TPU v7x, 32 devices: a whole 2x2x4 slice. The times are simulated.
32 devices in a mesh: dp: 8 (over z, x), blk: 4 (over y, core).
Axes of the slice: x: 2, y: 2, z: 4, core: 2. Of those that a mesh axis runs over, the one named last changes fastest.
Arguments:
- tokens: bfloat16 [8, 1024, 1024], P('dp', 'blk'), may hold values from -6 to 6
- cotangent: bfloat16 [8, 1024, 1024], P('dp', 'blk'), may hold values from -6 to 6
- stop_scale: int32 [8, 11], P('dp'), may hold values from 0 to 9, as said below
- labels: int32 [8, 12], P('dp'), may hold values from 0 to 1000
- class_table: bfloat16 [1001, 1024], replicated, may hold values from -6 to 6
- head_scale: float32 [2, 16], replicated, may hold values from 2.2 to 3
- w_qkv: bfloat16 [2, 1024, 3072], P(None, ('dp', 'blk')), may hold values from -0.1875 to 0.1875
- w_proj: bfloat16 [2, 1024, 1024], P(None, ('dp', 'blk')), may hold values from -0.75 to 0.75
- w_up: bfloat16 [2, 1024, 4096], P(None, ('dp', 'blk')), may hold values from -0.1875 to 0.1875
- w_down: bfloat16 [2, 4096, 1024], P(None, ('dp', 'blk')), may hold values from -0.09375 to 0.09375
- w_ada: bfloat16 [2, 1024, 6144], P(None, ('dp', 'blk')), may hold values from -0.1875 to 0.1875
Outputs:
- output: bfloat16 [8, 1024, 1024], P('dp', 'blk')
- tokens_grad: bfloat16 [8, 1024, 1024], P('dp', 'blk')
- class_table_grad: float32 [1001, 1024], replicated
- head_scale_grad: float32 [2, 16], replicated
- w_qkv_grad: float32 [2, 1024, 3072], P(None, ('dp', 'blk'))
- w_proj_grad: float32 [2, 1024, 1024], P(None, ('dp', 'blk'))
- w_up_grad: float32 [2, 1024, 4096], P(None, ('dp', 'blk'))
- w_down_grad: float32 [2, 4096, 1024], P(None, ('dp', 'blk'))
- w_ada_grad: float32 [2, 1024, 6144], P(None, ('dp', 'blk'))
Inputs may be any that keep to these rules, and one draw needn't show every extreme that they name: `stop_scale`: entries are 0 or 6 to 9; in every stream the nonzero entries come first, and their items hold at most 1024 tokens together.
All inputs are finite; a program needn't handle non-finite values.
Results may differ from a plain program's by a relative error of at most 0.035.
Values may be sent and summed in bfloat16 or wider, within the bound.
A program may use at most 512 MiB of HBM per device.

v0:
```python
from functools import partial

import jax
import jax.numpy as jnp
from jax import lax
from jax.sharding import PartitionSpec as P

patch_areas = (1, 4, 9, 16, 25, 36, 64, 100, 169)
scale_starts = (1, 5, 14, 30, 55, 91, 155, 255)


def token_meta(stops, length):
    areas = jnp.array(patch_areas, dtype=jnp.int32)
    levels = jnp.arange(9, dtype=jnp.int32)
    counts = jnp.sum(jnp.where(levels[None, :] < stops[:, None], areas[None, :], 0), axis=1)
    ends = jnp.cumsum(counts)
    places = jnp.arange(length, dtype=jnp.int32)
    passed = places[:, None] >= ends[None, :]
    item = jnp.sum(passed.astype(jnp.int32), axis=1)
    begin = jnp.sum(jnp.where(passed, counts[None, :], 0), axis=1)
    inner = places - begin
    bounds = jnp.array(scale_starts, dtype=jnp.int32)
    level = jnp.sum((inner[:, None] >= bounds[None, :]).astype(jnp.int32), axis=1)
    level = jnp.where(item == stops.shape[0], 0, level)
    return (item, level)


def modulate(values, scale, shift):
    centre = jnp.mean(values, axis=-1, keepdims=True)
    centred = values - centre
    spread = jnp.mean(centred * centred, axis=-1, keepdims=True)
    return centred * lax.rsqrt(spread + 1e-06) * (1.0 + scale) + shift


def qk_norm(query, keys, scale):
    query = (
        query
        * lax.rsqrt(jnp.sum(query * query, axis=-1, keepdims=True) + 1e-06)
        * jnp.exp(scale)[None, :, None]
    )
    keys = keys * lax.rsqrt(jnp.sum(keys * keys, axis=-1, keepdims=True) + 1e-06)
    return (query, keys)


def contract_rows(left, right, precision=None):
    return lax.dot_general(
        left,
        right,
        (((0,), (0,)), ((), ())),
        precision=precision,
        preferred_element_type=jnp.float32,
    )


def per_device(
    tokens,
    cotangent,
    stop_scale,
    labels,
    class_table,
    head_scale,
    w_qkv,
    w_proj,
    w_up,
    w_down,
    w_ada,
):
    rows = tokens.shape[1]
    width = tokens.shape[2]
    layers, heads = head_scale.shape
    size = width // heads
    group_count = heads // 4
    length = rows * lax.axis_size("blk")
    offset = lax.axis_index("blk") * rows
    owner = lax.axis_index("blk") == 0
    item_all, level_all = token_meta(stop_scale[0], length)
    item_own = lax.dynamic_slice_in_dim(item_all, offset, rows)
    level_own = lax.dynamic_slice_in_dim(level_all, offset, rows)
    slots = labels.shape[1]
    item_onehot = (item_own[:, None] == jnp.arange(slots, dtype=jnp.int32)[None, :]).astype(
        jnp.float32
    )
    chosen = (
        labels[0][:, None] == jnp.arange(class_table.shape[0], dtype=jnp.int32)[None, :]
    ).astype(jnp.float32)
    cond = jnp.dot(chosen.astype(jnp.bfloat16), class_table, preferred_element_type=jnp.float32)
    cond_act, silu_pull = jax.vjp(jax.nn.silu, cond)
    cond_low = cond_act.astype(jnp.bfloat16)
    full_mask = (item_own[:, None] == item_all[None, :]) & (
        level_all[None, :] <= level_own[:, None]
    )

    def to_groups(values, count):
        return values.reshape(count, group_count, 4, size).transpose(1, 0, 2, 3)

    def from_groups(values, count):
        return values.transpose(1, 0, 2, 3).reshape(count, width)

    def fetch(layer):
        return (
            lax.all_gather(w_qkv[layer], ("dp", "blk"), axis=0, tiled=True),
            lax.all_gather(w_proj[layer], ("dp", "blk"), axis=0, tiled=True),
            lax.all_gather(w_up[layer], ("dp", "blk"), axis=0, tiled=True),
            lax.all_gather(w_down[layer], ("dp", "blk"), axis=0, tiled=True),
            lax.all_gather(w_ada[layer], ("dp", "blk"), axis=0, tiled=True),
        )

    def modulations(w_mod):
        modulation = jnp.dot(cond_low, w_mod, preferred_element_type=jnp.float32)
        per_token = jnp.dot(item_onehot, modulation, precision=lax.Precision.HIGHEST)
        return jnp.split(per_token, 6, axis=1)

    def attend(query, keys, values, bound):
        query_groups = to_groups(query.reshape(rows, width), rows)
        start_state = (
            jnp.zeros((group_count, 4, rows), jnp.float32),
            jnp.zeros((group_count, rows, 4, size), jnp.float32),
        )
        key_piece = lax.all_gather(keys, "blk", axis=0, tiled=True)
        value_piece = lax.all_gather(values, "blk", axis=0, tiled=True)
        count = key_piece.shape[0]
        visible = (item_own[:, None] == item_all[None, :]) & (
            level_all[None, :] <= level_own[:, None]
        )

        def fold_single(parts):
            query_part, key_part, value_part, limit, total, summed = parts
            scores = jnp.einsum(
                "qhe,khe->hqk", query_part, key_part, preferred_element_type=jnp.float32
            )
            weights = jnp.where(visible[None], jnp.exp(scores - limit[:, None, None]), 0.0)
            added = jnp.einsum(
                "hqk,khe->qhe",
                weights.astype(jnp.bfloat16),
                value_part,
                preferred_element_type=jnp.float32,
            )
            return (total + jnp.sum(weights, axis=-1), summed + added)

        total, summed = lax.map(
            fold_single,
            (query_groups, to_groups(key_piece, count), to_groups(value_piece, count), bound)
            + tuple(start_state),
        )
        mixed = from_groups(summed / total.transpose(0, 2, 1)[..., None], rows)
        return (mixed, total)

    state = tokens[0].astype(jnp.float32)
    saved = []
    for layer in range(layers):
        w_query, w_out, w_first, w_second, w_mod = fetch(layer)
        bound = jnp.exp(head_scale[layer]).reshape(group_count, 4)
        gamma1, gamma2, scale1, scale2, shift1, shift2 = modulations(w_mod)
        normed = modulate(state, scale1, shift1).astype(jnp.bfloat16)
        packed = jnp.dot(normed, w_query, preferred_element_type=jnp.float32)
        query, keys, values = jnp.split(packed, 3, axis=1)
        query, keys = qk_norm(
            query.reshape(rows, heads, size), keys.reshape(rows, heads, size), head_scale[layer]
        )
        mixed, total = attend(
            query.astype(jnp.bfloat16),
            keys.astype(jnp.bfloat16).reshape(rows, width),
            values.astype(jnp.bfloat16),
            bound,
        )
        mixed_low = mixed.astype(jnp.bfloat16)
        state_mid = state + gamma1 * jnp.dot(mixed_low, w_out, preferred_element_type=jnp.float32)
        normed = modulate(state_mid, scale2, shift2).astype(jnp.bfloat16)
        hidden = jax.nn.gelu(
            jnp.dot(normed, w_first, preferred_element_type=jnp.float32), approximate=True
        )
        result = jnp.dot(hidden.astype(jnp.bfloat16), w_second, preferred_element_type=jnp.float32)
        saved.append((state, state_mid, mixed, total))
        state = state_mid + gamma2 * result
    output = state.astype(jnp.bfloat16)[None]
    grad = cotangent[0].astype(jnp.float32)
    cond_grad = jnp.zeros_like(cond)
    scale_grads = [None] * layers
    wide_grads = [None] * layers
    down_grads = [None] * layers
    shards = lax.axis_size(("dp", "blk"))
    for layer in reversed(range(layers)):
        w_query, w_out, w_first, w_second, w_mod = fetch(layer)
        state, state_mid, mixed, total = saved[layer]
        mixed_low = mixed.astype(jnp.bfloat16)
        bound = jnp.exp(head_scale[layer]).reshape(group_count, 4)
        gamma1, gamma2, scale1, scale2, shift1, shift2 = modulations(w_mod)
        normed_two, pull_second = jax.vjp(modulate, state_mid, scale2, shift2)
        normed_two = normed_two.astype(jnp.bfloat16)
        upward = jnp.dot(normed_two, w_first, preferred_element_type=jnp.float32)
        hidden, pull_gelu = jax.vjp(partial(jax.nn.gelu, approximate=True), upward)
        hidden_low = hidden.astype(jnp.bfloat16)
        result = jnp.dot(hidden_low, w_second, preferred_element_type=jnp.float32)
        gamma2_grad = grad * result
        result_grad = (gamma2 * grad).astype(jnp.bfloat16)
        hidden_grad = jnp.dot(result_grad, w_second.T, preferred_element_type=jnp.float32)
        upward_grad = pull_gelu(hidden_grad)[0].astype(jnp.bfloat16)
        normed_grad = jnp.dot(upward_grad, w_first.T, preferred_element_type=jnp.float32)
        mid_part, scale2_grad, shift2_grad = pull_second(normed_grad)
        mid_grad = grad + mid_part
        normed_one, pull_first = jax.vjp(modulate, state, scale1, shift1)
        normed_one = normed_one.astype(jnp.bfloat16)
        packed = jnp.dot(normed_one, w_query, preferred_element_type=jnp.float32)
        query, keys, values = jnp.split(packed, 3, axis=1)
        (query, keys), pull_norm = jax.vjp(
            qk_norm,
            query.reshape(rows, heads, size),
            keys.reshape(rows, heads, size),
            head_scale[layer],
        )
        branch = jnp.dot(mixed_low, w_out, preferred_element_type=jnp.float32)
        gamma1_grad = mid_grad * branch
        branch_grad = (gamma1 * mid_grad).astype(jnp.bfloat16)
        mixed_grad = jnp.dot(branch_grad, w_out.T, preferred_element_type=jnp.float32).astype(
            jnp.bfloat16
        )
        attend_query = query.astype(jnp.bfloat16)
        attend_keys = keys.astype(jnp.bfloat16).reshape(rows, width)
        attend_values = values.astype(jnp.bfloat16)
        key_all = lax.all_gather(attend_keys, "blk", axis=0, tiled=True)
        value_all = lax.all_gather(attend_values, "blk", axis=0, tiled=True)
        row_term = jnp.sum(
            (mixed_grad.astype(jnp.float32) * mixed).reshape(rows, heads, size), axis=-1
        )
        row_term = row_term.reshape(rows, group_count, 4).transpose(1, 2, 0)

        def attend_single(parts):
            query_part, key_part, value_part, out_grad, total_part, row_part, limit = parts
            scores = jnp.einsum(
                "qhe,khe->hqk", query_part, key_part, preferred_element_type=jnp.float32
            )
            weights = jnp.where(full_mask[None], jnp.exp(scores - limit[:, None, None]), 0.0)
            probs = weights / total_part[..., None]
            prob_grad = jnp.einsum(
                "qhe,khe->hqk", out_grad, value_part, preferred_element_type=jnp.float32
            )
            score_grad = (probs * (prob_grad - row_part[..., None])).astype(jnp.bfloat16)
            query_grad = jnp.einsum(
                "hqk,khe->qhe", score_grad, key_part, preferred_element_type=jnp.float32
            )
            key_grad = jnp.einsum(
                "hqk,qhe->khe", score_grad, query_part, preferred_element_type=jnp.float32
            )
            scaled_grad = out_grad.astype(jnp.float32) / total_part.transpose(1, 0)[:, :, None]
            value_grad = jnp.einsum(
                "hqk,qhe->khe",
                weights.astype(jnp.bfloat16).astype(jnp.float32),
                scaled_grad,
                preferred_element_type=jnp.float32,
            )
            return (query_grad, key_grad, value_grad)

        query_grad, key_grad, value_grad = lax.map(
            attend_single,
            (
                to_groups(attend_query.reshape(rows, width), rows),
                to_groups(key_all, length),
                to_groups(value_all, length),
                to_groups(mixed_grad, rows),
                total,
                row_term,
                bound,
            ),
        )
        query_grad, key_part, value_part = (
            from_groups(query_grad, rows).reshape(rows, heads, size),
            from_groups(key_grad, length),
            from_groups(value_grad, length),
        )
        key_grad, value_grad = (
            lax.psum_scatter(
                key_part.astype(jnp.bfloat16), "blk", scatter_dimension=0, tiled=True
            ).astype(jnp.float32),
            lax.psum_scatter(
                value_part.astype(jnp.bfloat16), "blk", scatter_dimension=0, tiled=True
            ).astype(jnp.float32),
        )
        raw_query, raw_keys, scale_grad = pull_norm(
            (query_grad, key_grad.reshape(rows, heads, size))
        )
        packed_grad = jnp.concatenate(
            [raw_query.reshape(rows, width), raw_keys.reshape(rows, width), value_grad], axis=1
        ).astype(jnp.bfloat16)
        normed_grad = jnp.dot(packed_grad, w_query.T, preferred_element_type=jnp.float32)
        input_part, scale1_grad, shift1_grad = pull_first(normed_grad)
        grad = mid_grad + input_part
        scale_grads[layer] = scale_grad
        token_mod_grad = jnp.concatenate(
            [gamma1_grad, gamma2_grad, scale1_grad, scale2_grad, shift1_grad, shift2_grad], axis=1
        )
        item_grad = contract_rows(item_onehot, token_mod_grad, lax.Precision.HIGHEST)
        item_grad = lax.psum(item_grad.astype(jnp.bfloat16), "blk")
        cond_grad = cond_grad + jnp.dot(item_grad, w_mod.T, preferred_element_type=jnp.float32)
        own_items = jnp.where(owner, item_grad, jnp.zeros_like(item_grad))
        wide_grads[layer] = lax.psum_scatter(
            jnp.concatenate(
                [
                    contract_rows(normed_one, packed_grad),
                    contract_rows(mixed_low, branch_grad),
                    contract_rows(normed_two, upward_grad),
                    contract_rows(cond_low, own_items),
                ],
                axis=1,
            ),
            ("dp", "blk"),
            scatter_dimension=0,
            tiled=True,
        )
        down_grads[layer] = lax.psum_scatter(
            contract_rows(
                lax.slice_in_dim(
                    hidden_low,
                    0,
                    w_second.shape[0] // shards * lax.axis_size(("dp", "blk")),
                    axis=1,
                ),
                result_grad,
            ),
            ("dp", "blk"),
            scatter_dimension=0,
            tiled=True,
        )
    cond_pre = silu_pull(cond_grad)[0]
    table_term = contract_rows(chosen, cond_pre, lax.Precision.HIGHEST)
    table_term = jnp.where(owner, table_term, jnp.zeros_like(table_term))
    table_grad, head_grad = lax.psum((table_term, jnp.stack(scale_grads)), ("dp", "blk"))
    ff_width = w_up.shape[2]
    cuts = [3 * width, 4 * width, 4 * width + ff_width]
    pieces = [jnp.split(one, cuts, axis=1) for one in wide_grads]
    qkv_grad = jnp.stack([one[0] for one in pieces])
    proj_grad = jnp.stack([one[1] for one in pieces])
    up_grad = jnp.stack([one[2] for one in pieces])
    ada_grad = jnp.stack([one[3] for one in pieces])
    down_grad = jnp.stack(down_grads)
    return (
        output,
        grad.astype(jnp.bfloat16)[None],
        table_grad,
        head_grad,
        qkv_grad,
        proj_grad,
        up_grad,
        down_grad,
        ada_grad,
    )


def solution(mesh):
    in_specs = (
        P("dp", "blk", None),
        P("dp", "blk", None),
        P("dp", None),
        P("dp", None),
        P(),
        P(),
        P(None, ("dp", "blk"), None),
        P(None, ("dp", "blk"), None),
        P(None, ("dp", "blk"), None),
        P(None, ("dp", "blk"), None),
        P(None, ("dp", "blk"), None),
    )
    out_specs = (
        P("dp", "blk", None),
        P("dp", "blk", None),
        P(),
        P(),
        P(None, ("dp", "blk"), None),
        P(None, ("dp", "blk"), None),
        P(None, ("dp", "blk"), None),
        P(None, ("dp", "blk"), None),
        P(None, ("dp", "blk"), None),
    )
    return jax.shard_map(
        per_device, mesh=mesh, in_specs=in_specs, out_specs=out_specs, check_vma=False
    )
```

profile of v0, /device:TPU:7, one launch (start us, length us, event | category | flops | bytes accessed | tf_op | source)
XLA Modules:
  0.0 3017.2 jit_solution(18310381702971236542)
XLA Ops:
  16.5 91.7 %all-gather.33.cloned.1.call-done = bf16[1,1024,6144]{2,1,0:T(8,128)(2,1)} async-done(((bf16[1,32,6144]{2,1,0:T(8,128)(2,1)}), bf16[1,1024,6144]{2,1,0:T(8,128)(2,1)}) %all-gather.33.cloned.1.call-update) | async-done | bytes 12582928 | tf_op jit(solution)/shard_map/all_gather | solution.py:105
  108.2 6.3 fusion.140
  120.3 59.3 %all-gather.35.cloned.1.call-done = bf16[1,1024,3072]{2,1,0:T(8,128)(2,1)} async-done(((bf16[1,32,3072]{2,1,0:T(8,128)(2,1)}), bf16[1,1024,3072]{2,1,0:T(8,128)(2,1)}) %all-gather.35.cloned.1.call-update) | async-done | bytes 6291472 | tf_op jit(solution)/shard_map/all_gather | solution.py:101
  179.6 4.6 fusion.164
  199.4 78.2 %all-gather.43.cloned.1.call-done = bf16[1,1024,6144]{2,1,0:T(8,128)(2,1)} async-done(((bf16[1,32,6144]{2,1,0:T(8,128)(2,1)}), bf16[1,1024,6144]{2,1,0:T(8,128)(2,1)}) %all-gather.43.cloned.1.call-update) | async-done | bytes 12582928 | tf_op jit(solution)/shard_map/all_gather | solution.py:105
  277.6 6.3 fusion.136
  284.0 4.5 fusion.251
  288.5 11.9 all-gather.25.cloned.1.call-done
  304.4 20.7 all-gather.27.cloned.1.call-done
  325.0 4.0 copy.85
  329.2 19.2 while.56
  349.3 35.5 %all-gather.37.cloned.1.call-done = bf16[1,1024,1024]{2,1,0:T(8,128)(2,1)} async-done(((bf16[1,32,1024]{2,1,0:T(8,128)(2,1)}), bf16[1,1024,1024]{2,1,0:T(8,128)(2,1)}) %all-gather.37.cloned.1.call-update) | async-done | bytes 2097168 | tf_op jit(solution)/shard_map/all_gather | solution.py:102
  390.6 74.1 %all-gather.39.cloned.1.call-done = bf16[1,1024,4096]{2,1,0:T(8,128)(2,1)} async-done(((bf16[1,32,4096]{2,1,0:T(8,128)(2,1)}), bf16[1,1024,4096]{2,1,0:T(8,128)(2,1)}) %all-gather.39.cloned.1.call-update) | async-done | bytes 8388624 | tf_op jit(solution)/shard_map/all_gather | solution.py:103
  464.7 7.8 fusion.156
  472.5 71.8 %all-gather.41.cloned.1.call-done = bf16[1,4096,1024]{2,1,0:T(8,128)(2,1)} async-done(((bf16[1,128,1024]{2,1,0:T(8,128)(2,1)}), bf16[1,4096,1024]{2,1,0:T(8,128)(2,1)}) %all-gather.41.cloned.1.call-update) | async-done | bytes 8388624 | tf_op jit(solution)/shard_map/all_gather | solution.py:104
  544.3 8.7 fusion.294
  555.8 59.6 %all-gather.45.cloned.1.call-done = bf16[1,1024,3072]{2,1,0:T(8,128)(2,1)} async-done(((bf16[1,32,3072]{2,1,0:T(8,128)(2,1)}), bf16[1,1024,3072]{2,1,0:T(8,128)(2,1)}) %all-gather.45.cloned.1.call-update) | async-done | bytes 6291472 | tf_op jit(solution)/shard_map/all_gather | solution.py:101
  615.4 4.6 fusion.160
  630.5 16.3 all-gather.29.cloned.1.call-done
  646.8 4.0 copy.90
  650.8 20.8 all-gather.31.cloned.1.call-done
  675.6 19.0 while.57
  698.4 32.4 %all-gather.47.cloned.1.call-done = bf16[1,1024,1024]{2,1,0:T(8,128)(2,1)} async-done(((bf16[1,32,1024]{2,1,0:T(8,128)(2,1)}), bf16[1,1024,1024]{2,1,0:T(8,128)(2,1)}) %all-gather.47.cloned.1.call-update) | async-done | bytes 2097168 | tf_op jit(solution)/shard_map/all_gather | solution.py:102
  730.8 4.2 fusion.293
  738.0 72.1 %all-gather.49.cloned.1.call-done = bf16[1,1024,4096]{2,1,0:T(8,128)(2,1)} async-done(((bf16[1,32,4096]{2,1,0:T(8,128)(2,1)}), bf16[1,1024,4096]{2,1,0:T(8,128)(2,1)}) %all-gather.49.cloned.1.call-update) | async-done | bytes 8388624 | tf_op jit(solution)/shard_map/all_gather | solution.py:103
  810.1 7.9 fusion.148
  818.0 71.6 %all-gather.51.cloned.1.call-done = bf16[1,4096,1024]{2,1,0:T(8,128)(2,1)} async-done(((bf16[1,128,1024]{2,1,0:T(8,128)(2,1)}), bf16[1,4096,1024]{2,1,0:T(8,128)(2,1)}) %all-gather.51.cloned.1.call-update) | async-done | bytes 8388624 | tf_op jit(solution)/shard_map/all_gather | solution.py:104
  889.6 9.4 fusion.179
  899.1 4.6 multiply_reduce_fusion.2
  903.7 6.7 fusion.144
  924.1 44.0 %while.58 = (s32[]{:T(128)}, f32[4,256,4,64]{1,3,2,0:T(8,128)S(1)}, bf16[4,1024,4,64]{1,3,2,0:T(8,128)(2,1)}, bf16[4,1024,4,64]{1,3,2,0:T(8,128)(2,1)}, bf16[4,1...) while((s32[]{:T(128)}, f32[4,256,4,64]{1,3,2,0:T(8,128)S(1)}, ...), condition=%wide.region_27.28_spmd.clone, body=%wide.region_26.27_spmd.clone.sunk | while | flops 681443328 | bytes 59818320 | solution.py:253
  968.0 4.3 copy.98
  991.1 11.1 reduce-scatter.9.cloned.1.call-done
  1002.1 4.2 fusion.214
  1017.1 19.1 reduce-scatter.11.cloned.1.call-done
  1036.2 5.7 multiply_reduce_fusion.1
  1045.4 8.5 fusion.172
  1054.0 7.2 multiply_reduce_fusion
  1072.8 45.4 %while.59 = (s32[]{:T(128)}, f32[4,256,4,64]{1,3,2,0:T(8,128)S(1)}, bf16[4,1024,4,64]{1,3,2,0:T(8,128)(2,1)}, bf16[4,1024,4,64]{1,3,2,0:T(8,128)(2,1)}, bf16[4,1...) while((s32[]{:T(128)}, f32[4,256,4,64]{1,3,2,0:T(8,128)S(1)}, ...), condition=%wide.region_38.39_spmd.clone, body=%wide.region_37.38_spmd.clone.sunk | while | flops 681443328 | bytes 59818320 | solution.py:253
  1118.2 4.3 copy.109
  1122.6 4.0 copy.113
  1150.7 5.7 convolution_convert_fusion.1
  1156.4 4.2 fusion.216
  1171.3 16.8 reduce-scatter.15.cloned.1.call-done
  1188.1 5.5 fusion.213
  1200.7 5.6 convolution_convert_fusion
  1206.8 11.2 fusion.285
  1219.0 10.8 fusion.288
  1233.9 8.2 fusion.303
  1242.2 6.3 fusion.234
  1248.5 10.6 fusion.245
  1259.1 37.7 %pad_maximum_fusion.1 = f32[1024,14336]{1,0:T(8,128)} fusion(f32[1024,6144]{1,0:T(8,128)} %fusion.245, f32[1024,4096]{1,0:T(8,128)} %fusion.303, f32[1024,1024]{1,0:T(8,128)S(1)} %copy-done.9, f32[1024,3072]{1,0:T(8,128)} %fusion.234), kind=kLoop, calls=%fused_computation.137 | loop fusion | flops 44040192 | bytes 117440512 | tf_op jit(solution)/shard_map/concatenate | solution.py:296
  1299.8 8.2 fusion.302
  1308.0 6.5 fusion.233
  1314.5 10.4 fusion.247
  1324.9 37.7 %pad_maximum_fusion = f32[1024,14336]{1,0:T(8,128)} fusion(f32[1024,6144]{1,0:T(8,128)} %fusion.247, f32[1024,4096]{1,0:T(8,128)} %fusion.302, f32[1024,1024]{1,0:T(8,128)S(1)} %fusion.242, f32[1024,3072]{1,0:T(8,128)} %fusion.233), kind=kLoop, calls=%fused_computation.136 | loop fusion | flops 44040192 | bytes 117440512 | tf_op jit(solution)/shard_map/concatenate | solution.py:296
  1363.4 47.1 %psum.31 = f32[2,16]{1,0:T(2,128)} all-reduce(f32[2,16]{1,0:T(2,128)S(1)} %pad_maximum_fusion.13), channel_id=1, replica_groups=mesh['dp'=8,'blk'=4] {'dp','blk'}, use_global_device_ids=true, to_apply=%region_50.51 | all-reduce | flops 32 | bytes 256 | tf_op jit(solution)/shard_map/psum | solution.py:326
  1411.5 8.0 fusion.134
  1419.5 8.1 fusion.206
  1431.5 182.0 %reduce-scatter.21.cloned.1.call-done = f32[128,1024]{1,0:T(8,128)} async-done(((f32[4096,1024]{1,0:T(8,128)}), f32[128,1024]{1,0:T(8,128)}) %reduce-scatter.21.cloned.1.call-update) | async-done | bytes 524304 | tf_op jit(solution)/shard_map/reduce_scatter | solution.py:309
  1615.8 612.9 %reduce-scatter.19.cloned.1.call-done = f32[32,14336]{1,0:T(8,128)} async-done(((f32[1024,14336]{1,0:T(8,128)}), f32[32,14336]{1,0:T(8,128)}) %reduce-scatter.19.cloned.1.call-update) | async-done | bytes 1835024 | tf_op jit(solution)/shard_map/reduce_scatter | solution.py:295
  2229.7 620.7 %reduce-scatter.17.cloned.1.call-done = f32[32,14336]{1,0:T(8,128)} async-done(((f32[1024,14336]{1,0:T(8,128)}), f32[32,14336]{1,0:T(8,128)}) %reduce-scatter.17.cloned.1.call-update) | async-done | bytes 1835024 | tf_op jit(solution)/shard_map/reduce_scatter | solution.py:295
  2859.7 145.6 %all-reduce.4.cloned.1.call-done = f32[1001,1024]{1,0:T(8,128)} async-done(((f32[1001,1024]{1,0:T(8,128)}), f32[1001,1024]{1,0:T(8,128)}) %all-reduce.4.cloned.1.call-update) | async-done | bytes 4100112 | tf_op jit(solution)/shard_map/psum | solution.py:326
  3005.4 4.7 copy.183
  (659 shorter events, 317.0 us)
Async XLA Ops:
  7.2 101.0 %all-gather.33.cloned.1.call-start = ((), (), s32[]{:S(2)}) async-start(), calls=%async_computation.21 | async-start | bytes 12976128 | tf_op jit(solution)/shard_map/all_gather | solution.py:105
  9.5 170.1 %all-gather.35.cloned.1.call-start = ((), (), s32[]{:S(2)}) async-start(), calls=%async_computation.22 | async-start | bytes 6488064 | tf_op jit(solution)/shard_map/all_gather | solution.py:101
  11.4 266.2 %all-gather.43.cloned.1.call-start = ((), (), s32[]{:S(2)}) async-start(), calls=%async_computation.26 | async-start | bytes 12976128 | tf_op jit(solution)/shard_map/all_gather | solution.py:105
  12.1 288.3 %all-gather.25.cloned.1.call-start = ((), (), s32[]{:S(2)}) async-start(), calls=%async_computation.8 | async-start | bytes 2621440 | tf_op jit(solution)/shard_map/all_gather | solution.py:119
  14.6 102.6 %copy-start.115 = (f32[256]{0:T(256)}, f32[256]{0:T(256)S(1)}, u32[]{:S(2)}) copy-start(f32[256]{0:T(256)S(1)} %broadcast_multiply_fusion.3) | copy-start | bytes 3076
  15.5 101.8 %copy-start.121 = (f32[256]{0:T(256)}, f32[256]{0:T(256)S(1)}, u32[]{:S(2)}) copy-start(f32[256]{0:T(256)S(1)} %fusion.268) | copy-start | bytes 3076
  16.5 261.1 %copy-start.85 = (bf16[12,1024]{1,0:T(8,128)(2,1)}, bf16[12,1024]{1,0:T(8,128)(2,1)S(1)}, u32[]{:S(2)}) copy-start(bf16[12,1024]{1,0:T(8,128)(2,1)S(1)} %get-tuple-element.526) | copy-start | bytes 73732
  120.3 63.9 %copy-start.76 = (bf16[256,1024]{1,0:T(8,128)(2,1)}, bf16[256,1024]{1,0:T(8,128)(2,1)S(1)}, u32[]{:S(2)}) copy-start(bf16[256,1024]{1,0:T(8,128)(2,1)S(1)} %fusion.210) | copy-start | bytes 1572868
  187.3 9.8 copy-start.125
  187.3 10.4 copy-start.132
  190.3 134.8 %all-gather.27.cloned.1.call-start = ((), (), s32[]{:S(2)}) async-start(), calls=%async_computation.9 | async-start | bytes 2621440 | tf_op jit(solution)/shard_map/all_gather | solution.py:120
  192.5 192.3 %all-gather.37.cloned.1.call-start = ((), (), s32[]{:S(2)}) async-start(), calls=%async_computation.23 | async-start | bytes 2162688 | tf_op jit(solution)/shard_map/all_gather | solution.py:102
  193.3 271.4 %all-gather.39.cloned.1.call-start = ((), (), s32[]{:S(2)}) async-start(), calls=%async_computation.24 | async-start | bytes 8650752 | tf_op jit(solution)/shard_map/all_gather | solution.py:103
  194.2 350.1 %all-gather.41.cloned.1.call-start = ((), (), s32[]{:S(2)}) async-start(), calls=%async_computation.25 | async-start | bytes 8650752 | tf_op jit(solution)/shard_map/all_gather | solution.py:104
  196.1 419.3 %all-gather.45.cloned.1.call-start = ((), (), s32[]{:S(2)}) async-start(), calls=%async_computation.27 | async-start | bytes 6488064 | tf_op jit(solution)/shard_map/all_gather | solution.py:101
  196.9 449.9 %all-gather.29.cloned.1.call-start = ((), (), s32[]{:S(2)}) async-start(), calls=%async_computation.10 | async-start | bytes 2621440 | tf_op jit(solution)/shard_map/all_gather | solution.py:119
  198.3 85.7 %copy-start.3 = (f32[256,1024]{0,1:T(8,128)}, f32[256,1024]{0,1:T(8,128)S(1)}, u32[]{:S(2)}) copy-start(f32[256,1024]{0,1:T(8,128)S(1)} %copy.80) | copy-start | bytes 3145732
  199.2 84.8 %copy-start.104 = (f32[256,16]{0,1:T(8,128)}, f32[256,16]{0,1:T(8,128)S(1)}, u32[]{:S(2)}) copy-start(f32[256,16]{0,1:T(8,128)S(1)} %add_rsqrt_fusion.3) | copy-start | bytes 49156
  199.2 84.8 %copy-start.96 = (f32[256,4,4]{0,2,1:T(4,128)}, f32[256,4,4]{0,2,1:T(4,128)S(1)}, u32[]{:S(2)}) copy-start(f32[256,4,4]{0,2,1:T(4,128)S(1)} %rsqrt.98) | copy-start | bytes 49156
  329.2 55.7 %copy-start.21 = (bf16[1,256,1024]{2,1,0:T(8,128)(2,1)S(1)}, bf16[1,256,1024]{2,1,0:T(8,128)(2,1)}, u32[]{:S(2)}) copy-start(bf16[1,256,1024]{2,1,0:T(8,128)(2,1)} %param.21) | copy-start | bytes 1572868
  348.4 40.0 %copy-start.95 = (f32[4,4,256]{2,1,0:T(4,128)}, f32[4,4,256]{2,1,0:T(4,128)S(1)}, u32[]{:S(2)}) copy-start(f32[4,4,256]{2,1,0:T(4,128)S(1)} %get-tuple-element.1006) | copy-start | bytes 49156
  348.4 40.0 %copy-start.123 = (f32[4,4]{1,0:T(4,128)}, f32[4,4]{1,0:T(4,128)S(1)}, u32[]{:S(2)}) copy-start(f32[4,4]{1,0:T(4,128)S(1)} %get-tuple-element.1171) | copy-start | bytes 196
  349.3 41.3 %copy-start.14 = (f32[4,256,4,64]{1,3,2,0:T(8,128)}, f32[4,256,4,64]{1,3,2,0:T(8,128)S(1)}, u32[]{:S(2)}) copy-start(f32[4,256,4,64]{1,3,2,0:T(8,128)S(1)} %broadcast_divide_fusion.1) | copy-start | bytes 3145732
  388.4 155.9 %copy-start.5 = (f32[256,1024]{1,0:T(8,128)}, f32[256,1024]{1,0:T(8,128)S(1)}, u32[]{:S(2)}) copy-start(f32[256,1024]{1,0:T(8,128)S(1)} %get-tuple-element.488) | copy-start | bytes 3145732
  388.4 84.1 %copy-start.107 = (f32[256]{0:T(256)}, f32[256]{0:T(256)S(1)}, u32[]{:S(2)}) copy-start(f32[256]{0:T(256)S(1)} %broadcast_multiply_fusion.2) | copy-start | bytes 3076
  388.7 83.8 %copy-start.119 = (f32[256]{0:T(256)}, f32[256]{0:T(256)S(1)}, u32[]{:S(2)}) copy-start(f32[256]{0:T(256)S(1)} %multiply_reduce_fusion.6) | copy-start | bytes 3076
  388.7 83.8 %copy-start.111 = (f32[256]{0:T(256)}, f32[256]{0:T(256)S(1)}, u32[]{:S(2)}) copy-start(f32[256]{0:T(256)S(1)} %fusion.269) | copy-start | bytes 3076
  390.6 81.9 %copy-start.67 = (bf16[256,1024]{1,0:T(8,128)(2,1)}, bf16[256,1024]{1,0:T(8,128)(2,1)S(1)}, u32[]{:S(2)}) copy-start(bf16[256,1024]{1,0:T(8,128)(2,1)S(1)} %fusion.222) | copy-start | bytes 1572868
  555.8 64.2 %copy-start.70 = (bf16[256,1024]{1,0:T(8,128)(2,1)}, bf16[256,1024]{1,0:T(8,128)(2,1)S(1)}, u32[]{:S(2)}) copy-start(bf16[256,1024]{1,0:T(8,128)(2,1)S(1)} %fusion.221) | copy-start | bytes 1572868
  625.6 46.0 %all-gather.31.cloned.1.call-start = ((), (), s32[]{:S(2)}) async-start(), calls=%async_computation.11 | async-start | bytes 2621440 | tf_op jit(solution)/shard_map/all_gather | solution.py:120
  627.8 103.0 %all-gather.47.cloned.1.call-start = ((), (), s32[]{:S(2)}) async-start(), calls=%async_computation.28 | async-start | bytes 2162688 | tf_op jit(solution)/shard_map/all_gather | solution.py:102
  628.4 181.8 %all-gather.49.cloned.1.call-start = ((), (), s32[]{:S(2)}) async-start(), calls=%async_computation.29 | async-start | bytes 8650752 | tf_op jit(solution)/shard_map/all_gather | solution.py:103
  629.1 260.5 %all-gather.51.cloned.1.call-start = ((), (), s32[]{:S(2)}) async-start(), calls=%async_computation.30 | async-start | bytes 8650752 | tf_op jit(solution)/shard_map/all_gather | solution.py:104
  629.7 372.5 %reduce-scatter.9.cloned.1.call-start = ((), (), s32[]{:S(2)}) async-start(), calls=%async_computation.12 | async-start | bytes 2621440 | tf_op jit(solution)/shard_map/reduce_scatter | solution.py:271
  630.2 353.2 %copy-start.7 = (f32[256,1024]{0,1:T(8,128)}, f32[256,1024]{0,1:T(8,128)S(1)}, u32[]{:S(2)}) copy-start(f32[256,1024]{0,1:T(8,128)S(1)} %copy.86) | copy-start | bytes 3145732
  630.3 45.2 %copy-start.98 = (f32[256,4,4]{0,2,1:T(4,128)}, f32[256,4,4]{0,2,1:T(4,128)S(1)}, u32[]{:S(2)}) copy-start(f32[256,4,4]{0,2,1:T(4,128)S(1)} %rsqrt.103) | copy-start | bytes 49156
  694.7 40.4 %copy-start.50 = (bf16[4,256,4,64]{1,3,2,0:T(8,128)(2,1)}, bf16[4,256,4,64]{1,3,2,0:T(8,128)(2,1)S(1)}, u32[]{:S(2)}) copy-start(bf16[4,256,4,64]{1,3,2,0:T(8,128)(2,1)S(1)} %get-tuple-element.1108) | copy-start | bytes 1572868
  735.0 175.4 %copy-start.8 = (f32[256,1024]{1,0:T(8,128)}, f32[256,1024]{1,0:T(8,128)S(1)}, u32[]{:S(2)}) copy-start(f32[256,1024]{1,0:T(8,128)S(1)} %get-tuple-element.484) | copy-start | bytes 3145732
  735.0 175.4 %copy-start.109 = (f32[256]{0:T(256)}, f32[256]{0:T(256)S(1)}, u32[]{:S(2)}) copy-start(f32[256]{0:T(256)S(1)} %broadcast_multiply_fusion) | copy-start | bytes 3076
  735.3 175.2 %copy-start.113 = (f32[256]{0:T(256)}, f32[256]{0:T(256)S(1)}, u32[]{:S(2)}) copy-start(f32[256]{0:T(256)S(1)} %fusion.271) | copy-start | bytes 3076
  738.0 151.6 %copy-start.45 = (bf16[1,256,1024]{2,1,0:T(8,128)(2,1)S(1)}, bf16[1,256,1024]{2,1,0:T(8,128)(2,1)}, u32[]{:S(2)}) copy-start(bf16[1,256,1024]{2,1,0:T(8,128)(2,1)} %param.22) | copy-start | bytes 1572868
  889.6 9.4 copy-start.133
  899.1 11.4 slice-start
  968.0 19.2 copy-start.11
  972.4 63.8 %reduce-scatter.11.cloned.1.call-start = ((), (), s32[]{:S(2)}) async-start(), calls=%async_computation.13 | async-start | bytes 2621440 | tf_op jit(solution)/shard_map/reduce_scatter | solution.py:274
  976.4 180.0 %reduce-scatter.13.cloned.1.call-start = ((), (), s32[]{:S(2)}) async-start(), calls=%async_computation.14 | async-start | bytes 2621440 | tf_op jit(solution)/shard_map/reduce_scatter | solution.py:271
  983.6 18.6 copy-start.60
  1009.0 27.2 copy-start.13
  1045.4 16.3 copy-start.23
  1122.6 65.6 %reduce-scatter.15.cloned.1.call-start = ((), (), s32[]{:S(2)}) async-start(), calls=%async_computation.15 | async-start | bytes 2621440 | tf_op jit(solution)/shard_map/reduce_scatter | solution.py:274
  1126.7 121.9 %all-reduce.6.cloned.1.call-start = ((), (), s32[]{:S(2)}) async-start(), calls=%async_computation.31 | async-start | bytes 786432 | tf_op jit(solution)/shard_map/psum | solution.py:292
  1163.2 24.9 copy-start.22
  1163.2 24.9 copy-start.116
  1206.3 225.2 %reduce-scatter.23.cloned.1.call-start = ((), (), s32[]{:S(2)}) async-start(), calls=%async_computation.20 | async-start | bytes 17301504 | tf_op jit(solution)/shard_map/reduce_scatter | solution.py:309
  1218.0 395.5 %reduce-scatter.21.cloned.1.call-start = ((), (), s32[]{:S(2)}) async-start(), calls=%async_computation.19 | async-start | bytes 17301504 | tf_op jit(solution)/shard_map/reduce_scatter | solution.py:309
  1229.9 998.8 %reduce-scatter.19.cloned.1.call-start = ((), (), s32[]{:S(2)}) async-start(), calls=%async_computation.18 | async-start | bytes 60555264 | tf_op jit(solution)/shard_map/reduce_scatter | solution.py:295
  1248.5 10.6 copy-start.9
  1296.8 1553.6 %reduce-scatter.17.cloned.1.call-start = ((), (), s32[]{:S(2)}) async-start(), calls=%async_computation.17 | async-start | bytes 60555264 | tf_op jit(solution)/shard_map/reduce_scatter | solution.py:295
  1362.7 47.8 %copy-start.127 = (f32[256]{0:T(256)S(1)}, f32[256]{0:T(256)}, u32[]{:S(2)}) copy-start(f32[256]{0:T(256)} %get-tuple-element.473) | copy-start | bytes 3076
  1362.7 47.8 %copy-start.26 = (f32[256,1024]{1,0:T(8,128)S(1)}, f32[256,1024]{1,0:T(8,128)}, u32[]{:S(2)}) copy-start(f32[256,1024]{1,0:T(8,128)} %copy-done.25) | copy-start | bytes 3145732
  1362.7 47.8 %copy-start.61 = (f32[256,1024]{1,0:T(8,128)S(1)}, f32[256,1024]{1,0:T(8,128)}, u32[]{:S(2)}) copy-start(f32[256,1024]{1,0:T(8,128)} %get-tuple-element.474) | copy-start | bytes 3145732
  1362.7 48.8 %copy-start.88 = (bf16[12,6144]{1,0:T(8,128)(2,1)S(1)}, bf16[12,6144]{1,0:T(8,128)(2,1)}, u32[]{:S(2)}) copy-start(bf16[12,6144]{1,0:T(8,128)(2,1)} %get-tuple-element.469) | copy-start | bytes 442372
  1362.7 1642.6 %all-reduce.4.cloned.1.call-start = ((), (), s32[]{:S(2)}) async-start(), calls=%async_computation.16 | async-start | bytes 8257536 | tf_op jit(solution)/shard_map/psum | solution.py:326
  2858.5 151.6 %copy-start.1 = (bf16[1001,1024]{1,0:T(8,128)(2,1)S(1)}, bf16[1001,1024]{1,0:T(8,128)(2,1)}, u32[]{:S(2)}) copy-start(bf16[1001,1024]{1,0:T(8,128)(2,1)} %param.25) | copy-start | bytes 6150148
  (128 other events, 543.8 us)
Sparse Core Ops, SparseCore 0:
  11.5 96.6 all-gather.32
  111.7 67.8 all-gather.34
  183.0 94.5 all-gather.42
  279.6 20.7 all-gather.24
  302.4 22.5 all-gather.26
  328.3 56.4 all-gather.36
  388.3 76.3 all-gather.38
  468.1 76.1 all-gather.40
  547.2 68.1 all-gather.44
  625.7 21.0 all-gather.28
  649.0 22.5 all-gather.30
  674.3 56.4 all-gather.46
  733.7 76.3 all-gather.48
  813.4 76.1 all-gather.50
  972.5 29.5 reduce-scatter.8
  1004.7 31.4 reduce-scatter.10
  1122.7 31.4 reduce-scatter.12
  1156.7 31.3 reduce-scatter.14
  1206.4 32.2 all-reduce.5
  1240.9 186.1 reduce-scatter.22
  1429.6 183.8 reduce-scatter.20
  1615.9 612.7 reduce-scatter.18
  2231.1 619.2 reduce-scatter.16
  2857.3 148.0 all-reduce.3
where the time goes:
time: 3030 us; the launch traced here: 3020 us
  waiting for transfers between devices  2330 us (77%)
  matrix products  324 us (11%)
  other arithmetic  152 us (5%)
  local copies, waits for them, and re-layouts  147 us (5%)
  blocking collectives  47.1 us (2%)
    reduce_scatter x2, waiting for transfers between devices, per_device(): lax.psum_scatter(jnp.concatenate([contract_rows(normed_one, packed_grad),...  1230 us
    reduce_scatter x2, waiting for transfers between devices, per_device(): lax.psum_scatter(contract_rows(lax.slice_in_dim(hidden_low, 0, w_second.s...  182 us
    all_gather x2, waiting for transfers between devices, fetch(): lax.all_gather(w_ada[layer], ('dp', 'blk'), axis=0, tiled=True)  170 us
    all_gather x2, waiting for transfers between devices, fetch(): lax.all_gather(w_up[layer], ('dp', 'blk'), axis=0, tiled=True)  146 us
    psum x1, waiting for transfers between devices, per_device(): lax.psum((table_term, jnp.stack(scale_grads)), ('dp', 'blk'))  146 us
    all_gather x2, waiting for transfers between devices, fetch(): lax.all_gather(w_down[layer], ('dp', 'blk'), axis=0, tiled=True)  143 us
    all_gather x2, waiting for transfers between devices, fetch(): lax.all_gather(w_qkv[layer], ('dp', 'blk'), axis=0, tiled=True)  119 us
    dot_general x13, matrix products, contract_rows(): lax.dot_general(left, right, (((0,), (0,)), ((), ())), precision=precisio...  90.8 us
  transfers between devices with their start and end apart: 24, of which 21 were waited for; matrix products, arithmetic and copies ran while one was open for 13% of the time, Pallas kernels for 0%

commit v1 on v0

v1 whole, which is shorter than its diff:
```python
from functools import partial

import jax
import jax.numpy as jnp
from jax import lax
from jax.sharding import PartitionSpec as P

patch_areas = (1, 4, 9, 16, 25, 36, 64, 100, 169)
scale_starts = (1, 5, 14, 30, 55, 91, 155, 255)
f32 = jnp.float32
bf16 = jnp.bfloat16


def token_meta(stops, length):
    areas = jnp.array(patch_areas, dtype=jnp.int32)
    levels = jnp.arange(9, dtype=jnp.int32)
    counts = jnp.sum(jnp.where(levels[None, :] < stops[:, None], areas[None, :], 0), axis=1)
    ends = jnp.cumsum(counts)
    places = jnp.arange(length, dtype=jnp.int32)
    passed = places[:, None] >= ends[None, :]
    item = jnp.sum(passed.astype(jnp.int32), axis=1)
    begin = jnp.sum(jnp.where(passed, counts[None, :], 0), axis=1)
    inner = places - begin
    bounds = jnp.array(scale_starts, dtype=jnp.int32)
    level = jnp.sum((inner[:, None] >= bounds[None, :]).astype(jnp.int32), axis=1)
    level = jnp.where(item == stops.shape[0], 0, level)
    return (item, level)


def modulate(values, scale, shift):
    centre = jnp.mean(values, axis=-1, keepdims=True)
    centred = values - centre
    spread = jnp.mean(centred * centred, axis=-1, keepdims=True)
    return centred * lax.rsqrt(spread + 1e-06) * (1.0 + scale) + shift


def qk_norm(query, keys, scale):
    query = (
        query
        * lax.rsqrt(jnp.sum(query * query, axis=-1, keepdims=True) + 1e-06)
        * jnp.exp(scale)[None, :, None]
    )
    keys = keys * lax.rsqrt(jnp.sum(keys * keys, axis=-1, keepdims=True) + 1e-06)
    return (query, keys)


def mm(left, right):
    return jnp.dot(left, right, preferred_element_type=f32)


def mm_t(left, right):
    return lax.dot_general(left, right, (((1,), (1,)), ((), ())), preferred_element_type=f32)


def rows_mm(left, right, precision=None):
    return lax.dot_general(
        left, right, (((0,), (0,)), ((), ())), precision=precision, preferred_element_type=f32
    )


def gather(values, axes):
    return lax.all_gather(values, axes, axis=0, tiled=True)


def scatter(values, axes):
    return lax.psum_scatter(values, axes, scatter_dimension=0, tiled=True)


def per_device(
    tokens,
    cotangent,
    stop_scale,
    labels,
    class_table,
    head_scale,
    w_qkv,
    w_proj,
    w_up,
    w_down,
    w_ada,
):
    rows, width = tokens.shape[1:]
    layers, heads = head_scale.shape
    size = width // heads
    dps, blks = lax.axis_size("dp"), lax.axis_size("blk")
    count = dps * blks
    length = rows * blks
    d, b = lax.axis_index("dp"), lax.axis_index("blk")
    own_heads = heads // blks
    piece = own_heads * size
    wrows = w_qkv.shape[1]
    ffrows = w_down.shape[1]
    ff = ffrows * dps
    slots = labels.shape[1]

    item_all, level_all = token_meta(stop_scale[0], length)
    item_own = lax.dynamic_slice_in_dim(item_all, b * rows, rows)
    visible = (item_all[:, None] == item_all[None, :]) & (level_all[None, :] <= level_all[:, None])
    item_onehot = (item_own[:, None] == jnp.arange(slots, dtype=jnp.int32)[None, :]).astype(f32)

    labels_all = gather(labels, "dp").reshape(-1)
    chosen = labels_all[:, None] == jnp.arange(class_table.shape[0], dtype=jnp.int32)[None, :]
    cond = mm(chosen.astype(bf16), class_table)
    cond_act, silu_pull = jax.vjp(jax.nn.silu, cond)
    cond_low = cond_act.astype(bf16)

    wide = w_ada.shape[2]
    columns = layers * wide // count
    ada_cols = w_ada.transpose(1, 0, 2).reshape(wrows, count, columns).transpose(1, 0, 2)
    ada_cols = lax.all_to_all(ada_cols, ("dp", "blk"), 0, 0, tiled=True)
    ada_part = mm(cond_low, ada_cols.reshape(count * wrows, columns))
    ada_part = lax.all_to_all(ada_part.reshape(dps, slots, columns), "dp", 0, 0, tiled=True)
    ada_all = lax.all_gather(ada_part, "blk", axis=1, tiled=False)
    ada_all = ada_all.transpose(2, 0, 1, 3).reshape(slots, layers, wide)

    qkv_cols = w_qkv.reshape(layers, wrows, 3, blks, piece).transpose(3, 0, 1, 2, 4)
    up_cols = w_up.reshape(layers, wrows, dps, blks, ffrows).transpose(3, 0, 1, 2, 4)
    moved = jnp.concatenate(
        [
            qkv_cols.reshape(blks, layers, wrows, 3 * piece),
            up_cols.reshape(blks, layers, wrows, ff),
        ],
        axis=3,
    )
    moved = lax.all_to_all(moved, "blk", 0, 0, tiled=True)
    moved = moved.transpose(1, 0, 2, 3).reshape(layers, blks * wrows, 3 * piece + ff)
    to_heads = [(i, (i % dps) * blks + i // dps) for i in range(count)]
    to_rows = [(j, i) for i, j in to_heads]
    proj_own = lax.ppermute(w_proj, ("dp", "blk"), to_heads)
    weights = []
    for layer in range(layers):
        weights.append(
            (
                gather(moved[layer, :, : 3 * piece], "dp"),
                gather(proj_own[layer], "dp"),
                gather(moved[layer, :, 3 * piece :], "dp"),
                gather(w_down[layer], "dp"),
            )
        )

    def modulations(layer):
        per_token = jnp.dot(item_onehot, ada_all[:, layer], precision=lax.Precision.HIGHEST)
        return jnp.split(per_token, 6, axis=1)

    def split_heads(values):
        return values.reshape(length, own_heads, size)

    state = tokens[0].astype(f32)
    saved = []
    for layer in range(layers):
        w_query, w_out, w_first, w_second = weights[layer]
        own_scale = lax.dynamic_slice_in_dim(head_scale[layer], b * own_heads, own_heads)
        bound = jnp.exp(own_scale)
        gamma1, gamma2, scale1, scale2, shift1, shift2 = modulations(layer)
        normed_one = gather(modulate(state, scale1, shift1).astype(bf16), "blk")
        packed = mm(normed_one, w_query)
        query, keys, values = jnp.split(packed, 3, axis=1)
        (query, keys), pull_norm = jax.vjp(
            qk_norm, split_heads(query), split_heads(keys), own_scale
        )
        q_low, k_low = query.astype(bf16), keys.astype(bf16)
        v_low = split_heads(values.astype(bf16))
        scores = jnp.einsum("qhe,khe->hqk", q_low, k_low, preferred_element_type=f32)
        exps = jnp.where(visible[None], jnp.exp(scores - bound[:, None, None]), 0.0)
        total = jnp.sum(exps, axis=-1)
        mixed = jnp.einsum("hqk,khe->qhe", exps.astype(bf16), v_low, preferred_element_type=f32)
        mixed = (mixed / total.transpose(1, 0)[..., None]).reshape(length, piece)
        mixed_low = mixed.astype(bf16)
        branch = scatter(mm(mixed_low, w_out).astype(bf16), "blk").astype(f32)
        state_mid = state + gamma1 * branch
        normed_two = gather(modulate(state_mid, scale2, shift2).astype(bf16), "blk")
        upward = mm(normed_two, w_first)
        hidden_low = jax.nn.gelu(upward, approximate=True).astype(bf16)
        result = scatter(mm(hidden_low, w_second).astype(bf16), "blk").astype(f32)
        saved.append(
            (
                state,
                state_mid,
                normed_one,
                normed_two,
                q_low,
                k_low,
                v_low,
                pull_norm,
                mixed,
                total,
                branch,
                upward,
                hidden_low,
                result,
            )
        )
        state = state_mid + gamma2 * result
    output = state.astype(bf16)[None]

    grad = cotangent[0].astype(f32)
    cond_grad = 0.0
    scale_grads, pieces = [None] * layers, [None] * layers
    for layer in reversed(range(layers)):
        w_query, w_out, w_first, w_second = weights[layer]
        (
            state,
            state_mid,
            normed_one,
            normed_two,
            q_low,
            k_low,
            v_low,
            pull_norm,
            mixed,
            total,
            branch,
            upward,
            hidden_low,
            result,
        ) = saved[layer]
        own_scale = lax.dynamic_slice_in_dim(head_scale[layer], b * own_heads, own_heads)
        bound = jnp.exp(own_scale)
        gamma1, gamma2, scale1, scale2, shift1, shift2 = modulations(layer)
        gamma2_grad = grad * result
        result_grad = gather((gamma2 * grad).astype(bf16), "blk")
        hidden_grad = mm_t(result_grad, w_second)
        _, pull_gelu = jax.vjp(partial(jax.nn.gelu, approximate=True), upward)
        upward_grad = pull_gelu(hidden_grad)[0].astype(bf16)
        normed_grad = scatter(mm_t(upward_grad, w_first).astype(bf16), "blk").astype(f32)
        down_grad = scatter(rows_mm(hidden_low, result_grad).astype(bf16), "dp").astype(f32)
        up_grad = scatter(rows_mm(normed_two, upward_grad).astype(bf16), "dp")
        _, pull_second = jax.vjp(modulate, state_mid, scale2, shift2)
        mid_part, scale2_grad, shift2_grad = pull_second(normed_grad)
        mid_grad = grad + mid_part
        gamma1_grad = mid_grad * branch
        branch_grad = gather((gamma1 * mid_grad).astype(bf16), "blk")
        mixed_grad = mm_t(branch_grad, w_out).astype(bf16)
        proj_grad = scatter(rows_mm(mixed.astype(bf16), branch_grad).astype(bf16), "dp")
        row_term = jnp.sum(split_heads(mixed_grad.astype(f32) * mixed), axis=-1).transpose(1, 0)
        out_grad = split_heads(mixed_grad)
        scores = jnp.einsum("qhe,khe->hqk", q_low, k_low, preferred_element_type=f32)
        exps = jnp.where(visible[None], jnp.exp(scores - bound[:, None, None]), 0.0)
        probs = exps / total[..., None]
        prob_grad = jnp.einsum("qhe,khe->hqk", out_grad, v_low, preferred_element_type=f32)
        score_grad = (probs * (prob_grad - row_term[..., None])).astype(bf16)
        query_grad = jnp.einsum("hqk,khe->qhe", score_grad, k_low, preferred_element_type=f32)
        key_grad = jnp.einsum("hqk,qhe->khe", score_grad, q_low, preferred_element_type=f32)
        scaled = (out_grad.astype(f32) / total.transpose(1, 0)[..., None]).astype(bf16)
        value_grad = jnp.einsum("hqk,qhe->khe", exps.astype(bf16), scaled, preferred_element_type=f32)
        raw_query, raw_keys, scale_grad = pull_norm((query_grad, key_grad))
        packed_grad = jnp.concatenate(
            [x.reshape(length, piece) for x in (raw_query, raw_keys, value_grad)], axis=1
        ).astype(bf16)
        normed_grad = scatter(mm_t(packed_grad, w_query).astype(bf16), "blk").astype(f32)
        qkv_grad = scatter(rows_mm(normed_one, packed_grad).astype(bf16), "dp")
        _, pull_first = jax.vjp(modulate, state, scale1, shift1)
        input_part, scale1_grad, shift1_grad = pull_first(normed_grad)
        grad = mid_grad + input_part
        scale_grads[layer] = lax.dynamic_update_slice_in_dim(
            jnp.zeros((heads,), f32), scale_grad, b * own_heads, 0
        )
        token_mod_grad = jnp.concatenate(
            [gamma1_grad, gamma2_grad, scale1_grad, scale2_grad, shift1_grad, shift2_grad], axis=1
        )
        item_grad = rows_mm(item_onehot, token_mod_grad, lax.Precision.HIGHEST)
        item_grad = item_grad.reshape(slots, blks, wide // blks).transpose(1, 0, 2)
        item_grad = scatter(item_grad, "blk").astype(bf16)
        item_grad = gather(item_grad, ("dp", "blk")).reshape(dps, blks, slots, wide // blks)
        item_grad = item_grad.transpose(0, 2, 1, 3).reshape(dps * slots, wide)
        cond_grad = cond_grad + mm_t(item_grad, w_ada[layer])
        own_cond = lax.dynamic_slice_in_dim(cond_low, (d * blks + b) * wrows, wrows, axis=1)
        ada_grad = rows_mm(own_cond, item_grad)
        back = jnp.concatenate([qkv_grad, up_grad], axis=1)
        back = lax.all_to_all(back.reshape(blks, wrows, 3 * piece + ff), "blk", 0, 0, tiled=True)
        qkv_grad = back[:, :, : 3 * piece].reshape(blks, wrows, 3, piece)
        qkv_grad = qkv_grad.transpose(1, 2, 0, 3).reshape(wrows, 3 * width).astype(f32)
        up_grad = back[:, :, 3 * piece :].reshape(blks, wrows, dps, ffrows)
        up_grad = up_grad.transpose(1, 2, 0, 3).reshape(wrows, ff * blks).astype(f32)
        proj_grad = lax.ppermute(proj_grad, ("dp", "blk"), to_rows).astype(f32)
        pieces[layer] = (qkv_grad, proj_grad, up_grad, down_grad, ada_grad)
    cond_grad = gather(cond_grad.T, ("dp", "blk")).T
    cond_pre = silu_pull(cond_grad)[0]
    table_grad = rows_mm(chosen.astype(f32), cond_pre, lax.Precision.HIGHEST)
    head_grad = lax.psum(jnp.stack(scale_grads), ("dp", "blk"))
    stacked = [jnp.stack([one[i] for one in pieces]) for i in range(5)]
    return (output, grad.astype(bf16)[None], table_grad, head_grad, *stacked)


def solution(mesh):
    in_specs = (
        P("dp", "blk", None),
        P("dp", "blk", None),
        P("dp", None),
        P("dp", None),
        P(),
        P(),
        P(None, ("dp", "blk"), None),
        P(None, ("dp", "blk"), None),
        P(None, ("dp", "blk"), None),
        P(None, ("dp", "blk"), None),
        P(None, ("dp", "blk"), None),
    )
    out_specs = (
        P("dp", "blk", None),
        P("dp", "blk", None),
        P(),
        P(),
        P(None, ("dp", "blk"), None),
        P(None, ("dp", "blk"), None),
        P(None, ("dp", "blk"), None),
        P(None, ("dp", "blk"), None),
        P(None, ("dp", "blk"), None),
    )
    return jax.shard_map(
        per_device, mesh=mesh, in_specs=in_specs, out_specs=out_specs, check_vma=False
    )
```

time: 3030 us -> 1720 us (0.57)
  waiting for transfers between devices: 2330 us -> 1120 us
  blocking collectives: 47.1 us -> 186 us
  matrix products: 324 us -> 211 us
  local copies, waits for them, and re-layouts: 147 us -> 50 us
  other arithmetic: 152 us -> 74.9 us
  starting transfers between devices: 2.39 us -> 43.9 us
    reduce_scatter x8 -> x16, waiting for transfers between devices: 1460 us -> 671 us  [scatter(): return lax.psum_scatter(values, axes, scatter_dimension=0, tiled=True)]
    all_gather x14 -> x16, waiting for transfers between devices: 716 us -> 429 us  [gather(): return lax.all_gather(values, axes, axis=0, tiled=True)]
    psum x2 -> x0, waiting for transfers between devices: 146 us -> none  [the longest x1 146 us: per_device(): lax.psum((table_term, jnp.stack(scale_grads)), ('dp', 'blk'))]
    all_gather x0 -> x5, blocking collectives: none -> 129 us  [the longest x4 116 us: gather(): return lax.all_gather(values, axes, axis=0, tiled=True)]
    dot_general x92 -> x47, matrix products: 324 us -> 211 us  [the longest x13 60.5 us: rows_mm(): lax.dot_general(left, right, (((0,), (0,)), ((), ())), precision=precisio...]
    concatenate x2 -> x5, other arithmetic: 75.4 us -> 6.84 us  [the longest x2 3.61 us: per_device(): back = jnp.concatenate([qkv_grad, up_grad], axis=1)]
  transfers between devices with their start and end apart: 24 -> 40, of which waited for: 21 -> 33; matrix products, arithmetic and copies ran while one was open for 13% -> 9% of each run, Pallas kernels for 0% -> 0%
where the time goes in v1:
time: 1720 us; the launch traced here: 1700 us
  waiting for transfers between devices  1120 us (65%)
  matrix products  211 us (12%)
  blocking collectives  186 us (11%)
  other arithmetic  74.9 us (4%)
  local copies, waits for them, and re-layouts  50 us (3%)
  starting transfers between devices  43.9 us (3%)
    reduce_scatter x16, waiting for transfers between devices, scatter(): return lax.psum_scatter(values, axes, scatter_dimension=0, tiled=True)  671 us
    all_gather x16, waiting for transfers between devices, gather(): return lax.all_gather(values, axes, axis=0, tiled=True)  429 us
    all_gather x4, blocking collectives, gather(): return lax.all_gather(values, axes, axis=0, tiled=True)  116 us
    dot_general x13, matrix products, rows_mm(): lax.dot_general(left, right, (((0,), (0,)), ((), ())), precision=precisio...  60.5 us
    dot_general x10, matrix products, mm(): return jnp.dot(left, right, preferred_element_type=f32)  42.2 us
    psum x1, blocking collectives, per_device(): head_grad = lax.psum(jnp.stack(scale_grads), ('dp', 'blk'))  40.6 us
    dot_general x10, matrix products, mm_t(): lax.dot_general(left, right, (((1,), (1,)), ((), ())), preferred_element_...  36.5 us
  transfers between devices with their start and end apart: 40, of which 33 were waited for; matrix products, arithmetic and copies ran while one was open for 9% of the time, Pallas kernels for 0%

profile of v1, /device:TPU:7, one launch (start us, length us, event | category | flops | bytes accessed | tf_op | source)
XLA Modules:
  0.0 1697.4 jit_solution(16343890458691682079)
XLA Ops:
  27.6 6.6 all-to-all-start
  34.6 23.9 %all-gather.9 = s32[8,1,12]{2,1,0:T(1,128)S(1)} all-gather(s32[1,1,12]{2,1,0:T(1,128)S(1)} %bitcast.371), channel_id=1, replica_groups=mesh['dp'=8,'blk'=4] {'dp'}, dimensions={0}, use_global_device_ids=true | all-gather | bytes 432 | tf_op jit(solution)/shard_map/all_gather | solution.py:62
  65.6 4.6 all-to-all-start.1
  70.4 4.7 all-to-all-done.1
  75.2 13.1 all-gather
  96.2 5.2 collective-permute-start
  102.8 4.9 collective-permute-done
  107.8 29.5 %all-gather.2 = bf16[1,256,1024]{2,1,0:T(8,128)(2,1)S(1)} all-gather(bf16[1,32,1024]{2,1,0:T(8,128)(2,1)S(1)} %get-tuple-element.69), channel_id=4, replica_groups=mesh['dp'=8,'blk'=4] {'dp'}, dimensions={1}, use_global_device_ids=true | all-gather | bytes 589824 | tf_op jit(solution)/shard_map/all_gather | solution.py:62
  146.9 9.1 fusion
  163.4 36.5 %reduce-scatter.19.cloned.1.call-done = bf16[256,1024]{1,0:T(8,128)(2,1)} async-done(((bf16[1024,1024]{1,0:T(8,128)(2,1)}), bf16[256,1024]{1,0:T(8,128)(2,1)}) %reduce-scatter.19.cloned.1.call-update) | async-done | bytes 524304 | tf_op jit(solution)/shard_map/reduce_scatter | solution.py:66
  205.4 45.5 %all-gather.49.cloned.1.call-done = bf16[1,1024,1024]{2,1,0:T(8,128)(2,1)} async-done(((bf16[1,128,1024]{2,1,0:T(8,128)(2,1)}), bf16[1,1024,1024]{2,1,0:T(8,128)(2,1)}) %all-gather.49.cloned.1.call-update) | async-done | bytes 2097168 | tf_op jit(solution)/shard_map/all_gather | solution.py:62
  250.9 24.7 %all-gather.29.cloned.1.call-done = bf16[1024,1024]{1,0:T(8,128)(2,1)} async-done(((bf16[256,1024]{1,0:T(8,128)(2,1)}), bf16[1024,1024]{1,0:T(8,128)(2,1)}) %all-gather.29.cloned.1.call-update) | async-done | bytes 2097168 | tf_op jit(solution)/shard_map/all_gather | solution.py:62
  275.6 6.6 fusion.36
  282.1 44.0 %all-gather.51.cloned.1.call-done = bf16[1,1024,1024]{2,1,0:T(8,128)(2,1)} async-done(((bf16[1,128,1024]{2,1,0:T(8,128)(2,1)}), bf16[1,1024,1024]{2,1,0:T(8,128)(2,1)}) %all-gather.51.cloned.1.call-update) | async-done | bytes 2097168 | tf_op jit(solution)/shard_map/all_gather | solution.py:62
  326.2 6.8 fusion.41
  338.4 25.9 %reduce-scatter.21.cloned.1.call-done = bf16[256,1024]{1,0:T(8,128)(2,1)} async-done(((bf16[1024,1024]{1,0:T(8,128)(2,1)}), bf16[256,1024]{1,0:T(8,128)(2,1)}) %reduce-scatter.21.cloned.1.call-update) | async-done | bytes 524304 | tf_op jit(solution)/shard_map/reduce_scatter | solution.py:66
  369.6 26.4 %all-gather.6 = bf16[1,256,1024]{2,1,0:T(8,128)(2,1)S(1)} all-gather(bf16[1,32,1024]{2,1,0:T(8,128)(2,1)S(1)} %get-tuple-element.68), channel_id=8, replica_groups=mesh['dp'=8,'blk'=4] {'dp'}, dimensions={1}, use_global_device_ids=true | all-gather | bytes 589824 | tf_op jit(solution)/shard_map/all_gather | solution.py:62
  396.0 15.7 all-gather.53.cloned.1.call-done
  411.7 25.2 %all-gather.31.cloned.1.call-done = bf16[1024,1024]{1,0:T(8,128)(2,1)} async-done(((bf16[256,1024]{1,0:T(8,128)(2,1)}), bf16[1024,1024]{1,0:T(8,128)(2,1)}) %all-gather.31.cloned.1.call-update) | async-done | bytes 2097168 | tf_op jit(solution)/shard_map/all_gather | solution.py:62
  442.9 9.1 fusion.2
  460.0 30.4 %reduce-scatter.23.cloned.1.call-done = bf16[256,1024]{1,0:T(8,128)(2,1)} async-done(((bf16[1024,1024]{1,0:T(8,128)(2,1)}), bf16[256,1024]{1,0:T(8,128)(2,1)}) %reduce-scatter.23.cloned.1.call-update) | async-done | bytes 524304 | tf_op jit(solution)/shard_map/reduce_scatter | solution.py:66
  497.2 43.7 %all-gather.55.cloned.1.call-done = bf16[1,1024,1024]{2,1,0:T(8,128)(2,1)} async-done(((bf16[1,128,1024]{2,1,0:T(8,128)(2,1)}), bf16[1,1024,1024]{2,1,0:T(8,128)(2,1)}) %all-gather.55.cloned.1.call-update) | async-done | bytes 2097168 | tf_op jit(solution)/shard_map/all_gather | solution.py:62
  540.9 24.7 %all-gather.33.cloned.1.call-done = bf16[1024,1024]{1,0:T(8,128)(2,1)} async-done(((bf16[256,1024]{1,0:T(8,128)(2,1)}), bf16[1024,1024]{1,0:T(8,128)(2,1)}) %all-gather.33.cloned.1.call-update) | async-done | bytes 2097168 | tf_op jit(solution)/shard_map/all_gather | solution.py:62
  565.6 6.5 fusion.26
  572.2 44.2 %all-gather.57.cloned.1.call-done = bf16[1,1024,1024]{2,1,0:T(8,128)(2,1)} async-done(((bf16[1,128,1024]{2,1,0:T(8,128)(2,1)}), bf16[1,1024,1024]{2,1,0:T(8,128)(2,1)}) %all-gather.57.cloned.1.call-update) | async-done | bytes 2097168 | tf_op jit(solution)/shard_map/all_gather | solution.py:62
  616.4 24.7 %all-gather.35.cloned.1.call-done = bf16[1024,1024]{1,0:T(8,128)(2,1)} async-done(((bf16[256,1024]{1,0:T(8,128)(2,1)}), bf16[1024,1024]{1,0:T(8,128)(2,1)}) %all-gather.35.cloned.1.call-update) | async-done | bytes 2097168 | tf_op jit(solution)/shard_map/all_gather | solution.py:62
  641.0 8.1 fusion.17
  654.3 6.9 fusion.47
  661.2 24.2 %reduce-scatter.27.cloned.1.call-done = bf16[256,1024]{1,0:T(8,128)(2,1)} async-done(((bf16[1024,1024]{1,0:T(8,128)(2,1)}), bf16[256,1024]{1,0:T(8,128)(2,1)}) %reduce-scatter.27.cloned.1.call-update) | async-done | bytes 524304 | tf_op jit(solution)/shard_map/reduce_scatter | solution.py:66
  687.1 32.2 %reduce-scatter.25.cloned.1.call-done = bf16[256,1024]{1,0:T(8,128)(2,1)} async-done(((bf16[1024,1024]{1,0:T(8,128)(2,1)}), bf16[256,1024]{1,0:T(8,128)(2,1)}) %reduce-scatter.25.cloned.1.call-update) | async-done | bytes 524304 | tf_op jit(solution)/shard_map/reduce_scatter | solution.py:66
  726.4 22.9 %all-gather.37.cloned.1.call-done = bf16[1024,1024]{1,0:T(8,128)(2,1)} async-done(((bf16[256,1024]{1,0:T(8,128)(2,1)}), bf16[1024,1024]{1,0:T(8,128)(2,1)}) %all-gather.37.cloned.1.call-update) | async-done | bytes 2097168 | tf_op jit(solution)/shard_map/all_gather | solution.py:62
  752.1 7.0 convolution_convert_fusion.11
  759.0 9.9 multiply_convert_fusion.1
  781.1 28.5 %reduce-scatter.29.cloned.1.call-done = bf16[256,1024]{1,0:T(8,128)(2,1)} async-done(((bf16[1024,1024]{1,0:T(8,128)(2,1)}), bf16[256,1024]{1,0:T(8,128)(2,1)}) %reduce-scatter.29.cloned.1.call-update) | async-done | bytes 524304 | tf_op jit(solution)/shard_map/reduce_scatter | solution.py:66
  817.6 23.1 %all-gather.39.cloned.1.call-done = bf16[1024,1024]{1,0:T(8,128)(2,1)} async-done(((bf16[256,1024]{1,0:T(8,128)(2,1)}), bf16[1024,1024]{1,0:T(8,128)(2,1)}) %all-gather.39.cloned.1.call-update) | async-done | bytes 2097168 | tf_op jit(solution)/shard_map/all_gather | solution.py:62
  840.7 8.1 fusion.10
  853.9 31.1 %reduce-scatter.31.cloned.1.call-done = bf16[256,1024]{1,0:T(8,128)(2,1)} async-done(((bf16[1024,1024]{1,0:T(8,128)(2,1)}), bf16[256,1024]{1,0:T(8,128)(2,1)}) %reduce-scatter.31.cloned.1.call-update) | async-done | bytes 524304 | tf_op jit(solution)/shard_map/reduce_scatter | solution.py:66
  894.4 22.9 %all-gather.41.cloned.1.call-done = bf16[1024,1024]{1,0:T(8,128)(2,1)} async-done(((bf16[256,1024]{1,0:T(8,128)(2,1)}), bf16[1024,1024]{1,0:T(8,128)(2,1)}) %all-gather.41.cloned.1.call-update) | async-done | bytes 2097168 | tf_op jit(solution)/shard_map/all_gather | solution.py:62
  920.2 7.0 convolution_convert_fusion.10
  927.1 9.9 multiply_convert_fusion
  946.7 5.9 convolution_convert_fusion.2
  952.7 5.1 convolution_convert_fusion.8
  961.1 6.1 convolution_convert_fusion.3
  967.2 5.1 convolution_convert_fusion.9
  975.9 7.0 convolution_convert_fusion
  983.0 7.0 convolution_convert_fusion.1
  995.2 5.0 fusion.120
  1011.1 4.9 fusion.119
  1016.2 17.1 %all-reduce.4 = (bf16[4,12,1536]{2,0,1:T(4,128)(2,1)S(1)}, bf16[4,12,1536]{2,0,1:T(4,128)(2,1)S(1)}) all-reduce(f32[4,12,1536]{2,0,1:T(4,128)S(1)} %bitcast.345, f32[4,12,1536]{2,0,1:T(4,128)S(1)} %bitcast.346), channel_id=19, replica_groups=mesh['dp'=8,'blk'=4] {'blk'}, use_global_device_ids=true, to_apply=%region_41.42.clone | all-reduce | flops 147456 | bytes 884736
  1034.7 13.7 reduce-scatter.41.cloned.1.call-done
  1048.4 67.1 %reduce-scatter.39.cloned.1.call-done = bf16[128,768]{1,0:T(8,128)(2,1)} async-done(((bf16[1024,768]{1,0:T(8,128)(2,1)}), bf16[128,768]{1,0:T(8,128)(2,1)}) %reduce-scatter.39.cloned.1.call-update) | async-done | bytes 196624 | tf_op jit(solution)/shard_map/reduce_scatter | solution.py:66
  1117.2 6.1 all-to-all-start.4
  1124.8 56.0 %reduce-scatter.45.cloned.1.call-done = bf16[32,1024]{1,0:T(8,128)(2,1)} async-done(((bf16[256,1024]{1,0:T(8,128)(2,1)}), bf16[32,1024]{1,0:T(8,128)(2,1)}) %reduce-scatter.45.cloned.1.call-update) | async-done | bytes 65552 | tf_op jit(solution)/shard_map/reduce_scatter | solution.py:66
  1187.0 64.5 %reduce-scatter.37.cloned.1.call-done = bf16[128,1024]{1,0:T(8,128)(2,1)} async-done(((bf16[1024,1024]{1,0:T(8,128)(2,1)}), bf16[128,1024]{1,0:T(8,128)(2,1)}) %reduce-scatter.37.cloned.1.call-update) | async-done | bytes 262160 | tf_op jit(solution)/shard_map/reduce_scatter | solution.py:66
  1251.4 66.5 %reduce-scatter.35.cloned.1.call-done = bf16[128,768]{1,0:T(8,128)(2,1)} async-done(((bf16[1024,768]{1,0:T(8,128)(2,1)}), bf16[128,768]{1,0:T(8,128)(2,1)}) %reduce-scatter.35.cloned.1.call-update) | async-done | bytes 196624 | tf_op jit(solution)/shard_map/reduce_scatter | solution.py:66
  1319.7 6.2 all-to-all-start.3
  1325.9 57.4 %reduce-scatter.43.cloned.1.call-done = bf16[32,1024]{1,0:T(8,128)(2,1)} async-done(((bf16[256,1024]{1,0:T(8,128)(2,1)}), bf16[32,1024]{1,0:T(8,128)(2,1)}) %reduce-scatter.43.cloned.1.call-update) | async-done | bytes 65552 | tf_op jit(solution)/shard_map/reduce_scatter | solution.py:66
  1387.3 66.8 %reduce-scatter.49.cloned.1.call-done = bf16[128,1024]{1,0:T(8,128)(2,1)} async-done(((bf16[1024,1024]{1,0:T(8,128)(2,1)}), bf16[128,1024]{1,0:T(8,128)(2,1)}) %reduce-scatter.49.cloned.1.call-update) | async-done | bytes 262160 | tf_op jit(solution)/shard_map/reduce_scatter | solution.py:66
  1454.1 70.0 %reduce-scatter.47.cloned.1.call-done = bf16[128,1024]{1,0:T(8,128)(2,1)} async-done(((bf16[1024,1024]{1,0:T(8,128)(2,1)}), bf16[128,1024]{1,0:T(8,128)(2,1)}) %reduce-scatter.47.cloned.1.call-update) | async-done | bytes 262160 | tf_op jit(solution)/shard_map/reduce_scatter | solution.py:66
  1526.4 40.6 %psum.7 = f32[2,16]{1,0:T(2,128)} all-reduce(f32[2,16]{1,0:T(2,128)S(1)} %pad_maximum_fusion.10), channel_id=1, replica_groups=mesh['dp'=8,'blk'=4] {'dp','blk'}, use_global_device_ids=true, to_apply=%region_45.46 | all-reduce | flops 32 | bytes 256 | tf_op jit(solution)/shard_map/psum | solution.py:280
  1572.5 9.7 all-gather.43.cloned.1.call-done
  1584.8 54.9 %all-gather.45.cloned.1.call-done = bf16[32,12,1536]{2,1,0:T(8,128)(2,1)} async-done(((bf16[1,12,1536]{2,1,0:T(8,128)(2,1)}), bf16[32,12,1536]{2,1,0:T(8,128)(2,1)}) %all-gather.45.cloned.1.call-update) | async-done | bytes 1179664 | tf_op jit(solution)/shard_map/all_gather | solution.py:62
  1646.5 35.8 %all_gather.87 = f32[1024,96]{1,0:T(8,128)S(1)} all-gather(f32[32,96]{1,0:T(8,128)S(1)} %fusion.65), channel_id=1, replica_groups=mesh['dp'=8,'blk'=4] {'dp','blk'}, dimensions={0}, use_global_device_ids=true | all-gather | bytes 405504 | tf_op jit(solution)/shard_map/all_gather | solution.py:62
  1685.6 5.0 fusion.100
  (423 shorter events, 214.3 us)
Async XLA Ops:
  7.2 52.6 %copy-start = (bf16[1001,1024]{1,0:T(8,128)(2,1)S(1)}, bf16[1001,1024]{1,0:T(8,128)(2,1)}, u32[]{:S(2)}) copy-start(bf16[1001,1024]{1,0:T(8,128)(2,1)} %param.17) | copy-start | bytes 6150148
  12.0 22.2 %copy-start.83 = (s32[1,11]{1,0:T(1,128)S(1)}, s32[1,11]{1,0:T(1,128)}, u32[]{:S(2)}) copy-start(s32[1,11]{1,0:T(1,128)} %param.15) | copy-start | bytes 136
  12.0 22.2 %copy-start.87 = (s32[9]{0:T(128)S(1)}, s32[9]{0:T(128)}, u32[]{:S(2)}) copy-start(s32[9]{0:T(128)} %constant.77.clone) | copy-start | bytes 112
  12.0 22.6 %copy-start.76 = (s32[1,12]{1,0:T(1,128)S(1)}, s32[1,12]{1,0:T(1,128)}, u32[]{:S(2)}) copy-start(s32[1,12]{1,0:T(1,128)} %param.16) | copy-start | bytes 148
  12.0 15.6 all-to-all-start.2
  19.3 42.9 %copy-start.10 = (bf16[1,256,1024]{2,1,0:T(8,128)(2,1)S(1)}, bf16[1,256,1024]{2,1,0:T(8,128)(2,1)}, u32[]{:S(2)}) copy-start(bf16[1,256,1024]{2,1,0:T(8,128)(2,1)} %param.13) | copy-start | bytes 1572868
  27.6 35.9 %all-to-all-start = ((bf16[32,32,384]{2,1,0:T(8,128)(2,1)}), bf16[32,32,384]{2,1,0:T(8,128)(2,1)}, u32[]{:S(2)}, u32[]{:S(2)}) async-start(bf16[32,32,384]{2,1,0:T(8,128)(2,1)} %copy.113), calls=%async_computation | async-start | bytes 1572864 | tf_op jit(solution)/shard_map/all_to_all | solution.py:110
  34.2 103.1 %all-gather.47.cloned.1.call-start = ((), (), s32[]{:S(2)}) async-start(), calls=%async_computation.47 | async-start | bytes 1769472 | tf_op jit(solution)/shard_map/all_gather | solution.py:62
  62.3 30.0 %copy-start.61 = (f32[256]{0:T(256)}, f32[256]{0:T(256)S(1)}, u32[]{:S(2)}) copy-start(f32[256]{0:T(256)S(1)} %broadcast_multiply_fusion.3) | copy-start | bytes 3076
  62.6 27.0 %copy-start.67 = (f32[256]{0:T(256)}, f32[256]{0:T(256)S(1)}, u32[]{:S(2)}) copy-start(f32[256]{0:T(256)S(1)} %fusion.68) | copy-start | bytes 3076
  65.6 9.5 all-to-all-start.1
  70.2 70.6 %all-gather.27.cloned.1.call-start = ((), (), s32[]{:S(2)}) async-start(), calls=%async_computation.21 | async-start | bytes 2621440 | tf_op jit(solution)/shard_map/all_gather | solution.py:62
  70.4 263.5 %copy-start.59 = (s32[256]{0:T(256)}, s32[256]{0:T(256)S(1)}, u32[]{:S(2)}) copy-start(s32[256]{0:T(256)S(1)} %dynamic_slice.15) | copy-start | bytes 3076
  70.4 22.0 %copy-start.65 = (f32[256]{0:T(256)}, f32[256]{0:T(256)S(1)}, u32[]{:S(2)}) copy-start(f32[256]{0:T(256)S(1)} %fusion.129) | copy-start | bytes 3076
  96.1 103.8 %reduce-scatter.19.cloned.1.call-start = ((), (), s32[]{:S(2)}) async-start(), calls=%async_computation.22 | async-start | bytes 2621440 | tf_op jit(solution)/shard_map/reduce_scatter | solution.py:66
  96.2 11.6 collective-permute-start
  102.7 44.2 %copy-start.14 = (pred[1024,1024]{0,1:T(8,128)(4,1)}, pred[1024,1024]{0,1:T(8,128)(4,1)S(1)}, u32[]{:S(2)}) copy-start(pred[1024,1024]{0,1:T(8,128)(4,1)S(1)} %compare_and_fusion) | copy-start | bytes 3145732
  102.7 42.0 %copy-start.73 = (f32[1,16]{1,0:T(1,128)}, f32[1,16]{1,0:T(1,128)S(1)}, u32[]{:S(2)}) copy-start(f32[1,16]{1,0:T(1,128)S(1)} %get-tuple-element.71) | copy-start | bytes 196
  102.7 266.8 %copy-start.71 = (f32[1,16]{1,0:T(1,128)}, f32[1,16]{1,0:T(1,128)S(1)}, u32[]{:S(2)}) copy-start(f32[1,16]{1,0:T(1,128)S(1)} %get-tuple-element.70) | copy-start | bytes 196
  102.8 44.1 %copy-start.63 = (f32[4]{0:T(128)}, f32[4]{0:T(128)S(1)}, u32[]{:S(2)}) copy-start(f32[4]{0:T(128)S(1)} %fusion.141) | copy-start | bytes 52
  137.2 22.2 %copy-start.44 = (bf16[1,256,1024]{2,1,0:T(8,128)(2,1)}, bf16[1,256,1024]{2,1,0:T(8,128)(2,1)S(1)}, u32[]{:S(2)}) copy-start(bf16[1,256,1024]{2,1,0:T(8,128)(2,1)S(1)} %all-gather.2) | copy-start | bytes 1572868
  162.4 88.5 %all-gather.49.cloned.1.call-start = ((), (), s32[]{:S(2)}) async-start(), calls=%async_computation.48 | async-start | bytes 2359296 | tf_op jit(solution)/shard_map/all_gather | solution.py:62
  163.3 41.2 %copy-start.50 = (bf16[2,128,1024]{2,1,0:T(8,128)(2,1)S(1)}, bf16[2,128,1024]{2,1,0:T(8,128)(2,1)}, u32[]{:S(2)}) copy-start(bf16[2,128,1024]{2,1,0:T(8,128)(2,1)} %param.22) | copy-start | bytes 1572868
  163.3 112.2 %all-gather.29.cloned.1.call-start = ((), (), s32[]{:S(2)}) async-start(), calls=%async_computation.23 | async-start | bytes 2621440 | tf_op jit(solution)/shard_map/all_gather | solution.py:62
  204.5 121.7 %all-gather.51.cloned.1.call-start = ((), (), s32[]{:S(2)}) async-start(), calls=%async_computation.49 | async-start | bytes 2359296 | tf_op jit(solution)/shard_map/all_gather | solution.py:62
  205.4 158.8 %reduce-scatter.21.cloned.1.call-start = ((), (), s32[]{:S(2)}) async-start(), calls=%async_computation.24 | async-start | bytes 2621440 | tf_op jit(solution)/shard_map/reduce_scatter | solution.py:66
  333.0 78.7 %all-gather.53.cloned.1.call-start = ((), (), s32[]{:S(2)}) async-start(), calls=%async_computation.50 | async-start | bytes 1769472 | tf_op jit(solution)/shard_map/all_gather | solution.py:62
  333.8 103.2 %all-gather.31.cloned.1.call-start = ((), (), s32[]{:S(2)}) async-start(), calls=%async_computation.25 | async-start | bytes 2621440 | tf_op jit(solution)/shard_map/all_gather | solution.py:62
  369.4 120.9 %reduce-scatter.23.cloned.1.call-start = ((), (), s32[]{:S(2)}) async-start(), calls=%async_computation.26 | async-start | bytes 2621440 | tf_op jit(solution)/shard_map/reduce_scatter | solution.py:66
  396.0 59.3 %copy-start.45 = (bf16[1,256,1024]{2,1,0:T(8,128)(2,1)}, bf16[1,256,1024]{2,1,0:T(8,128)(2,1)S(1)}, u32[]{:S(2)}) copy-start(bf16[1,256,1024]{2,1,0:T(8,128)(2,1)S(1)} %all-gather.6) | copy-start | bytes 1572868
  459.2 33.4 %copy-start.26 = (bf16[1,256,1024]{2,1,0:T(8,128)(2,1)S(1)}, bf16[1,256,1024]{2,1,0:T(8,128)(2,1)}, u32[]{:S(2)}) copy-start(bf16[1,256,1024]{2,1,0:T(8,128)(2,1)} %param.14) | copy-start | bytes 1572868
  459.2 81.8 %all-gather.55.cloned.1.call-start = ((), (), s32[]{:S(2)}) async-start(), calls=%async_computation.51 | async-start | bytes 2359296 | tf_op jit(solution)/shard_map/all_gather | solution.py:62
  459.9 105.7 %all-gather.33.cloned.1.call-start = ((), (), s32[]{:S(2)}) async-start(), calls=%async_computation.27 | async-start | bytes 2621440 | tf_op jit(solution)/shard_map/all_gather | solution.py:62
  495.7 120.7 %all-gather.57.cloned.1.call-start = ((), (), s32[]{:S(2)}) async-start(), calls=%async_computation.52 | async-start | bytes 2359296 | tf_op jit(solution)/shard_map/all_gather | solution.py:62
  496.5 144.6 %all-gather.35.cloned.1.call-start = ((), (), s32[]{:S(2)}) async-start(), calls=%async_computation.29 | async-start | bytes 2621440 | tf_op jit(solution)/shard_map/all_gather | solution.py:62
  497.0 188.4 %reduce-scatter.27.cloned.1.call-start = ((), (), s32[]{:S(2)}) async-start(), calls=%async_computation.30 | async-start | bytes 2621440 | tf_op jit(solution)/shard_map/reduce_scatter | solution.py:66
  654.2 65.0 %reduce-scatter.25.cloned.1.call-start = ((), (), s32[]{:S(2)}) async-start(), calls=%async_computation.28 | async-start | bytes 2621440 | tf_op jit(solution)/shard_map/reduce_scatter | solution.py:66
  661.2 88.1 %all-gather.37.cloned.1.call-start = ((), (), s32[]{:S(2)}) async-start(), calls=%async_computation.31 | async-start | bytes 2621440 | tf_op jit(solution)/shard_map/all_gather | solution.py:62
  726.1 83.4 %reduce-scatter.29.cloned.1.call-start = ((), (), s32[]{:S(2)}) async-start(), calls=%async_computation.32 | async-start | bytes 2621440 | tf_op jit(solution)/shard_map/reduce_scatter | solution.py:66
  778.4 62.3 %all-gather.39.cloned.1.call-start = ((), (), s32[]{:S(2)}) async-start(), calls=%async_computation.33 | async-start | bytes 2621440 | tf_op jit(solution)/shard_map/all_gather | solution.py:62
  817.5 67.5 %reduce-scatter.31.cloned.1.call-start = ((), (), s32[]{:S(2)}) async-start(), calls=%async_computation.34 | async-start | bytes 2621440 | tf_op jit(solution)/shard_map/reduce_scatter | solution.py:66
  853.9 34.7 %copy-start.41 = (bf16[256,1024]{1,0:T(8,128)(2,1)S(1)}, bf16[256,1024]{1,0:T(8,128)(2,1)}, u32[]{:S(2)}) copy-start(bf16[256,1024]{1,0:T(8,128)(2,1)} %reduce-scatter.19.cloned.1.call-done) | copy-start | bytes 1572868
  853.9 63.5 %all-gather.41.cloned.1.call-start = ((), (), s32[]{:S(2)}) async-start(), calls=%async_computation.35 | async-start | bytes 2621440 | tf_op jit(solution)/shard_map/all_gather | solution.py:62
  894.2 108.4 %reduce-scatter.33.cloned.1.call-start = ((), (), s32[]{:S(2)}) async-start(), calls=%async_computation.36 | async-start | bytes 2621440 | tf_op jit(solution)/shard_map/reduce_scatter | solution.py:66
  946.4 101.9 %reduce-scatter.41.cloned.1.call-start = ((), (), s32[]{:S(2)}) async-start(), calls=%async_computation.42 | async-start | bytes 2359296 | tf_op jit(solution)/shard_map/reduce_scatter | solution.py:66
  952.6 162.8 %reduce-scatter.39.cloned.1.call-start = ((), (), s32[]{:S(2)}) async-start(), calls=%async_computation.41 | async-start | bytes 1769472 | tf_op jit(solution)/shard_map/reduce_scatter | solution.py:66
  957.8 222.9 %reduce-scatter.45.cloned.1.call-start = ((), (), s32[]{:S(2)}) async-start(), calls=%async_computation.44 | async-start | bytes 589824 | tf_op jit(solution)/shard_map/reduce_scatter | solution.py:66
  961.0 290.4 %reduce-scatter.37.cloned.1.call-start = ((), (), s32[]{:S(2)}) async-start(), calls=%async_computation.40 | async-start | bytes 2359296 | tf_op jit(solution)/shard_map/reduce_scatter | solution.py:66
  967.2 350.7 %reduce-scatter.35.cloned.1.call-start = ((), (), s32[]{:S(2)}) async-start(), calls=%async_computation.39 | async-start | bytes 1769472 | tf_op jit(solution)/shard_map/reduce_scatter | solution.py:66
  972.3 410.9 %reduce-scatter.43.cloned.1.call-start = ((), (), s32[]{:S(2)}) async-start(), calls=%async_computation.43 | async-start | bytes 589824 | tf_op jit(solution)/shard_map/reduce_scatter | solution.py:66
  975.5 478.6 %reduce-scatter.49.cloned.1.call-start = ((), (), s32[]{:S(2)}) async-start(), calls=%async_computation.46 | async-start | bytes 2359296 | tf_op jit(solution)/shard_map/reduce_scatter | solution.py:66
  983.0 541.2 %reduce-scatter.47.cloned.1.call-start = ((), (), s32[]{:S(2)}) async-start(), calls=%async_computation.45 | async-start | bytes 2359296 | tf_op jit(solution)/shard_map/reduce_scatter | solution.py:66
  990.0 592.2 %all-gather.43.cloned.1.call-start = ((), (), s32[]{:S(2)}) async-start(), calls=%async_computation.37 | async-start | bytes 1622016 | tf_op jit(solution)/shard_map/all_gather | solution.py:62
  1016.0 170.4 %copy-start.72 = (f32[1,16]{1,0:T(1,128)S(1)}, f32[1,16]{1,0:T(1,128)}, u32[]{:S(2)}) copy-start(f32[1,16]{1,0:T(1,128)} %copy-done.71) | copy-start | bytes 196
  1016.0 170.4 %copy-start.74 = (f32[1,16]{1,0:T(1,128)S(1)}, f32[1,16]{1,0:T(1,128)}, u32[]{:S(2)}) copy-start(f32[1,16]{1,0:T(1,128)} %copy-done.73) | copy-start | bytes 196
  1117.2 67.6 %all-to-all-start.4 = ((bf16[4,32,1792]{2,1,0:T(8,128)(2,1)}), bf16[4,32,1792]{2,1,0:T(8,128)(2,1)S(1)}, u32[]{:S(2)}, u32[]{:S(2)}) async-start(bf16[4,32,1792]{2,1,0:T(8,128)(2,1)} %bitcast.75), calls=%async_computation.16 | async-start | bytes 917504 | tf_op jit(solution)/shard_map/all_to_all | solution.py:270
  1123.4 516.3 %all-gather.45.cloned.1.call-start = ((), (), s32[]{:S(2)}) async-start(), calls=%async_computation.38 | async-start | bytes 1622016 | tf_op jit(solution)/shard_map/all_gather | solution.py:62
  1180.8 386.2 %collective-permute-start.2 = (bf16[32,1024]{1,0:T(8,128)(2,1)}, bf16[32,1024]{1,0:T(8,128)(2,1)S(1)}, u32[]{:S(2)}, u32[]{:S(2)}) collective-permute-start(bf16[32,1024]{1,0:T(8,128)(2,1)} %reduce-scatter.45.cloned.1.call-done), channel_id=1, source_target_pairs={{0,0},{4,1},{8,2},{12,3},{16,4},{20,5},{24,6},{28,7},{1,8},{5,9},{... | collective-permute-start | bytes 196616 | tf_op jit(solution)/shard_map/ppermute | solution.py:275
  1319.7 248.0 %all-to-all-start.3 = ((bf16[4,32,1792]{2,1,0:T(8,128)(2,1)}), bf16[4,32,1792]{2,1,0:T(8,128)(2,1)S(1)}, u32[]{:S(2)}, u32[]{:S(2)}) async-start(bf16[4,32,1792]{2,1,0:T(8,128)(2,1)} %bitcast.73), calls=%async_computation.13 | async-start | bytes 917504 | tf_op jit(solution)/shard_map/all_to_all | solution.py:270
  1383.3 183.7 %collective-permute-start.1 = (bf16[32,1024]{1,0:T(8,128)(2,1)}, bf16[32,1024]{1,0:T(8,128)(2,1)S(1)}, u32[]{:S(2)}, u32[]{:S(2)}) collective-permute-start(bf16[32,1024]{1,0:T(8,128)(2,1)} %reduce-scatter.43.cloned.1.call-done), channel_id=1, source_target_pairs={{0,0},{4,1},{8,2},{12,3},{16,4},{20,5},{24,6},{28,7},{1,8},{5,9},{... | collective-permute-start | bytes 196616 | tf_op jit(solution)/shard_map/ppermute | solution.py:275
  1524.1 47.4 %copy-start.19 = (f32[256,1024]{1,0:T(8,128)S(1)}, f32[256,1024]{1,0:T(8,128)}, u32[]{:S(2)}) copy-start(f32[256,1024]{1,0:T(8,128)} %copy-done.18) | copy-start | bytes 3145732
  1524.1 47.4 %copy-start.29 = (f32[256,1024]{1,0:T(8,128)S(1)}, f32[256,1024]{1,0:T(8,128)}, u32[]{:S(2)}) copy-start(f32[256,1024]{1,0:T(8,128)} %get-tuple-element.26) | copy-start | bytes 3145732
  1584.6 57.6 %copy-start.34 = (bf16[2,32,6144]{2,1,0:T(8,128)(2,1)S(1)}, bf16[2,32,6144]{2,1,0:T(8,128)(2,1)}, u32[]{:S(2)}) copy-start(bf16[2,32,6144]{2,1,0:T(8,128)(2,1)} %param.23) | copy-start | bytes 2359300
  1643.9 41.7 %copy-start.70 = (s32[96]{0:T(128)S(1)}, s32[96]{0:T(128)}, u32[]{:S(2)}) copy-start(s32[96]{0:T(128)} %copy-done.69) | copy-start | bytes 1156
  (66 other events, 344.6 us)
Sparse Core Ops, SparseCore 0:
  63.6 45.6 all-gather.46
  111.5 29.2 all-gather.26
  162.5 37.3 reduce-scatter.18
  202.7 48.1 all-gather.48
  253.0 22.5 all-gather.28
  278.4 47.7 all-gather.50
  333.2 31.0 reduce-scatter.20
  366.4 45.2 all-gather.52
  413.8 23.0 all-gather.30
  459.3 31.0 reduce-scatter.22
  492.7 48.1 all-gather.54
  543.0 22.5 all-gather.32
  568.5 47.7 all-gather.56
  618.4 22.5 all-gather.34
  654.4 31.0 reduce-scatter.26
  687.8 31.4 reduce-scatter.24
  726.3 22.9 all-gather.36
  778.5 31.0 reduce-scatter.28
  817.7 22.9 all-gather.38
  854.0 31.0 reduce-scatter.30
  894.3 22.9 all-gather.40
  946.6 31.0 reduce-scatter.32
  981.2 67.1 reduce-scatter.40
  1052.2 63.1 reduce-scatter.38
  1119.7 61.0 reduce-scatter.44
  1184.2 67.2 reduce-scatter.36
  1254.7 63.1 reduce-scatter.34
  1322.2 61.0 reduce-scatter.42
  1386.8 67.2 reduce-scatter.48
  1457.5 66.5 reduce-scatter.46
  1527.0 55.1 all-gather.42
  1585.7 53.9 all-gather.44

commit v2 on v1

v2 whole, which is shorter than its diff:
```python
from functools import partial

import jax
import jax.numpy as jnp
from jax import lax
from jax.experimental import pallas as pl
from jax.experimental.pallas import tpu as pltpu
from jax.sharding import PartitionSpec as P

patch_areas = (1, 4, 9, 16, 25, 36, 64, 100, 169)
scale_starts = (1, 5, 14, 30, 55, 91, 155, 255)
f32 = jnp.float32
bf16 = jnp.bfloat16
MESH = pl.DeviceIdType.MESH
TILE = 256
HALF = 128
STEP = 32


def token_meta(stops, length):
    areas = jnp.array(patch_areas, dtype=jnp.int32)
    levels = jnp.arange(9, dtype=jnp.int32)
    counts = jnp.sum(jnp.where(levels[None, :] < stops[:, None], areas[None, :], 0), axis=1)
    ends = jnp.cumsum(counts)
    places = jnp.arange(length, dtype=jnp.int32)
    passed = places[:, None] >= ends[None, :]
    item = jnp.sum(passed.astype(jnp.int32), axis=1)
    begin = jnp.sum(jnp.where(passed, counts[None, :], 0), axis=1)
    inner = places - begin
    bounds = jnp.array(scale_starts, dtype=jnp.int32)
    level = jnp.sum((inner[:, None] >= bounds[None, :]).astype(jnp.int32), axis=1)
    level = jnp.where(item == stops.shape[0], 0, level)
    return (item, level)


def mm(left, right):
    return jnp.dot(left, right, preferred_element_type=f32)


def mm_t(left, right):
    return lax.dot_general(left, right, (((1,), (1,)), ((), ())), preferred_element_type=f32)


def rows_mm(left, right, precision=None):
    return lax.dot_general(
        left, right, (((0,), (0,)), ((), ())), precision=precision, preferred_element_type=f32
    )


def gather(values, axes):
    return lax.all_gather(values, axes, axis=0, tiled=True)


def scatter(values, axes):
    return lax.psum_scatter(values, axes, scatter_dimension=0, tiled=True)


def partners():
    d, b = lax.axis_index("dp"), lax.axis_index("blk")
    return (d, b + 1 - 2 * (b % 2)), (d, (b + 2) % 4)


def greet(sibling, peer):
    barrier = pltpu.get_barrier_semaphore()
    for other in (sibling, peer):
        pl.semaphore_signal(barrier, inc=1, device_id=other, device_id_type=MESH)
    pl.semaphore_wait(barrier, 2)


def remote(src, dst, send, recv, target):
    return pltpu.make_async_remote_copy(
        src_ref=src, dst_ref=dst, send_sem=send, recv_sem=recv, device_id=target, device_id_type=MESH
    )


class Spread:
    def __init__(self, buf, send, recv, sibling, peer):
        def copy(src, dst, k, target):
            return remote(
                buf.at[pl.ds(src, HALF)], buf.at[pl.ds(dst, HALF)], send.at[k], recv.at[k], target
            )

        self.to_peer = [copy(HALF * c, 2 * TILE + TILE * c, c, peer) for c in range(2)]
        self.to_sibling = [copy(HALF * c, TILE + HALF * c, 2 + c, sibling) for c in range(2)]
        self.forward = [
            copy(2 * TILE + TILE * c, 2 * TILE + TILE * c + HALF, 4 + c, sibling) for c in range(2)
        ]

    def start(self, c):
        self.to_peer[c].start()
        self.to_sibling[c].start()

    def wait_block(self, i):
        @pl.when(i == 1)
        def _():
            for c in range(2):
                self.to_sibling[c].wait_recv()

        for c in range(2):

            @pl.when(i == 2 + c)
            def _():
                self.to_peer[c].wait_recv()
                self.forward[c].start()
                self.forward[c].wait_recv()

    def finish(self):
        for c in range(2):
            self.to_peer[c].wait_send()
            self.to_sibling[c].wait_send()
            self.forward[c].wait_send()


class Collect:
    def __init__(self, parts, out, mid, own, far, send, recv, sibling, peer):
        self.parts, self.out, self.mid, self.own, self.far = parts, out, mid, own, far
        self.cross = [
            remote(
                parts.at[pl.ds(2 * TILE + TILE * c + HALF, HALF)],
                mid.at[pl.ds(HALF * c, HALF)],
                send.at[c],
                recv.at[c],
                sibling,
            )
            for c in range(2)
        ]
        self.over = [
            remote(
                out.at[pl.ds(HALF * c, HALF)],
                far.at[pl.ds(HALF * c, HALF)],
                send.at[2 + c],
                recv.at[2 + c],
                peer,
            )
            for c in range(2)
        ]
        self.home = remote(parts.at[pl.ds(TILE, TILE)], own, send.at[4], recv.at[4], sibling)

    def block_done(self, j):
        for c in range(2):

            @pl.when(j == 2 + c)
            def _():
                self.cross[c].start()
                self.cross[c].wait_recv()

                @pl.loop(0, HALF // STEP)
                def _(s):
                    at = pl.multiple_of(s * STEP, STEP)
                    mine = self.parts[pl.ds(2 * TILE + TILE * c + at, STEP), :].astype(f32)
                    theirs = self.mid[pl.ds(HALF * c + at, STEP), :].astype(f32)
                    self.out[pl.ds(HALF * c + at, STEP), :] = (mine + theirs).astype(bf16)

                self.over[c].start()

        @pl.when(j == 1)
        def _():
            self.home.start()

    def wait(self):
        self.home.wait_recv()
        for c in range(2):
            self.over[c].wait_recv()

    def rows(self, at):
        span = pl.ds(at, STEP)
        total = self.parts[span, :].astype(f32) + self.own[span, :].astype(f32)
        return total + self.far[span, :].astype(f32)

    def finish(self):
        self.home.wait_send()
        for c in range(2):
            self.cross[c].wait_send()
            self.over[c].wait_send()


def spread_scratch(width):
    return [
        pltpu.VMEM((4 * TILE, width), bf16),
        pltpu.SemaphoreType.DMA((6,)),
        pltpu.SemaphoreType.DMA((6,)),
    ]


def collect_scratch(width):
    return [pltpu.VMEM((4 * TILE, width), bf16)] + [pltpu.VMEM((TILE, width), bf16)] * 4 + [
        pltpu.SemaphoreType.DMA((5,)),
        pltpu.SemaphoreType.DMA((5,)),
    ]


class Moves:
    def __init__(self, sems):
        self.sems, self.used = sems, 0

    def copy(self, src, dst):
        made = pltpu.make_async_copy(src, dst, self.sems.at[self.used])
        self.used += 1
        made.start()
        return made


def expand(onehot, ada, which, outs):
    width = outs[0].shape[1]
    for k, out in zip(which, outs):
        for n in range(0, width, TILE):
            out[:, n : n + TILE] = mm(onehot[...], ada[:, k * width + n : k * width + n + TILE])


def normed(values):
    centre = jnp.mean(values, axis=-1, keepdims=True)
    centred = values - centre
    spread = jnp.mean(centred * centred, axis=-1, keepdims=True)
    rate = lax.rsqrt(spread + 1e-06)
    return centred * rate, rate


def norm_back(grad, values_hat, rate):
    first = jnp.mean(grad, axis=-1, keepdims=True)
    second = jnp.mean(grad * values_hat, axis=-1, keepdims=True)
    return rate * (grad - first - values_hat * second)


def row_steps(start, rows, body):
    @pl.loop(0, rows // STEP)
    def _(s):
        body(pl.multiple_of(start + s * STEP, STEP))


def block_ones(size):
    shape = (TILE, TILE)
    one = lax.broadcasted_iota(jnp.int32, shape, 0) // size
    two = lax.broadcasted_iota(jnp.int32, shape, 1) // size
    return (one == two).astype(bf16)


def split_mm(dot, values, ones):
    high = values.astype(bf16)
    low = (values - high.astype(f32)).astype(bf16)
    return dot(high, ones) + dot(low, ones)


def head_lanes(values, h, size):
    lane = lax.broadcasted_iota(jnp.int32, values.shape, 1) // size
    return jnp.where(lane == h, values, jnp.zeros_like(values))


def hidden_bias(keyc, keyr, rows, cols):
    keys = keyc[pl.ds(rows, TILE), :]
    top = keyr[cols]
    low = top - top % 16
    return jnp.where((keys >= low) & (keys <= top), 0.0, -1e30)


def attend_kernel(
    size,
    x,
    onehot,
    ada,
    qscale,
    keyc,
    keyr,
    wqkv_in,
    wproj_in,
    h_out,
    qkv_out,
    rate_out,
    o_out,
    inv_out,
    branch_out,
    mid_out,
    wqkv,
    wproj,
    qkv,
    vt,
    rates,
    gamma,
    scale,
    shift,
    moves,
    hbuf,
    ag_send,
    ag_recv,
    parts,
    out,
    mid,
    own,
    far,
    rs_send,
    rs_recv,
):
    sibling, peer = partners()
    mover = Moves(moves)
    load_qkv = mover.copy(wqkv_in, wqkv)
    load_proj = mover.copy(wproj_in, wproj)
    expand(onehot, ada, (0, 2, 4), (gamma, scale, shift))
    greet(sibling, peer)
    spread = Spread(hbuf, ag_send, ag_recv, sibling, peer)
    collect = Collect(parts, out, mid, own, far, rs_send, rs_recv, sibling, peer)

    def modulated(at):
        span = pl.ds(at, STEP)
        hat, _ = normed(x[span, :])
        hbuf[span, :] = (hat * (1.0 + scale[span, :]) + shift[span, :]).astype(bf16)

    for c in range(2):
        row_steps(HALF * c, HALF, modulated)
        spread.start(c)
    load_qkv.wait()
    ones = block_ones(size)

    @pl.loop(0, 4)
    def _(i):
        spread.wait_block(i)
        span = pl.ds(pl.multiple_of(i * TILE, TILE), TILE)
        h = hbuf[span, :]
        for part in range(3):
            columns = slice(part * TILE, (part + 1) * TILE)
            value = mm(h, wqkv[:, columns])
            if part < 2:
                rate = lax.rsqrt(split_mm(mm, value * value, ones) + 1e-06)
                if part == 0:
                    rate = rate * qscale[...]
                rates[span, columns] = rate
                value = value * rate
            else:
                vt[:, span] = value.T.astype(bf16)
            qkv[span, columns] = value.astype(bf16)

    save_h = mover.copy(hbuf, h_out)
    save_qkv = mover.copy(qkv, qkv_out)
    save_rates = mover.copy(rates, rate_out)
    load_proj.wait()
    heads = TILE // size

    @pl.loop(0, 4)
    def _(i):
        j = (i + 2) % 4
        span = pl.ds(pl.multiple_of(j * TILE, TILE), TILE)
        queries = [head_lanes(qkv[span, 0:TILE], h, size) for h in range(heads)]
        sums = [jnp.zeros((1, TILE), f32)] * heads
        mixed = [jnp.zeros((size, TILE), f32)] * heads
        for k in range(4):
            keys = qkv[k * TILE : (k + 1) * TILE, TILE : 2 * TILE]
            bias = hidden_bias(keyc, keyr, k * TILE, j)
            for h in range(heads):
                grown = jnp.exp(mm_t(keys, queries[h]) + bias)
                sums[h] = sums[h] + jnp.sum(grown, axis=0, keepdims=True)
                mixed[h] = mixed[h] + mm(
                    vt[h * size : (h + 1) * size, k * TILE : (k + 1) * TILE], grown.astype(bf16)
                )
        inverse = [1.0 / one for one in sums]
        for h in range(heads):
            inv_out[j, h : h + 1, :] = inverse[h]
        whole = jnp.concatenate([mixed[h] * inverse[h] for h in range(heads)], axis=0)
        low = whole.T.astype(bf16)
        o_out[span, :] = low
        for n in range(0, parts.shape[1], TILE):
            parts[span, n : n + TILE] = mm(low, wproj[:, n : n + TILE]).astype(bf16)
        collect.block_done(j)

    collect.wait()

    def added(at):
        span = pl.ds(at, STEP)
        branch = collect.rows(at)
        branch_out[span, :] = branch
        mid_out[span, :] = x[span, :] + gamma[span, :] * branch

    row_steps(0, TILE, added)
    spread.finish()
    collect.finish()
    for one in (save_h, save_qkv, save_rates):
        one.wait()


def mlp_kernel(
    x,
    onehot,
    ada,
    wup_in,
    wdown_in,
    h_out,
    g_out,
    slope_out,
    result_out,
    x_out,
    wup,
    wdown,
    hidden,
    slope,
    gamma,
    scale,
    shift,
    moves,
    hbuf,
    ag_send,
    ag_recv,
    parts,
    out,
    mid,
    own,
    far,
    rs_send,
    rs_recv,
):
    sibling, peer = partners()
    mover = Moves(moves)
    load_up = mover.copy(wup_in, wup)
    load_down = mover.copy(wdown_in, wdown)
    expand(onehot, ada, (1, 3, 5), (gamma, scale, shift))
    greet(sibling, peer)
    spread = Spread(hbuf, ag_send, ag_recv, sibling, peer)
    collect = Collect(parts, out, mid, own, far, rs_send, rs_recv, sibling, peer)

    def modulated(at):
        span = pl.ds(at, STEP)
        hat, _ = normed(x[span, :])
        hbuf[span, :] = (hat * (1.0 + scale[span, :]) + shift[span, :]).astype(bf16)

    for c in range(2):
        row_steps(HALF * c, HALF, modulated)
        spread.start(c)
    load_up.wait()
    load_down.wait()

    @pl.loop(0, 4)
    def _(i):
        spread.wait_block(i)
        span = pl.ds(pl.multiple_of(i * TILE, TILE), TILE)
        h = hbuf[span, :]
        for n in range(0, wup.shape[1], TILE):
            columns = slice(n, n + TILE)
            up = mm(h, wup[:, columns])
            square = up * up
            bent = jnp.tanh(0.7978845608 * (up * (1.0 + 0.044715 * square)))
            half = 0.5 * (1.0 + bent)
            hidden[span, columns] = (up * half).astype(bf16)
            inner = 0.7978845608 + (3.0 * 0.044715 * 0.7978845608) * square
            slope[span, columns] = (half + 0.5 * up * (1.0 - bent * bent) * inner).astype(bf16)
        g = hidden[span, :]
        for n in range(0, parts.shape[1], TILE):
            parts[span, n : n + TILE] = mm(g, wdown[:, n : n + TILE]).astype(bf16)
        collect.block_done(i)

    saves = [mover.copy(a, b) for a, b in ((hbuf, h_out), (hidden, g_out), (slope, slope_out))]
    collect.wait()

    def added(at):
        span = pl.ds(at, STEP)
        result = collect.rows(at)
        result_out[span, :] = result
        x_out[span, :] = x[span, :] + gamma[span, :] * result

    row_steps(0, TILE, added)
    spread.finish()
    collect.finish()
    for one in saves:
        one.wait()


def item_sums(onehot_t, terms, out):
    for k, term in enumerate(terms):
        width = term.shape[1]
        out[:, k * width : (k + 1) * width] = mm(onehot_t[...], term[...])


def mlp_back_kernel(
    dx,
    result,
    mid_state,
    onehot,
    onehot_t,
    ada,
    wup_in,
    wdown_in,
    h_in,
    g_in,
    slope_in,
    dmid_out,
    dwup_out,
    dwdown_out,
    items_out,
    wup,
    wdown,
    hall,
    gall,
    slope,
    dwup,
    dwdown,
    dgamma,
    dscale,
    dshift,
    gamma,
    scale,
    moves,
    hbuf,
    ag_send,
    ag_recv,
    parts,
    out,
    mid,
    own,
    far,
    rs_send,
    rs_recv,
):
    sibling, peer = partners()
    mover = Moves(moves)
    load_down = mover.copy(wdown_in, wdown)
    load_slope = mover.copy(slope_in, slope)
    load_up = mover.copy(wup_in, wup)
    load_g = mover.copy(g_in, gall)
    load_h = mover.copy(h_in, hall)
    expand(onehot, ada, (1, 3), (gamma, scale))
    greet(sibling, peer)
    spread = Spread(hbuf, ag_send, ag_recv, sibling, peer)
    collect = Collect(parts, out, mid, own, far, rs_send, rs_recv, sibling, peer)

    def scaled(at):
        span = pl.ds(at, STEP)
        hbuf[span, :] = (gamma[span, :] * dx[span, :]).astype(bf16)

    for c in range(2):
        row_steps(HALF * c, HALF, scaled)
        spread.start(c)
    for one in (load_down, load_slope, load_up):
        one.wait()

    @pl.loop(0, 4)
    def _(i):
        spread.wait_block(i)
        span = pl.ds(pl.multiple_of(i * TILE, TILE), TILE)
        dm = hbuf[span, :]
        for n in range(0, slope.shape[1], TILE):
            columns = slice(n, n + TILE)
            dg = mm_t(dm, wdown[columns, :])
            slope[span, columns] = (dg * slope[span, columns].astype(f32)).astype(bf16)
        du = slope[span, :]
        for n in range(0, parts.shape[1], TILE):
            parts[span, n : n + TILE] = mm_t(du, wup[n : n + TILE, :]).astype(bf16)
        collect.block_done(i)

    load_g.wait()
    load_h.wait()

    @pl.loop(0, gall.shape[1] // TILE)
    def _(k):
        columns = pl.ds(pl.multiple_of(k * TILE, TILE), TILE)
        for n in range(0, hbuf.shape[1], 2 * TILE):
            dwdown[columns, n : n + 2 * TILE] = rows_mm(
                gall[:, columns], hbuf[:, n : n + 2 * TILE]
            ).astype(bf16)

    save_down = mover.copy(dwdown, dwdown_out)

    @pl.loop(0, hall.shape[1] // TILE)
    def _(k):
        columns = pl.ds(pl.multiple_of(k * TILE, TILE), TILE)
        for n in range(0, slope.shape[1], 2 * TILE):
            dwup[columns, n : n + 2 * TILE] = rows_mm(
                hall[:, columns], slope[:, n : n + 2 * TILE]
            ).astype(bf16)

    save_up = mover.copy(dwup, dwup_out)
    collect.wait()

    def added(at):
        span = pl.ds(at, STEP)
        dh = collect.rows(at)
        hat, rate = normed(mid_state[span, :])
        grad = dx[span, :]
        dgamma[span, :] = (grad * result[span, :]).astype(bf16)
        dscale[span, :] = (dh * hat).astype(bf16)
        dshift[span, :] = dh.astype(bf16)
        dmid_out[span, :] = grad + norm_back(dh * (1.0 + scale[span, :]), hat, rate)

    row_steps(0, TILE, added)
    item_sums(onehot_t, (dgamma, dscale, dshift), items_out)
    spread.finish()
    collect.finish()
    save_down.wait()
    save_up.wait()


def attend_back_kernel(
    size,
    dmid,
    branch,
    x,
    onehot,
    onehot_t,
    ada,
    qscale,
    keyc,
    keyr,
    inverse,
    wqkv_in,
    wproj_in,
    h_in,
    qkv_in,
    rate_in,
    o_in,
    dx_out,
    dwqkv_out,
    dwproj_out,
    items_out,
    head_out,
    wqkv,
    wproj,
    hall,
    qkv,
    rates,
    oall,
    kt,
    dkeys,
    dvalues,
    dqkv,
    dwqkv,
    dwproj,
    dgamma,
    dscale,
    dshift,
    gamma,
    scale,
    moves,
    hbuf,
    ag_send,
    ag_recv,
    parts,
    out,
    mid,
    own,
    far,
    rs_send,
    rs_recv,
):
    sibling, peer = partners()
    mover = Moves(moves)
    load_proj = mover.copy(wproj_in, wproj)
    load_qkv = mover.copy(qkv_in, qkv)
    load_o = mover.copy(o_in, oall)
    load_rates = mover.copy(rate_in, rates)
    load_w = mover.copy(wqkv_in, wqkv)
    load_h = mover.copy(h_in, hall)
    expand(onehot, ada, (0, 2), (gamma, scale))
    greet(sibling, peer)
    spread = Spread(hbuf, ag_send, ag_recv, sibling, peer)
    collect = Collect(parts, out, mid, own, far, rs_send, rs_recv, sibling, peer)

    def scaled(at):
        span = pl.ds(at, STEP)
        hbuf[span, :] = (gamma[span, :] * dmid[span, :]).astype(bf16)

    for c in range(2):
        row_steps(HALF * c, HALF, scaled)
        spread.start(c)
    for one in (load_proj, load_qkv, load_o, load_rates):
        one.wait()
    heads = TILE // size
    ones = block_ones(size)
    inv_square = 1.0 / (qscale[...] * qscale[...])
    select = (
        lax.broadcasted_iota(jnp.int32, (8, TILE), 1) // size
        == lax.broadcasted_iota(jnp.int32, (8, TILE), 0)
    ).astype(bf16)
    dkeys[...] = jnp.zeros_like(dkeys)
    dvalues[...] = jnp.zeros_like(dvalues)
    head_out[...] = jnp.zeros_like(head_out)
    for k in range(4):
        rows = slice(k * TILE, (k + 1) * TILE)
        kt[:, rows] = qkv[rows, TILE : 2 * TILE].astype(f32).T.astype(bf16)

    @pl.loop(0, 4)
    def _(i):
        spread.wait_block(i)
        span = pl.ds(pl.multiple_of(i * TILE, TILE), TILE)
        dout = mm_t(hbuf[span, :], wproj[...]).astype(bf16)
        product = dout.astype(f32) * oall[span, :].astype(f32)
        row_term = split_mm(lambda a, b: mm_t(b, a), product, select)
        q_low = qkv[span, 0:TILE]
        queries = [head_lanes(q_low, h, size) for h in range(heads)]
        douts = [head_lanes(dout, h, size) for h in range(heads)]
        dquery = [jnp.zeros((size, TILE), f32)] * heads
        for k in range(4):
            rows = slice(k * TILE, (k + 1) * TILE)
            keys = qkv[rows, TILE : 2 * TILE]
            values = qkv[rows, 2 * TILE : 3 * TILE]
            bias = hidden_bias(keyc, keyr, k * TILE, i)
            dkey = jnp.zeros((TILE, TILE), f32)
            dvalue = jnp.zeros((TILE, TILE), f32)
            for h in range(heads):
                share = jnp.exp(mm_t(keys, queries[h]) + bias) * inverse[i, h : h + 1, :]
                dshare = mm_t(values, douts[h])
                dscore = (share * (dshare - row_term[h : h + 1, :])).astype(bf16)
                dvalue = dvalue + mm(share.astype(bf16), douts[h])
                dkey = dkey + mm(dscore, queries[h])
                dquery[h] = dquery[h] + mm(kt[h * size : (h + 1) * size, rows], dscore)
            dkeys[rows, :] += dkey
            dvalues[rows, :] += dvalue
        dq = jnp.concatenate(dquery, axis=0).T
        qhat = q_low.astype(f32)
        along = split_mm(mm, dq * qhat, ones)
        head_out[...] += jnp.sum(along, axis=0, keepdims=True)
        dqkv[span, 0:TILE] = (rates[span, 0:TILE] * (dq - qhat * (along * inv_square))).astype(bf16)

    load_w.wait()

    @pl.loop(0, 4)
    def _(i):
        j = (i + 2) % 4
        span = pl.ds(pl.multiple_of(j * TILE, TILE), TILE)
        dk = dkeys[span, :]
        khat = qkv[span, TILE : 2 * TILE].astype(f32)
        along = split_mm(mm, dk * khat, ones)
        dqkv[span, TILE : 2 * TILE] = (
            rates[span, TILE : 2 * TILE] * (dk - khat * along)
        ).astype(bf16)
        dqkv[span, 2 * TILE : 3 * TILE] = dvalues[span, :].astype(bf16)
        low = dqkv[span, :]
        for n in range(0, parts.shape[1], TILE):
            parts[span, n : n + TILE] = mm_t(low, wqkv[n : n + TILE, :]).astype(bf16)
        collect.block_done(j)

    for n in range(0, hbuf.shape[1], 2 * TILE):
        dwproj[:, n : n + 2 * TILE] = rows_mm(oall[...], hbuf[:, n : n + 2 * TILE]).astype(bf16)
    save_proj = mover.copy(dwproj, dwproj_out)
    load_h.wait()

    @pl.loop(0, hall.shape[1] // TILE)
    def _(k):
        columns = pl.ds(pl.multiple_of(k * TILE, TILE), TILE)
        dwqkv[columns, :] = rows_mm(hall[:, columns], dqkv[...]).astype(bf16)

    save_w = mover.copy(dwqkv, dwqkv_out)
    collect.wait()

    def added(at):
        span = pl.ds(at, STEP)
        dh = collect.rows(at)
        hat, rate = normed(x[span, :])
        grad = dmid[span, :]
        dgamma[span, :] = (grad * branch[span, :]).astype(bf16)
        dscale[span, :] = (dh * hat).astype(bf16)
        dshift[span, :] = dh.astype(bf16)
        dx_out[span, :] = grad + norm_back(dh * (1.0 + scale[span, :]), hat, rate)

    row_steps(0, TILE, added)
    item_sums(onehot_t, (dgamma, dscale, dshift), items_out)
    spread.finish()
    collect.finish()
    save_proj.wait()
    save_w.wait()


ANY = pl.BlockSpec(memory_space=pl.ANY)
VMEM = pl.BlockSpec(memory_space=pltpu.VMEM)


def shaped(*shape, dtype=f32):
    return jax.ShapeDtypeStruct(shape, dtype)


def run(kernel, ident, inputs, outs, scratch, flops):
    return pl.pallas_call(
        kernel,
        out_shape=[one for one, _ in outs],
        in_specs=[where for _, where in inputs],
        out_specs=[where for _, where in outs],
        scratch_shapes=scratch,
        compiler_params=pltpu.CompilerParams(
            collective_id=ident, has_side_effects=True, vmem_limit_bytes=56 * 2**20
        ),
        cost_estimate=pl.CostEstimate(flops=flops, bytes_accessed=2**24, transcendentals=0),
    )(*[one for one, _ in inputs])


def attend(layer, size, x, onehot, ada, qscale, keyc, keyr, wqkv, wproj):
    rows, width = x.shape
    length, wide = wqkv.shape
    big = pltpu.VMEM((rows, width), f32)
    return run(
        partial(attend_kernel, size),
        layer,
        [(a, VMEM) for a in (x, onehot, ada, qscale, keyc, keyr)] + [(wqkv, ANY), (wproj, ANY)],
        [
            (shaped(length, width, dtype=bf16), ANY),
            (shaped(length, wide, dtype=bf16), ANY),
            (shaped(length, 2 * TILE), ANY),
            (shaped(length, TILE, dtype=bf16), VMEM),
            (shaped(4, 8, TILE), VMEM),
            (shaped(rows, width), VMEM),
            (shaped(rows, width), VMEM),
        ],
        [
            pltpu.VMEM(wqkv.shape, bf16),
            pltpu.VMEM(wproj.shape, bf16),
            pltpu.VMEM((length, wide), bf16),
            pltpu.VMEM((TILE, length), bf16),
            pltpu.VMEM((length, 2 * TILE), f32),
            big,
            big,
            big,
            pltpu.SemaphoreType.DMA((5,)),
        ]
        + spread_scratch(width)
        + collect_scratch(width),
        2**35,
    )


def mlp(layer, x, onehot, ada, wup, wdown):
    rows, width = x.shape
    length, ff = 4 * rows, wup.shape[1]
    big = pltpu.VMEM((rows, width), f32)
    return run(
        mlp_kernel,
        2 + layer,
        [(a, VMEM) for a in (x, onehot, ada)] + [(wup, ANY), (wdown, ANY)],
        [
            (shaped(length, width, dtype=bf16), ANY),
            (shaped(length, ff, dtype=bf16), ANY),
            (shaped(length, ff, dtype=bf16), ANY),
            (shaped(rows, width), VMEM),
            (shaped(rows, width), VMEM),
        ],
        [
            pltpu.VMEM(wup.shape, bf16),
            pltpu.VMEM(wdown.shape, bf16),
            pltpu.VMEM((length, ff), bf16),
            pltpu.VMEM((length, ff), bf16),
            big,
            big,
            big,
            pltpu.SemaphoreType.DMA((5,)),
        ]
        + spread_scratch(width)
        + collect_scratch(width),
        2**35,
    )


def mlp_back(layer, dx, result, mid, onehot, onehot_t, ada, wup, wdown, h, g, slope):
    rows, width = dx.shape
    length, ff = 4 * rows, wup.shape[1]
    big = pltpu.VMEM((rows, width), f32)
    small = pltpu.VMEM((rows, width), bf16)
    return run(
        mlp_back_kernel,
        4 + layer,
        [(a, VMEM) for a in (dx, result, mid, onehot, onehot_t, ada)]
        + [(a, ANY) for a in (wup, wdown, h, g, slope)],
        [
            (shaped(rows, width), VMEM),
            (shaped(*wup.shape, dtype=bf16), ANY),
            (shaped(*wdown.shape, dtype=bf16), ANY),
            (shaped(onehot_t.shape[0], 3 * width), VMEM),
        ],
        [
            pltpu.VMEM(wup.shape, bf16),
            pltpu.VMEM(wdown.shape, bf16),
            pltpu.VMEM((length, width), bf16),
            pltpu.VMEM((length, ff), bf16),
            pltpu.VMEM((length, ff), bf16),
            pltpu.VMEM(wup.shape, bf16),
            pltpu.VMEM(wdown.shape, bf16),
            small,
            small,
            small,
            big,
            big,
            pltpu.SemaphoreType.DMA((7,)),
        ]
        + spread_scratch(width)
        + collect_scratch(width),
        2**35,
    )


def attend_back(
    layer, size, dmid, branch, x, onehot, onehot_t, ada, qscale, keyc, keyr, inverse, wqkv, wproj, h, qkv, rates, o
):
    rows, width = dmid.shape
    length, wide = qkv.shape
    big = pltpu.VMEM((rows, width), f32)
    small = pltpu.VMEM((rows, width), bf16)
    return run(
        partial(attend_back_kernel, size),
        6 + layer,
        [(a, VMEM) for a in (dmid, branch, x, onehot, onehot_t, ada, qscale, keyc, keyr, inverse)]
        + [(a, ANY) for a in (wqkv, wproj, h, qkv, rates, o)],
        [
            (shaped(rows, width), VMEM),
            (shaped(*wqkv.shape, dtype=bf16), ANY),
            (shaped(*wproj.shape, dtype=bf16), ANY),
            (shaped(onehot_t.shape[0], 3 * width), VMEM),
            (shaped(1, TILE), VMEM),
        ],
        [
            pltpu.VMEM(wqkv.shape, bf16),
            pltpu.VMEM(wproj.shape, bf16),
            pltpu.VMEM((length, width), bf16),
            pltpu.VMEM((length, wide), bf16),
            pltpu.VMEM((length, 2 * TILE), f32),
            pltpu.VMEM((length, TILE), bf16),
            pltpu.VMEM((TILE, length), bf16),
            pltpu.VMEM((length, TILE), f32),
            pltpu.VMEM((length, TILE), f32),
            pltpu.VMEM((length, wide), bf16),
            pltpu.VMEM(wqkv.shape, bf16),
            pltpu.VMEM(wproj.shape, bf16),
            small,
            small,
            small,
            big,
            big,
            pltpu.SemaphoreType.DMA((8,)),
        ]
        + spread_scratch(width)
        + collect_scratch(width),
        2**35,
    )


def per_device(
    tokens,
    cotangent,
    stop_scale,
    labels,
    class_table,
    head_scale,
    w_qkv,
    w_proj,
    w_up,
    w_down,
    w_ada,
):
    rows, width = tokens.shape[1:]
    layers, heads = head_scale.shape
    size = width // heads
    dps, blks = lax.axis_size("dp"), lax.axis_size("blk")
    count = dps * blks
    length = rows * blks
    d, b = lax.axis_index("dp"), lax.axis_index("blk")
    own_heads = heads // blks
    piece = own_heads * size
    wrows = w_qkv.shape[1]
    ffrows = w_down.shape[1]
    ff = ffrows * dps
    slots = labels.shape[1]
    padded = 16

    item_all, level_all = token_meta(stop_scale[0], length)
    item_own = lax.dynamic_slice_in_dim(item_all, b * rows, rows)
    key = (item_all * 16 + level_all).reshape(blks, rows)
    sib = b + 1 - 2 * (b % 2)
    far, far_sib = (b + 2) % 4, (sib + 2) % 4
    key = jnp.concatenate(
        [key[b], key[sib], key[far, :HALF], key[far_sib, :HALF], key[far, HALF:], key[far_sib, HALF:]]
    )
    keyc, keyr = key[:, None], key.reshape(4, 1, TILE)
    slot_id = jnp.arange(padded, dtype=jnp.int32)
    onehot_t = (slot_id[:, None] == item_own[None, :]).astype(bf16)
    onehot = (item_own[:, None] == jnp.concatenate([slot_id, slot_id])[None, :]).astype(bf16)

    labels_all = gather(labels, "dp").reshape(-1)
    chosen = labels_all[:, None] == jnp.arange(class_table.shape[0], dtype=jnp.int32)[None, :]
    cond = mm(chosen.astype(bf16), class_table)
    cond_act, silu_pull = jax.vjp(jax.nn.silu, cond)
    cond_low = cond_act.astype(bf16)

    wide = w_ada.shape[2]
    columns = layers * wide // count
    ada_cols = w_ada.transpose(1, 0, 2).reshape(wrows, count, columns).transpose(1, 0, 2)
    ada_cols = lax.all_to_all(ada_cols, ("dp", "blk"), 0, 0, tiled=True)
    ada_part = mm(cond_low, ada_cols.reshape(count * wrows, columns))
    ada_part = lax.all_to_all(ada_part.reshape(dps, slots, columns), "dp", 0, 0, tiled=True)
    ada_all = lax.all_gather(ada_part, "blk", axis=1, tiled=False)
    ada_all = ada_all.transpose(2, 0, 1, 3).reshape(slots, layers, wide)
    ada_all = jnp.pad(ada_all.transpose(1, 0, 2), ((0, 0), (0, padded - slots), (0, 0)))
    ada_high = ada_all.astype(bf16)
    ada_low = (ada_all - ada_high.astype(f32)).astype(bf16)
    ada = jnp.concatenate([ada_high, ada_low], axis=1)

    qkv_cols = w_qkv.reshape(layers, wrows, 3, blks, piece).transpose(3, 0, 1, 2, 4)
    up_cols = w_up.reshape(layers, wrows, dps, blks, ffrows).transpose(3, 0, 1, 2, 4)
    moved = jnp.concatenate(
        [
            qkv_cols.reshape(blks, layers, wrows, 3 * piece),
            up_cols.reshape(blks, layers, wrows, ff),
        ],
        axis=3,
    )
    moved = lax.all_to_all(moved, "blk", 0, 0, tiled=True)
    moved = moved.transpose(1, 0, 2, 3).reshape(layers, blks * wrows, 3 * piece + ff)
    to_heads = [(i, (i % dps) * blks + i // dps) for i in range(count)]
    to_rows = [(j, i) for i, j in to_heads]
    proj_own = lax.ppermute(w_proj, ("dp", "blk"), to_heads)
    weights = []
    for layer in range(layers):
        weights.append(
            (
                gather(moved[layer, :, : 3 * piece], "dp"),
                gather(proj_own[layer], "dp"),
                gather(moved[layer, :, 3 * piece :], "dp"),
                gather(w_down[layer], "dp"),
            )
        )

    own_scale = lax.dynamic_slice_in_dim(head_scale, b * own_heads, own_heads, axis=1)
    qscales = jnp.repeat(jnp.exp(own_scale), size, axis=1)

    state = tokens[0].astype(f32)
    saved = []
    for layer in range(layers):
        w_query, w_out, w_first, w_second = weights[layer]
        qscale = qscales[layer][None, :]
        h, qkv, rates, o, inverse, branch, mid = attend(
            layer, size, state, onehot, ada[layer], qscale, keyc, keyr, w_query, w_out
        )
        h2, g, slope, result, following = mlp(layer, mid, onehot, ada[layer], w_first, w_second)
        saved.append((state, h, qkv, rates, o, inverse, branch, mid, h2, g, slope, result))
        state = following
    output = state.astype(bf16)[None]

    grad = cotangent[0].astype(f32)
    cond_grad = 0.0
    scale_grads, pieces = [None] * layers, [None] * layers
    for layer in reversed(range(layers)):
        w_query, w_out, w_first, w_second = weights[layer]
        qscale = qscales[layer][None, :]
        state, h, qkv, rates, o, inverse, branch, mid, h2, g, slope, result = saved[layer]
        mid_grad, up_grad, down_grad, items_two = mlp_back(
            layer, grad, result, mid, onehot, onehot_t, ada[layer], w_first, w_second, h2, g, slope
        )
        wide_grad = scatter(
            jnp.concatenate(
                [down_grad.reshape(dps, ffrows, width), up_grad.reshape(dps, blks * wrows, ff)], axis=1
            ).reshape(-1, width),
            "dp",
        )
        down_grad, up_grad = wide_grad[:ffrows].astype(f32), wide_grad[ffrows:]
        grad, qkv_grad, proj_grad, items_one, scale_grad = attend_back(
            layer,
            size,
            mid_grad,
            branch,
            state,
            onehot,
            onehot_t,
            ada[layer],
            qscale,
            keyc,
            keyr,
            inverse,
            w_query,
            w_out,
            h,
            qkv,
            rates,
            o,
        )
        qkv_grad = scatter(qkv_grad, "dp")
        proj_grad = scatter(proj_grad, "dp")
        scale_grads[layer] = lax.dynamic_update_slice_in_dim(
            jnp.zeros((heads,), f32), scale_grad[0, ::size], b * own_heads, 0
        )
        parts_one, parts_two = jnp.split(items_one, 3, axis=1), jnp.split(items_two, 3, axis=1)
        item_grad = jnp.concatenate(
            [part for pair in zip(parts_one, parts_two) for part in pair], axis=1
        )[:slots]
        item_grad = item_grad.reshape(slots, blks, wide // blks).transpose(1, 0, 2)
        item_grad = scatter(item_grad, "blk").astype(bf16)
        item_grad = gather(item_grad, ("dp", "blk")).reshape(dps, blks, slots, wide // blks)
        item_grad = item_grad.transpose(0, 2, 1, 3).reshape(dps * slots, wide)
        cond_grad = cond_grad + mm_t(item_grad, w_ada[layer])
        own_cond = lax.dynamic_slice_in_dim(cond_low, (d * blks + b) * wrows, wrows, axis=1)
        ada_grad = rows_mm(own_cond, item_grad)
        back = jnp.concatenate([qkv_grad, up_grad], axis=1)
        back = lax.all_to_all(back.reshape(blks, wrows, 3 * piece + ff), "blk", 0, 0, tiled=True)
        qkv_grad = back[:, :, : 3 * piece].reshape(blks, wrows, 3, piece)
        qkv_grad = qkv_grad.transpose(1, 2, 0, 3).reshape(wrows, 3 * width).astype(f32)
        up_grad = back[:, :, 3 * piece :].reshape(blks, wrows, dps, ffrows)
        up_grad = up_grad.transpose(1, 2, 0, 3).reshape(wrows, ff * blks).astype(f32)
        proj_grad = lax.ppermute(proj_grad, ("dp", "blk"), to_rows).astype(f32)
        pieces[layer] = (qkv_grad, proj_grad, up_grad, down_grad, ada_grad)
    cond_grad = gather(cond_grad.T, ("dp", "blk")).T
    cond_pre = silu_pull(cond_grad)[0]
    table_grad = rows_mm(chosen.astype(f32), cond_pre, lax.Precision.HIGHEST)
    head_grad = lax.psum(jnp.stack(scale_grads), ("dp", "blk"))
    stacked = [jnp.stack([one[i] for one in pieces]) for i in range(5)]
    return (output, grad.astype(bf16)[None], table_grad, head_grad, *stacked)


def solution(mesh):
    in_specs = (
        P("dp", "blk", None),
        P("dp", "blk", None),
        P("dp", None),
        P("dp", None),
        P(),
        P(),
        P(None, ("dp", "blk"), None),
        P(None, ("dp", "blk"), None),
        P(None, ("dp", "blk"), None),
        P(None, ("dp", "blk"), None),
        P(None, ("dp", "blk"), None),
    )
    out_specs = (
        P("dp", "blk", None),
        P("dp", "blk", None),
        P(),
        P(),
        P(None, ("dp", "blk"), None),
        P(None, ("dp", "blk"), None),
        P(None, ("dp", "blk"), None),
        P(None, ("dp", "blk"), None),
        P(None, ("dp", "blk"), None),
    )
    return jax.shard_map(
        per_device, mesh=mesh, in_specs=in_specs, out_specs=out_specs, check_vma=False
    )
```

time: 1720 us -> 1060 us (0.62)
  waiting for transfers between devices: 1120 us -> 401 us
  Pallas kernels: 0 us -> 289 us
  matrix products: 211 us -> 9.6 us
  other arithmetic: 74.9 us -> 25.4 us
  blocking collectives: 186 us -> 228 us
    reduce_scatter x16 -> x6, waiting for transfers between devices: 671 us -> 283 us  [scatter(): return lax.psum_scatter(values, axes, scatter_dimension=0, tiled=True)]
    all_gather x16 -> x8, waiting for transfers between devices: 429 us -> 115 us  [gather(): return lax.all_gather(values, axes, axis=0, tiled=True)]
    pallas_call x0 -> x8, Pallas kernels: none -> 289 us  [run(): pl.pallas_call(kernel, out_shape=[one for one, _ in outs], in_specs=[wher...]
    dot_general x14 -> x0, matrix products: 71.4 us -> none  [the longest x2 19.8 us: per_device(): jnp.einsum('qhe,khe->hqk', out_grad, v_low, preferred_element_type=f32)]
    dot_general x13 -> x3, matrix products: 60.5 us -> 6.19 us  [rows_mm(): lax.dot_general(left, right, (((0,), (0,)), ((), ())), precision=precisio...]
    dot_general x10 -> x2, matrix products: 42.2 us -> 2.34 us  [mm(): return jnp.dot(left, right, preferred_element_type=f32)]
    dot_general x10 -> x2, matrix products: 36.5 us -> 1.06 us  [mm_t(): lax.dot_general(left, right, (((1,), (1,)), ((), ())), preferred_element_...]
    reduce_sum x18 -> x0, other arithmetic: 25.2 us -> none  [the longest x4 11.2 us: modulate(): centred = values - centre]
  transfers between devices with their start and end apart: 40 -> 21, of which waited for: 33 -> 9; matrix products, arithmetic and copies ran while one was open for 9% -> 6% of each run, Pallas kernels for 0% -> 17%
where the time goes in v2:
time: 1060 us; the launch traced here: 1040 us
  waiting for transfers between devices  401 us (38%)
  Pallas kernels  289 us (27%)
  blocking collectives  228 us (22%)
  local copies, waits for them, and re-layouts  38.5 us (4%)
  starting transfers between devices  38.3 us (4%)
  other arithmetic  25.4 us (2%)
  between operations  15.2 us (1%)
    pallas_call x8, Pallas kernels, run(): pl.pallas_call(kernel, out_shape=[one for one, _ in outs], in_specs=[wher...  289 us
    reduce_scatter x6, waiting for transfers between devices, scatter(): return lax.psum_scatter(values, axes, scatter_dimension=0, tiled=True)  283 us
    all_gather x4, blocking collectives, gather(): return lax.all_gather(values, axes, axis=0, tiled=True)  135 us
    all_gather x8, waiting for transfers between devices, gather(): return lax.all_gather(values, axes, axis=0, tiled=True)  115 us
    psum x1, blocking collectives, per_device(): head_grad = lax.psum(jnp.stack(scale_grads), ('dp', 'blk'))  40.1 us
    all_gather x1, blocking collectives, per_device(): ada_all = lax.all_gather(ada_part, 'blk', axis=1, tiled=False)  21.8 us
  transfers between devices with their start and end apart: 21, of which 9 were waited for; matrix products, arithmetic and copies ran while one was open for 6% of the time, Pallas kernels for 17%

profile of v2, /device:TPU:7, one launch (start us, length us, event | category | flops | bytes accessed | tf_op | source)
XLA Modules:
  0.0 1044.5 jit_solution(4939086900444221368)
XLA Ops:
  7.2 1.5 reshape.230
  9.1 1.3 reshape.228
  11.1 14.7 %all_to_all.25 = bf16[4,2,32,1792]{3,2,1,0:T(8,128)(2,1)S(1)} all-to-all(bf16[4,2,32,1792]{3,2,1,0:T(8,128)(2,1)S(1)} %pad_maximum_fusion.3), channel_id=1, replica_groups=mesh['dp'=8,'blk'=4] {'blk'}, dimensions={0} | all-to-all | bytes 1835008 | tf_op jit(solution)/shard_map/all_to_all | solution.py:994
  27.7 0.9 fusion.28
  29.1 2.8 copy.89
  32.0 2.4 reshape.224
  34.5 1.1 copy.90
  35.6 6.5 all-to-all-start
  42.1 5.2 collective-permute-start
  47.9 39.6 %all-gather.9 = s32[8,1,12]{2,1,0:T(1,128)S(1)} all-gather(s32[1,1,12]{2,1,0:T(1,128)S(1)} %bitcast.196), channel_id=1, replica_groups=mesh['dp'=8,'blk'=4] {'dp'}, dimensions={0}, use_global_device_ids=true | all-gather | bytes 432 | tf_op jit(solution)/shard_map/all_gather | solution.py:51
  88.7 1.4 multiply_convert_fusion
  90.1 1.0 dot_general.24
  92.4 1.0 copy.97.keyc
  95.5 1.1 bitcast_convert_fusion.1.x
  96.6 1.1 bitcast_convert_fusion.dx
  98.3 1.0 fusion.32
  99.3 5.0 all-to-all-start.1
  104.4 29.1 %all-gather.2 = bf16[1,256,1024]{2,1,0:T(8,128)(2,1)} all-gather(bf16[1,32,1024]{2,1,0:T(8,128)(2,1)S(1)} %get-tuple-element.110), channel_id=4, replica_groups=mesh['dp'=8,'blk'=4] {'dp'}, dimensions={1}, use_global_device_ids=true | all-gather | bytes 589824 | tf_op jit(solution)/shard_map/all_gather | solution.py:51
  133.5 28.2 %all-gather.6 = bf16[1,256,1024]{2,1,0:T(8,128)(2,1)} all-gather(bf16[1,32,1024]{2,1,0:T(8,128)(2,1)S(1)} %get-tuple-element.109), channel_id=8, replica_groups=mesh['dp'=8,'blk'=4] {'dp'}, dimensions={1}, use_global_device_ids=true | all-gather | bytes 589824 | tf_op jit(solution)/shard_map/all_gather | solution.py:51
  161.8 21.8 %all-gather = f32[8,48,384]{2,0,1:T(8,128)S(1)} all-gather(f32[8,12,384]{2,0,1:T(8,128)S(1)} %copy.91), channel_id=2, replica_groups=mesh['dp'=8,'blk'=4] {'blk'}, dimensions={1}, use_global_device_ids=true | all-gather | bytes 737280 | tf_op jit(solution)/shard_map/all_gather | solution.py:978
  184.9 0.9 fusion.7
  185.8 37.0 %shard_map.196 = (bf16[1024,1024]{1,0:T(8,128)(2,1)}, bf16[1024,768]{1,0:T(8,128)(2,1)}, f32[1024,512]{1,0:T(8,128)}, bf16[1024,256]{1,0:T(8,128)(2,1)}, f32[4,8...) custom-call(f32[256,1024]{1,0:T(8,128)} %bitcast_convert_fusion.1.x, ...), custom_call_target="tpu_custom_call" | custom-call | flops 34359738368 | bytes 16777216 | tf_op jit(solution)/shard_map/pallas_call | solution.py:765
  223.0 30.4 %shard_map.197 = (bf16[1024,1024]{1,0:T(8,128)(2,1)}, bf16[1024,1024]{1,0:T(8,128)(2,1)}, bf16[1024,1024]{1,0:T(8,128)(2,1)}, f32[256,1024]{1,0:T(8,128)}, f32[256,1024]{1,0:T(8,128)}) custom-call(f32[256,1024]{1,0:T(8,128)} %get-tuple-element.51.x.mid_state, bf16[256,32]{1,0:T(8,128)(2,1)} %compare_convert_fusion.onehot, ...), custom_call_target="tpu_custom_call" | custom-call | flops 34359738368 | bytes 16777216 | tf_op jit(solution)/shard_map/pallas_call | solution.py:765
  253.4 36.5 %shard_map.198 = (bf16[1024,1024]{1,0:T(8,128)(2,1)}, bf16[1024,768]{1,0:T(8,128)(2,1)}, f32[1024,512]{1,0:T(8,128)}, bf16[1024,256]{1,0:T(8,128)(2,1)}, f32[4,8...) custom-call(f32[256,1024]{1,0:T(8,128)} %get-tuple-element.52.x, ...), custom_call_target="tpu_custom_call" | custom-call | flops 34359738368 | bytes 16777216 | tf_op jit(solution)/shard_map/pallas_call | solution.py:765
  290.0 47.0 %all-gather.31.cloned.1.call-done = bf16[1,1024,1024]{2,1,0:T(8,128)(2,1)} async-done(((bf16[1,128,1024]{2,1,0:T(8,128)(2,1)}), bf16[1,1024,1024]{2,1,0:T(8,128)(2,1)}) %all-gather.31.cloned.1.call-update) | async-done | bytes 2097168 | tf_op jit(solution)/shard_map/all_gather | solution.py:51
  336.9 30.0 %shard_map.199 = (bf16[1024,1024]{1,0:T(8,128)(2,1)}, bf16[1024,1024]{1,0:T(8,128)(2,1)}, bf16[1024,1024]{1,0:T(8,128)(2,1)}, f32[256,1024]{1,0:T(8,128)}, f32[256,1024]{1,0:T(8,128)}) custom-call(f32[256,1024]{1,0:T(8,128)} %get-tuple-element.53.x.mid_state, bf16[256,32]{1,0:T(8,128)(2,1)} %compare_convert_fusion.onehot, ...), custom_call_target="tpu_custom_call" | custom-call | flops 34359738368 | bytes 16777216 | tf_op jit(solution)/shard_map/pallas_call | solution.py:765
  367.0 32.0 %shard_map.200 = (f32[256,1024]{1,0:T(8,128)}, bf16[1024,1024]{1,0:T(8,128)(2,1)}, bf16[1024,1024]{1,0:T(8,128)(2,1)}, f32[16,3072]{1,0:T(8,128)}) custom-call(f32[256,1024]{1,0:T(8,128)} %bitcast_convert_fusion.dx, f32[256,1024]{1,0:T(8,128)} %get-tuple-element.55.result, f32[256,1024]{1,0:T(8,128)} %get-tuple-element.53.x.mid_state, ...), custom_call_target="tpu_custom_call" | custom-call | flops 34359738368 | bytes 16777216 | tf_op jit(solution)/shard_map/pallas_call | solution.py:765
  399.0 45.4 %shard_map.201 = (f32[256,1024]{1,0:T(8,128)}, bf16[1024,768]{1,0:T(8,128)(2,1)}, bf16[256,1024]{1,0:T(8,128)(2,1)}, f32[16,3072]{1,0:T(8,128)}, f32[1,256]{1,0:T(1,128)}) custom-call(f32[256,1024]{1,0:T(8,128)} %get-tuple-element.59.dmid, f32[256,1024]{1,0:T(8,128)} %get-tuple-element.60.branch, f32[256,1024]{1,0:T(8,128)} %get-tuple-element.52.x, ...), custom_call_target="tpu_custom_call" | custom-call | flops 34359738368 | bytes 16777216 | tf_op jit(solution)/shard_map/pallas_call | solution.py:765
  445.2 0.8 slice_dynamic-update-slice_fusion.9
  446.2 31.6 %shard_map.202 = (f32[256,1024]{1,0:T(8,128)}, bf16[1024,1024]{1,0:T(8,128)(2,1)}, bf16[1024,1024]{1,0:T(8,128)(2,1)}, f32[16,3072]{1,0:T(8,128)}) custom-call(f32[256,1024]{1,0:T(8,128)} %get-tuple-element.66.dx, f32[256,1024]{1,0:T(8,128)} %get-tuple-element.67.result, f32[256,1024]{1,0:T(8,128)} %get-tuple-element.51.x.mid_state, ...), custom_call_target="tpu_custom_call" | custom-call | flops 34359738368 | bytes 16777216 | tf_op jit(solution)/shard_map/pallas_call | solution.py:765
  477.8 46.0 %shard_map.203 = (f32[256,1024]{1,0:T(8,128)}, bf16[1024,768]{1,0:T(8,128)(2,1)}, bf16[256,1024]{1,0:T(8,128)(2,1)}, f32[16,3072]{1,0:T(8,128)}, f32[1,256]{1,0:T(1,128)}) custom-call(f32[256,1024]{1,0:T(8,128)} %get-tuple-element.71.dmid, f32[256,1024]{1,0:T(8,128)} %get-tuple-element.72.branch, f32[256,1024]{1,0:T(8,128)} %bitcast_convert_fusion.1.x, ...), custom_call_target="tpu_custom_call" | custom-call | flops 34359738368 | bytes 16777216 | tf_op jit(solution)/shard_map/pallas_call | solution.py:765
  527.7 16.8 %all-reduce.5 = (bf16[4,12,1536]{2,0,1:T(4,128)(2,1)S(1)}, bf16[4,12,1536]{2,0,1:T(4,128)(2,1)S(1)}) all-reduce(f32[4,12,1536]{2,0,1:T(4,128)S(1)} %bitcast.171, f32[4,12,1536]{2,0,1:T(4,128)S(1)} %bitcast.172), channel_id=11, replica_groups=mesh['dp'=8,'blk'=4] {'blk'}, use_global_device_ids=true, to_apply=%region_5.6.clone | all-reduce | flops 147456 | bytes 884736
  547.2 4.7 pad_maximum_fusion.1
  552.5 4.7 pad_maximum_fusion
  558.8 0.9 convert_bitcast_fusion.1
  559.7 4.6 collective-permute-start.2
  564.3 21.3 %reduce-scatter.17.cloned.1.call-done = bf16[32,1024]{1,0:T(8,128)(2,1)} async-done(((bf16[256,1024]{1,0:T(8,128)(2,1)}), bf16[32,1024]{1,0:T(8,128)(2,1)}) %reduce-scatter.17.cloned.1.call-update) | async-done | bytes 65552 | tf_op jit(solution)/shard_map/reduce_scatter | solution.py:55
  585.6 4.0 collective-permute-start.1
  589.6 0.9 convert_bitcast_fusion
  590.4 40.1 %psum.7 = f32[2,16]{1,0:T(2,128)} all-reduce(f32[2,16]{1,0:T(2,128)S(1)} %pad_maximum_fusion.7), channel_id=1, replica_groups=mesh['dp'=8,'blk'=4] {'dp','blk'}, use_global_device_ids=true, to_apply=%region_7.8 | all-reduce | flops 32 | bytes 256 | tf_op jit(solution)/shard_map/psum | solution.py:1090
  631.3 13.4 %all-gather.19.cloned.1.call-done = bf16[32,12,1536]{2,1,0:T(8,128)(2,1)} async-done(((bf16[1,12,1536]{2,1,0:T(8,128)(2,1)}), bf16[32,12,1536]{2,1,0:T(8,128)(2,1)}) %all-gather.19.cloned.1.call-update) | async-done | bytes 1179664 | tf_op jit(solution)/shard_map/all_gather | solution.py:51
  644.7 2.3 copy.113
  647.2 54.7 %all-gather.21.cloned.1.call-done = bf16[32,12,1536]{2,1,0:T(8,128)(2,1)} async-done(((bf16[1,12,1536]{2,1,0:T(8,128)(2,1)}), bf16[32,12,1536]{2,1,0:T(8,128)(2,1)}) %all-gather.21.cloned.1.call-update) | async-done | bytes 1179664 | tf_op jit(solution)/shard_map/all_gather | solution.py:51
  701.9 2.4 copy.115
  705.6 37.6 %all_gather.55 = f32[1024,96]{1,0:T(8,128)S(1)} all-gather(f32[32,96]{1,0:T(8,128)S(1)} %fusion), channel_id=1, replica_groups=mesh['dp'=8,'blk'=4] {'dp','blk'}, dimensions={0}, use_global_device_ids=true | all-gather | bytes 405504 | tf_op jit(solution)/shard_map/all_gather | solution.py:51
  743.3 0.9 copy.107
  744.2 1.1 convolution_bitcast_fusion
  745.4 1.1 convolution_bitcast_fusion.1
  746.5 1.3 pad_maximum_fusion.2
  747.8 47.5 %reduce-scatter.15.cloned.1.call-done = bf16[256,1024]{1,0:T(8,128)(2,1)} async-done(((bf16[2048,1024]{1,0:T(8,128)(2,1)}), bf16[256,1024]{1,0:T(8,128)(2,1)}) %reduce-scatter.15.cloned.1.call-update) | async-done | bytes 524304 | tf_op jit(solution)/shard_map/reduce_scatter | solution.py:55
  795.3 1.1 slice_bitcast_fusion
  796.3 64.9 %reduce-scatter.13.cloned.1.call-done = bf16[128,768]{1,0:T(8,128)(2,1)} async-done(((bf16[1024,768]{1,0:T(8,128)(2,1)}), bf16[128,768]{1,0:T(8,128)(2,1)}) %reduce-scatter.13.cloned.1.call-update) | async-done | bytes 196624 | tf_op jit(solution)/shard_map/reduce_scatter | solution.py:55
  861.3 1.7 pad_maximum_fusion.5
  863.0 6.3 all-to-all-start.4
  869.3 84.8 %reduce-scatter.11.cloned.1.call-done = bf16[256,1024]{1,0:T(8,128)(2,1)} async-done(((bf16[2048,1024]{1,0:T(8,128)(2,1)}), bf16[256,1024]{1,0:T(8,128)(2,1)}) %reduce-scatter.11.cloned.1.call-update) | async-done | bytes 524304 | tf_op jit(solution)/shard_map/reduce_scatter | solution.py:55
  954.1 1.1 slice_bitcast_fusion.1
  955.2 64.8 %reduce-scatter.9.cloned.1.call-done = bf16[128,768]{1,0:T(8,128)(2,1)} async-done(((bf16[1024,768]{1,0:T(8,128)(2,1)}), bf16[128,768]{1,0:T(8,128)(2,1)}) %reduce-scatter.9.cloned.1.call-update) | async-done | bytes 196624 | tf_op jit(solution)/shard_map/reduce_scatter | solution.py:55
  1020.0 1.7 pad_maximum_fusion.4
  1021.7 6.2 all-to-all-start.3
  1027.9 3.9 fusion.3
  1031.8 1.0 maximum_convert_fusion.1
  1033.3 0.8 all-to-all-done.3
  1035.5 0.9 maximum_convert_fusion.2
  1036.5 1.0 maximum_convert_fusion
  (176 shorter events, 24.2 us)
Async XLA Ops:
  7.2 81.5 %copy-start = (bf16[1001,1024]{1,0:T(8,128)(2,1)S(1)}, bf16[1001,1024]{1,0:T(8,128)(2,1)}, u32[]{:S(2)}) copy-start(bf16[1001,1024]{1,0:T(8,128)(2,1)} %param.17) | copy-start | bytes 6150148
  7.2 178.6 %all-gather.23.cloned.1.call-start = ((), (), s32[]{:S(2)}) async-start(), calls=%async_computation.19 | async-start | bytes 1769472 | tf_op jit(solution)/shard_map/all_gather | solution.py:51
  11.1 15.6 %copy-start.8 = (bf16[2,128,1024]{2,1,0:T(8,128)(2,1)S(1)}, bf16[2,128,1024]{2,1,0:T(8,128)(2,1)}, u32[]{:S(2)}) copy-start(bf16[2,128,1024]{2,1,0:T(8,128)(2,1)} %param.22) | copy-start | bytes 1572868
  26.7 196.2 %all-gather.27.cloned.1.call-start = ((), (), s32[]{:S(2)}) async-start(), calls=%async_computation.21 | async-start | bytes 2359296 | tf_op jit(solution)/shard_map/all_gather | solution.py:51
  27.6 195.3 %all-gather.25.cloned.1.call-start = ((), (), s32[]{:S(2)}) async-start(), calls=%async_computation.20 | async-start | bytes 2359296 | tf_op jit(solution)/shard_map/all_gather | solution.py:51
  28.6 224.8 %all-gather.29.cloned.1.call-start = ((), (), s32[]{:S(2)}) async-start(), calls=%async_computation.22 | async-start | bytes 1769472 | tf_op jit(solution)/shard_map/all_gather | solution.py:51
  34.4 13.1 %copy-start.18 = (s32[1,11]{1,0:T(1,128)S(1)}, s32[1,11]{1,0:T(1,128)}, u32[]{:S(2)}) copy-start(s32[1,11]{1,0:T(1,128)} %param.15) | copy-start | bytes 136
  34.4 13.1 %copy-start.20 = (s32[9]{0:T(128)S(1)}, s32[9]{0:T(128)}, u32[]{:S(2)}) copy-start(s32[9]{0:T(128)} %constant.66.clone) | copy-start | bytes 112
  34.4 13.4 %copy-start.16 = (s32[1,12]{1,0:T(1,128)S(1)}, s32[1,12]{1,0:T(1,128)}, u32[]{:S(2)}) copy-start(s32[1,12]{1,0:T(1,128)} %param.16) | copy-start | bytes 148
  35.6 62.7 %all-to-all-start = ((bf16[32,32,384]{2,1,0:T(8,128)(2,1)}), bf16[32,32,384]{2,1,0:T(8,128)(2,1)S(1)}, u32[]{:S(2)}, u32[]{:S(2)}) async-start(bf16[32,32,384]{2,1,0:T(8,128)(2,1)} %copy.90), calls=%async_computation | async-start | bytes 1572864 | tf_op jit(solution)/shard_map/all_to_all | solution.py:975
  42.1 247.9 %all-gather.33.cloned.1.call-start = ((), (), s32[]{:S(2)}) async-start(), calls=%async_computation.24 | async-start | bytes 2359296 | tf_op jit(solution)/shard_map/all_gather | solution.py:51
  42.1 56.2 %collective-permute-start = (bf16[2,32,1024]{2,1,0:T(8,128)(2,1)}, bf16[2,32,1024]{2,1,0:T(8,128)(2,1)S(1)}, u32[]{:S(2)}, u32[]{:S(2)}) collective-permute-start(bf16[2,32,1024]{2,1,0:T(8,128)(2,1)} %param.20), channel_id=1, source_target_pairs={{0,0},{1,4},{2,8},{3,12},{4,16},{5,20},{6,24},{7,28},{8,1},{9,5},{... | collective-permute-start | bytes 393224 | tf_op jit(solution)/shard_map/ppermute | solution.py:998
  47.4 43.7 %copy-start.15 = (f32[2,16]{1,0:T(2,128)S(1)}, f32[2,16]{1,0:T(2,128)}, u32[]{:S(2)}) copy-start(f32[2,16]{1,0:T(2,128)} %param.18) | copy-start | bytes 388
  47.4 44.7 %copy-start.17 = (s32[8]{0:T(128)S(1)}, s32[8]{0:T(128)}, u32[]{:S(2)}) copy-start(s32[8]{0:T(128)} %constant.67.clone) | copy-start | bytes 100
  88.7 4.7 copy-start.13
  88.7 5.5 copy-start.19
  88.7 6.8 copy-start.6
  90.1 6.6 copy-start.7
  92.4 7.0 copy-start.12
  99.3 62.5 %all-to-all-start.1 = ((f32[8,12,384]{2,1,0:T(8,128)}), f32[8,12,384]{2,1,0:T(8,128)S(1)}, u32[]{:S(2)}, u32[]{:S(2)}) async-start(f32[8,12,384]{2,1,0:T(8,128)} %fusion.32), calls=%async_computation.1 | async-start | bytes 393216 | tf_op jit(solution)/shard_map/all_to_all | solution.py:977
  104.3 232.6 %all-gather.31.cloned.1.call-start = ((), (), s32[]{:S(2)}) async-start(), calls=%async_computation.23 | async-start | bytes 2359296 | tf_op jit(solution)/shard_map/all_gather | solution.py:51
  161.7 398.0 %reduce-scatter.19.cloned.1.call-start = ((), (), s32[]{:S(2)}) async-start(), calls=%async_computation.18 | async-start | bytes 589824 | tf_op jit(solution)/shard_map/reduce_scatter | solution.py:55
  399.0 46.2 %copy-start.10 = (f32[16,3072]{1,0:T(8,128)S(1)}, f32[16,3072]{1,0:T(8,128)}, u32[]{:S(2)}) copy-start(f32[16,3072]{1,0:T(8,128)} %get-tuple-element.80) | copy-start | bytes 589828
  446.1 139.5 %reduce-scatter.17.cloned.1.call-start = ((), (), s32[]{:S(2)}) async-start(), calls=%async_computation.17 | async-start | bytes 589824 | tf_op jit(solution)/shard_map/reduce_scatter | solution.py:55
  477.7 47.7 %copy-start.11 = (f32[16,3072]{1,0:T(8,128)S(1)}, f32[16,3072]{1,0:T(8,128)}, u32[]{:S(2)}) copy-start(f32[16,3072]{1,0:T(8,128)} %get-tuple-element.82) | copy-start | bytes 589828
  526.3 118.3 %all-gather.19.cloned.1.call-start = ((), (), s32[]{:S(2)}) async-start(), calls=%async_computation.11 | async-start | bytes 1622016 | tf_op jit(solution)/shard_map/all_gather | solution.py:51
  545.8 156.2 %all-gather.21.cloned.1.call-start = ((), (), s32[]{:S(2)}) async-start(), calls=%async_computation.12 | async-start | bytes 1622016 | tf_op jit(solution)/shard_map/all_gather | solution.py:51
  547.1 248.1 %reduce-scatter.15.cloned.1.call-start = ((), (), s32[]{:S(2)}) async-start(), calls=%async_computation.16 | async-start | bytes 4718592 | tf_op jit(solution)/shard_map/reduce_scatter | solution.py:55
  551.9 309.4 %reduce-scatter.13.cloned.1.call-start = ((), (), s32[]{:S(2)}) async-start(), calls=%async_computation.15 | async-start | bytes 1769472 | tf_op jit(solution)/shard_map/reduce_scatter | solution.py:55
  552.5 401.6 %reduce-scatter.11.cloned.1.call-start = ((), (), s32[]{:S(2)}) async-start(), calls=%async_computation.14 | async-start | bytes 4718592 | tf_op jit(solution)/shard_map/reduce_scatter | solution.py:55
  557.2 0.6 copy-start.21
  557.2 0.7 copy-start.22
  557.2 1.6 copy-start.4
  557.2 32.3 %copy-start.5 = (f32[256,1024]{1,0:T(8,128)S(1)}, f32[256,1024]{1,0:T(8,128)}, u32[]{:S(2)}) copy-start(f32[256,1024]{1,0:T(8,128)} %get-tuple-element.78) | copy-start | bytes 3145732
  557.2 462.7 %reduce-scatter.9.cloned.1.call-start = ((), (), s32[]{:S(2)}) async-start(), calls=%async_computation.13 | async-start | bytes 1769472 | tf_op jit(solution)/shard_map/reduce_scatter | solution.py:55
  559.7 70.9 %collective-permute-start.2 = (bf16[32,1024]{1,0:T(8,128)(2,1)}, bf16[32,1024]{1,0:T(8,128)(2,1)S(1)}, u32[]{:S(2)}, u32[]{:S(2)}) collective-permute-start(bf16[32,1024]{1,0:T(8,128)(2,1)} %reduce-scatter.19.cloned.1.call-done), channel_id=1, source_target_pairs={{0,0},{4,1},{8,2},{12,3},{16,4},{20,5},{24,6},{28,7},{1,8},{5,9},{... | collective-permute-start | bytes 196616 | tf_op jit(solution)/shard_map/ppermute | solution.py:1085
  585.6 45.0 %collective-permute-start.1 = (bf16[32,1024]{1,0:T(8,128)(2,1)}, bf16[32,1024]{1,0:T(8,128)(2,1)S(1)}, u32[]{:S(2)}, u32[]{:S(2)}) collective-permute-start(bf16[32,1024]{1,0:T(8,128)(2,1)} %reduce-scatter.17.cloned.1.call-done), channel_id=1, source_target_pairs={{0,0},{4,1},{8,2},{12,3},{16,4},{20,5},{24,6},{28,7},{1,8},{5,9},{... | collective-permute-start | bytes 196616 | tf_op jit(solution)/shard_map/ppermute | solution.py:1085
  701.9 2.6 copy-start.2
  863.0 164.9 %copy-start.3 = (f32[1024,96]{0,1:T(8,128)S(1)}, f32[1024,96]{0,1:T(8,128)}, u32[]{:S(2)}) copy-start(f32[1024,96]{0,1:T(8,128)} %copy.107) | copy-start | bytes 1179652
  863.0 164.9 %copy-start.9 = (f32[96,1024]{1,0:T(8,128)S(1)}, f32[96,1024]{1,0:T(8,128)}, u32[]{:S(2)}) copy-start(f32[96,1024]{1,0:T(8,128)} %get-tuple-element.116) | copy-start | bytes 1179652
  863.0 164.9 %copy-start.14 = (s32[96]{0:T(128)S(1)}, s32[96]{0:T(128)}, u32[]{:S(2)}) copy-start(s32[96]{0:T(128)} %copy-done.13) | copy-start | bytes 1156
  863.0 158.7 %all-to-all-start.4 = ((bf16[4,32,1792]{2,1,0:T(8,128)(2,1)}), bf16[4,32,1792]{2,1,0:T(8,128)(2,1)S(1)}, u32[]{:S(2)}, u32[]{:S(2)}) async-start(bf16[4,32,1792]{2,1,0:T(8,128)(2,1)} %bitcast.60), calls=%async_computation.8 | async-start | bytes 917504 | tf_op jit(solution)/shard_map/all_to_all | solution.py:1080
  1021.7 12.4 %all-to-all-start.3 = ((bf16[4,32,1792]{2,1,0:T(8,128)(2,1)}), bf16[4,32,1792]{2,1,0:T(8,128)(2,1)S(1)}, u32[]{:S(2)}, u32[]{:S(2)}) async-start(bf16[4,32,1792]{2,1,0:T(8,128)(2,1)} %bitcast.55), calls=%async_computation.5 | async-start | bytes 917504 | tf_op jit(solution)/shard_map/all_to_all | solution.py:1080
  1035.1 2.4 copy-start.1
Sparse Core Ops, SparseCore 0:
  26.8 51.0 all-gather.22
  80.1 58.9 all-gather.26
  141.8 49.5 all-gather.24
  193.5 43.4 all-gather.28
  238.9 47.5 all-gather.32
  289.1 47.8 all-gather.30
  446.2 59.0 reduce-scatter.18
  526.5 59.0 reduce-scatter.16
  589.1 55.5 all-gather.18
  648.0 53.9 all-gather.20
  705.6 89.6 reduce-scatter.14
  798.9 62.2 reduce-scatter.12
  864.9 89.1 reduce-scatter.10
  957.8 62.1 reduce-scatter.8

commit v3 on v2

--- a/solution.py
+++ b/solution.py
@@ -60,11 +60,11 @@
     return (d, b + 1 - 2 * (b % 2)), (d, (b + 2) % 4)
 
 
-def greet(sibling, peer):
+def greet(others):
     barrier = pltpu.get_barrier_semaphore()
-    for other in (sibling, peer):
+    for other in others:
         pl.semaphore_signal(barrier, inc=1, device_id=other, device_id_type=MESH)
-    pl.semaphore_wait(barrier, 2)
+    pl.semaphore_wait(barrier, len(others))
 
 
 def remote(src, dst, send, recv, target):
@@ -254,6 +254,7 @@
 
 def attend_kernel(
     size,
+    jobs,
     x,
     onehot,
     ada,
@@ -294,7 +295,8 @@
     load_qkv = mover.copy(wqkv_in, wqkv)
     load_proj = mover.copy(wproj_in, wproj)
     expand(onehot, ada, (0, 2, 4), (gamma, scale, shift))
-    greet(sibling, peer)
+    jobs.greet(sibling, peer)
+    jobs.start()
     spread = Spread(hbuf, ag_send, ag_recv, sibling, peer)
     collect = Collect(parts, out, mid, own, far, rs_send, rs_recv, sibling, peer)
 
@@ -327,6 +329,7 @@
                 vt[:, span] = value.T.astype(bf16)
             qkv[span, columns] = value.astype(bf16)
 
+    jobs.step(0)
     save_h = mover.copy(hbuf, h_out)
     save_qkv = mover.copy(qkv, qkv_out)
     save_rates = mover.copy(rates, rate_out)
@@ -359,6 +362,8 @@
             parts[span, n : n + TILE] = mm(low, wproj[:, n : n + TILE]).astype(bf16)
         collect.block_done(j)
 
+    jobs.step(1)
+    jobs.step(2)
     collect.wait()
 
     def added(at):
@@ -372,9 +377,19 @@
     collect.finish()
     for one in (save_h, save_qkv, save_rates):
         one.wait()
+    jobs.finish()
+
+
+def early_hooks(jobs, i):
+    for hook in range(2):
+
+        @pl.when(i == 2 + hook)
+        def _():
+            jobs.step(hook)
 
 
 def mlp_kernel(
+    jobs,
     x,
     onehot,
     ada,
@@ -409,7 +424,8 @@
     load_up = mover.copy(wup_in, wup)
     load_down = mover.copy(wdown_in, wdown)
     expand(onehot, ada, (1, 3, 5), (gamma, scale, shift))
-    greet(sibling, peer)
+    jobs.greet(sibling, peer)
+    jobs.start()
     spread = Spread(hbuf, ag_send, ag_recv, sibling, peer)
     collect = Collect(parts, out, mid, own, far, rs_send, rs_recv, sibling, peer)
 
@@ -427,6 +443,7 @@
     @pl.loop(0, 4)
     def _(i):
         spread.wait_block(i)
+        early_hooks(jobs, i)
         span = pl.ds(pl.multiple_of(i * TILE, TILE), TILE)
         h = hbuf[span, :]
         for n in range(0, wup.shape[1], TILE):
@@ -443,6 +460,7 @@
             parts[span, n : n + TILE] = mm(g, wdown[:, n : n + TILE]).astype(bf16)
         collect.block_done(i)
 
+    jobs.step(2)
     saves = [mover.copy(a, b) for a, b in ((hbuf, h_out), (hidden, g_out), (slope, slope_out))]
     collect.wait()
 
@@ -457,6 +475,7 @@
     collect.finish()
     for one in saves:
         one.wait()
+    jobs.finish()
 
 
 def item_sums(onehot_t, terms, out):
@@ -466,6 +485,7 @@
 
 
 def mlp_back_kernel(
+    jobs,
     dx,
     result,
     mid_state,
@@ -513,7 +533,8 @@
     load_g = mover.copy(g_in, gall)
     load_h = mover.copy(h_in, hall)
     expand(onehot, ada, (1, 3), (gamma, scale))
-    greet(sibling, peer)
+    jobs.greet(sibling, peer)
+    jobs.start()
     spread = Spread(hbuf, ag_send, ag_recv, sibling, peer)
     collect = Collect(parts, out, mid, own, far, rs_send, rs_recv, sibling, peer)
 
@@ -530,6 +551,7 @@
     @pl.loop(0, 4)
     def _(i):
         spread.wait_block(i)
+        early_hooks(jobs, i)
         span = pl.ds(pl.multiple_of(i * TILE, TILE), TILE)
         dm = hbuf[span, :]
         for n in range(0, slope.shape[1], TILE):
@@ -541,6 +563,7 @@
             parts[span, n : n + TILE] = mm_t(du, wup[n : n + TILE, :]).astype(bf16)
         collect.block_done(i)
 
+    jobs.step(2)
     load_g.wait()
     load_h.wait()
 
@@ -581,10 +604,12 @@
     collect.finish()
     save_down.wait()
     save_up.wait()
+    jobs.finish()
 
 
 def attend_back_kernel(
     size,
+    jobs,
     dmid,
     branch,
     x,
@@ -644,7 +669,8 @@
     load_w = mover.copy(wqkv_in, wqkv)
     load_h = mover.copy(h_in, hall)
     expand(onehot, ada, (0, 2), (gamma, scale))
-    greet(sibling, peer)
+    jobs.greet(sibling, peer)
+    jobs.start()
     spread = Spread(hbuf, ag_send, ag_recv, sibling, peer)
     collect = Collect(parts, out, mid, own, far, rs_send, rs_recv, sibling, peer)
 
@@ -674,6 +700,11 @@
     @pl.loop(0, 4)
     def _(i):
         spread.wait_block(i)
+
+        @pl.when(i == 3)
+        def _():
+            jobs.step(0)
+
         span = pl.ds(pl.multiple_of(i * TILE, TILE), TILE)
         dout = mm_t(hbuf[span, :], wproj[...]).astype(bf16)
         product = dout.astype(f32) * oall[span, :].astype(f32)
@@ -705,6 +736,7 @@
         dqkv[span, 0:TILE] = (rates[span, 0:TILE] * (dq - qhat * (along * inv_square))).astype(bf16)
 
     load_w.wait()
+    jobs.step(1)
 
     @pl.loop(0, 4)
     def _(i):
@@ -722,6 +754,7 @@
             parts[span, n : n + TILE] = mm_t(low, wqkv[n : n + TILE, :]).astype(bf16)
         collect.block_done(j)
 
+    jobs.step(2)
     for n in range(0, hbuf.shape[1], 2 * TILE):
         dwproj[:, n : n + 2 * TILE] = rows_mm(oall[...], hbuf[:, n : n + 2 * TILE]).astype(bf16)
     save_proj = mover.copy(dwproj, dwproj_out)
@@ -751,6 +784,452 @@
     collect.finish()
     save_proj.wait()
     save_w.wait()
+    jobs.finish()
+
+
+def groups(dps):
+    d, b = lax.axis_index("dp"), lax.axis_index("blk")
+    side, pairs = d % 2, dps // 2
+    pair = d // 2
+    ahead = [((pair + k) % pairs) * 2 + side for k in range(pairs)]
+    behind = [((pair - k + pairs) % pairs) * 2 + side for k in range(pairs)]
+    return d, b, d + 1 - 2 * side, ahead, behind
+
+
+class DpGather:
+    def __init__(self, shards):
+        self.shards = list(shards)
+        self.dps = lax.axis_size("dp")
+        self.inputs = [(one, ANY) for one in self.shards]
+        self.outs = [
+            (shaped(self.dps, *one.shape, dtype=one.dtype), ANY) for one in self.shards
+        ]
+        count = len(self.shards)
+        sems = pltpu.SemaphoreType.DMA((count, self.dps))
+        self.scratch = [sems, sems, pltpu.SemaphoreType.DMA((count,))]
+
+    def bind(self, ins, outs, scratch):
+        send, recv, local = scratch
+        d, b, other, ahead, behind = groups(self.dps)
+        pairs = self.dps // 2
+        self.partners = [(other, b)] + [(t, b) for t in ahead[1:]]
+        self.first, self.direct, self.forward, self.local = [], [], [], []
+        for a, (src, dst) in enumerate(zip(ins, outs)):
+            self.local.append(pltpu.make_async_copy(src, dst.at[d], local.at[a]))
+            self.first.append(remote(src, dst.at[d], send.at[a, 0], recv.at[a, 0], (other, b)))
+            self.direct.append([None])
+            self.forward.append([None])
+            for k in range(1, pairs):
+                self.direct[a].append(
+                    remote(src, dst.at[d], send.at[a, k], recv.at[a, k], (ahead[k], b))
+                )
+                at = pairs + k
+                self.forward[a].append(
+                    remote(
+                        dst.at[behind[k]], dst.at[behind[k]], send.at[a, at], recv.at[a, at], (other, b)
+                    )
+                )
+        self.order = [(k, a) for k in range(1, pairs) for a in range(len(ins))]
+
+    def start(self):
+        for k, a in self.order:
+            self.direct[a][k].start()
+        for one in self.first + self.local:
+            one.start()
+
+    def step(self, hook, hooks):
+        low, high = (len(self.order) * hook) // hooks, (len(self.order) * (hook + 1)) // hooks
+        for k, a in self.order[low:high]:
+            self.direct[a][k].wait_recv()
+            self.forward[a][k].start()
+
+    def finish(self):
+        for one in self.local:
+            one.wait()
+        for one in self.first:
+            one.wait()
+        for k, a in self.order:
+            self.direct[a][k].wait_send()
+            self.forward[a][k].wait()
+
+
+class DpScatter:
+    def __init__(self, values, dtypes):
+        self.values = list(values)
+        self.dps = lax.axis_size("dp")
+        self.inputs = [(one, ANY) for one in self.values]
+        self.outs = [
+            (shaped(*one.shape[1:], dtype=dtype), VMEM) for one, dtype in zip(self.values, dtypes)
+        ]
+        pairs = self.dps // 2
+        self.scratch = []
+        for one in self.values:
+            self.scratch += [pltpu.VMEM((pairs, *one.shape[1:]), bf16)] * 3
+            self.scratch += [pltpu.SemaphoreType.DMA((2 * pairs,))] * 2
+            self.scratch += [pltpu.SemaphoreType.DMA((pairs,))]
+
+    def bind(self, ins, outs, scratch):
+        d, b, other, ahead, behind = groups(self.dps)
+        pairs = self.dps // 2
+        self.partners = [(other, b)] + [(t, b) for t in ahead[1:]]
+        self.results = outs
+        self.bufs, self.local, self.cross, self.direct = [], [], [], []
+        for a, src in enumerate(ins):
+            mine, near, far, send, recv, local = scratch[6 * a : 6 * a + 6]
+            self.bufs.append((mine, near, far))
+            self.local.append([])
+            self.cross.append([])
+            self.direct.append([None])
+            for k in range(pairs):
+                target = ahead[k]
+                theirs = target + 1 - 2 * (target % 2)
+                self.local[a].append(
+                    pltpu.make_async_copy(src.at[target], mine.at[k], local.at[k])
+                )
+                self.cross[a].append(
+                    remote(src.at[theirs], near.at[k], send.at[k], recv.at[k], (other, b))
+                )
+                if k:
+                    at = pairs + k
+                    self.direct[a].append(
+                        remote(mine.at[k], far.at[k], send.at[at], recv.at[at], (target, b))
+                    )
+        self.order = [(k, a) for k in range(1, pairs) for a in range(len(ins))]
+        self.last = [(0, a) for a in range(len(ins))]
+
+    def start(self):
+        for k, a in self.order + self.last:
+            self.cross[a][k].start()
+            self.local[a][k].start()
+
+    def add(self, a, k):
+        self.local[a][k].wait()
+        self.cross[a][k].wait_recv()
+        mine, near, _ = self.bufs[a]
+        rows = mine.shape[1]
+        step = min(rows, STEP)
+
+        @pl.loop(0, rows // step)
+        def _(s):
+            span = pl.ds(pl.multiple_of(s * step, step), step)
+            total = mine[k, span, :].astype(f32) + near[k, span, :].astype(f32)
+            mine[k, span, :] = total.astype(bf16)
+
+    def step(self, hook, hooks):
+        low, high = (len(self.order) * hook) // hooks, (len(self.order) * (hook + 1)) // hooks
+        for k, a in self.order[low:high]:
+            self.add(a, k)
+            self.direct[a][k].start()
+
+    def finish(self):
+        for k, a in self.last:
+            self.add(a, k)
+        for k, a in self.order:
+            self.direct[a][k].wait()
+        for k, a in self.order + self.last:
+            self.cross[a][k].wait_send()
+        for a, result in enumerate(self.results):
+            mine, _, far = self.bufs[a]
+            rows = mine.shape[1]
+            step = min(rows, STEP)
+
+            @pl.loop(0, rows // step)
+            def _(s):
+                span = pl.ds(pl.multiple_of(s * step, step), step)
+                total = mine[0, span, :].astype(f32)
+                for k in range(1, self.dps // 2):
+                    total = total + far[k, span, :].astype(f32)
+                result[span, :] = total.astype(result.dtype)
+
+
+class Swap:
+    def __init__(self, values):
+        self.values = list(values)
+        self.inputs = [(one, ANY) for one in self.values]
+        self.outs = [(shaped(*one.shape, dtype=one.dtype), ANY) for one in self.values]
+        sems = pltpu.SemaphoreType.DMA((len(self.values), 4))
+        self.scratch = [sems, sems]
+
+    def bind(self, ins, outs, scratch):
+        send, recv = scratch
+        d, b = lax.axis_index("dp"), lax.axis_index("blk")
+        self.partners = [(d, (b + k) % 4) for k in range(1, 4)]
+        self.local, self.sent = [], []
+        for a, (src, dst) in enumerate(zip(ins, outs)):
+            self.local.append(pltpu.make_async_copy(src.at[b], dst.at[b], send.at[a, 0]))
+            for k in range(1, 4):
+                to = (b + k) % 4
+                self.sent.append(
+                    remote(src.at[to], dst.at[b], send.at[a, k], recv.at[a, k], (d, to))
+                )
+
+    def start(self):
+        for one in self.sent + self.local:
+            one.start()
+
+    def step(self, hook, hooks):
+        pass
+
+    def finish(self):
+        for one in self.sent + self.local:
+            one.wait()
+
+
+class Jobs:
+    def __init__(self, jobs):
+        self.jobs = jobs
+
+    def greet(self, sibling, peer):
+        d, b = lax.axis_index("dp"), lax.axis_index("blk")
+        others = [sibling, peer]
+        if any(isinstance(job, Swap) for job in self.jobs):
+            others.append((d, 3 - b))
+        dps = [job for job in self.jobs if not isinstance(job, Swap)]
+        if dps:
+            others += dps[0].partners
+        greet(others)
+
+    def start(self):
+        for job in self.jobs:
+            job.start()
+
+    def step(self, hook):
+        for job in self.jobs:
+            job.step(hook, 3)
+
+    def finish(self):
+        for job in self.jobs:
+            job.finish()
+
+
+def prepare_kernel(
+    gather_job,
+    cond,
+    ada_in,
+    qkv_in,
+    up_in,
+    ada_out,
+    cond_out,
+    qkv_out,
+    up_out,
+    conds,
+    columns,
+    answers,
+    ada,
+    cond_send,
+    cond_recv,
+    ada_send,
+    ada_recv,
+    answer_send,
+    answer_recv,
+    blk_send,
+    blk_recv,
+    local,
+):
+    dps, blks = lax.axis_size("dp"), lax.axis_size("blk")
+    count = dps * blks
+    d, b = lax.axis_index("dp"), lax.axis_index("blk")
+    me = d * blks + b
+    layers = qkv_in.shape[1]
+    rows, wide = ada_in.shape[1:]
+    slots = cond.shape[0]
+    others = [(me + k) % count for k in range(count)]
+    barrier = pltpu.get_barrier_semaphore()
+    for t in others[1:]:
+        pl.semaphore_signal(barrier, inc=1, device_id=(t // blks, t % blks), device_id_type=MESH)
+    pl.semaphore_wait(barrier, count - 1)
+
+    locals_ = [pltpu.make_async_copy(cond, conds.at[d], local.at[0])]
+    sends = []
+    for k in range(1, dps):
+        to = (d + k) % dps
+        sends.append(remote(cond, conds.at[d], cond_send.at[k], cond_recv.at[k], (to, b)))
+    swaps = []
+    for layer in range(layers):
+        pieces = []
+        for a, (src, dst) in enumerate(((qkv_in, qkv_out), (up_in, up_out))):
+            at = layer * 2 + a
+            locals_.append(
+                pltpu.make_async_copy(src.at[b, layer], dst.at[layer, b], local.at[1 + at])
+            )
+            for k in range(1, blks):
+                to = (b + k) % blks
+                pieces.append(
+                    remote(
+                        src.at[to, layer],
+                        dst.at[layer, b],
+                        blk_send.at[at, k],
+                        blk_recv.at[at, k],
+                        (d, to),
+                    )
+                )
+        swaps.append(pieces)
+    moves = []
+    for k in range(1, count):
+        t = others[k]
+        moves.append(
+            remote(
+                ada_in.at[t],
+                columns.at[pl.ds(pl.multiple_of(me * rows, rows), rows)],
+                ada_send.at[k],
+                ada_recv.at[k],
+                (t // blks, t % blks),
+            )
+        )
+    locals_.append(
+        pltpu.make_async_copy(
+            ada_in.at[me],
+            columns.at[pl.ds(pl.multiple_of(me * rows, rows), rows)],
+            local.at[1 + 2 * layers],
+        )
+    )
+    for one in locals_ + sends + swaps[0] + moves:
+        one.start()
+    for one in swaps[1:]:
+        for piece in one:
+            piece.start()
+    for one in swaps[0]:
+        one.wait_recv()
+    for one in locals_:
+        one.wait()
+    gather_job.start()
+    for one in sends:
+        one.wait_recv()
+    for one in moves:
+        one.wait_recv()
+    whole = mm(conds[...].reshape(dps * slots, conds.shape[2]), columns[...])
+    answers[...] = whole.reshape(dps, slots, wide)
+    place = pl.ds(pl.multiple_of(me * wide, 128), wide)
+    replies = []
+    for k in range(1, count):
+        t = others[k]
+        replies.append(
+            remote(
+                answers.at[t // blks],
+                ada.at[:, place],
+                answer_send.at[k],
+                answer_recv.at[k],
+                (t // blks, t % blks),
+            )
+        )
+    for one in replies:
+        one.start()
+    ada[:, place] = answers[d]
+    gather_job.step(0)
+    gather_job.step(1)
+    for one in replies:
+        one.wait_recv()
+    each = ada_out.shape[2]
+    for layer in range(layers):
+        value = ada[:, layer * each : (layer + 1) * each]
+        high = value.astype(bf16)
+        ada_out[layer, 0:slots, :] = high
+        ada_out[layer, slots : 2 * slots, :] = (value - high.astype(f32)).astype(bf16)
+    cond_out[...] = conds[...]
+    gather_job.step(2)
+    for one in sends + moves + replies:
+        one.wait_send()
+    for layer, pieces in enumerate(swaps):
+        for one in pieces:
+            one.wait_send()
+            if layer:
+                one.wait_recv()
+    gather_job.finish()
+
+
+def prepare(cond, ada_in, qkv_in, up_in, proj):
+    dps, blks = lax.axis_size("dp"), lax.axis_size("blk")
+    count = dps * blks
+    slots, width = cond.shape
+    layers = qkv_in.shape[1]
+    rows, wide = ada_in.shape[1:]
+    sems = pltpu.SemaphoreType.DMA
+    qkv_shard = (layers, blks, *qkv_in.shape[2:])
+    up_shard = (layers, blks, *up_in.shape[2:])
+    gather_outs = [
+        shaped(dps, *qkv_shard[1:], dtype=bf16),
+        shaped(dps, *proj.shape, dtype=bf16),
+    ]
+
+    def body(cond, ada_in, qkv_in, up_in, proj, ada_out, cond_out, qkv_out, up_out, whole_qkv, whole_proj, *scratch):
+        job = DpGather([jax.ShapeDtypeStruct(qkv_shard[1:], bf16), proj])
+        job.bind([qkv_out.at[0], proj], [whole_qkv, whole_proj], scratch[-3:])
+        prepare_kernel(
+            Jobs([job]), cond, ada_in, qkv_in, up_in, ada_out, cond_out, qkv_out, up_out, *scratch[:-3]
+        )
+
+    outs = [
+        (shaped(layers, 2 * slots, count * wide // layers, dtype=bf16), VMEM),
+        (shaped(dps, slots, width, dtype=bf16), VMEM),
+        (shaped(*qkv_shard, dtype=bf16), ANY),
+        (shaped(*up_shard, dtype=bf16), ANY),
+    ] + [(one, ANY) for one in gather_outs]
+    results = pl.pallas_call(
+        body,
+        out_shape=[one for one, _ in outs],
+        in_specs=[VMEM, ANY, ANY, ANY, ANY],
+        out_specs=[where for _, where in outs],
+        scratch_shapes=[
+            pltpu.VMEM((dps, slots, width), bf16),
+            pltpu.VMEM((count * rows, wide), bf16),
+            pltpu.VMEM((dps, slots, wide), f32),
+            pltpu.VMEM((slots, count * wide), f32),
+            sems((dps,)),
+            sems((dps,)),
+            sems((count,)),
+            sems((count,)),
+            sems((count,)),
+            sems((count,)),
+            sems((2 * layers, blks)),
+            sems((2 * layers, blks)),
+            sems((2 + 2 * layers,)),
+            sems((2, dps)),
+            sems((2, dps)),
+            sems((2,)),
+        ],
+        compiler_params=pltpu.CompilerParams(
+            collective_id=8, has_side_effects=True, vmem_limit_bytes=40 * 2**20
+        ),
+        cost_estimate=pl.CostEstimate(flops=2**35, bytes_accessed=2**24, transcendentals=0),
+    )(cond, ada_in, qkv_in, up_in, proj)
+    return results[:4], results[4:]
+
+
+def finish_kernel(jobs, out, staged, local, send, recv):
+    sibling, peer = partners()
+    jobs.greet(sibling, peer)
+    jobs.start()
+    for hook in range(3):
+        jobs.step(hook)
+    jobs.finish()
+    d, b = lax.axis_index("dp"), lax.axis_index("blk")
+    result = jobs.jobs[0].results[0]
+    rows = staged.shape[1]
+    for i in range(4):
+        staged[i] = result[i * rows : (i + 1) * rows, :]
+    sent = [pltpu.make_async_copy(staged.at[b], out.at[b], local)]
+    for k in range(1, 4):
+        to = (b + k) % 4
+        sent.append(remote(staged.at[to], out.at[b], send.at[k], recv.at[k], (d, to)))
+    for one in sent:
+        one.start()
+    for one in sent:
+        one.wait()
+
+
+def finish(scatter_job, swap_job):
+    rows, columns = scatter_job.values[0].shape[1:]
+    shape = (4, rows // 4, columns)
+    sems = pltpu.SemaphoreType.DMA
+    return run(
+        finish_kernel,
+        9,
+        [],
+        [(shaped(*shape, dtype=bf16), VMEM)],
+        [pltpu.VMEM(shape, bf16), sems, sems((4,)), sems((4,))],
+        2**30,
+        [scatter_job, swap_job],
+    )
 
 
 ANY = pl.BlockSpec(memory_space=pl.ANY)
@@ -761,9 +1240,26 @@
     return jax.ShapeDtypeStruct(shape, dtype)
 
 
-def run(kernel, ident, inputs, outs, scratch, flops):
-    return pl.pallas_call(
-        kernel,
+def run(kernel, ident, inputs, outs, scratch, flops, jobs=()):
+    sizes = [(len(inputs), len(outs), len(scratch))]
+    sizes += [(len(job.inputs), len(job.outs), len(job.scratch)) for job in jobs]
+    own_outs = len(outs)
+    for job in jobs:
+        inputs, outs, scratch = inputs + job.inputs, outs + job.outs, scratch + job.scratch
+
+    def body(*refs):
+        at = 0
+        shares = [[] for _ in sizes]
+        for kind in range(3):
+            for i, size in enumerate(sizes):
+                shares[i].append(refs[at : at + size[kind]])
+                at += size[kind]
+        for job, share in zip(jobs, shares[1:]):
+            job.bind(*share)
+        kernel(Jobs(jobs), *shares[0][0], *shares[0][1], *shares[0][2])
+
+    results = pl.pallas_call(
+        body,
         out_shape=[one for one, _ in outs],
         in_specs=[where for _, where in inputs],
         out_specs=[where for _, where in outs],
@@ -773,9 +1269,10 @@
         ),
         cost_estimate=pl.CostEstimate(flops=flops, bytes_accessed=2**24, transcendentals=0),
     )(*[one for one, _ in inputs])
-
-
-def attend(layer, size, x, onehot, ada, qscale, keyc, keyr, wqkv, wproj):
+    return results[:own_outs], results[own_outs:]
+
+
+def attend(layer, size, x, onehot, ada, qscale, keyc, keyr, wqkv, wproj, jobs=()):
     rows, width = x.shape
     length, wide = wqkv.shape
     big = pltpu.VMEM((rows, width), f32)
@@ -806,10 +1303,11 @@
         + spread_scratch(width)
         + collect_scratch(width),
         2**35,
+        jobs,
     )
 
 
-def mlp(layer, x, onehot, ada, wup, wdown):
+def mlp(layer, x, onehot, ada, wup, wdown, jobs=()):
     rows, width = x.shape
     length, ff = 4 * rows, wup.shape[1]
     big = pltpu.VMEM((rows, width), f32)
@@ -837,10 +1335,11 @@
         + spread_scratch(width)
         + collect_scratch(width),
         2**35,
+        jobs,
     )
 
 
-def mlp_back(layer, dx, result, mid, onehot, onehot_t, ada, wup, wdown, h, g, slope):
+def mlp_back(layer, dx, result, mid, onehot, onehot_t, ada, wup, wdown, h, g, slope, jobs=()):
     rows, width = dx.shape
     length, ff = 4 * rows, wup.shape[1]
     big = pltpu.VMEM((rows, width), f32)
@@ -874,11 +1373,30 @@
         + spread_scratch(width)
         + collect_scratch(width),
         2**35,
+        jobs,
     )
 
 
 def attend_back(
-    layer, size, dmid, branch, x, onehot, onehot_t, ada, qscale, keyc, keyr, inverse, wqkv, wproj, h, qkv, rates, o
+    layer,
+    size,
+    dmid,
+    branch,
+    x,
+    onehot,
+    onehot_t,
+    ada,
+    qscale,
+    keyc,
+    keyr,
+    inverse,
+    wqkv,
+    wproj,
+    h,
+    qkv,
+    rates,
+    o,
+    jobs=(),
 ):
     rows, width = dmid.shape
     length, wide = qkv.shape
@@ -919,6 +1437,7 @@
         + spread_scratch(width)
         + collect_scratch(width),
         2**35,
+        jobs,
     )
 
 
@@ -963,84 +1482,110 @@
     onehot_t = (slot_id[:, None] == item_own[None, :]).astype(bf16)
     onehot = (item_own[:, None] == jnp.concatenate([slot_id, slot_id])[None, :]).astype(bf16)
 
-    labels_all = gather(labels, "dp").reshape(-1)
-    chosen = labels_all[:, None] == jnp.arange(class_table.shape[0], dtype=jnp.int32)[None, :]
-    cond = mm(chosen.astype(bf16), class_table)
-    cond_act, silu_pull = jax.vjp(jax.nn.silu, cond)
-    cond_low = cond_act.astype(bf16)
+    def one_hot(names):
+        return (names[:, None] == jnp.arange(class_table.shape[0], dtype=jnp.int32)[None, :]).astype(bf16)
 
     wide = w_ada.shape[2]
     columns = layers * wide // count
     ada_cols = w_ada.transpose(1, 0, 2).reshape(wrows, count, columns).transpose(1, 0, 2)
-    ada_cols = lax.all_to_all(ada_cols, ("dp", "blk"), 0, 0, tiled=True)
-    ada_part = mm(cond_low, ada_cols.reshape(count * wrows, columns))
-    ada_part = lax.all_to_all(ada_part.reshape(dps, slots, columns), "dp", 0, 0, tiled=True)
-    ada_all = lax.all_gather(ada_part, "blk", axis=1, tiled=False)
-    ada_all = ada_all.transpose(2, 0, 1, 3).reshape(slots, layers, wide)
-    ada_all = jnp.pad(ada_all.transpose(1, 0, 2), ((0, 0), (0, padded - slots), (0, 0)))
-    ada_high = ada_all.astype(bf16)
-    ada_low = (ada_all - ada_high.astype(f32)).astype(bf16)
-    ada = jnp.concatenate([ada_high, ada_low], axis=1)
-
     qkv_cols = w_qkv.reshape(layers, wrows, 3, blks, piece).transpose(3, 0, 1, 2, 4)
+    qkv_cols = qkv_cols.reshape(blks, layers, wrows, 3 * piece)
     up_cols = w_up.reshape(layers, wrows, dps, blks, ffrows).transpose(3, 0, 1, 2, 4)
-    moved = jnp.concatenate(
-        [
-            qkv_cols.reshape(blks, layers, wrows, 3 * piece),
-            up_cols.reshape(blks, layers, wrows, ff),
-        ],
-        axis=3,
-    )
-    moved = lax.all_to_all(moved, "blk", 0, 0, tiled=True)
-    moved = moved.transpose(1, 0, 2, 3).reshape(layers, blks * wrows, 3 * piece + ff)
+    up_cols = up_cols.reshape(blks, layers, wrows, ff)
     to_heads = [(i, (i % dps) * blks + i // dps) for i in range(count)]
     to_rows = [(j, i) for i, j in to_heads]
     proj_own = lax.ppermute(w_proj, ("dp", "blk"), to_heads)
-    weights = []
-    for layer in range(layers):
-        weights.append(
-            (
-                gather(moved[layer, :, : 3 * piece], "dp"),
-                gather(proj_own[layer], "dp"),
-                gather(moved[layer, :, 3 * piece :], "dp"),
-                gather(w_down[layer], "dp"),
-            )
+    own_cond = jax.nn.silu(mm(one_hot(labels[0]), class_table)).astype(bf16)
+    own_cond = jnp.pad(own_cond, ((0, padded - slots), (0, 0)))
+    if columns % 128 == 0 and wrows % 16 == 0:
+        (ada, cond_all, qkv_shards, up_shards), (first_qkv, first_proj) = prepare(
+            own_cond, ada_cols, qkv_cols, up_cols, proj_own[0]
         )
+        cond_all = cond_all.reshape(dps * padded, width)
+    else:
+        cond_all = gather(own_cond, "dp")
+        ada_cols = lax.all_to_all(ada_cols, ("dp", "blk"), 0, 0, tiled=True)
+        ada_part = mm(cond_all, ada_cols.reshape(count * wrows, columns))
+        ada_part = lax.all_to_all(ada_part.reshape(dps, padded, columns), "dp", 0, 0, tiled=True)
+        ada_all = lax.all_gather(ada_part, "blk", axis=1, tiled=False)
+        ada_all = ada_all.transpose(2, 0, 1, 3).reshape(padded, layers, wide).transpose(1, 0, 2)
+        ada_high = ada_all.astype(bf16)
+        ada_low = (ada_all - ada_high.astype(f32)).astype(bf16)
+        ada = jnp.concatenate([ada_high, ada_low], axis=1)
+        qkv_shards = lax.all_to_all(qkv_cols, "blk", 0, 0, tiled=True).transpose(1, 0, 2, 3)
+        up_shards = lax.all_to_all(up_cols, "blk", 0, 0, tiled=True).transpose(1, 0, 2, 3)
+        first_qkv, first_proj = gather(qkv_shards[:1], "dp"), gather(proj_own[:1], "dp")
 
     own_scale = lax.dynamic_slice_in_dim(head_scale, b * own_heads, own_heads, axis=1)
     qscales = jnp.repeat(jnp.exp(own_scale), size, axis=1)
 
     state = tokens[0].astype(f32)
-    saved = []
+    saved, weights = [], []
+    w_query, w_out = first_qkv, first_proj
     for layer in range(layers):
-        w_query, w_out, w_first, w_second = weights[layer]
+        w_query = w_query.reshape(length, 3 * piece)
+        w_out = w_out.reshape(piece, width)
         qscale = qscales[layer][None, :]
-        h, qkv, rates, o, inverse, branch, mid = attend(
-            layer, size, state, onehot, ada[layer], qscale, keyc, keyr, w_query, w_out
+        (h, qkv, rates, o, inverse, branch, mid), (w_first, w_second) = attend(
+            layer,
+            size,
+            state,
+            onehot,
+            ada[layer],
+            qscale,
+            keyc,
+            keyr,
+            w_query,
+            w_out,
+            [DpGather([up_shards[layer], w_down[layer]])],
         )
-        h2, g, slope, result, following = mlp(layer, mid, onehot, ada[layer], w_first, w_second)
+        w_first, w_second = w_first.reshape(width, ff), w_second.reshape(ff, width)
+        weights.append((w_query, w_out, w_first, w_second))
+        more = layer + 1 < layers
+        (h2, g, slope, result, following), gathered = mlp(
+            layer,
+            mid,
+            onehot,
+            ada[layer],
+            w_first,
+            w_second,
+            [DpGather([qkv_shards[layer + 1], proj_own[layer + 1]])] if more else [],
+        )
+        if more:
+            w_query, w_out = gathered
         saved.append((state, h, qkv, rates, o, inverse, branch, mid, h2, g, slope, result))
         state = following
     output = state.astype(bf16)[None]
 
     grad = cotangent[0].astype(f32)
+    own_rows = lax.dynamic_slice_in_dim(cond_all, (d * blks + b) * wrows, wrows, axis=1)
     cond_grad = 0.0
-    scale_grads, pieces = [None] * layers, [None] * layers
+    scale_grads = [None] * layers
+    ada_grads, up_grads, down_grads, qkv_grads, proj_grads = ([None] * layers for _ in range(5))
+
+    def item_term(items):
+        columns = items.shape[1] // blks
+        items = items.reshape(padded, blks, columns).transpose(1, 0, 2)
+        items = scatter(items, "blk").astype(bf16)
+        items = gather(items, ("dp", "blk")).reshape(dps, blks, padded, columns)
+        return items.transpose(0, 2, 1, 3).reshape(dps * padded, blks * columns)
+
+    waiting_scatter, waiting_swap = None, None
     for layer in reversed(range(layers)):
         w_query, w_out, w_first, w_second = weights[layer]
         qscale = qscales[layer][None, :]
         state, h, qkv, rates, o, inverse, branch, mid, h2, g, slope, result = saved[layer]
-        mid_grad, up_grad, down_grad, items_two = mlp_back(
-            layer, grad, result, mid, onehot, onehot_t, ada[layer], w_first, w_second, h2, g, slope
+        jobs = []
+        if waiting_scatter is not None:
+            jobs = [DpScatter(waiting_scatter, (bf16, f32)), Swap([waiting_swap])]
+        (mid_grad, up_grad, down_grad, items_two), done = mlp_back(
+            layer, grad, result, mid, onehot, onehot_t, ada[layer], w_first, w_second, h2, g, slope, jobs
         )
-        wide_grad = scatter(
-            jnp.concatenate(
-                [down_grad.reshape(dps, ffrows, width), up_grad.reshape(dps, blks * wrows, ff)], axis=1
-            ).reshape(-1, width),
-            "dp",
-        )
-        down_grad, up_grad = wide_grad[:ffrows].astype(f32), wide_grad[ffrows:]
-        grad, qkv_grad, proj_grad, items_one, scale_grad = attend_back(
+        swaps = []
+        if waiting_scatter is not None:
+            qkv_sum, proj_grads[layer + 1], up_grads[layer + 1] = done
+            swaps = [Swap([qkv_sum.reshape(blks, wrows, 3 * piece)])]
+        (grad, qkv_grad, proj_grad, items_one, scale_grad), done = attend_back(
             layer,
             size,
             mid_grad,
@@ -1059,37 +1604,55 @@
             qkv,
             rates,
             o,
+            [
+                DpScatter(
+                    [up_grad.reshape(dps, blks * wrows, ff), down_grad.reshape(dps, ffrows, width)],
+                    (bf16, f32),
+                )
+            ]
+            + swaps,
         )
-        qkv_grad = scatter(qkv_grad, "dp")
-        proj_grad = scatter(proj_grad, "dp")
+        up_sum, down_grads[layer] = done[:2]
+        if swaps:
+            qkv_grads[layer + 1] = done[2]
+        waiting_scatter = [
+            qkv_grad.reshape(dps, blks * wrows, 3 * piece),
+            proj_grad.reshape(dps, piece // dps, width),
+        ]
+        waiting_swap = up_sum.reshape(blks, wrows, ff)
         scale_grads[layer] = lax.dynamic_update_slice_in_dim(
             jnp.zeros((heads,), f32), scale_grad[0, ::size], b * own_heads, 0
         )
-        parts_one, parts_two = jnp.split(items_one, 3, axis=1), jnp.split(items_two, 3, axis=1)
-        item_grad = jnp.concatenate(
-            [part for pair in zip(parts_one, parts_two) for part in pair], axis=1
-        )[:slots]
-        item_grad = item_grad.reshape(slots, blks, wide // blks).transpose(1, 0, 2)
-        item_grad = scatter(item_grad, "blk").astype(bf16)
-        item_grad = gather(item_grad, ("dp", "blk")).reshape(dps, blks, slots, wide // blks)
-        item_grad = item_grad.transpose(0, 2, 1, 3).reshape(dps * slots, wide)
+        terms = [jnp.split(item_term(one), 3, axis=1) for one in (items_one, items_two)]
+        item_grad = jnp.concatenate([part for pair in zip(*terms) for part in pair], axis=1)
         cond_grad = cond_grad + mm_t(item_grad, w_ada[layer])
-        own_cond = lax.dynamic_slice_in_dim(cond_low, (d * blks + b) * wrows, wrows, axis=1)
-        ada_grad = rows_mm(own_cond, item_grad)
-        back = jnp.concatenate([qkv_grad, up_grad], axis=1)
-        back = lax.all_to_all(back.reshape(blks, wrows, 3 * piece + ff), "blk", 0, 0, tiled=True)
-        qkv_grad = back[:, :, : 3 * piece].reshape(blks, wrows, 3, piece)
-        qkv_grad = qkv_grad.transpose(1, 2, 0, 3).reshape(wrows, 3 * width).astype(f32)
-        up_grad = back[:, :, 3 * piece :].reshape(blks, wrows, dps, ffrows)
-        up_grad = up_grad.transpose(1, 2, 0, 3).reshape(wrows, ff * blks).astype(f32)
-        proj_grad = lax.ppermute(proj_grad, ("dp", "blk"), to_rows).astype(f32)
-        pieces[layer] = (qkv_grad, proj_grad, up_grad, down_grad, ada_grad)
-    cond_grad = gather(cond_grad.T, ("dp", "blk")).T
-    cond_pre = silu_pull(cond_grad)[0]
+        ada_grads[layer] = rows_mm(own_rows, item_grad)
+    (qkv_grads[0],), (_, proj_grads[0], up_grads[0]) = finish(
+        DpScatter(waiting_scatter, (bf16, f32)), Swap([waiting_swap])
+    )
+    for layer in range(layers):
+        one = qkv_grads[layer].reshape(blks, wrows, 3, piece)
+        qkv_grads[layer] = one.transpose(1, 2, 0, 3).reshape(wrows, 3 * width).astype(f32)
+        one = up_grads[layer].reshape(blks, wrows, dps, ffrows)
+        up_grads[layer] = one.transpose(1, 2, 0, 3).reshape(wrows, ff * blks).astype(f32)
+    proj_whole = lax.ppermute(jnp.stack(proj_grads), ("dp", "blk"), to_rows)
+    cond_grad = gather(cond_grad.T, ("dp", "blk")).T.reshape(dps, padded, width)[:, :slots]
+    chosen = one_hot(gather(labels, "dp").reshape(-1))
+    _, silu_pull = jax.vjp(jax.nn.silu, mm(chosen, class_table))
+    cond_pre = silu_pull(cond_grad.reshape(dps * slots, width))[0]
     table_grad = rows_mm(chosen.astype(f32), cond_pre, lax.Precision.HIGHEST)
     head_grad = lax.psum(jnp.stack(scale_grads), ("dp", "blk"))
-    stacked = [jnp.stack([one[i] for one in pieces]) for i in range(5)]
-    return (output, grad.astype(bf16)[None], table_grad, head_grad, *stacked)
+    return (
+        output,
+        grad.astype(bf16)[None],
+        table_grad,
+        head_grad,
+        jnp.stack(qkv_grads),
+        proj_whole,
+        jnp.stack(up_grads),
+        jnp.stack(down_grads),
+        jnp.stack(ada_grads),
+    )
 
 
 def solution(mesh):

time: 1060 us -> 907 us (0.86)
  waiting for transfers between devices: 401 us -> 2.68 us
  Pallas kernels: 289 us -> 559 us
  starting transfers between devices: 38.3 us -> 9.24 us
  blocking collectives: 228 us -> 250 us
    reduce_scatter x6 -> x4, waiting for transfers between devices: 283 us -> 0.05 us  [scatter(): return lax.psum_scatter(values, axes, scatter_dimension=0, tiled=True)]
    pallas_call x8 -> x10, Pallas kernels: 289 us -> 559 us  [the longest x9 482 us: run(): pl.pallas_call(body, out_shape=[one for one, _ in outs], in_specs=[where...]
    all_gather x8 -> x0, waiting for transfers between devices: 115 us -> none  [gather(): return lax.all_gather(values, axes, axis=0, tiled=True)]
    all_gather x4 -> x6, blocking collectives: 135 us -> 210 us  [gather(): return lax.all_gather(values, axes, axis=0, tiled=True)]
    all_to_all x4 -> x0, starting transfers between devices: 24 us -> none  [the longest x2 12.5 us: per_device(): lax.all_to_all(back.reshape(blks, wrows, 3 * piece + ff), 'blk', 0, 0, ti...]
    all_gather x1 -> x0, blocking collectives: 21.8 us -> none  [per_device(): ada_all = lax.all_gather(ada_part, 'blk', axis=1, tiled=False)]
    unnamed x1 -> x0, blocking collectives: 16.8 us -> none
    all_to_all x1 -> x0, blocking collectives: 14.7 us -> none  [per_device(): moved = lax.all_to_all(moved, 'blk', 0, 0, tiled=True)]
  transfers between devices with their start and end apart: 21 -> 6, of which waited for: 9 -> 1; matrix products, arithmetic and copies ran while one was open for 6% -> 4% of each run, Pallas kernels for 17% -> 18%
where the time goes in v3:
time: 907 us; the launch traced here: 896 us
  Pallas kernels  559 us (62%)
  blocking collectives  250 us (28%)
  local copies, waits for them, and re-layouts  33.7 us (4%)
  other arithmetic  16.2 us (2%)
  between operations  15.1 us (2%)
  matrix products  9.79 us (1%)
  starting transfers between devices  9.24 us (1%)
    pallas_call x9, Pallas kernels, run(): pl.pallas_call(body, out_shape=[one for one, _ in outs], in_specs=[where...  482 us
    all_gather x6, blocking collectives, gather(): return lax.all_gather(values, axes, axis=0, tiled=True)  210 us
    pallas_call x1, Pallas kernels, prepare(): pl.pallas_call(body, out_shape=[one for one, _ in outs], in_specs=[VMEM,...  77.5 us
    psum x1, blocking collectives, per_device(): head_grad = lax.psum(jnp.stack(scale_grads), ('dp', 'blk'))  40.1 us
  transfers between devices with their start and end apart: 6, of which 1 were waited for; matrix products, arithmetic and copies ran while one was open for 4% of the time, Pallas kernels for 18%

profile of v3, /device:TPU:7, one launch (start us, length us, event | category | flops | bytes accessed | tf_op | source)
XLA Modules:
  0.0 895.9 jit_solution(2945792767137617787)
XLA Ops:
  7.3 5.9 collective-permute-start
  13.2 2.1 bitcast_convert_fusion.1.refs_0_.refs_2_
  15.9 1.9 copy.82
  17.8 1.4 reshape.274
  19.2 1.4 copy.120
  20.6 1.0 reshape.275
  21.7 1.2 copy.122
  22.9 1.2 reshape.276.qkv_in
  24.1 1.4 reshape.277
  25.5 0.9 copy.121
  26.4 1.3 reshape.278.up_in
  27.8 0.7 broadcast_in_dim.62.refs_3_.refs_6_
  28.8 1.0 copy.86.refs_4_.refs_7_
  29.8 1.8 slice_bitcast_fusion.2
  31.7 0.7 broadcast_in_dim.68.refs_3_.refs_6_
  32.4 2.1 bitcast_convert_fusion.refs_0_
  34.5 11.8 %all-gather = s32[8,1,12]{2,1,0:T(1,128)S(1)} all-gather(s32[1,1,12]{2,1,0:T(1,128)S(1)} %bitcast.241), channel_id=1, replica_groups=mesh['dp'=8,'blk'=4] {'dp'}, dimensions={0}, use_global_device_ids=true | all-gather | bytes 432 | tf_op jit(solution)/shard_map/all_gather | solution.py:51
  46.9 0.7 reduce.3
  48.1 1.3 fusion.16
  49.3 0.7 compare_convert_fusion.refs_1_.refs_3_
  50.7 0.6 slice_bitcast_fusion.7
  51.3 1.0 copy-done.2
  52.3 77.5 %shard_map.196 = (bf16[2,32,6144]{2,1,0:T(8,128)(2,1)S(1)}, bf16[8,16,1024]{2,1,0:T(8,128)(2,1)S(1)}, bf16[2,4,32,768]{3,2,1,0:T(8,128)(2,1)S(1)}, bf16[2,4,32,1...) custom-call(bf16[16,1024]{1,0:T(8,128)(2,1)S(1)} %pad.4.cond, ...), custom_call_target="tpu_custom_call" | custom-call | flops 34359738368 | bytes 16777216 | tf_op jit(solution)/shard_map/pallas_call | solution.py:1167
  129.8 1.0 slice_bitcast_fusion
  130.8 0.8 slice_bitcast_fusion.3
  131.6 0.7 slice_bitcast_fusion.6.refs_5_
  132.3 62.1 %shard_map.197 = (bf16[1024,1024]{1,0:T(8,128)(2,1)}, bf16[1024,768]{1,0:T(8,128)(2,1)}, f32[1024,512]{1,0:T(8,128)}, bf16[1024,256]{1,0:T(8,128)(2,1)}, f32[4,8...) custom-call(f32[256,1024]{1,0:T(8,128)} %bitcast_convert_fusion.1.re, ...), custom_call_target="tpu_custom_call" | custom-call | flops 34359738368 | bytes 16777216 | tf_op jit(solution)/shard_map/pallas_call | solution.py:1261
  194.4 54.1 %shard_map.198 = (bf16[1024,1024]{1,0:T(8,128)(2,1)}, bf16[1024,1024]{1,0:T(8,128)(2,1)}, bf16[1024,1024]{1,0:T(8,128)(2,1)}, f32[256,1024]{1,0:T(8,128)}, f32[2...) custom-call(f32[256,1024]{1,0:T(8,128)} %get-tuple-element.78.refs_0_.refs_2_, ...), custom_call_target="tpu_custom_call" | custom-call | flops 34359738368 | bytes 16777216 | tf_op jit(solution)/shard_map/pallas_call | solution.py:1261
  248.5 66.8 %shard_map.199 = (bf16[1024,1024]{1,0:T(8,128)(2,1)}, bf16[1024,768]{1,0:T(8,128)(2,1)}, f32[1024,512]{1,0:T(8,128)}, bf16[1024,256]{1,0:T(8,128)(2,1)}, f32[4,8...) custom-call(f32[256,1024]{1,0:T(8,128)} %get-tuple-element.82.refs_0, ...), custom_call_target="tpu_custom_call" | custom-call | flops 34359738368 | bytes 16777216 | tf_op jit(solution)/shard_map/pallas_call | solution.py:1261
  315.3 30.1 %shard_map.200 = (bf16[1024,1024]{1,0:T(8,128)(2,1)}, bf16[1024,1024]{1,0:T(8,128)(2,1)}, bf16[1024,1024]{1,0:T(8,128)(2,1)}, f32[256,1024]{1,0:T(8,128)}, f32[256,1024]{1,0:T(8,128)}) custom-call(f32[256,1024]{1,0:T(8,128)} %get-tuple-element.85.refs_0_.refs_2_, bf16[256,32]{1,0:T(8,128)(2,1)} %compare_convert_fusion.refs_1_.refs_3_, ...), custom_call_target="tpu_custom_call" | custom-call | flops 34359738368 | bytes 16777216 | tf_op jit(solution)/shard_map/pallas_call | solution.py:1261
  345.4 31.2 %shard_map.201 = (f32[256,1024]{1,0:T(8,128)}, bf16[1024,1024]{1,0:T(8,128)(2,1)}, bf16[1024,1024]{1,0:T(8,128)(2,1)}, f32[16,3072]{1,0:T(8,128)}) custom-call(f32[256,1024]{1,0:T(8,128)} %bitcast_convert_fusion.refs_0_, f32[256,1024]{1,0:T(8,128)} %get-tuple-element.89.refs_1_, f32[256,1024]{1,0:T(8,128)} %get-tuple-element.85.refs_0_.refs_2_, ...), custom_call_target="tpu_custom_call" | custom-call | flops 34359738368 | bytes 16777216 | tf_op jit(solution)/shard_map/pallas_call | solution.py:1261
  376.6 77.0 %shard_map.202 = (f32[256,1024]{1,0:T(8,128)}, bf16[1024,768]{1,0:T(8,128)(2,1)}, bf16[256,1024]{1,0:T(8,128)(2,1)}, f32[16,3072]{1,0:T(8,128)}, f32[1,256]{1,0:...) custom-call(f32[256,1024]{1,0:T(8,128)} %get-tuple-element.93.refs_0_, f32[256,1024]{1,0:T(8,128)} %get-tuple-element.94.refs_1_, ...), custom_call_target="tpu_custom_call" | custom-call | flops 34359738368 | bytes 16777216 | tf_op jit(solution)/shard_map/pallas_call | solution.py:1261
  453.6 1.6 copy.126
  455.3 48.0 %shard_map.203 = (f32[256,1024]{1,0:T(8,128)}, bf16[1024,1024]{1,0:T(8,128)(2,1)}, bf16[1024,1024]{1,0:T(8,128)(2,1)}, f32[16,3072]{1,0:T(8,128)}, bf16[128,768]...) custom-call(f32[256,1024]{1,0:T(8,128)} %get-tuple-element.102.refs_0_, ...), custom_call_target="tpu_custom_call" | custom-call | flops 34359738368 | bytes 16777216 | tf_op jit(solution)/shard_map/pallas_call | solution.py:1261
  503.4 66.1 %shard_map.204 = (f32[256,1024]{1,0:T(8,128)}, bf16[1024,768]{1,0:T(8,128)(2,1)}, bf16[256,1024]{1,0:T(8,128)(2,1)}, f32[16,3072]{1,0:T(8,128)}, f32[1,256]{1,0:...) custom-call(f32[256,1024]{1,0:T(8,128)} %get-tuple-element.110.refs_0_, ...), custom_call_target="tpu_custom_call" | custom-call | flops 34359738368 | bytes 16777216 | tf_op jit(solution)/shard_map/pallas_call | solution.py:1261
  569.5 0.7 copy.125
  570.2 0.7 slice.80
  571.8 46.7 %shard_map.205 = (bf16[4,32,768]{2,1,0:T(8,128)(2,1)}, bf16[128,768]{1,0:T(8,128)(2,1)}, f32[32,1024]{1,0:T(8,128)}, bf16[4,32,1024]{2,1,0:T(8,128)(2,1)}) custom-call(bf16[8,128,768]{2,1,0:T(8,128)(2,1)} %bitcast.258, bf16[8,32,1024]{2,1,0:T(8,128)(2,1)} %bitcast.262, bf16[4,32,1024]{2,1,0:T(8,128)(2,1)} %bitcast.266), custom_call_target="tpu_custom_call" | custom-call | flops 1073741824 | bytes 16777216 | tf_op jit(solution)/shard_map/pallas_call | solution.py:1261
  618.5 40.1 %psum.7 = f32[2,16]{1,0:T(2,128)} all-reduce(f32[2,16]{1,0:T(2,128)S(1)} %pad_maximum_fusion.3), channel_id=1, replica_groups=mesh['dp'=8,'blk'=4] {'dp','blk'}, use_global_device_ids=true, to_apply=%region_9.10 | all-reduce | flops 32 | bytes 256 | tf_op jit(solution)/shard_map/psum | solution.py:1644
  658.6 0.7 copy.124
  659.3 0.7 copy.123
  660.9 3.2 collective-permute-start.1
  665.5 0.9 convert_bitcast_fusion.1
  666.4 0.9 maximum_convert_fusion.1
  667.3 1.0 maximum_convert_fusion
  668.3 1.0 pad_maximum_fusion.1
  669.4 0.9 convert_bitcast_fusion
  670.2 2.6 collective-permute-done.1
  672.8 0.8 convert_element_type.127
  673.6 39.2 %all_gather.19 = bf16[32,16,768]{2,1,0:T(8,128)(2,1)S(1)} all-gather(bf16[1,16,768]{2,1,0:T(8,128)(2,1)S(1)} %convert_element_type.127), channel_id=1, replica_groups=mesh['dp'=8,'blk'=4] {'dp','blk'}, dimensions={0}, use_global_device_ids=true | all-gather | bytes 811008 | tf_op jit(solution)/shard_map/all_gather | solution.py:51
  713.5 0.8 convert_element_type.128
  714.3 41.1 %all_gather.20 = bf16[32,16,768]{2,1,0:T(8,128)(2,1)S(1)} all-gather(bf16[1,16,768]{2,1,0:T(8,128)(2,1)S(1)} %convert_element_type.128), channel_id=1, replica_groups=mesh['dp'=8,'blk'=4] {'dp','blk'}, dimensions={0}, use_global_device_ids=true | all-gather | bytes 811008 | tf_op jit(solution)/shard_map/all_gather | solution.py:51
  756.1 0.8 convert_element_type.129
  756.9 39.0 %all_gather.21 = bf16[32,16,768]{2,1,0:T(8,128)(2,1)S(1)} all-gather(bf16[1,16,768]{2,1,0:T(8,128)(2,1)S(1)} %convert_element_type.129), channel_id=1, replica_groups=mesh['dp'=8,'blk'=4] {'dp','blk'}, dimensions={0}, use_global_device_ids=true | all-gather | bytes 811008 | tf_op jit(solution)/shard_map/all_gather | solution.py:51
  796.4 0.9 copy-done.5
  798.0 0.8 convert_element_type.130
  798.8 40.0 %all_gather.22 = bf16[32,16,768]{2,1,0:T(8,128)(2,1)S(1)} all-gather(bf16[1,16,768]{2,1,0:T(8,128)(2,1)S(1)} %convert_element_type.130), channel_id=1, replica_groups=mesh['dp'=8,'blk'=4] {'dp','blk'}, dimensions={0}, use_global_device_ids=true | all-gather | bytes 811008 | tf_op jit(solution)/shard_map/all_gather | solution.py:51
  840.0 1.3 convolution_bitcast_fusion
  841.8 0.7 copy-done.9
  842.5 0.6 fusion
  843.1 38.4 %all_gather.23 = f32[1024,128]{1,0:T(8,128)S(1)} all-gather(f32[32,128]{1,0:T(8,128)S(1)} %fusion), channel_id=1, replica_groups=mesh['dp'=8,'blk'=4] {'dp','blk'}, dimensions={0}, use_global_device_ids=true | all-gather | bytes 540672 | tf_op jit(solution)/shard_map/all_gather | solution.py:51
  881.9 5.0 fusion.3
  886.9 1.2 pad_maximum_fusion
  888.2 0.7 copy.146
  (152 shorter events, 10.1 us)
Async XLA Ops:
  7.2 40.5 %copy-start = (bf16[1001,1024]{1,0:T(8,128)(2,1)S(1)}, bf16[1001,1024]{1,0:T(8,128)(2,1)}, u32[]{:S(2)}) copy-start(bf16[1001,1024]{1,0:T(8,128)(2,1)} %param.17) | copy-start | bytes 6150148
  7.2 8.2 copy-start.33
  7.2 8.2 copy-start.32
  7.2 665.6 %reduce-scatter.5.cloned.1.call-start = ((), (), s32[]{:S(2)}) async-start(), calls=%async_computation.4 | async-start | bytes 245760 | tf_op jit(solution)/shard_map/reduce_scatter | solution.py:55
  7.3 43.4 %collective-permute-start = (bf16[2,32,1024]{2,1,0:T(8,128)(2,1)}, bf16[2,32,1024]{2,1,0:T(8,128)(2,1)S(1)}, u32[]{:S(2)}, u32[]{:S(2)}) collective-permute-start(bf16[2,32,1024]{2,1,0:T(8,128)(2,1)} %param.20), channel_id=1, source_target_pairs={{0,0},{1,4},{2,8},{3,12},{4,16},{5,20},{6,24},{7,28},{8,1},{9,5},{... | collective-permute-start | bytes 393224 | tf_op jit(solution)/shard_map/ppermute | solution.py:1497
  17.8 2.8 copy-start.14
  24.1 3.6 copy-start.30
  24.1 4.5 copy-start.31
  28.8 5.8 copy-start.28
  28.8 5.8 copy-start.29
  47.6 1.7 copy-start.26
  51.3 1.0 copy-start.2
  129.8 2.5 copy-start.4
  129.8 2.5 copy-start.3
  455.3 258.2 %reduce-scatter.7.cloned.1.call-start = ((), (), s32[]{:S(2)}) async-start(), calls=%async_computation.5 | async-start | bytes 245760 | tf_op jit(solution)/shard_map/reduce_scatter | solution.py:55
  503.3 66.1 %copy-start.21 = (f32[16,3072]{1,0:T(8,128)S(1)}, f32[16,3072]{1,0:T(8,128)}, u32[]{:S(2)}) copy-start(f32[16,3072]{1,0:T(8,128)} %get-tuple-element.122) | copy-start | bytes 589828
  503.4 66.8 %copy-start.34 = (f32[1,256]{1,0:T(1,128)S(1)}, f32[1,256]{1,0:T(1,128)}, u32[]{:S(2)}) copy-start(f32[1,256]{1,0:T(1,128)} %get-tuple-element.126) | copy-start | bytes 3076
  571.0 185.1 %reduce-scatter.9.cloned.1.call-start = ((), (), s32[]{:S(2)}) async-start(), calls=%async_computation.6 | async-start | bytes 245760 | tf_op jit(solution)/shard_map/reduce_scatter | solution.py:55
  571.8 86.8 %copy-start.23 = (f32[16,3072]{1,0:T(8,128)S(1)}, f32[16,3072]{1,0:T(8,128)}, u32[]{:S(2)}) copy-start(f32[16,3072]{1,0:T(8,128)} %get-tuple-element.123) | copy-start | bytes 589828
  571.8 87.5 %copy-start.22 = (f32[16,3072]{1,0:T(8,128)S(1)}, f32[16,3072]{1,0:T(8,128)}, u32[]{:S(2)}) copy-start(f32[16,3072]{1,0:T(8,128)} %get-tuple-element.124) | copy-start | bytes 589828
  571.8 88.2 %copy-start.19 = (bf16[4,32,768]{2,1,0:T(8,128)(2,1)S(1)}, bf16[4,32,768]{2,1,0:T(8,128)(2,1)}, u32[]{:S(2)}) copy-start(bf16[4,32,768]{2,1,0:T(8,128)(2,1)} %get-tuple-element.131) | copy-start | bytes 589828
  618.5 41.9 %copy-start.20 = (bf16[4,32,768]{2,1,0:T(8,128)(2,1)S(1)}, bf16[4,32,768]{2,1,0:T(8,128)(2,1)}, u32[]{:S(2)}) copy-start(bf16[4,32,768]{2,1,0:T(8,128)(2,1)} %get-tuple-element.130) | copy-start | bytes 589828
  659.3 1.5 copy-start.24
  659.3 1.6 copy-start.25
  660.0 4.1 copy-start.17
  660.7 3.9 copy-start.18
  660.9 11.9 %collective-permute-start.1 = (f32[2,32,1024]{2,1,0:T(8,128)S(1)}, f32[2,32,1024]{2,1,0:T(8,128)S(1)}, u32[]{:S(2)}, u32[]{:S(2)}) collective-permute-start(f32[2,32,1024]{2,1,0:T(8,128)S(1)} %pad_maximum_fusion.2), channel_id=1, source_target_pairs={{0,0},{4,1},{8,2},{12,3},{16,4},{20,5},{24,6},{28,7},{1,8},{5,9},{... | collective-permute-start | bytes 786440 | tf_op jit(solution)/shard_map/ppermute | solution.py:1638
  664.2 1.2 copy-start.10
  664.7 133.2 %reduce-scatter.11.cloned.1.call-start = ((), (), s32[]{:S(2)}) async-start(), calls=%async_computation.7 | async-start | bytes 245760 | tf_op jit(solution)/shard_map/reduce_scatter | solution.py:55
  666.3 2.0 copy-start.12
  666.3 2.0 copy-start.13
  667.3 2.1 copy-start.11
  672.8 40.6 %copy-start.15 = (f32[2,32,1024]{2,1,0:T(8,128)}, f32[2,32,1024]{2,1,0:T(8,128)S(1)}, u32[]{:S(2)}) copy-start(f32[2,32,1024]{2,1,0:T(8,128)S(1)} %collective-permute-done.1) | copy-start | bytes 786436
  795.9 1.4 copy-start.8
  796.4 0.9 copy-start.5
  838.8 1.1 copy-start.6
  841.4 1.1 copy-start.9
  843.1 38.7 %copy-start.27 = (s32[96]{0:T(128)S(1)}, s32[96]{0:T(128)}, u32[]{:S(2)}) copy-start(s32[96]{0:T(128)} %copy-done.26) | copy-start | bytes 1156
  881.8 5.1 copy-start.7
  881.9 7.0 copy-start.1
  886.9 1.3 copy-start.16
Sparse Core Ops, SparseCore 0:
  455.4 29.9 reduce-scatter.4
  571.1 28.5 reduce-scatter.6
  664.8 20.1 reduce-scatter.8
  687.3 19.8 reduce-scatter.10

commit v4 on v3

--- a/solution.py
+++ b/solution.py
@@ -975,6 +975,109 @@
             one.wait()
 
 
+class Items:
+    def __init__(self, items):
+        self.dps = lax.axis_size("dp")
+        slots, columns = items.shape
+        self.quarter = columns // 4
+        self.inputs = [(items, ANY)]
+        self.outs = [(shaped(4, self.dps, slots, self.quarter, dtype=bf16), VMEM)]
+        sems = pltpu.SemaphoreType.DMA
+        self.scratch = [
+            pltpu.VMEM((4, slots, self.quarter), f32),
+            pltpu.VMEM((self.dps, slots, self.quarter), bf16),
+            sems((8,)),
+            sems((8,)),
+            sems((self.dps,)),
+            sems((self.dps,)),
+        ]
+
+    def bind(self, ins, outs, scratch):
+        (src,), (out,) = ins, outs
+        self.terms, self.held, send, recv, dp_send, dp_recv = scratch
+        d, b = lax.axis_index("dp"), lax.axis_index("blk")
+        self.here, self.out = (d, b), out
+        self.partners = [((d + k) % self.dps, b) for k in range(1, self.dps)]
+
+        def quarter(i):
+            return src.at[:, pl.ds(pl.multiple_of(i * self.quarter, 128), self.quarter)]
+
+        self.first = [pltpu.make_async_copy(quarter(b), self.terms.at[0], send.at[0])]
+        self.last = []
+        for k in range(1, 4):
+            to = (b + k) % 4
+            self.first.append(
+                remote(quarter(to), self.terms.at[k], send.at[k], recv.at[k], (d, to))
+            )
+            self.last.append(
+                remote(self.held, out.at[b], send.at[4 + k], recv.at[4 + k], (d, to))
+            )
+        self.over = [
+            remote(self.held.at[d], self.held.at[d], dp_send.at[k], dp_recv.at[k], to)
+            for k, to in enumerate(self.partners)
+        ]
+
+    def start(self):
+        for one in self.first:
+            one.start()
+
+    def step(self, hook, hooks):
+        d, b = self.here
+        if hook == 0:
+            for one in self.first:
+                one.wait()
+            total = (self.terms[0] + self.terms[1]) + (self.terms[2] + self.terms[3])
+            self.held[d] = total.astype(bf16)
+            for one in self.over:
+                one.start()
+        if hook == 1:
+            for one in self.over:
+                one.wait()
+            for one in self.last:
+                one.start()
+            self.out[b] = self.held[...]
+
+    def finish(self):
+        for one in self.last:
+            one.wait()
+
+
+def greet_all():
+    dps, blks = lax.axis_size("dp"), lax.axis_size("blk")
+    me = lax.axis_index("dp") * blks + lax.axis_index("blk")
+    others = [(me + k) % (dps * blks) for k in range(1, dps * blks)]
+    greet([(t // blks, t % blks) for t in others])
+
+
+class Permute:
+    def __init__(self, src, dst, send, recv, back):
+        dps, blks = lax.axis_size("dp"), lax.axis_size("blk")
+        d, b = lax.axis_index("dp"), lax.axis_index("blk")
+        owner, user = d * blks + b, b * dps + d
+        self.moves = owner != user
+        to = (user // blks, user % blks) if back else (owner % dps, owner // dps)
+        self.away = remote(src, dst, send, recv, to)
+        self.stay = pltpu.make_async_copy(src, dst, send)
+
+    def start(self):
+        @pl.when(self.moves)
+        def _():
+            self.away.start()
+
+        @pl.when(jnp.logical_not(self.moves))
+        def _():
+            self.stay.start()
+
+    def wait(self):
+        @pl.when(self.moves)
+        def _():
+            self.away.wait()
+
+        @pl.when(jnp.logical_not(self.moves))
+        def _():
+            self.stay.wait()
+
+
 class Jobs:
     def __init__(self, jobs):
         self.jobs = jobs
@@ -982,11 +1085,11 @@
     def greet(self, sibling, peer):
         d, b = lax.axis_index("dp"), lax.axis_index("blk")
         others = [sibling, peer]
-        if any(isinstance(job, Swap) for job in self.jobs):
+        if any(isinstance(job, (Swap, Items)) for job in self.jobs):
             others.append((d, 3 - b))
         dps = [job for job in self.jobs if not isinstance(job, Swap)]
         if dps:
-            others += dps[0].partners
+            others += max((job.partners for job in dps), key=len)
         greet(others)
 
     def start(self):
@@ -1003,232 +1106,260 @@
 
 
 def prepare_kernel(
-    gather_job,
-    cond,
+    rows_in,
     ada_in,
     qkv_in,
     up_in,
+    proj_in,
     ada_out,
-    cond_out,
+    rows_out,
+    qkv_shard,
+    up_shard,
+    proj_shard,
     qkv_out,
-    up_out,
-    conds,
+    proj_out,
     columns,
     answers,
     ada,
-    cond_send,
-    cond_recv,
+    dp_send,
+    dp_recv,
     ada_send,
     ada_recv,
     answer_send,
     answer_recv,
     blk_send,
     blk_recv,
+    proj_send,
+    proj_recv,
     local,
+    *gather_scratch,
 ):
     dps, blks = lax.axis_size("dp"), lax.axis_size("blk")
     count = dps * blks
     d, b = lax.axis_index("dp"), lax.axis_index("blk")
     me = d * blks + b
-    layers = qkv_in.shape[1]
+    layers, double, each = ada_out.shape
+    slots = double // 2
     rows, wide = ada_in.shape[1:]
-    slots = cond.shape[0]
-    others = [(me + k) % count for k in range(count)]
-    barrier = pltpu.get_barrier_semaphore()
-    for t in others[1:]:
-        pl.semaphore_signal(barrier, inc=1, device_id=(t // blks, t % blks), device_id_type=MESH)
-    pl.semaphore_wait(barrier, count - 1)
-
-    locals_ = [pltpu.make_async_copy(cond, conds.at[d], local.at[0])]
+    greet_all()
+    job = DpGather([shaped(*qkv_shard.shape, dtype=bf16), shaped(*proj_shard.shape[1:], dtype=bf16)])
+    job.bind([qkv_shard, proj_shard.at[0]], [qkv_out, proj_out], gather_scratch)
+
+    permutes = [
+        Permute(proj_in.at[i], proj_shard.at[i], proj_send.at[i], proj_recv.at[i], False)
+        for i in range(layers)
+    ]
+    copies = [pltpu.make_async_copy(rows_in, rows_out.at[d], local.at[0])]
     sends = []
     for k in range(1, dps):
-        to = (d + k) % dps
-        sends.append(remote(cond, conds.at[d], cond_send.at[k], cond_recv.at[k], (to, b)))
+        sends.append(
+            remote(rows_in, rows_out.at[d], dp_send.at[k], dp_recv.at[k], ((d + k) % dps, b))
+        )
     swaps = []
-    for layer in range(layers):
-        pieces = []
-        for a, (src, dst) in enumerate(((qkv_in, qkv_out), (up_in, up_out))):
-            at = layer * 2 + a
-            locals_.append(
-                pltpu.make_async_copy(src.at[b, layer], dst.at[layer, b], local.at[1 + at])
+    for a, (src, dst) in enumerate(((qkv_in, qkv_shard), (up_in, up_shard))):
+        copies.append(pltpu.make_async_copy(src.at[b], dst.at[b], local.at[1 + a]))
+        for k in range(1, blks):
+            to = (b + k) % blks
+            swaps.append(
+                remote(src.at[to], dst.at[b], blk_send.at[a, k], blk_recv.at[a, k], (d, to))
             )
-            for k in range(1, blks):
-                to = (b + k) % blks
-                pieces.append(
-                    remote(
-                        src.at[to, layer],
-                        dst.at[layer, b],
-                        blk_send.at[at, k],
-                        blk_recv.at[at, k],
-                        (d, to),
-                    )
-                )
-        swaps.append(pieces)
     moves = []
+    span = pl.ds(pl.multiple_of(me * rows, rows), rows)
+    copies.append(pltpu.make_async_copy(ada_in.at[me], columns.at[span], local.at[3]))
     for k in range(1, count):
-        t = others[k]
-        moves.append(
-            remote(
-                ada_in.at[t],
-                columns.at[pl.ds(pl.multiple_of(me * rows, rows), rows)],
-                ada_send.at[k],
-                ada_recv.at[k],
-                (t // blks, t % blks),
-            )
-        )
-    locals_.append(
-        pltpu.make_async_copy(
-            ada_in.at[me],
-            columns.at[pl.ds(pl.multiple_of(me * rows, rows), rows)],
-            local.at[1 + 2 * layers],
-        )
-    )
-    for one in locals_ + sends + swaps[0] + moves:
+        t = (me + k) % count
+        to = (t // blks, t % blks)
+        moves.append(remote(ada_in.at[t], columns.at[span], ada_send.at[k], ada_recv.at[k], to))
+    for one in permutes[:1] + swaps[: blks - 1] + copies + sends + moves:
         one.start()
-    for one in swaps[1:]:
-        for piece in one:
-            piece.start()
-    for one in swaps[0]:
+    for one in swaps[: blks - 1]:
         one.wait_recv()
-    for one in locals_:
+    for one in copies:
         one.wait()
-    gather_job.start()
-    for one in sends:
+    permutes[0].wait()
+    job.start()
+    for one in swaps[blks - 1 :] + permutes[1:]:
+        one.start()
+    for one in sends + moves:
         one.wait_recv()
-    for one in moves:
-        one.wait_recv()
-    whole = mm(conds[...].reshape(dps * slots, conds.shape[2]), columns[...])
+    value = rows_out[...].astype(f32)
+    value = (value / (1.0 + jnp.exp(-value))).astype(bf16)
+    whole = mm(value.reshape(dps * slots, rows_out.shape[2]), columns[...])
     answers[...] = whole.reshape(dps, slots, wide)
     place = pl.ds(pl.multiple_of(me * wide, 128), wide)
     replies = []
     for k in range(1, count):
-        t = others[k]
+        t = (me + k) % count
+        to = (t // blks, t % blks)
         replies.append(
             remote(
-                answers.at[t // blks],
-                ada.at[:, place],
-                answer_send.at[k],
-                answer_recv.at[k],
-                (t // blks, t % blks),
+                answers.at[t // blks], ada.at[:, place], answer_send.at[k], answer_recv.at[k], to
             )
         )
     for one in replies:
         one.start()
     ada[:, place] = answers[d]
-    gather_job.step(0)
-    gather_job.step(1)
     for one in replies:
         one.wait_recv()
-    each = ada_out.shape[2]
     for layer in range(layers):
         value = ada[:, layer * each : (layer + 1) * each]
         high = value.astype(bf16)
         ada_out[layer, 0:slots, :] = high
-        ada_out[layer, slots : 2 * slots, :] = (value - high.astype(f32)).astype(bf16)
-    cond_out[...] = conds[...]
-    gather_job.step(2)
-    for one in sends + moves + replies:
+        ada_out[layer, slots:double, :] = (value - high.astype(f32)).astype(bf16)
+    for hook in range(3):
+        job.step(hook, 3)
+    for one in sends + moves + replies + swaps:
         one.wait_send()
-    for layer, pieces in enumerate(swaps):
-        for one in pieces:
-            one.wait_send()
-            if layer:
-                one.wait_recv()
-    gather_job.finish()
-
-
-def prepare(cond, ada_in, qkv_in, up_in, proj):
+    for one in swaps[blks - 1 :]:
+        one.wait_recv()
+    for one in permutes[1:]:
+        one.wait()
+    job.finish()
+
+
+def prepare(rows_in, ada_in, qkv_in, up_in, proj):
     dps, blks = lax.axis_size("dp"), lax.axis_size("blk")
     count = dps * blks
-    slots, width = cond.shape
-    layers = qkv_in.shape[1]
+    slots, width = rows_in.shape
+    layers = proj.shape[0]
     rows, wide = ada_in.shape[1:]
     sems = pltpu.SemaphoreType.DMA
-    qkv_shard = (layers, blks, *qkv_in.shape[2:])
-    up_shard = (layers, blks, *up_in.shape[2:])
-    gather_outs = [
-        shaped(dps, *qkv_shard[1:], dtype=bf16),
-        shaped(dps, *proj.shape, dtype=bf16),
-    ]
-
-    def body(cond, ada_in, qkv_in, up_in, proj, ada_out, cond_out, qkv_out, up_out, whole_qkv, whole_proj, *scratch):
-        job = DpGather([jax.ShapeDtypeStruct(qkv_shard[1:], bf16), proj])
-        job.bind([qkv_out.at[0], proj], [whole_qkv, whole_proj], scratch[-3:])
-        prepare_kernel(
-            Jobs([job]), cond, ada_in, qkv_in, up_in, ada_out, cond_out, qkv_out, up_out, *scratch[:-3]
-        )
-
     outs = [
         (shaped(layers, 2 * slots, count * wide // layers, dtype=bf16), VMEM),
         (shaped(dps, slots, width, dtype=bf16), VMEM),
-        (shaped(*qkv_shard, dtype=bf16), ANY),
-        (shaped(*up_shard, dtype=bf16), ANY),
-    ] + [(one, ANY) for one in gather_outs]
-    results = pl.pallas_call(
-        body,
-        out_shape=[one for one, _ in outs],
-        in_specs=[VMEM, ANY, ANY, ANY, ANY],
-        out_specs=[where for _, where in outs],
-        scratch_shapes=[
-            pltpu.VMEM((dps, slots, width), bf16),
-            pltpu.VMEM((count * rows, wide), bf16),
-            pltpu.VMEM((dps, slots, wide), f32),
-            pltpu.VMEM((slots, count * wide), f32),
-            sems((dps,)),
-            sems((dps,)),
-            sems((count,)),
-            sems((count,)),
-            sems((count,)),
-            sems((count,)),
-            sems((2 * layers, blks)),
-            sems((2 * layers, blks)),
-            sems((2 + 2 * layers,)),
-            sems((2, dps)),
-            sems((2, dps)),
-            sems((2,)),
-        ],
-        compiler_params=pltpu.CompilerParams(
-            collective_id=8, has_side_effects=True, vmem_limit_bytes=40 * 2**20
-        ),
-        cost_estimate=pl.CostEstimate(flops=2**35, bytes_accessed=2**24, transcendentals=0),
-    )(cond, ada_in, qkv_in, up_in, proj)
-    return results[:4], results[4:]
-
-
-def finish_kernel(jobs, out, staged, local, send, recv):
-    sibling, peer = partners()
-    jobs.greet(sibling, peer)
-    jobs.start()
-    for hook in range(3):
-        jobs.step(hook)
-    jobs.finish()
+        (shaped(*qkv_in.shape, dtype=bf16), ANY),
+        (shaped(*up_in.shape, dtype=bf16), ANY),
+        (shaped(*proj.shape, dtype=bf16), ANY),
+        (shaped(dps, *qkv_in.shape, dtype=bf16), ANY),
+        (shaped(dps, *proj.shape[1:], dtype=bf16), ANY),
+    ]
+    scratch = [
+        pltpu.VMEM((count * rows, wide), bf16),
+        pltpu.VMEM((dps, slots, wide), f32),
+        pltpu.VMEM((slots, count * wide), f32),
+    ]
+    scratch += [sems((dps,))] * 2 + [sems((count,))] * 4
+    scratch += [sems((2, blks))] * 2 + [sems((layers,))] * 2 + [sems((4,))]
+    scratch += [sems((2, dps))] * 2 + [sems((2,))]
+    return run(
+        lambda jobs, *refs: prepare_kernel(*refs),
+        8,
+        [(rows_in, ANY), (ada_in, ANY), (qkv_in, ANY), (up_in, ANY), (proj, ANY)],
+        outs,
+        scratch,
+        2**35,
+    )[0]
+
+
+def finish_kernel(
+    jobs,
+    cond,
+    w_ada,
+    notes,
+    proj_next,
+    two_next,
+    one_next,
+    two,
+    qkv_out,
+    proj_out,
+    ada_grad,
+    message_out,
+    staged,
+    message,
+    blk_send,
+    blk_recv,
+    proj_send,
+    proj_recv,
+    all_send,
+    all_recv,
+    local,
+):
+    items, scatter_job, swap = jobs.jobs
+    dps, blks = lax.axis_size("dp"), lax.axis_size("blk")
+    count = dps * blks
     d, b = lax.axis_index("dp"), lax.axis_index("blk")
-    result = jobs.jobs[0].results[0]
-    rows = staged.shape[1]
+    me = d * blks + b
+    greet_all()
+    for job in jobs.jobs:
+        job.start()
+    permute_next = Permute(proj_next, proj_out.at[1], proj_send.at[1], proj_recv.at[1], True)
+    permute_next.start()
+    rows = w_ada.shape[1]
+    width = w_ada.shape[2] // 6
+    people = cond.shape[1]
+
+    def fold(layer, second, dada, total):
+        quarter = dada.shape[3]
+        for c in range(0, 3 * width, TILE):
+            at = (c // width) * 2 * width + second * width + c % width
+            inner = c % quarter
+            value = dada[c // quarter, :, :, inner : inner + TILE].reshape(people, TILE)
+            ada_grad[layer, :, at : at + TILE] = mm(cond[...], value)
+            total = total + mm_t(w_ada[layer, :, at : at + TILE], value)
+        return total
+
+    items.step(0, 3)
+    total = fold(1, 1, two_next, jnp.zeros((rows, people), f32))
+    items.step(1, 3)
+    total = fold(1, 0, one_next, total)
+    scatter_job.step(0, 3)
+    total = fold(0, 1, two, total)
+    items.finish()
+    total = fold(0, 0, items.out, total)
+    message[0:rows, :] = total
+    message[rows:, :] = notes[...]
+    told = [pltpu.make_async_copy(message, message_out.at[me], local.at[0])]
+    for k in range(1, count):
+        t = (me + k) % count
+        to = (t // blks, t % blks)
+        told.append(remote(message, message_out.at[me], all_send.at[k], all_recv.at[k], to))
+    for one in told:
+        one.start()
+    scatter_job.step(1, 3)
+    scatter_job.step(2, 3)
+    scatter_job.finish()
+    qkv_sum, proj_sum = scatter_job.results
+    permute = Permute(proj_sum, proj_out.at[0], proj_send.at[0], proj_recv.at[0], True)
+    permute.start()
+    height = staged.shape[1]
     for i in range(4):
-        staged[i] = result[i * rows : (i + 1) * rows, :]
-    sent = [pltpu.make_async_copy(staged.at[b], out.at[b], local)]
+        staged[i] = qkv_sum[i * height : (i + 1) * height, :]
+    sent = [pltpu.make_async_copy(staged.at[b], qkv_out.at[b], local.at[1])]
     for k in range(1, 4):
         to = (b + k) % 4
-        sent.append(remote(staged.at[to], out.at[b], send.at[k], recv.at[k], (d, to)))
+        sent.append(remote(staged.at[to], qkv_out.at[b], blk_send.at[k], blk_recv.at[k], (d, to)))
     for one in sent:
         one.start()
-    for one in sent:
+    swap.finish()
+    for one in sent + told + [permute, permute_next]:
         one.wait()
 
 
-def finish(scatter_job, swap_job):
+def finish(scatter_job, swap_job, items_job, cond, w_ada, notes, proj_next, dadas):
+    dps, blks = lax.axis_size("dp"), lax.axis_size("blk")
+    count = dps * blks
     rows, columns = scatter_job.values[0].shape[1:]
     shape = (4, rows // 4, columns)
     sems = pltpu.SemaphoreType.DMA
+    message = shaped(w_ada.shape[1] + notes.shape[0], cond.shape[1])
+    inputs = [cond, w_ada, notes, proj_next, *dadas]
     return run(
         finish_kernel,
         9,
-        [],
-        [(shaped(*shape, dtype=bf16), VMEM)],
-        [pltpu.VMEM(shape, bf16), sems, sems((4,)), sems((4,))],
+        [(one, VMEM) for one in inputs],
+        [
+            (shaped(*shape, dtype=bf16), VMEM),
+            (shaped(2, *proj_next.shape), VMEM),
+            (shaped(*w_ada.shape), VMEM),
+            (shaped(count, *message.shape), VMEM),
+        ],
+        [pltpu.VMEM(shape, bf16), pltpu.VMEM(message.shape, f32)]
+        + [sems((4,))] * 2
+        + [sems((2,))] * 2
+        + [sems((count,))] * 2
+        + [sems((2,))],
         2**30,
-        [scatter_job, swap_job],
+        [items_job, scatter_job, swap_job],
     )
 
 
@@ -1482,28 +1613,30 @@
     onehot_t = (slot_id[:, None] == item_own[None, :]).astype(bf16)
     onehot = (item_own[:, None] == jnp.concatenate([slot_id, slot_id])[None, :]).astype(bf16)
 
+    names = jnp.pad(labels[0], (0, padded - slots), constant_values=-1)
+
     def one_hot(names):
         return (names[:, None] == jnp.arange(class_table.shape[0], dtype=jnp.int32)[None, :]).astype(bf16)
 
     wide = w_ada.shape[2]
     columns = layers * wide // count
     ada_cols = w_ada.transpose(1, 0, 2).reshape(wrows, count, columns).transpose(1, 0, 2)
-    qkv_cols = w_qkv.reshape(layers, wrows, 3, blks, piece).transpose(3, 0, 1, 2, 4)
-    qkv_cols = qkv_cols.reshape(blks, layers, wrows, 3 * piece)
-    up_cols = w_up.reshape(layers, wrows, dps, blks, ffrows).transpose(3, 0, 1, 2, 4)
-    up_cols = up_cols.reshape(blks, layers, wrows, ff)
-    to_heads = [(i, (i % dps) * blks + i // dps) for i in range(count)]
-    to_rows = [(j, i) for i, j in to_heads]
-    proj_own = lax.ppermute(w_proj, ("dp", "blk"), to_heads)
-    own_cond = jax.nn.silu(mm(one_hot(labels[0]), class_table)).astype(bf16)
-    own_cond = jnp.pad(own_cond, ((0, padded - slots), (0, 0)))
+    qkv_cols = w_qkv.reshape(layers, wrows, 3, blks, piece).transpose(0, 3, 1, 2, 4)
+    qkv_cols = qkv_cols.reshape(layers, blks, wrows, 3 * piece)
+    up_cols = w_up.reshape(layers, wrows, dps, blks, ffrows).transpose(0, 3, 1, 2, 4)
+    up_cols = up_cols.reshape(layers, blks, wrows, ff)
+    class_rows = mm(one_hot(names), class_table).astype(bf16)
     if columns % 128 == 0 and wrows % 16 == 0:
-        (ada, cond_all, qkv_shards, up_shards), (first_qkv, first_proj) = prepare(
-            own_cond, ada_cols, qkv_cols, up_cols, proj_own[0]
+        ada, class_rows, qkv_shard, up_shard, proj_own, first_qkv, first_proj = prepare(
+            class_rows, ada_cols, qkv_cols[0], up_cols[0], w_proj
         )
-        cond_all = cond_all.reshape(dps * padded, width)
+        class_rows = class_rows.reshape(dps * padded, width)
+        cond_all = jax.nn.silu(class_rows.astype(f32)).astype(bf16)
     else:
-        cond_all = gather(own_cond, "dp")
+        to_heads = [(i, (i % dps) * blks + i // dps) for i in range(count)]
+        proj_own = lax.ppermute(w_proj, ("dp", "blk"), to_heads)
+        class_rows = gather(class_rows, "dp")
+        cond_all = jax.nn.silu(class_rows.astype(f32)).astype(bf16)
         ada_cols = lax.all_to_all(ada_cols, ("dp", "blk"), 0, 0, tiled=True)
         ada_part = mm(cond_all, ada_cols.reshape(count * wrows, columns))
         ada_part = lax.all_to_all(ada_part.reshape(dps, padded, columns), "dp", 0, 0, tiled=True)
@@ -1512,9 +1645,9 @@
         ada_high = ada_all.astype(bf16)
         ada_low = (ada_all - ada_high.astype(f32)).astype(bf16)
         ada = jnp.concatenate([ada_high, ada_low], axis=1)
-        qkv_shards = lax.all_to_all(qkv_cols, "blk", 0, 0, tiled=True).transpose(1, 0, 2, 3)
-        up_shards = lax.all_to_all(up_cols, "blk", 0, 0, tiled=True).transpose(1, 0, 2, 3)
-        first_qkv, first_proj = gather(qkv_shards[:1], "dp"), gather(proj_own[:1], "dp")
+        qkv_shard = lax.all_to_all(qkv_cols[0], "blk", 0, 0, tiled=True)
+        up_shard = lax.all_to_all(up_cols[0], "blk", 0, 0, tiled=True)
+        first_qkv, first_proj = gather(qkv_shard[None], "dp"), gather(proj_own[:1], "dp")
 
     own_scale = lax.dynamic_slice_in_dim(head_scale, b * own_heads, own_heads, axis=1)
     qscales = jnp.repeat(jnp.exp(own_scale), size, axis=1)
@@ -1526,7 +1659,11 @@
         w_query = w_query.reshape(length, 3 * piece)
         w_out = w_out.reshape(piece, width)
         qscale = qscales[layer][None, :]
-        (h, qkv, rates, o, inverse, branch, mid), (w_first, w_second) = attend(
+        more = layer + 1 < layers
+        jobs = [DpGather([up_shard, w_down[layer]])]
+        if more:
+            jobs.append(Swap([qkv_cols[layer + 1], up_cols[layer + 1]]))
+        (h, qkv, rates, o, inverse, branch, mid), (w_first, w_second, *shards) = attend(
             layer,
             size,
             state,
@@ -1537,11 +1674,12 @@
             keyr,
             w_query,
             w_out,
-            [DpGather([up_shards[layer], w_down[layer]])],
+            jobs,
         )
         w_first, w_second = w_first.reshape(width, ff), w_second.reshape(ff, width)
         weights.append((w_query, w_out, w_first, w_second))
-        more = layer + 1 < layers
+        if more:
+            qkv_shard, up_shard = shards
         (h2, g, slope, result, following), gathered = mlp(
             layer,
             mid,
@@ -1549,7 +1687,7 @@
             ada[layer],
             w_first,
             w_second,
-            [DpGather([qkv_shards[layer + 1], proj_own[layer + 1]])] if more else [],
+            [DpGather([qkv_shard, proj_own[layer + 1]])] if more else [],
         )
         if more:
             w_query, w_out = gathered
@@ -1558,34 +1696,29 @@
     output = state.astype(bf16)[None]
 
     grad = cotangent[0].astype(f32)
-    own_rows = lax.dynamic_slice_in_dim(cond_all, (d * blks + b) * wrows, wrows, axis=1)
-    cond_grad = 0.0
-    scale_grads = [None] * layers
-    ada_grads, up_grads, down_grads, qkv_grads, proj_grads = ([None] * layers for _ in range(5))
-
-    def item_term(items):
-        columns = items.shape[1] // blks
-        items = items.reshape(padded, blks, columns).transpose(1, 0, 2)
-        items = scatter(items, "blk").astype(bf16)
-        items = gather(items, ("dp", "blk")).reshape(dps, blks, padded, columns)
-        return items.transpose(0, 2, 1, 3).reshape(dps * padded, blks * columns)
-
-    waiting_scatter, waiting_swap = None, None
+    up_grads, down_grads, qkv_grads, proj_grads = ([None] * layers for _ in range(4))
+    notes, dadas = [], []
+    waiting_scatter, waiting_swap, waiting_items = None, None, None
     for layer in reversed(range(layers)):
         w_query, w_out, w_first, w_second = weights[layer]
         qscale = qscales[layer][None, :]
         state, h, qkv, rates, o, inverse, branch, mid, h2, g, slope, result = saved[layer]
         jobs = []
         if waiting_scatter is not None:
-            jobs = [DpScatter(waiting_scatter, (bf16, f32)), Swap([waiting_swap])]
+            jobs = [
+                DpScatter(waiting_scatter, (bf16, f32)),
+                Swap([waiting_swap]),
+                Items(waiting_items),
+            ]
         (mid_grad, up_grad, down_grad, items_two), done = mlp_back(
             layer, grad, result, mid, onehot, onehot_t, ada[layer], w_first, w_second, h2, g, slope, jobs
         )
         swaps = []
         if waiting_scatter is not None:
-            qkv_sum, proj_grads[layer + 1], up_grads[layer + 1] = done
+            qkv_sum, proj_grads[layer + 1], up_grads[layer + 1], dada = done
+            dadas.append(dada)
             swaps = [Swap([qkv_sum.reshape(blks, wrows, 3 * piece)])]
-        (grad, qkv_grad, proj_grad, items_one, scale_grad), done = attend_back(
+        (grad, qkv_grad, proj_grad, waiting_items, scale_grad), done = attend_back(
             layer,
             size,
             mid_grad,
@@ -1608,40 +1741,52 @@
                 DpScatter(
                     [up_grad.reshape(dps, blks * wrows, ff), down_grad.reshape(dps, ffrows, width)],
                     (bf16, f32),
-                )
+                ),
+                Items(items_two),
             ]
             + swaps,
         )
-        up_sum, down_grads[layer] = done[:2]
+        up_sum, down_grads[layer], dada = done[:3]
+        dadas.append(dada)
         if swaps:
-            qkv_grads[layer + 1] = done[2]
+            qkv_grads[layer + 1] = done[3]
         waiting_scatter = [
             qkv_grad.reshape(dps, blks * wrows, 3 * piece),
             proj_grad.reshape(dps, piece // dps, width),
         ]
         waiting_swap = up_sum.reshape(blks, wrows, ff)
-        scale_grads[layer] = lax.dynamic_update_slice_in_dim(
-            jnp.zeros((heads,), f32), scale_grad[0, ::size], b * own_heads, 0
-        )
-        terms = [jnp.split(item_term(one), 3, axis=1) for one in (items_one, items_two)]
-        item_grad = jnp.concatenate([part for pair in zip(*terms) for part in pair], axis=1)
-        cond_grad = cond_grad + mm_t(item_grad, w_ada[layer])
-        ada_grads[layer] = rows_mm(own_rows, item_grad)
-    (qkv_grads[0],), (_, proj_grads[0], up_grads[0]) = finish(
-        DpScatter(waiting_scatter, (bf16, f32)), Swap([waiting_swap])
+        notes.append(scale_grad[:, ::size])
+    lanes = dps * padded
+    notes = [jnp.pad(one, ((0, 0), (0, lanes - own_heads))) for one in notes[::-1]]
+    notes.append(jnp.pad(names.astype(f32)[None, :], ((0, 0), (0, lanes - padded))))
+    notes = jnp.pad(jnp.concatenate(notes), ((0, 8 - len(notes)), (0, 0)))
+    cond_own = lax.dynamic_slice_in_dim(cond_all, (d * blks + b) * wrows, wrows, axis=1).T
+    (qkv_grads[0], proj_whole, ada_grads, told), done = finish(
+        DpScatter(waiting_scatter, (bf16, f32)),
+        Swap([waiting_swap]),
+        Items(waiting_items),
+        cond_own,
+        w_ada,
+        notes,
+        proj_grads[1],
+        dadas,
     )
+    up_grads[0] = done[3]
     for layer in range(layers):
         one = qkv_grads[layer].reshape(blks, wrows, 3, piece)
         qkv_grads[layer] = one.transpose(1, 2, 0, 3).reshape(wrows, 3 * width).astype(f32)
         one = up_grads[layer].reshape(blks, wrows, dps, ffrows)
         up_grads[layer] = one.transpose(1, 2, 0, 3).reshape(wrows, ff * blks).astype(f32)
-    proj_whole = lax.ppermute(jnp.stack(proj_grads), ("dp", "blk"), to_rows)
-    cond_grad = gather(cond_grad.T, ("dp", "blk")).T.reshape(dps, padded, width)[:, :slots]
-    chosen = one_hot(gather(labels, "dp").reshape(-1))
-    _, silu_pull = jax.vjp(jax.nn.silu, mm(chosen, class_table))
-    cond_pre = silu_pull(cond_grad.reshape(dps * slots, width))[0]
-    table_grad = rows_mm(chosen.astype(f32), cond_pre, lax.Precision.HIGHEST)
-    head_grad = lax.psum(jnp.stack(scale_grads), ("dp", "blk"))
+    head_grad = told[:, wrows : wrows + layers, :own_heads].reshape(dps, blks, layers, own_heads)
+    head_grad = jnp.sum(head_grad, axis=0).transpose(1, 0, 2).reshape(layers, heads)
+    every_name = told[::blks, wrows + layers, :padded].reshape(-1).astype(jnp.int32)
+    cond_grad = told[:, :wrows, :].reshape(width, lanes).T
+    _, silu_pull = jax.vjp(jax.nn.silu, class_rows.astype(f32))
+    cond_pre = silu_pull(cond_grad)[0]
+    pre_high = cond_pre.astype(bf16)
+    pre_low = (cond_pre - pre_high.astype(f32)).astype(bf16)
+    chosen = one_hot(jnp.concatenate([every_name, every_name]))
+    table_grad = rows_mm(chosen, jnp.concatenate([pre_high, pre_low]))
     return (
         output,
         grad.astype(bf16)[None],
@@ -1651,7 +1796,7 @@
         proj_whole,
         jnp.stack(up_grads),
         jnp.stack(down_grads),
-        jnp.stack(ada_grads),
+        ada_grads,
     )
 
 

time: 907 us -> 709 us (0.78)
  blocking collectives: 250 us -> 0 us
  Pallas kernels: 559 us -> 658 us
  between operations: 15.1 us -> 1.49 us
  starting transfers between devices: 9.24 us -> 0 us
  local copies, waits for them, and re-layouts: 33.7 us -> 24.6 us
    all_gather x6 -> x0, blocking collectives: 210 us -> none  [gather(): return lax.all_gather(values, axes, axis=0, tiled=True)]
    pallas_call x9 -> x10, Pallas kernels: 482 us -> 658 us  [run(): pl.pallas_call(body, out_shape=[one for one, _ in outs], in_specs=[where...]
    pallas_call x1 -> x0, Pallas kernels: 77.5 us -> none  [prepare(): pl.pallas_call(body, out_shape=[one for one, _ in outs], in_specs=[VMEM,...]
    psum x1 -> x0, blocking collectives: 40.1 us -> none  [per_device(): head_grad = lax.psum(jnp.stack(scale_grads), ('dp', 'blk'))]
    ppermute x2 -> x0, starting transfers between devices: 9.08 us -> none  [the longest x1 5.86 us: per_device(): proj_own = lax.ppermute(w_proj, ('dp', 'blk'), to_heads)]
  transfers between devices with their start and end apart: 6 -> 0, of which waited for: 1 -> 0; matrix products, arithmetic and copies ran while one was open for 4% -> 0% of each run, Pallas kernels for 18% -> 0%
where the time goes in v4:
time: 709 us; the launch traced here: 701 us
  Pallas kernels  658 us (93%)
  local copies, waits for them, and re-layouts  24.6 us (3%)
  other arithmetic  14 us (2%)
    pallas_call x10, Pallas kernels, run(): pl.pallas_call(body, out_shape=[one for one, _ in outs], in_specs=[where...  658 us

profile of v4, /device:TPU:7, one launch (start us, length us, event | category | flops | bytes accessed | tf_op | source)
XLA Modules:
  0.0 701.5 jit_solution(13882824911493504398)
XLA Ops:
  0.7 1.0 select_reduce_fusion.1
  1.7 0.2 reduce-window.8
  1.9 0.1 select_reduce_fusion
  2.0 0.7 convert_reduce_fusion.1
  2.9 1.0 copy.77.refs_4_.refs_7_
  4.1 0.7 compare_convert_fusion.refs_1_.refs_3_
  4.8 0.8 fusion.14
  5.7 0.6 broadcast_in_dim.67.refs_3_.refs_6_
  6.3 1.4 reshape.242
  7.8 0.7 fusion.21
  8.5 0.8 squeeze.58.refs_3_
  9.4 0.3 reshape.241
  9.7 0.2 copy.96
  9.9 0.2 fusion.22
  10.1 0.9 squeeze.57.refs_2_
  11.0 0.6 convert_bitcast_fusion.2
  11.6 1.0 convolution_convert_fusion.refs_0_
  12.6 0.8 copy.73
  13.4 0.5 reshape.240
  13.9 1.1 copy.94
  15.1 91.0 %shard_map.196 = (bf16[2,32,6144]{2,1,0:T(8,128)(2,1)}, bf16[8,16,1024]{2,1,0:T(8,128)(2,1)}, bf16[4,32,768]{2,1,0:T(8,128)(2,1)}, bf16[4,32,1024]{2,1,0:T(8,128...) custom-call(bf16[16,1024]{1,0:T(8,128)(2,1)} %convolution_convert_fusion.refs_0_, ...), custom_call_target="tpu_custom_call" | custom-call | flops 34359738368 | bytes 16777216 | tf_op jit(solution)/shard_map/pallas_call | solution.py:1392
  106.1 2.1 slice_bitcast_fusion
  108.3 0.8 squeeze.68.refs_11_
  109.1 0.9 squeeze.67.refs_10_
  110.0 1.1 bitcast_convert_fusion.1.refs_0_.refs_2_
  111.1 0.8 slice_bitcast_fusion.2
  111.9 66.6 %shard_map.197 = (bf16[1024,1024]{1,0:T(8,128)(2,1)}, bf16[1024,768]{1,0:T(8,128)(2,1)}, f32[1024,512]{1,0:T(8,128)}, bf16[1024,256]{1,0:T(8,128)(2,1)}, f32[4,8...) custom-call(f32[256,1024]{1,0:T(8,128)} %bitcast_convert_fusion.1.re, ...), custom_call_target="tpu_custom_call" | custom-call | flops 34359738368 | bytes 16777216 | tf_op jit(solution)/shard_map/pallas_call | solution.py:1392
  178.5 0.6 slice_bitcast_fusion.4.refs_6_
  179.1 49.8 %shard_map.198 = (bf16[1024,1024]{1,0:T(8,128)(2,1)}, bf16[1024,1024]{1,0:T(8,128)(2,1)}, bf16[1024,1024]{1,0:T(8,128)(2,1)}, f32[256,1024]{1,0:T(8,128)}, f32[2...) custom-call(f32[256,1024]{1,0:T(8,128)} %get-tuple-element.85.refs_0_.refs_2_, ...), custom_call_target="tpu_custom_call" | custom-call | flops 34359738368 | bytes 16777216 | tf_op jit(solution)/shard_map/pallas_call | solution.py:1392
  229.0 0.6 broadcast_in_dim.73.refs_3_.refs_6_
  229.7 66.7 %shard_map.199 = (bf16[1024,1024]{1,0:T(8,128)(2,1)}, bf16[1024,768]{1,0:T(8,128)(2,1)}, f32[1024,512]{1,0:T(8,128)}, bf16[1024,256]{1,0:T(8,128)(2,1)}, f32[4,8...) custom-call(f32[256,1024]{1,0:T(8,128)} %get-tuple-element.90.refs_0, ...), custom_call_target="tpu_custom_call" | custom-call | flops 34359738368 | bytes 16777216 | tf_op jit(solution)/shard_map/pallas_call | solution.py:1392
  296.4 30.7 %shard_map.200 = (bf16[1024,1024]{1,0:T(8,128)(2,1)}, bf16[1024,1024]{1,0:T(8,128)(2,1)}, bf16[1024,1024]{1,0:T(8,128)(2,1)}, f32[256,1024]{1,0:T(8,128)}, f32[256,1024]{1,0:T(8,128)}) custom-call(f32[256,1024]{1,0:T(8,128)} %get-tuple-element.94.refs_0_.refs_2_, bf16[256,32]{1,0:T(8,128)(2,1)} %compare_convert_fusion.refs_1_.refs_3_, ...), custom_call_target="tpu_custom_call" | custom-call | flops 34359738368 | bytes 16777216 | tf_op jit(solution)/shard_map/pallas_call | solution.py:1392
  327.1 0.6 fusion.11.refs_4_
  327.7 1.1 bitcast_convert_fusion.refs_0_
  328.8 31.3 %shard_map.201 = (f32[256,1024]{1,0:T(8,128)}, bf16[1024,1024]{1,0:T(8,128)(2,1)}, bf16[1024,1024]{1,0:T(8,128)(2,1)}, f32[16,3072]{1,0:T(8,128)}) custom-call(f32[256,1024]{1,0:T(8,128)} %bitcast_convert_fusion.refs_0_, f32[256,1024]{1,0:T(8,128)} %get-tuple-element.98.refs_1_, f32[256,1024]{1,0:T(8,128)} %get-tuple-element.94.refs_0_.refs_2_, ...), custom_call_target="tpu_custom_call" | custom-call | flops 34359738368 | bytes 16777216 | tf_op jit(solution)/shard_map/pallas_call | solution.py:1392
  360.1 93.3 %shard_map.202 = (f32[256,1024]{1,0:T(8,128)}, bf16[1024,768]{1,0:T(8,128)(2,1)}, bf16[256,1024]{1,0:T(8,128)(2,1)}, f32[16,3072]{1,0:T(8,128)}, f32[1,256]{1,0:...) custom-call(f32[256,1024]{1,0:T(8,128)} %get-tuple-element.102.refs_0_, ...), custom_call_target="tpu_custom_call" | custom-call | flops 34359738368 | bytes 16777216 | tf_op jit(solution)/shard_map/pallas_call | solution.py:1392
  453.4 54.2 %shard_map.203 = (f32[256,1024]{1,0:T(8,128)}, bf16[1024,1024]{1,0:T(8,128)(2,1)}, bf16[1024,1024]{1,0:T(8,128)(2,1)}, f32[16,3072]{1,0:T(8,128)}, bf16[128,768]...) custom-call(f32[256,1024]{1,0:T(8,128)} %get-tuple-element.112.refs_0_, ...), custom_call_target="tpu_custom_call" | custom-call | flops 34359738368 | bytes 16777216 | tf_op jit(solution)/shard_map/pallas_call | solution.py:1392
  507.6 89.2 %shard_map.204 = (f32[256,1024]{1,0:T(8,128)}, bf16[1024,768]{1,0:T(8,128)(2,1)}, bf16[256,1024]{1,0:T(8,128)(2,1)}, f32[16,3072]{1,0:T(8,128)}, f32[1,256]{1,0:...) custom-call(f32[256,1024]{1,0:T(8,128)} %get-tuple-element.121.refs_, ...), custom_call_target="tpu_custom_call" | custom-call | flops 34359738368 | bytes 16777216 | tf_op jit(solution)/shard_map/pallas_call | solution.py:1392
  596.8 2.2 pad_maximum_fusion
  599.0 0.1 slice.81
  599.1 0.1 slice.82
  599.2 0.6 pad.23.refs_2_
  599.8 0.2 copy.82
  600.0 0.1 add_divide_fusion
  600.2 0.6 fusion.12.refs_0_
  600.8 84.8 %shard_map.205 = (bf16[4,32,768]{2,1,0:T(8,128)(2,1)}, f32[2,32,1024]{2,1,0:T(8,128)}, f32[2,32,6144]{2,1,0:T(8,128)}, f32[32,40,128]{2,1,0:T(8,128)}, bf16[4,8,...) custom-call(bf16[32,128]{1,0:T(8,128)(2,1)} %fusion.12.refs_0_, ...), custom_call_target="tpu_custom_call" | custom-call | flops 1073741824 | bytes 16777216 | tf_op jit(solution)/shard_map/pallas_call | solution.py:1392
  685.6 1.0 copy.89
  686.7 0.2 copy.87
  686.9 0.2 convert_element_type.164
  687.2 0.2 copy.88
  687.4 0.2 convert_element_type.167
  687.6 1.0 maximum_convert_fusion
  688.8 0.2 copy.85
  688.9 0.1 convert_element_type.158
  689.2 0.2 copy.86
  689.4 0.1 convert_element_type.161
  689.5 0.9 maximum_convert_fusion.1
  690.5 0.2 fusion.20
  690.9 2.8 fusion.3
  693.7 1.0 slice.85
  694.7 0.6 reshape.265
  695.4 2.5 convert_bitcast_fusion
  697.9 0.7 copy.105
  698.6 2.7 copy.106
  (79 shorter events, 1.1 us)
Async XLA Ops:
  0.6 10.9 %copy-start = (bf16[1001,1024]{1,0:T(8,128)(2,1)S(1)}, bf16[1001,1024]{1,0:T(8,128)(2,1)}, u32[]{:S(2)}) copy-start(bf16[1001,1024]{1,0:T(8,128)(2,1)} %param.17) | copy-start | bytes 6150148
  2.9 6.5 copy-start.19
  2.9 6.4 copy-start.10
  4.0 1.6 copy-start.17
  8.5 2.4 copy-start.21
  9.6 3.0 copy-start.2
  15.1 93.2 %copy-start.4 = (bf16[1,4,32,8,128]{4,3,2,1,0:T(8,128)(2,1)S(1)}, bf16[1,4,32,8,128]{4,3,2,1,0:T(8,128)(2,1)}, u32[]{:S(2)}) copy-start(bf16[1,4,32,8,128]{4,3,2,1,0:T(8,128)(2,1)} %get-tuple-element.161) | copy-start | bytes 786436
  106.1 3.9 copy-start.5
  106.1 4.9 copy-start.7
  111.9 66.6 %copy-start.16 = (bf16[2,32,1024]{2,1,0:T(8,128)(2,1)S(1)}, bf16[2,32,1024]{2,1,0:T(8,128)(2,1)}, u32[]{:S(2)}) copy-start(bf16[2,32,1024]{2,1,0:T(8,128)(2,1)} %get-tuple-element.89) | copy-start | bytes 393220
  296.4 30.8 %copy-start.18 = (s32[256]{0:T(256)S(1)}, s32[256]{0:T(256)}, u32[]{:S(2)}) copy-start(s32[256]{0:T(256)} %copy-done.17) | copy-start | bytes 3076
  296.4 31.4 %copy-start.6 = (bf16[1,256,1024]{2,1,0:T(8,128)(2,1)S(1)}, bf16[1,256,1024]{2,1,0:T(8,128)(2,1)}, u32[]{:S(2)}) copy-start(bf16[1,256,1024]{2,1,0:T(8,128)(2,1)} %param.14) | copy-start | bytes 1572868
  507.6 89.2 %copy-start.8 = (f32[128,1024]{1,0:T(8,128)S(1)}, f32[128,1024]{1,0:T(8,128)}, u32[]{:S(2)}) copy-start(f32[128,1024]{1,0:T(8,128)} %get-tuple-element.151) | copy-start | bytes 1572868
  596.7 2.2 copy-start.23
  596.7 2.3 copy-start.22
  596.8 2.4 copy-start.20
  596.8 3.0 copy-start.11
  685.6 1.5 copy-start.12
  686.9 1.7 copy-start.15
  687.2 1.9 copy-start.14
  688.7 1.8 copy-start.9
  690.9 4.5 copy-start.3
  693.7 4.1 copy-start.13
  695.4 5.9 copy-start.1

commit v5 on v2

v5 whole, which is shorter than its diff:
```python
from functools import partial
from types import SimpleNamespace

import jax
import jax.numpy as jnp
from jax import lax
from jax.experimental import pallas as pl
from jax.experimental.pallas import tpu as pltpu
from jax.sharding import PartitionSpec as P

patch_areas = (1, 4, 9, 16, 25, 36, 64, 100, 169)
scale_starts = (1, 5, 14, 30, 55, 91, 155, 255)
f32 = jnp.float32
bf16 = jnp.bfloat16
MESH = pl.DeviceIdType.MESH
TILE = 256
HALF = 128
STEP = 32


def sizes():
    return lax.axis_size("dp"), lax.axis_size("blk")


def place():
    return lax.axis_index("dp"), lax.axis_index("blk")


def flat_place():
    return place()[0] * sizes()[1] + place()[1]


def token_meta(stops, length):
    areas = jnp.array(patch_areas, dtype=jnp.int32)
    levels = jnp.arange(9, dtype=jnp.int32)
    counts = jnp.sum(jnp.where(levels[None, :] < stops[:, None], areas[None, :], 0), axis=1)
    ends = jnp.cumsum(counts)
    places = jnp.arange(length, dtype=jnp.int32)
    passed = places[:, None] >= ends[None, :]
    item = jnp.sum(passed.astype(jnp.int32), axis=1)
    begin = jnp.sum(jnp.where(passed, counts[None, :], 0), axis=1)
    inner = places - begin
    bounds = jnp.array(scale_starts, dtype=jnp.int32)
    level = jnp.sum((inner[:, None] >= bounds[None, :]).astype(jnp.int32), axis=1)
    level = jnp.where(item == stops.shape[0], 0, level)
    return (item, level)


def mm(left, right):
    return jnp.dot(left, right, preferred_element_type=f32)


def mm_t(left, right):
    return lax.dot_general(left, right, (((1,), (1,)), ((), ())), preferred_element_type=f32)


def rows_mm(left, right, precision=None):
    return lax.dot_general(
        left, right, (((0,), (0,)), ((), ())), precision=precision, preferred_element_type=f32
    )


def gather(values, axes):
    return lax.all_gather(values, axes, axis=0, tiled=True)


def scatter(values, axes):
    return lax.psum_scatter(values, axes, scatter_dimension=0, tiled=True)


def partners():
    d, b = place()
    return (d, b + 1 - 2 * (b % 2)), (d, (b + 2) % 4)


def greet(others):
    barrier = pltpu.get_barrier_semaphore()
    for other in others:
        pl.semaphore_signal(barrier, inc=1, device_id=other, device_id_type=MESH)
    return lambda: pl.semaphore_wait(barrier, len(others))


def greet_all():
    dps, blks = sizes()
    me = flat_place()
    others = [(me + k) % (dps * blks) for k in range(1, dps * blks)]
    return greet([(t // blks, t % blks) for t in others])


def remote(src, dst, send, recv, target):
    return pltpu.make_async_remote_copy(
        src_ref=src, dst_ref=dst, send_sem=send, recv_sem=recv, device_id=target, device_id_type=MESH
    )


class Spread:
    def __init__(self, buf, send, recv, sibling, peer):
        def copy(src, dst, k, target):
            return remote(
                buf.at[pl.ds(src, HALF)], buf.at[pl.ds(dst, HALF)], send.at[k], recv.at[k], target
            )

        self.to_peer = [copy(HALF * c, 2 * TILE + TILE * c, c, peer) for c in range(2)]
        self.to_sibling = [copy(HALF * c, TILE + HALF * c, 2 + c, sibling) for c in range(2)]
        self.forward = [
            copy(2 * TILE + TILE * c, 2 * TILE + TILE * c + HALF, 4 + c, sibling) for c in range(2)
        ]

    def start(self, c):
        self.to_peer[c].start()
        self.to_sibling[c].start()

    def wait_block(self, i):
        @pl.when(i == 1)
        def _():
            for c in range(2):
                self.to_sibling[c].wait_recv()

        for c in range(2):

            @pl.when(i == 2 + c)
            def _():
                self.to_peer[c].wait_recv()
                self.forward[c].start()
                self.forward[c].wait_recv()

    def finish(self):
        for c in range(2):
            self.to_peer[c].wait_send()
            self.to_sibling[c].wait_send()
            self.forward[c].wait_send()


class Collect:
    def __init__(self, parts, out, mid, own, far, send, recv, sibling, peer):
        self.parts, self.out, self.mid, self.own, self.far = parts, out, mid, own, far
        self.cross = [
            remote(
                parts.at[pl.ds(2 * TILE + TILE * c + HALF, HALF)],
                mid.at[pl.ds(HALF * c, HALF)],
                send.at[c],
                recv.at[c],
                sibling,
            )
            for c in range(2)
        ]
        self.over = [
            remote(
                out.at[pl.ds(HALF * c, HALF)],
                far.at[pl.ds(HALF * c, HALF)],
                send.at[2 + c],
                recv.at[2 + c],
                peer,
            )
            for c in range(2)
        ]
        self.home = remote(parts.at[pl.ds(TILE, TILE)], own, send.at[4], recv.at[4], sibling)

    def block_done(self, j):
        for c in range(2):

            @pl.when(j == 2 + c)
            def _():
                self.cross[c].start()
                self.cross[c].wait_recv()

                @pl.loop(0, HALF // STEP)
                def _(s):
                    at = pl.multiple_of(s * STEP, STEP)
                    mine = self.parts[pl.ds(2 * TILE + TILE * c + at, STEP), :].astype(f32)
                    theirs = self.mid[pl.ds(HALF * c + at, STEP), :].astype(f32)
                    self.out[pl.ds(HALF * c + at, STEP), :] = (mine + theirs).astype(bf16)

                self.over[c].start()

        @pl.when(j == 1)
        def _():
            self.home.start()

    def wait(self):
        self.home.wait_recv()
        for c in range(2):
            self.over[c].wait_recv()

    def rows(self, at):
        span = pl.ds(at, STEP)
        total = self.parts[span, :].astype(f32) + self.own[span, :].astype(f32)
        return total + self.far[span, :].astype(f32)

    def finish(self):
        self.home.wait_send()
        for c in range(2):
            self.cross[c].wait_send()
            self.over[c].wait_send()


def spread_scratch(width):
    return [
        pltpu.VMEM((4 * TILE, width), bf16),
        pltpu.SemaphoreType.DMA((6,)),
        pltpu.SemaphoreType.DMA((6,)),
    ]


def collect_scratch(width):
    return [pltpu.VMEM((4 * TILE, width), bf16)] + [pltpu.VMEM((TILE, width), bf16)] * 4 + [
        pltpu.SemaphoreType.DMA((5,)),
        pltpu.SemaphoreType.DMA((5,)),
    ]


class Moves:
    def __init__(self, sems):
        self.sems, self.used = sems, 0

    def copy(self, src, dst):
        made = pltpu.make_async_copy(src, dst, self.sems.at[self.used])
        self.used += 1
        made.start()
        return made


def expand(onehot, ada, which, outs):
    width = outs[0].shape[1]
    for k, out in zip(which, outs):
        for n in range(0, width, TILE):
            out[:, n : n + TILE] = mm(onehot[...], ada[:, k * width + n : k * width + n + TILE])


def normed(values):
    centre = jnp.mean(values, axis=-1, keepdims=True)
    centred = values - centre
    spread = jnp.mean(centred * centred, axis=-1, keepdims=True)
    rate = lax.rsqrt(spread + 1e-06)
    return centred * rate, rate


def norm_back(grad, values_hat, rate):
    first = jnp.mean(grad, axis=-1, keepdims=True)
    second = jnp.mean(grad * values_hat, axis=-1, keepdims=True)
    return rate * (grad - first - values_hat * second)


def row_steps(start, rows, body):
    @pl.loop(0, rows // STEP)
    def _(s):
        body(pl.multiple_of(start + s * STEP, STEP))


def block_ones(size):
    shape = (TILE, TILE)
    one = lax.broadcasted_iota(jnp.int32, shape, 0) // size
    two = lax.broadcasted_iota(jnp.int32, shape, 1) // size
    return (one == two).astype(bf16)


def split_mm(dot, values, ones):
    high = values.astype(bf16)
    low = (values - high.astype(f32)).astype(bf16)
    return dot(high, ones) + dot(low, ones)


def head_lanes(values, h, size):
    lane = lax.broadcasted_iota(jnp.int32, values.shape, 1) // size
    return jnp.where(lane == h, values, jnp.zeros_like(values))


def hidden_bias(keyc, keyr, rows, cols):
    keys = keyc[pl.ds(rows, TILE), :]
    top = keyr[cols]
    low = top - top % 16
    return jnp.where((keys >= low) & (keys <= top), 0.0, -1e30)


def nothing():
    pass


class Hooks:
    def __init__(self, **table):
        self.start = self.sent = self.need = self.a = self.b = self.c = self.d = self.dw = nothing
        vars(self).update(table)


def modulate_rows(x, scale, shift, hbuf, spread):
    def modulated(at):
        span = pl.ds(at, STEP)
        hat, _ = normed(x[span, :])
        hbuf[span, :] = (hat * (1.0 + scale[span, :]) + shift[span, :]).astype(bf16)

    for c in range(2):
        row_steps(HALF * c, HALF, modulated)
        spread.start(c)


def exchange(refs):
    hbuf, ag_send, ag_recv, parts, out, mid, own, far, rs_send, rs_recv = refs
    sibling, peer = partners()
    spread = Spread(hbuf, ag_send, ag_recv, sibling, peer)
    collect = Collect(parts, out, mid, own, far, rs_send, rs_recv, sibling, peer)
    return hbuf, parts, spread, collect


def attend_segment(
    hooks,
    size,
    x,
    onehot,
    ada,
    qscale,
    keyc,
    keyr,
    weights_in,
    weights,
    saves_out,
    inv_out,
    branch_out,
    mid_out,
    held,
    mods,
    moves,
    refs,
):
    qkv, vt, rates, o_out = held
    gamma, scale, shift = mods
    wqkv, wproj = weights
    hbuf, parts, spread, collect = exchange(refs)
    mover = Moves(moves)
    expand(onehot, ada, (0, 2, 4), (gamma, scale, shift))
    modulate_rows(x, scale, shift, hbuf, spread)
    hooks.need()
    load_qkv = mover.copy(weights_in[0], wqkv)
    load_proj = mover.copy(weights_in[1], wproj)
    load_qkv.wait()
    ones = block_ones(size)

    @pl.loop(0, 4)
    def _(i):
        spread.wait_block(i)
        span = pl.ds(pl.multiple_of(i * TILE, TILE), TILE)
        h = hbuf[span, :]
        for part in range(3):
            columns = slice(part * TILE, (part + 1) * TILE)
            value = mm(h, wqkv[:, columns])
            if part < 2:
                rate = lax.rsqrt(split_mm(mm, value * value, ones) + 1e-06)
                if part == 0:
                    rate = rate * qscale[...]
                rates[span, columns] = rate
                value = value * rate
            else:
                vt[:, span] = value.T.astype(bf16)
            qkv[span, columns] = value.astype(bf16)

    hooks.a()
    saves = [mover.copy(a, b) for a, b in zip((hbuf, qkv, rates), saves_out)]
    load_proj.wait()
    heads = TILE // size

    @pl.loop(0, 4)
    def _(i):
        j = (i + 2) % 4
        span = pl.ds(pl.multiple_of(j * TILE, TILE), TILE)
        queries = [head_lanes(qkv[span, 0:TILE], h, size) for h in range(heads)]
        sums = [jnp.zeros((1, TILE), f32)] * heads
        mixed = [jnp.zeros((size, TILE), f32)] * heads
        for k in range(4):
            keys = qkv[k * TILE : (k + 1) * TILE, TILE : 2 * TILE]
            bias = hidden_bias(keyc, keyr, k * TILE, j)
            for h in range(heads):
                grown = jnp.exp(mm_t(keys, queries[h]) + bias)
                sums[h] = sums[h] + jnp.sum(grown, axis=0, keepdims=True)
                mixed[h] = mixed[h] + mm(
                    vt[h * size : (h + 1) * size, k * TILE : (k + 1) * TILE], grown.astype(bf16)
                )
        inverse = [1.0 / one for one in sums]
        for h in range(heads):
            inv_out[j, h : h + 1, :] = inverse[h]
        whole = jnp.concatenate([mixed[h] * inverse[h] for h in range(heads)], axis=0)
        low = whole.T.astype(bf16)
        o_out[span, :] = low
        for n in range(0, parts.shape[1], TILE):
            parts[span, n : n + TILE] = mm(low, wproj[:, n : n + TILE]).astype(bf16)
        collect.block_done(j)

    hooks.b()
    collect.wait()
    hooks.c()

    def added(at):
        span = pl.ds(at, STEP)
        branch = collect.rows(at)
        branch_out[span, :] = branch
        mid_out[span, :] = x[span, :] + gamma[span, :] * branch

    row_steps(0, TILE, added)
    spread.finish()
    collect.finish()
    for one in saves:
        one.wait()


def mlp_segment(
    hooks, x, onehot, ada, weights_in, weights, saves_out, result_out, x_out, held, mods, moves, refs
):
    hidden, slope = held
    gamma, scale, shift = mods
    wup, wdown = weights
    hbuf, parts, spread, collect = exchange(refs)
    mover = Moves(moves)
    expand(onehot, ada, (1, 3, 5), (gamma, scale, shift))
    modulate_rows(x, scale, shift, hbuf, spread)
    hooks.need()
    loads = [mover.copy(a, b) for a, b in zip(weights_in, weights)]
    for one in loads:
        one.wait()

    @pl.loop(0, 4)
    def _(i):
        spread.wait_block(i)
        for at, hook in ((2, hooks.a), (3, hooks.b)):

            @pl.when(i == at)
            def _():
                hook()

        span = pl.ds(pl.multiple_of(i * TILE, TILE), TILE)
        h = hbuf[span, :]
        for n in range(0, wup.shape[1], TILE):
            columns = slice(n, n + TILE)
            up = mm(h, wup[:, columns])
            square = up * up
            bent = jnp.tanh(0.7978845608 * (up * (1.0 + 0.044715 * square)))
            half = 0.5 * (1.0 + bent)
            hidden[span, columns] = (up * half).astype(bf16)
            inner = 0.7978845608 + (3.0 * 0.044715 * 0.7978845608) * square
            slope[span, columns] = (half + 0.5 * up * (1.0 - bent * bent) * inner).astype(bf16)
        g = hidden[span, :]
        for n in range(0, parts.shape[1], TILE):
            parts[span, n : n + TILE] = mm(g, wdown[:, n : n + TILE]).astype(bf16)
        collect.block_done(i)

    hooks.c()
    saves = [mover.copy(a, b) for a, b in zip((hbuf, hidden, slope), saves_out)]
    collect.wait()

    def added(at):
        span = pl.ds(at, STEP)
        result = collect.rows(at)
        result_out[span, :] = result
        x_out[span, :] = x[span, :] + gamma[span, :] * result

    row_steps(0, TILE, added)
    spread.finish()
    collect.finish()
    for one in saves:
        one.wait()


def item_sums(onehot_t, terms, out):
    for k, term in enumerate(terms):
        width = term.shape[1]
        out[:, k * width : (k + 1) * width] = mm(onehot_t[...], term[...])


def scaled_rows(x, gamma, hbuf, spread):
    def scaled(at):
        span = pl.ds(at, STEP)
        hbuf[span, :] = (gamma[span, :] * x[span, :]).astype(bf16)

    for c in range(2):
        row_steps(HALF * c, HALF, scaled)
        spread.start(c)


def back_rows(collect, x, grad, branch, scale, terms, out):
    dgamma, dscale, dshift = terms

    def added(at):
        span = pl.ds(at, STEP)
        dh = collect.rows(at)
        hat, rate = normed(x[span, :])
        above = grad[span, :]
        dgamma[span, :] = (above * branch[span, :]).astype(bf16)
        dscale[span, :] = (dh * hat).astype(bf16)
        dshift[span, :] = dh.astype(bf16)
        out[span, :] = above + norm_back(dh * (1.0 + scale[span, :]), hat, rate)

    row_steps(0, TILE, added)


def mlp_back_segment(
    hooks, dx, onehot, onehot_t, ada, ins, outs, dmid, items, held, mods, terms, moves, refs
):
    wup_in, wdown_in, h_in, g_in, slope_in, result_in, mid_in = ins
    wup, wdown, hall, gall, slope, dwup, dwdown, result, mid_state = held
    gamma, scale = mods
    hbuf, parts, spread, collect = exchange(refs)
    mover = Moves(moves)
    load_down = mover.copy(wdown_in, wdown)
    load_slope = mover.copy(slope_in, slope)
    load_up = mover.copy(wup_in, wup)
    later = [mover.copy(g_in, gall), mover.copy(h_in, hall)]
    later += [mover.copy(result_in, result), mover.copy(mid_in, mid_state)]
    expand(onehot, ada, (1, 3), (gamma, scale))
    hooks.start()
    scaled_rows(dx, gamma, hbuf, spread)
    hooks.sent()
    for one in (load_down, load_slope, load_up):
        one.wait()

    @pl.loop(0, 4)
    def _(i):
        spread.wait_block(i)
        for at, hook in ((2, hooks.a), (3, hooks.b)):

            @pl.when(i == at)
            def _():
                hook()

        span = pl.ds(pl.multiple_of(i * TILE, TILE), TILE)
        dm = hbuf[span, :]
        for n in range(0, slope.shape[1], TILE):
            columns = slice(n, n + TILE)
            dg = mm_t(dm, wdown[columns, :])
            slope[span, columns] = (dg * slope[span, columns].astype(f32)).astype(bf16)
        du = slope[span, :]
        for n in range(0, parts.shape[1], TILE):
            parts[span, n : n + TILE] = mm_t(du, wup[n : n + TILE, :]).astype(bf16)
        collect.block_done(i)

    hooks.c()
    for one in later:
        one.wait()

    @pl.loop(0, gall.shape[1] // TILE)
    def _(k):
        columns = pl.ds(pl.multiple_of(k * TILE, TILE), TILE)
        for n in range(0, hbuf.shape[1], 2 * TILE):
            dwdown[columns, n : n + 2 * TILE] = rows_mm(
                gall[:, columns], hbuf[:, n : n + 2 * TILE]
            ).astype(bf16)

    save_down = mover.copy(dwdown, outs[1])

    @pl.loop(0, hall.shape[1] // TILE)
    def _(k):
        columns = pl.ds(pl.multiple_of(k * TILE, TILE), TILE)
        for n in range(0, slope.shape[1], 2 * TILE):
            dwup[columns, n : n + 2 * TILE] = rows_mm(
                hall[:, columns], slope[:, n : n + 2 * TILE]
            ).astype(bf16)

    save_up = mover.copy(dwup, outs[0])
    save_down.wait()
    save_up.wait()
    hooks.dw()
    collect.wait()
    back_rows(collect, mid_state, dx, result, scale, terms, dmid)
    item_sums(onehot_t, terms, items)
    spread.finish()
    collect.finish()


def attend_back_segment(
    hooks,
    size,
    dmid,
    onehot,
    onehot_t,
    ada,
    qscale,
    keyc,
    keyr,
    inverse,
    ins,
    outs,
    dx,
    items,
    head_out,
    held,
    mods,
    terms,
    moves,
    refs,
):
    wqkv_in, wproj_in, h_in, qkv_in, rate_in, o_in, branch_in, x_in = ins
    wqkv, wproj, hall, qkv, rates, oall, kt, dkeys, dvalues, dqkv, dwqkv, dwproj, branch, x = held
    gamma, scale = mods
    hbuf, parts, spread, collect = exchange(refs)
    mover = Moves(moves)
    loads = [mover.copy(wproj_in, wproj), mover.copy(qkv_in, qkv)]
    loads += [mover.copy(o_in, oall), mover.copy(rate_in, rates)]
    load_w = mover.copy(wqkv_in, wqkv)
    later = [mover.copy(h_in, hall), mover.copy(branch_in, branch)]
    if x_in is not None:
        later.append(mover.copy(x_in, x))
    expand(onehot, ada, (0, 2), (gamma, scale))
    hooks.start()
    scaled_rows(dmid, gamma, hbuf, spread)
    hooks.sent()
    for one in loads:
        one.wait()
    heads = TILE // size
    ones = block_ones(size)
    inv_square = 1.0 / (qscale[...] * qscale[...])
    select = (
        lax.broadcasted_iota(jnp.int32, (8, TILE), 1) // size
        == lax.broadcasted_iota(jnp.int32, (8, TILE), 0)
    ).astype(bf16)
    dkeys[...] = jnp.zeros_like(dkeys)
    dvalues[...] = jnp.zeros_like(dvalues)
    head_out[...] = jnp.zeros_like(head_out)
    for k in range(4):
        rows = slice(k * TILE, (k + 1) * TILE)
        kt[:, rows] = qkv[rows, TILE : 2 * TILE].astype(f32).T.astype(bf16)

    @pl.loop(0, 4)
    def _(i):
        spread.wait_block(i)
        for at, hook in ((2, hooks.a), (3, hooks.b)):

            @pl.when(i == at)
            def _():
                hook()

        span = pl.ds(pl.multiple_of(i * TILE, TILE), TILE)
        dout = mm_t(hbuf[span, :], wproj[...]).astype(bf16)
        product = dout.astype(f32) * oall[span, :].astype(f32)
        row_term = split_mm(lambda a, b: mm_t(b, a), product, select)
        q_low = qkv[span, 0:TILE]
        queries = [head_lanes(q_low, h, size) for h in range(heads)]
        douts = [head_lanes(dout, h, size) for h in range(heads)]
        dquery = [jnp.zeros((size, TILE), f32)] * heads
        for k in range(4):
            rows = slice(k * TILE, (k + 1) * TILE)
            keys = qkv[rows, TILE : 2 * TILE]
            values = qkv[rows, 2 * TILE : 3 * TILE]
            bias = hidden_bias(keyc, keyr, k * TILE, i)
            dkey = jnp.zeros((TILE, TILE), f32)
            dvalue = jnp.zeros((TILE, TILE), f32)
            for h in range(heads):
                share = jnp.exp(mm_t(keys, queries[h]) + bias) * inverse[i, h : h + 1, :]
                dshare = mm_t(values, douts[h])
                dscore = (share * (dshare - row_term[h : h + 1, :])).astype(bf16)
                dvalue = dvalue + mm(share.astype(bf16), douts[h])
                dkey = dkey + mm(dscore, queries[h])
                dquery[h] = dquery[h] + mm(kt[h * size : (h + 1) * size, rows], dscore)
            dkeys[rows, :] += dkey
            dvalues[rows, :] += dvalue
        dq = jnp.concatenate(dquery, axis=0).T
        qhat = q_low.astype(f32)
        along = split_mm(mm, dq * qhat, ones)
        head_out[...] += jnp.sum(along, axis=0, keepdims=True)
        dqkv[span, 0:TILE] = (rates[span, 0:TILE] * (dq - qhat * (along * inv_square))).astype(bf16)

    load_w.wait()
    hooks.c()

    @pl.loop(0, 4)
    def _(i):
        j = (i + 2) % 4
        span = pl.ds(pl.multiple_of(j * TILE, TILE), TILE)
        dk = dkeys[span, :]
        khat = qkv[span, TILE : 2 * TILE].astype(f32)
        along = split_mm(mm, dk * khat, ones)
        dqkv[span, TILE : 2 * TILE] = (
            rates[span, TILE : 2 * TILE] * (dk - khat * along)
        ).astype(bf16)
        dqkv[span, 2 * TILE : 3 * TILE] = dvalues[span, :].astype(bf16)
        low = dqkv[span, :]
        for n in range(0, parts.shape[1], TILE):
            parts[span, n : n + TILE] = mm_t(low, wqkv[n : n + TILE, :]).astype(bf16)
        collect.block_done(j)

    hooks.d()
    for n in range(0, hbuf.shape[1], 2 * TILE):
        dwproj[:, n : n + 2 * TILE] = rows_mm(oall[...], hbuf[:, n : n + 2 * TILE]).astype(bf16)
    save_proj = mover.copy(dwproj, outs[1])
    for one in later:
        one.wait()

    @pl.loop(0, hall.shape[1] // TILE)
    def _(k):
        columns = pl.ds(pl.multiple_of(k * TILE, TILE), TILE)
        dwqkv[columns, :] = rows_mm(hall[:, columns], dqkv[...]).astype(bf16)

    save_w = mover.copy(dwqkv, outs[0])
    save_proj.wait()
    save_w.wait()
    hooks.dw()
    collect.wait()
    back_rows(collect, x, dmid, branch, scale, terms, dx)
    item_sums(onehot_t, terms, items)
    spread.finish()
    collect.finish()


def groups(dps):
    d, b = place()
    side, pairs = d % 2, dps // 2
    pair = d // 2
    ahead = [((pair + k) % pairs) * 2 + side for k in range(pairs)]
    behind = [((pair - k + pairs) % pairs) * 2 + side for k in range(pairs)]
    return d, b, d + 1 - 2 * side, ahead, behind


class DpGather:
    def __init__(self):
        self.dps = sizes()[0]

    def bind(self, ins, outs, scratch):
        send, recv, local = scratch
        d, b, other, ahead, behind = groups(self.dps)
        pairs = self.dps // 2
        self.partners = [(other, b)] + [(t, b) for t in ahead[1:]]
        self.first, self.direct, self.forward, self.local = [], [], [], []
        for a, (src, dst) in enumerate(zip(ins, outs)):
            self.local.append(pltpu.make_async_copy(src, dst.at[d], local.at[a]))
            self.first.append(remote(src, dst.at[d], send.at[a, 0], recv.at[a, 0], (other, b)))
            self.direct.append([None])
            self.forward.append([None])
            for k in range(1, pairs):
                self.direct[a].append(
                    remote(src, dst.at[d], send.at[a, k], recv.at[a, k], (ahead[k], b))
                )
                at = pairs + k
                self.forward[a].append(
                    remote(
                        dst.at[behind[k]], dst.at[behind[k]], send.at[a, at], recv.at[a, at], (other, b)
                    )
                )
        self.order = [(k, a) for k in range(1, pairs) for a in range(len(ins))]

    def start_far(self):
        for k, a in self.order:
            self.direct[a][k].start()
        for one in self.local:
            one.start()

    def start_near(self):
        for one in self.first:
            one.start()

    def step(self, hook, hooks=3):
        low, high = (len(self.order) * hook) // hooks, (len(self.order) * (hook + 1)) // hooks
        for k, a in self.order[low:high]:
            self.direct[a][k].wait_recv()
            self.forward[a][k].start()

    def finish(self):
        for one in self.local:
            one.wait()
        for one in self.first:
            one.wait()
        for k, a in self.order:
            self.direct[a][k].wait_send()
            self.forward[a][k].wait()


class DpScatter:
    def __init__(self):
        self.dps = sizes()[0]

    def bind(self, ins, outs, scratch):
        d, b, other, ahead, behind = groups(self.dps)
        pairs = self.dps // 2
        self.partners = [(other, b)] + [(t, b) for t in ahead[1:]]
        self.results = outs
        self.bufs, self.local, self.cross, self.direct = [], [], [], []
        for a, src in enumerate(ins):
            mine, near, far, send, recv, local = scratch[6 * a : 6 * a + 6]
            self.bufs.append((mine, near, far))
            self.local.append([])
            self.cross.append([])
            self.direct.append([None])
            for k in range(pairs):
                target = ahead[k]
                theirs = target + 1 - 2 * (target % 2)
                self.local[a].append(
                    pltpu.make_async_copy(src.at[target], mine.at[k], local.at[k])
                )
                self.cross[a].append(
                    remote(src.at[theirs], near.at[k], send.at[k], recv.at[k], (other, b))
                )
                if k:
                    at = pairs + k
                    self.direct[a].append(
                        remote(mine.at[k], far.at[k], send.at[at], recv.at[at], (target, b))
                    )
        self.order = [(k, a) for k in range(1, pairs) for a in range(len(ins))]
        self.last = [(0, a) for a in range(len(ins))]

    def start(self):
        for k, a in self.order + self.last:
            self.cross[a][k].start()
            self.local[a][k].start()

    def add(self, a, k):
        self.local[a][k].wait()
        self.cross[a][k].wait_recv()
        mine, near, _ = self.bufs[a]
        rows = mine.shape[1]
        step = min(rows, STEP)

        @pl.loop(0, rows // step)
        def _(s):
            span = pl.ds(pl.multiple_of(s * step, step), step)
            total = mine[k, span, :].astype(f32) + near[k, span, :].astype(f32)
            mine[k, span, :] = total.astype(bf16)

    def step(self, hook, hooks=3):
        low, high = (len(self.order) * hook) // hooks, (len(self.order) * (hook + 1)) // hooks
        for k, a in self.order[low:high]:
            self.add(a, k)
            self.direct[a][k].start()

    def own(self):
        for k, a in self.last:
            self.add(a, k)
        for k, a in self.order + self.last:
            self.cross[a][k].wait_send()

    def finish(self):
        for k, a in self.order:
            self.direct[a][k].wait()
        for a, result in enumerate(self.results):
            mine, _, far = self.bufs[a]
            step = result.shape[1] if len(result.shape) == 3 else min(mine.shape[1], STEP)

            @pl.loop(0, mine.shape[1] // step)
            def _(s):
                span = pl.ds(pl.multiple_of(s * step, step), step)
                total = mine[0, span, :].astype(f32)
                for k in range(1, self.dps // 2):
                    total = total + far[k, span, :].astype(f32)
                if len(result.shape) == 3:
                    result[s] = total.astype(result.dtype)
                else:
                    result[span, :] = total.astype(result.dtype)

    def release(self, credit):
        for other in self.partners:
            pl.semaphore_signal(credit, inc=1, device_id=other, device_id_type=MESH)

    def acquire(self, credit):
        pl.semaphore_wait(credit, len(self.partners))


class Items:
    def __init__(self, src, out, scratch):
        self.terms, self.held, send, recv, dp_send, dp_recv = scratch
        dps = sizes()[0]
        d, b = place()
        self.here, self.out = (d, b), out
        wide = self.held.shape[2]

        def quarter(i):
            return src.at[:, pl.ds(pl.multiple_of(i * wide, 128), wide)]

        self.first = [pltpu.make_async_copy(quarter(b), self.terms.at[0], send.at[0])]
        for k in range(1, 4):
            to = (b + k) % 4
            self.first.append(
                remote(quarter(to), self.terms.at[k], send.at[k], recv.at[k], (d, to))
            )
        self.over = [
            remote(self.held.at[0], out.at[b, d], dp_send.at[k], dp_recv.at[k], ((d + k) % dps, b))
            for k in range(1, dps)
        ]
        self.keep = pltpu.make_async_copy(self.held.at[0], out.at[b, d], send.at[7])
        self.share = Share(out, send.at[pl.ds(4, 3)], recv.at[pl.ds(4, 3)])

    def start(self):
        for one in self.first:
            one.start()

    def sum(self):
        d, b = self.here
        for one in self.first:
            one.wait()
        total = (self.terms[0] + self.terms[1]) + (self.terms[2] + self.terms[3])
        low = total.astype(bf16)
        self.held[0] = low
        for one in self.over + [self.keep]:
            one.start()

    def spread(self):
        for one in self.over + [self.keep]:
            one.wait()
        self.share.start()

    def forward(self):
        self.share.forward()

    def finish(self):
        self.share.finish()


class Permute:
    def __init__(self, src, dst, send, recv, back):
        dps, blks = sizes()
        d, b = place()
        owner, user = d * blks + b, b * dps + d
        self.moves = owner != user
        to = (user // blks, user % blks) if back else (owner % dps, owner // dps)
        self.away = remote(src, dst, send, recv, to)
        self.stay = pltpu.make_async_copy(src, dst, send)

    def start(self):
        @pl.when(self.moves)
        def _():
            self.away.start()

        @pl.when(jnp.logical_not(self.moves))
        def _():
            self.stay.start()

    def finish(self):
        @pl.when(self.moves)
        def _():
            self.away.wait()

        @pl.when(jnp.logical_not(self.moves))
        def _():
            self.stay.wait()


def modulations_start(rows_in, ada_in, rows_out, columns, sems):
    dp_send, dp_recv, ada_send, ada_recv, local = sems
    dps, blks = sizes()
    count = dps * blks
    d, b = place()
    me = d * blks + b
    rows = ada_in.shape[1]
    span = pl.ds(pl.multiple_of(me * rows, rows), rows)
    sends = [
        pltpu.make_async_copy(rows_in, rows_out.at[d], local.at[0]),
        pltpu.make_async_copy(ada_in.at[me], columns.at[span], local.at[1]),
    ]
    for k in range(1, dps):
        to = ((d + k) % dps, b)
        sends.append(remote(rows_in, rows_out.at[d], dp_send.at[k], dp_recv.at[k], to))
    for k in range(1, count):
        t = (me + k) % count
        to = (t // blks, t % blks)
        sends.append(remote(ada_in.at[t], columns.at[span], ada_send.at[k], ada_recv.at[k], to))
    for one in sends:
        one.start()
    return sends


def modulations_answer(rows_out, columns, answers, quarters, sems):
    send, recv = sems
    dps = sizes()[0]
    d, b = place()
    slots, wide = answers.shape[1:]
    value = rows_out[...].astype(f32)
    value = (value / (1.0 + jnp.exp(-value))).astype(bf16)
    whole = mm(value.reshape(dps * slots, rows_out.shape[2]), columns[...])
    answers[...] = whole.reshape(dps, slots, wide)
    replies = []
    for k in range(1, dps):
        to = (d + k) % dps
        replies.append(
            remote(answers.at[to], quarters.at[b, d], send.at[k], recv.at[k], (to, b))
        )
    for one in replies:
        one.start()
    quarters[b, d] = answers[d]
    return replies


class Share:
    def __init__(self, buf, send, recv):
        d, b = place()
        sibling, peer = partners()
        far = peer[1]
        self.moves = [
            remote(buf.at[b], buf.at[b], send.at[0], recv.at[0], peer),
            remote(buf.at[b], buf.at[b], send.at[1], recv.at[1], sibling),
            remote(buf.at[far], buf.at[far], send.at[2], recv.at[2], sibling),
        ]

    def start(self):
        self.moves[0].start()
        self.moves[1].start()

    def forward(self):
        self.moves[0].wait_recv()
        self.moves[2].start()

    def finish(self):
        self.moves[1].wait_recv()
        self.moves[2].wait_recv()
        for one in self.moves:
            one.wait_send()


class PieceSwap:
    def __init__(self, pairs, send, recv):
        d, b = place()
        self.sent = []
        for a, (src, dst) in enumerate(pairs):
            self.sent.append(pltpu.make_async_copy(src.at[b], dst.at[b], send.at[a, 0]))
            for k in range(1, 4):
                to = (b + k) % 4
                self.sent.append(
                    remote(src.at[to], dst.at[b], send.at[a, k], recv.at[a, k], (d, to))
                )

    def start(self):
        for one in self.sent:
            one.start()

    def finish(self):
        for one in self.sent:
            one.wait()


def flat(value):
    return [leaf for one in value for leaf in flat(one)] if isinstance(value, list) else [value]


def refill(value, leaves):
    return [refill(one, leaves) for one in value] if isinstance(value, list) else next(leaves)


class Names:
    def __init__(self):
        self.ins, self.outs, self.scratch = SimpleNamespace(), SimpleNamespace(), SimpleNamespace()

    def call(self, kernel, ident, vmem):
        ins, outs, scratch = (flat(list(vars(one).values())) for one in (self.ins, self.outs, self.scratch))

        def fill(bags, refs):
            leaves, found = iter(refs), SimpleNamespace()
            for bag in bags:
                for name, value in vars(bag).items():
                    vars(found)[name] = refill(value, leaves)
            return found

        results = pl.pallas_call(
            lambda *refs: kernel(fill((self.ins, self.outs, self.scratch), refs)),
            out_shape=[one for one, _ in outs],
            in_specs=[where for _, where in ins],
            out_specs=[where for _, where in outs],
            scratch_shapes=scratch,
            compiler_params=pltpu.CompilerParams(
                collective_id=ident, has_side_effects=True, vmem_limit_bytes=vmem * 2**20
            ),
            cost_estimate=pl.CostEstimate(flops=2**36, bytes_accessed=2**26, transcendentals=0),
        )(*[one for one, _ in ins])
        return fill((self.outs,), results)


def add_exchanges(names, width):
    names.scratch.spreads = [spread_scratch(width) for _ in range(2)]
    names.scratch.parts, names.scratch.out = collect_scratch(width)[:2]
    names.scratch.collects = [collect_scratch(width)[2:] for _ in range(2)]


def exchange_set(r, turn):
    return r.spreads[turn] + [r.parts, r.out] + r.collects[turn]


def forward_kernel(lead, layers, size, r):
    dps, blks = sizes()
    d, b = place()
    sibling, peer = partners()
    ada = r.ada
    qkv_shard = r.qkv_shard if lead else [r.qkv_first] + r.qkv_shard
    up_shard = r.up_shard if lead else [r.up_first] + r.up_shard
    gathers = []
    for layer in range(layers):
        first = [qkv_shard[layer], r.proj_shard.at[layer]]
        second = [up_shard[layer], r.w_down.at[layer]]
        for part, (srcs, dsts) in enumerate(((first, (r.wq, r.wp)), (second, (r.wu, r.wd)))):
            job = DpGather()
            job.bind(srcs, [one[layer] for one in dsts], r.gather_sems[2 * layer + part])
            gathers.append(job)
    if lead:
        arrived = greet_all()
    else:
        arrived = greet([sibling, peer, (d, 3 - b)] + gathers[0].partners)
    r.state[...] = r.tokens[...].astype(f32)
    arrived()
    swaps = [
        PieceSwap(
            [(r.qkv_cols[n], r.qkv_shard[n]), (r.up_cols[n], r.up_shard[n])],
            r.swap_send[n],
            r.swap_recv[n],
        )
        for n in range(len(r.qkv_cols))
    ]
    if lead:
        permutes = [
            Permute(
                r.w_proj.at[n], r.proj_shard.at[n], r.permute_send.at[n], r.permute_recv.at[n], False
            )
            for n in range(layers)
        ]
        permutes[0].start()
        swaps[0].start()
        moves = modulations_start(
            r.rows_in,
            r.ada_in,
            r.rows,
            r.columns,
            (r.dp_send, r.dp_recv, r.ada_send, r.ada_recv, r.ada_local),
        )
        for one in moves:
            one.wait()
        replies = modulations_answer(
            r.rows, r.columns, r.answers, r.quarters, (r.answer_send, r.answer_recv)
        )
        swaps[0].finish()
        permutes[0].finish()
        gathers[0].start_far()
        gathers[0].start_near()
        for one in permutes[1:]:
            one.start()
        share = Share(r.quarters, r.share_send, r.share_recv)
        for one in replies:
            one.wait()
        share.start()
        share.forward()
        gathers[0].step(0)
        share.finish()
        slots = r.answers.shape[1]
        wide = r.answers.shape[2]
        each = ada.shape[2]
        for i in range(dps * blks):
            value = r.quarters[i % blks, i // blks]
            layer, at = (i * wide) // each, (i * wide) % each
            high = value.astype(bf16)
            ada[layer, 0:slots, at : at + wide] = high
            ada[layer, slots : 2 * slots, at : at + wide] = (value - high.astype(f32)).astype(bf16)
    else:
        gathers[0].start_far()
        gathers[0].start_near()
        gathers[0].step(0)
    gathers[1].start_far()
    for one in swaps[-(layers - 1) :]:
        one.start()

    def need_first(layer):
        job, following = gathers[2 * layer], gathers[2 * layer + 1]
        if layer == 0:
            job.step(1)
            job.step(2)
        following.start_near()
        job.finish()

    def early(layer):
        if layer == 0:
            for one in swaps[-(layers - 1) :]:
                one.finish()
            if lead:
                for one in permutes[1:]:
                    one.finish()
            for one in gathers[2:]:
                one.start_far()
        else:
            gathers[2 * layer + 1].step(0)

    def middle(layer):
        gathers[2 * layer + 1].step(0 if layer == 0 else 1)

    def late(layer):
        gathers[2 * layer + 1].step(1 if layer == 0 else 2)

    def need_second(layer):
        if layer == 0:
            gathers[1].step(2)
        if layer + 1 < layers:
            gathers[2 * layer + 2].start_near()
        gathers[2 * layer + 1].finish()

    def weights(ref, rows):
        return ref.reshape(rows, ref.shape[-1])

    pending = []
    saver = Moves(r.save_sems)
    width = r.state.shape[1]
    for layer in range(layers):
        last = layer + 1 == layers
        attend_segment(
            Hooks(
                need=partial(need_first, layer),
                a=partial(early, layer),
                b=partial(middle, layer),
                c=partial(late, layer),
            ),
            size,
            r.state,
            r.onehot,
            ada.at[layer],
            r.qscale.at[layer],
            r.keyc,
            r.keyr,
            (weights(r.wq[layer], width), weights(r.wp[layer], width // 4)),
            (r.wqkv, r.wproj),
            (r.h.at[layer], r.qkv.at[layer], r.rates.at[layer]),
            r.inverse.at[layer],
            r.branch_buf,
            r.middle,
            (r.qkv_buf, r.vt, r.rate_buf, r.o_buf),
            (r.gamma, r.scale, r.shift),
            r.moves.at[2 * layer],
            exchange_set(r, 0),
        )
        for one in pending:
            one.wait()
        pending = [
            saver.copy(r.o_buf, r.o.at[layer]),
            saver.copy(r.branch_buf, r.branch.at[layer]),
            saver.copy(r.middle, r.mids.at[layer]),
        ]
        hooks = Hooks(need=partial(need_second, layer))
        if not last:
            hooks.a, hooks.b, hooks.c = [partial(gathers[2 * layer + 2].step, i) for i in range(3)]
        mlp_segment(
            hooks,
            r.middle,
            r.onehot,
            ada.at[layer],
            (weights(r.wu[layer], width), weights(r.wd[layer], width)),
            (r.wup, r.wdown),
            (r.h2.at[layer], r.g.at[layer], r.slope.at[layer]),
            r.result_buf,
            r.state,
            (r.hidden, r.slope_buf),
            (r.gamma, r.scale, r.shift),
            r.moves.at[2 * layer + 1],
            exchange_set(r, 1),
        )
        for one in pending:
            one.wait()
        pending = [saver.copy(r.result_buf, r.result.at[layer])]
        if not last:
            pending.append(saver.copy(r.state, r.states.at[layer]))
    r.output[...] = r.state[...].astype(bf16)
    for one in pending:
        one.wait()


def forward(size, tokens, onehot, keyc, keyr, qscale, w_down, proj, qkv_cols, up_cols, rows_in, ada_in, ada, qkv_shard, up_shard):
    lead = ada_in is not None
    dps, blks = sizes()
    count = dps * blks
    rows, width = tokens.shape
    layers = proj.shape[0]
    length = rows * blks
    wide, ff = qkv_cols[0].shape[2], up_cols[0].shape[2]
    sems = pltpu.SemaphoreType.DMA
    n = Names()
    vars(n.ins).update(
        tokens=(tokens, VMEM), onehot=(onehot, VMEM), keyc=(keyc, VMEM), keyr=(keyr, VMEM), qscale=(qscale, VMEM)
    )
    n.ins.w_down = (w_down, ANY)
    low = partial(shaped, dtype=bf16)
    if lead:
        vars(n.ins).update(rows_in=(rows_in, ANY), ada_in=(ada_in, ANY), w_proj=(proj, ANY))
        slots = rows_in.shape[0]
        columns = ada_in.shape[2]
        vars(n.outs).update(
            ada=(low(layers, 2 * slots, count * columns // layers), VMEM),
            rows=(low(dps, slots, width), VMEM),
            proj_shard=(low(*proj.shape), ANY),
        )
        vars(n.scratch).update(
            columns=pltpu.VMEM((width, columns), bf16),
            answers=pltpu.VMEM((dps, slots, columns), f32),
            quarters=pltpu.VMEM((blks, dps, slots, columns), f32),
            dp_send=sems((dps,)),
            dp_recv=sems((dps,)),
            answer_send=sems((dps,)),
            answer_recv=sems((dps,)),
            ada_send=sems((count,)),
            ada_recv=sems((count,)),
            ada_local=sems((2,)),
            share_send=sems((3,)),
            share_recv=sems((3,)),
            permute_send=sems((layers,)),
            permute_recv=sems((layers,)),
        )
    else:
        vars(n.ins).update(
            ada=(ada, VMEM), proj_shard=(proj, ANY), qkv_first=(qkv_shard, ANY), up_first=(up_shard, ANY)
        )
    moved_qkv, moved_up = (one if lead else one[1:] for one in (qkv_cols, up_cols))
    n.ins.qkv_cols = [(one, ANY) for one in moved_qkv]
    n.ins.up_cols = [(one, ANY) for one in moved_up]
    n.outs.qkv_shard = [(low(*one.shape), ANY) for one in moved_qkv]
    n.outs.up_shard = [(low(*one.shape), ANY) for one in moved_up]
    n.scratch.swap_send = [sems((2, 4)) for _ in moved_qkv]
    n.scratch.swap_recv = [sems((2, 4)) for _ in moved_qkv]
    n.outs.wq = [(low(dps, *one.shape), ANY) for one in qkv_cols]
    n.outs.wp = [(low(dps, *proj.shape[1:]), ANY)] * layers
    n.outs.wu = [(low(dps, *one.shape), ANY) for one in up_cols]
    n.outs.wd = [(low(dps, *w_down.shape[1:]), ANY)] * layers
    n.scratch.gather_sems = [[sems((2, dps)), sems((2, dps)), sems((2,))] for _ in range(2 * layers)]
    vars(n.outs).update(
        output=(low(rows, width), VMEM),
        inverse=(shaped(layers, 4, 8, TILE), VMEM),
        h=(low(layers, length, width), ANY),
        qkv=(low(layers, length, wide), ANY),
        rates=(shaped(layers, length, 2 * TILE), ANY),
        o=(low(layers, length, TILE), ANY),
        branch=(shaped(layers, rows, width), ANY),
        mids=(shaped(layers, rows, width), ANY),
        h2=(low(layers, length, width), ANY),
        g=(low(layers, length, ff), ANY),
        slope=(low(layers, length, ff), ANY),
        result=(shaped(layers, rows, width), ANY),
        states=(shaped(layers, rows, width), ANY),
    )
    big = pltpu.VMEM((rows, width), f32)
    vars(n.scratch).update(
        state=big, middle=big, branch_buf=big, result_buf=big, gamma=big, scale=big, shift=big
    )
    vars(n.scratch).update(
        wqkv=pltpu.VMEM((width, wide), bf16),
        wproj=pltpu.VMEM((TILE, width), bf16),
        wup=pltpu.VMEM((width, ff), bf16),
        wdown=pltpu.VMEM((ff, width), bf16),
        qkv_buf=pltpu.VMEM((length, wide), bf16),
        vt=pltpu.VMEM((TILE, length), bf16),
        rate_buf=pltpu.VMEM((length, 2 * TILE), f32),
        o_buf=pltpu.VMEM((length, TILE), bf16),
        hidden=pltpu.VMEM((length, ff), bf16),
        slope_buf=pltpu.VMEM((length, ff), bf16),
        moves=sems((2 * layers, 5)),
        save_sems=sems((5 * layers,)),
    )
    add_exchanges(n, width)
    return n.call(partial(forward_kernel, lead, layers, size), 8, 56)


def backward_kernel(layers, size, r):
    dps, blks = sizes()
    d, b = place()
    arrived = greet_all()
    width = r.grad.shape[1]
    rows = r.w_ada.shape[1]
    people = r.cond.shape[1]
    r.grad[...] = r.cotangent[...].astype(f32)
    arrived()

    wides, narrows, swaps, permutes, items = {}, {}, {}, {}, {}
    r.dadas = [r.near_dada] + r.far_dadas
    for n in range(layers):
        wides[n], narrows[n] = DpScatter(), DpScatter()
        shared = r.wide
        wides[n].bind([r.dwu[n], r.dwd[n]], [r.up_sum[n], r.down_grad.at[n]], shared)
        shared = r.narrow
        narrows[n].bind([r.dwq[n], r.dwp[n]], [r.qkv_sum[n], r.proj_sum[n]], shared)
        for k, (src, dst) in enumerate(((r.up_sum, r.up_grad), (r.qkv_sum, r.qkv_grad))):
            swaps[k, n] = PieceSwap(
                [(src[n], dst.at[n])], r.swap_send.at[2 * n + k], r.swap_recv.at[2 * n + k]
            )
        permutes[n] = Permute(
            r.proj_sum[n], r.proj_grad.at[n], r.permute_send.at[n], r.permute_recv.at[n], True
        )
        for part in range(2):
            at = 2 * n + part
            items[n, part] = Items(r.items[at], r.dadas[at], r.items_scratch[at])

    def wide_done(n):
        wides[n].finish()
        swaps[0, n].start()
        if n:
            wides[n].release(r.credit.at[0])

    def narrow_done(n):
        narrows[n].finish()
        swaps[1, n].start()
        permutes[n].start()
        if n:
            narrows[n].release(r.credit.at[1])

    def weights(ref, count):
        return ref.reshape(count, ref.shape[-1])

    wide = 3 * TILE
    length = 4 * TILE
    for layer in reversed(range(layers)):
        top = layer + 1 == layers
        above = layer + 1

        def begin_mlp():
            if not top:
                items[above, 0].start()

        def late_mlp():
            if not top:
                narrows[above].step(2)
                items[above, 1].spread()
                items[above, 0].sum()

        def done_mlp():
            if not top:
                wide_done(above)
                wides[layer].acquire(r.credit.at[0])
            wides[layer].start()

        hooks = Hooks(start=begin_mlp, c=late_mlp, dw=done_mlp)
        if not top:
            hooks.sent = wides[above].own
            hooks.a, hooks.b = [partial(narrows[above].step, i) for i in range(2)]
        ff = r.slope.shape[2]
        mlp_back_segment(
            hooks,
            r.grad,
            r.onehot,
            r.onehot_t,
            r.ada.at[layer],
            (
                weights(r.wu[layer], width),
                weights(r.wd[layer], ff),
                r.h2.at[layer],
                r.g.at[layer],
                r.slope.at[layer],
                r.result.at[layer],
                r.mids.at[layer],
            ),
            (weights(r.dwu[layer], width), weights(r.dwd[layer], ff)),
            r.dmid,
            r.items[2 * layer + 1],
            (r.wup, r.wdown, r.hall, r.gall, r.du, r.dwup, r.dwdown, r.load_a, r.load_b),
            (r.gamma, r.scale),
            (r.dgamma, r.dscale, r.dshift),
            r.moves.at[2 * layer],
            exchange_set(r, 0),
        )

        def begin_attend():
            items[layer, 1].start()

        def sent_attend():
            if not top:
                narrows[above].own()

        def second_attend():
            wides[layer].step(1)
            if not top:
                narrow_done(above)

        def late_attend():
            wides[layer].step(2)
            items[layer, 1].sum()
            if not top:
                items[above, 1].forward()
                items[above, 0].spread()

        def done_attend():
            if not top:
                narrows[layer].acquire(r.credit.at[1])
            narrows[layer].start()

        attend_back_segment(
            Hooks(
                start=begin_attend,
                sent=sent_attend,
                a=partial(wides[layer].step, 0),
                b=second_attend,
                d=late_attend,
                dw=done_attend,
            ),
            size,
            r.dmid,
            r.onehot,
            r.onehot_t,
            r.ada.at[layer],
            r.qscale.at[layer],
            r.keyc,
            r.keyr,
            r.inverse.at[layer],
            (
                weights(r.wq[layer], width),
                weights(r.wp[layer], TILE),
                r.h.at[layer],
                r.qkv.at[layer],
                r.rates.at[layer],
                r.o.at[layer],
                r.branch.at[layer],
                r.states.at[layer - 1] if layer else None,
            ),
            (weights(r.dwq[layer], width), weights(r.dwp[layer], TILE)),
            r.grad,
            r.items[2 * layer],
            r.heads.at[layer],
            (
                r.wup.at[:, 0:wide],
                r.wdown.at[0:TILE],
                r.hall,
                r.gall.at[:, 0:wide],
                r.rates_buf,
                r.gall.at[:, wide : wide + TILE],
                r.dwdown.at[TILE : 2 * TILE],
                r.dkeys,
                r.dvalues,
                r.du.at[:, 0:wide],
                r.dwup.at[:, 0:wide],
                r.dwdown.at[0:TILE],
                r.load_a,
                r.load_b if layer else r.tokens,
            ),
            (r.gamma, r.scale),
            (r.dgamma, r.dscale, r.dshift),
            r.moves.at[2 * layer + 1],
            exchange_set(r, 1),
        )
    items[0, 0].start()
    r.tokens_grad[...] = r.grad[...].astype(bf16)
    wides[0].own()
    items[0, 0].sum()

    def fold(layer, part, total):
        dada = r.dadas[2 * layer + part]
        if layer or part:
            load = pltpu.make_async_copy(dada, r.dada, r.dada_sem)
            load.start()
            load.wait()
            dada = r.dada
        quarter = dada.shape[3]
        for c in range(0, 3 * width, TILE):
            at = (c // width) * 2 * width + part * width + c % width
            inner = c % quarter
            value = dada[c // quarter, :, :, inner : inner + TILE].reshape(people, TILE)
            r.ada_grad[layer, :, at : at + TILE] = mm(r.cond[...], value)
            total = total + mm_t(r.w_ada[layer, :, at : at + TILE], value)
        return total

    items[1, 1].finish()
    total = fold(1, 1, jnp.zeros((rows, people), f32))
    items[1, 0].forward()
    items[0, 1].spread()
    narrows[0].step(0)
    items[1, 0].finish()
    total = fold(1, 0, total)
    items[0, 1].forward()
    items[0, 0].spread()
    narrows[0].step(1)
    items[0, 1].finish()
    total = fold(0, 1, total)
    items[0, 0].forward()
    narrows[0].step(2)
    items[0, 0].finish()
    total = fold(0, 0, total)
    message = r.message
    message[0:rows, :] = total
    message[rows:, :] = r.notes[...]
    lane = lax.broadcasted_iota(jnp.int32, (TILE, people), 0)
    pick = (lane == lax.broadcasted_iota(jnp.int32, (TILE, people), 1) * size).astype(bf16)
    for layer in range(layers):
        message[rows + layer : rows + layer + 1, :] = split_three(r.heads[layer], pick)
    told = [
        remote(message, r.heard.at[b, d], r.told_send.at[k], r.told_recv.at[k], ((d + k) % dps, b))
        for k in range(1, dps)
    ]
    told.append(pltpu.make_async_copy(message, r.heard.at[b, d], r.told_send.at[0]))
    for one in told:
        one.start()
    narrows[0].own()
    wide_done(0)
    for one in told:
        one.wait()
    share = Share(r.heard, r.share_send, r.share_recv)
    share.start()
    share.forward()
    narrow_done(0)
    share.finish()
    for one in list(swaps.values()) + list(permutes.values()):
        one.finish()


def split_three(values, ones):
    high = values.astype(bf16)
    rest = values - high.astype(f32)
    low = rest.astype(bf16)
    least = (rest - low.astype(f32)).astype(bf16)
    return mm(high, ones) + (mm(low, ones) + mm(least, ones))


def backward(size, keep, extra):
    dps, blks = sizes()
    layers = keep.h.shape[0]
    rows, width = extra.cotangent.shape
    length = rows * blks
    wide, ff = keep.qkv.shape[2], keep.slope.shape[2]
    wrows = extra.w_ada.shape[1]
    slots, people = extra.onehot_t.shape[0], extra.cond.shape[1]
    sems = pltpu.SemaphoreType.DMA
    low = partial(shaped, dtype=bf16)
    n = Names()
    for name, one in vars(extra).items():
        vars(n.ins)[name] = (one, VMEM)
    for name in vars(keep):
        vars(n.ins)[name] = [(one, ANY) for one in flat(vars(keep)[name])]
        if not isinstance(vars(keep)[name], list):
            vars(n.ins)[name] = vars(n.ins)[name][0]
    pairs = dps // 2

    def scatter_scratch(shapes):
        found = []
        for shape in shapes:
            found += [pltpu.VMEM((pairs, *shape), bf16)] * 3
            found += [sems((2 * pairs,)), sems((2 * pairs,)), sems((pairs,))]
        return found

    quarter = 3 * width // 4
    whole = (4, dps, slots, quarter)
    sets = 2 * layers
    n.outs.dwu = [(low(dps, blks * wrows, ff), ANY)] * layers
    n.outs.dwd = [(low(dps, ff // dps, width), ANY)] * layers
    n.outs.dwq = [(low(dps, blks * wrows, wide), ANY)] * layers
    n.outs.dwp = [(low(dps, TILE // dps, width), ANY)] * layers
    n.outs.far_dadas = [(low(*whole), ANY)] * (sets - 1)
    n.scratch.near_dada = pltpu.VMEM(whole, bf16)
    n.scratch.dada = pltpu.VMEM(whole, bf16)
    n.scratch.dada_sem = sems
    n.scratch.up_sum = [pltpu.VMEM((blks, wrows, ff), bf16)] * layers
    n.scratch.qkv_sum = [pltpu.VMEM((blks, wrows, wide), bf16)] * layers
    n.scratch.proj_sum = [pltpu.VMEM((TILE // dps, width), f32)] * layers
    n.scratch.items = [pltpu.VMEM((slots, 3 * width), f32)] * sets
    n.scratch.items_scratch = [
        [
            pltpu.VMEM((4, slots, quarter), f32),
            pltpu.VMEM((1, slots, quarter), bf16),
            sems((8,)),
            sems((7,)),
            sems((dps,)),
            sems((dps,)),
        ]
    ] * sets
    n.scratch.wide = scatter_scratch([(blks * wrows, ff), (ff // dps, width)])
    n.scratch.narrow = scatter_scratch([(blks * wrows, wide), (TILE // dps, width)])
    vars(n.outs).update(
        tokens_grad=(low(rows, width), VMEM),
        ada_grad=(shaped(layers, wrows, 6 * width), VMEM),
        up_grad=(low(layers, blks, wrows, ff), ANY),
        qkv_grad=(low(layers, blks, wrows, wide), ANY),
        proj_grad=(shaped(layers, TILE // dps, width), ANY),
        down_grad=(shaped(layers, ff // dps, width), VMEM),
        heard=(shaped(blks, dps, wrows + 8, people), ANY),
    )
    big, small = pltpu.VMEM((rows, width), f32), pltpu.VMEM((rows, width), bf16)
    vars(n.scratch).update(
        grad=big,
        dmid=big,
        load_a=big,
        load_b=big,
        gamma=big,
        scale=big,
        dgamma=small,
        dscale=small,
        dshift=small,
        wup=pltpu.VMEM((width, ff), bf16),
        wdown=pltpu.VMEM((ff, width), bf16),
        hall=pltpu.VMEM((length, width), bf16),
        gall=pltpu.VMEM((length, ff), bf16),
        du=pltpu.VMEM((length, ff), bf16),
        dwup=pltpu.VMEM((width, ff), bf16),
        dwdown=pltpu.VMEM((ff, width), bf16),
        rates_buf=pltpu.VMEM((length, 2 * TILE), f32),
        dkeys=pltpu.VMEM((length, TILE), f32),
        dvalues=pltpu.VMEM((length, TILE), f32),
        heads=pltpu.VMEM((layers, 1, TILE), f32),
        message=pltpu.VMEM((wrows + 8, people), f32),
        moves=sems((2 * layers, 10)),
        credit=pltpu.SemaphoreType.REGULAR((2,)),
        permute_send=sems((layers,)),
        permute_recv=sems((layers,)),
        told_send=sems((dps,)),
        told_recv=sems((dps,)),
        share_send=sems((3,)),
        share_recv=sems((3,)),
    )
    n.scratch.swap_send = sems((2 * layers, 1, 4))
    n.scratch.swap_recv = sems((2 * layers, 1, 4))
    add_exchanges(n, width)
    return n.call(partial(backward_kernel, layers, size), 9, 60)


ANY = pl.BlockSpec(memory_space=pl.ANY)
VMEM = pl.BlockSpec(memory_space=pltpu.VMEM)


def shaped(*shape, dtype=f32):
    return jax.ShapeDtypeStruct(shape, dtype)


def per_device(
    tokens,
    cotangent,
    stop_scale,
    labels,
    class_table,
    head_scale,
    w_qkv,
    w_proj,
    w_up,
    w_down,
    w_ada,
):
    rows, width = tokens.shape[1:]
    layers, heads = head_scale.shape
    size = width // heads
    dps, blks = sizes()
    count = dps * blks
    length = rows * blks
    d, b = place()
    own_heads = heads // blks
    piece = own_heads * size
    wrows = w_qkv.shape[1]
    ffrows = w_down.shape[1]
    ff = ffrows * dps
    slots = labels.shape[1]
    padded = 16

    item_all, level_all = token_meta(stop_scale[0], length)
    item_own = lax.dynamic_slice_in_dim(item_all, b * rows, rows)
    key = (item_all * 16 + level_all).reshape(blks, rows)
    sib = b + 1 - 2 * (b % 2)
    far, far_sib = (b + 2) % 4, (sib + 2) % 4
    key = jnp.concatenate(
        [key[b], key[sib], key[far, :HALF], key[far_sib, :HALF], key[far, HALF:], key[far_sib, HALF:]]
    )
    keyc, keyr = key[:, None], key.reshape(4, 1, TILE)
    slot_id = jnp.arange(padded, dtype=jnp.int32)
    onehot_t = (slot_id[:, None] == item_own[None, :]).astype(bf16)
    onehot = (item_own[:, None] == jnp.concatenate([slot_id, slot_id])[None, :]).astype(bf16)

    names = jnp.pad(labels[0], (0, padded - slots), constant_values=-1)

    def one_hot(names):
        return (names[:, None] == jnp.arange(class_table.shape[0], dtype=jnp.int32)[None, :]).astype(bf16)

    wide = w_ada.shape[2]
    columns = layers * wide // count
    ada_cols = w_ada.transpose(1, 0, 2).reshape(wrows, count, columns).transpose(1, 0, 2)
    qkv_cols = w_qkv.reshape(layers, wrows, 3, blks, piece).transpose(0, 3, 1, 2, 4)
    qkv_cols = qkv_cols.reshape(layers, blks, wrows, 3 * piece)
    up_cols = w_up.reshape(layers, wrows, dps, blks, ffrows).transpose(0, 3, 1, 2, 4)
    up_cols = up_cols.reshape(layers, blks, wrows, ff)
    class_rows = mm(one_hot(names), class_table).astype(bf16)
    own_scale = lax.dynamic_slice_in_dim(head_scale, b * own_heads, own_heads, axis=1)
    qscales = jnp.repeat(jnp.exp(own_scale), size, axis=1)
    common = (size, tokens[0], onehot, keyc, keyr, qscales[:, None, :], w_down)
    qkv_list, up_list = [qkv_cols[i] for i in range(layers)], [up_cols[i] for i in range(layers)]
    if columns % 128 == 0 and wrows % 16 == 0:
        kept = forward(*common, w_proj, qkv_list, up_list, class_rows, ada_cols, None, None, None)
        ada = kept.ada
        class_rows = kept.rows.reshape(dps * padded, width)
        cond_all = jax.nn.silu(class_rows.astype(f32)).astype(bf16)
    else:
        to_heads = [(i, (i % dps) * blks + i // dps) for i in range(count)]
        proj_own = lax.ppermute(w_proj, ("dp", "blk"), to_heads)
        class_rows = gather(class_rows, "dp")
        cond_all = jax.nn.silu(class_rows.astype(f32)).astype(bf16)
        ada_cols = lax.all_to_all(ada_cols, ("dp", "blk"), 0, 0, tiled=True)
        ada_part = mm(cond_all, ada_cols.reshape(count * wrows, columns))
        ada_part = lax.all_to_all(ada_part.reshape(dps, padded, columns), "dp", 0, 0, tiled=True)
        ada_all = lax.all_gather(ada_part, "blk", axis=1, tiled=False)
        ada_all = ada_all.transpose(2, 0, 1, 3).reshape(padded, layers, wide).transpose(1, 0, 2)
        ada_high = ada_all.astype(bf16)
        ada_low = (ada_all - ada_high.astype(f32)).astype(bf16)
        ada = jnp.concatenate([ada_high, ada_low], axis=1)
        qkv_shard = lax.all_to_all(qkv_cols[0], "blk", 0, 0, tiled=True)
        up_shard = lax.all_to_all(up_cols[0], "blk", 0, 0, tiled=True)
        kept = forward(*common, proj_own, qkv_list, up_list, None, None, ada, qkv_shard, up_shard)
    output = kept.output[None]
    lanes = dps * padded
    notes = jnp.pad(names.astype(f32)[None, :], ((layers, 7 - layers), (0, lanes - padded)))
    cond_own = lax.dynamic_slice_in_dim(cond_all, (d * blks + b) * wrows, wrows, axis=1).T
    keep = SimpleNamespace(
        h=kept.h,
        qkv=kept.qkv,
        rates=kept.rates,
        o=kept.o,
        branch=kept.branch,
        mids=kept.mids,
        h2=kept.h2,
        g=kept.g,
        slope=kept.slope,
        result=kept.result,
        states=kept.states,
        wq=kept.wq,
        wp=kept.wp,
        wu=kept.wu,
        wd=kept.wd,
    )
    extra = SimpleNamespace(
        tokens=tokens[0],
        cotangent=cotangent[0],
        onehot=onehot,
        onehot_t=onehot_t,
        keyc=keyc,
        keyr=keyr,
        qscale=qscales[:, None, :],
        ada=ada,
        inverse=kept.inverse,
        cond=cond_own,
        w_ada=w_ada,
        notes=notes,
    )
    grads = backward(size, keep, extra)
    one = grads.qkv_grad.reshape(layers, blks, wrows, 3, piece)
    qkv_grad = one.transpose(0, 2, 3, 1, 4).reshape(layers, wrows, 3 * width).astype(f32)
    one = grads.up_grad.reshape(layers, blks, wrows, dps, ffrows)
    up_grad = one.transpose(0, 2, 3, 1, 4).reshape(layers, wrows, ff * blks).astype(f32)
    told = grads.heard
    head_grad = jnp.sum(told[:, :, wrows : wrows + layers, :own_heads], axis=1)
    head_grad = head_grad.transpose(1, 0, 2).reshape(layers, heads)
    every_name = told[0, :, wrows + layers, :padded].reshape(-1).astype(jnp.int32)
    cond_grad = told[:, :, :wrows, :].transpose(1, 0, 2, 3).reshape(width, lanes).T
    _, silu_pull = jax.vjp(jax.nn.silu, class_rows.astype(f32))
    cond_pre = silu_pull(cond_grad)[0]
    pre_high = cond_pre.astype(bf16)
    pre_low = (cond_pre - pre_high.astype(f32)).astype(bf16)
    chosen = one_hot(jnp.concatenate([every_name, every_name]))
    table_grad = rows_mm(chosen, jnp.concatenate([pre_high, pre_low]))
    return (
        output,
        grads.tokens_grad[None],
        table_grad,
        head_grad,
        qkv_grad,
        grads.proj_grad,
        up_grad,
        grads.down_grad,
        grads.ada_grad,
    )


def solution(mesh):
    in_specs = (
        P("dp", "blk", None),
        P("dp", "blk", None),
        P("dp", None),
        P("dp", None),
        P(),
        P(),
        P(None, ("dp", "blk"), None),
        P(None, ("dp", "blk"), None),
        P(None, ("dp", "blk"), None),
        P(None, ("dp", "blk"), None),
        P(None, ("dp", "blk"), None),
    )
    out_specs = (
        P("dp", "blk", None),
        P("dp", "blk", None),
        P(),
        P(),
        P(None, ("dp", "blk"), None),
        P(None, ("dp", "blk"), None),
        P(None, ("dp", "blk"), None),
        P(None, ("dp", "blk"), None),
        P(None, ("dp", "blk"), None),
    )
    return jax.shard_map(
        per_device, mesh=mesh, in_specs=in_specs, out_specs=out_specs, check_vma=False
    )
```

time: 1060 us -> 554 us (0.52)
  waiting for transfers between devices: 401 us -> 0 us
  blocking collectives: 228 us -> 0 us
  Pallas kernels: 289 us -> 512 us
  starting transfers between devices: 38.3 us -> 0 us
  other arithmetic: 25.4 us -> 7.87 us
  local copies, waits for them, and re-layouts: 38.5 us -> 21.2 us
  between operations: 15.2 us -> 1.17 us
    reduce_scatter x6 -> x0, waiting for transfers between devices: 283 us -> none  [scatter(): return lax.psum_scatter(values, axes, scatter_dimension=0, tiled=True)]
    pallas_call x8 -> x2, Pallas kernels: 289 us -> 512 us  [call(): pl.pallas_call(lambda *refs: kernel(fill((self.ins, self.outs, self.scrat...]
    all_gather x5 -> x0, blocking collectives: 156 us -> none  [the longest x4 135 us: gather(): return lax.all_gather(values, axes, axis=0, tiled=True)]
    all_gather x8 -> x0, waiting for transfers between devices: 115 us -> none  [gather(): return lax.all_gather(values, axes, axis=0, tiled=True)]
    psum x1 -> x0, blocking collectives: 40.1 us -> none  [per_device(): head_grad = lax.psum(jnp.stack(scale_grads), ('dp', 'blk'))]
    all_to_all x4 -> x0, starting transfers between devices: 24 us -> none  [the longest x2 12.5 us: per_device(): lax.all_to_all(back.reshape(blks, wrows, 3 * piece + ff), 'blk', 0, 0, ti...]
    unnamed x1 -> x0, blocking collectives: 16.8 us -> none
    all_to_all x1 -> x0, blocking collectives: 14.7 us -> none  [per_device(): moved = lax.all_to_all(moved, 'blk', 0, 0, tiled=True)]
  transfers between devices with their start and end apart: 21 -> 0, of which waited for: 9 -> 0; matrix products, arithmetic and copies ran while one was open for 6% -> 0% of each run, Pallas kernels for 17% -> 0%
where the time goes in v5:
time: 554 us; the launch traced here: 546 us
  Pallas kernels  512 us (92%)
  local copies, waits for them, and re-layouts  21.2 us (4%)
  other arithmetic  7.87 us (1%)
    pallas_call x2, Pallas kernels, call(): pl.pallas_call(lambda *refs: kernel(fill((self.ins, self.outs, self.scrat...  512 us

profile of v5, /device:TPU:7, one launch (start us, length us, event | category | flops | bytes accessed | tf_op | source)
XLA Modules:
  0.0 545.7 jit_solution(13644947515750462560)
XLA Ops:
  0.6 0.0 copy-start
  0.7 0.0 copy-start.9
  0.7 1.0 select_reduce_fusion.1
  1.7 0.2 reduce-window.8
  1.9 0.8 fusion.13
  2.7 0.1 pad_add_fusion.1
  2.8 0.7 convert_bitcast_fusion
  3.4 0.1 broadcast_in_dim.64
  3.5 0.7 broadcast_in_dim_reshape.4.refs_4_.refs_6_
  4.2 0.6 pad.9.refs_11_
  4.8 0.1 select_reduce_fusion
  4.9 0.7 convert_reduce_fusion.1
  5.6 0.1 dynamic_slice.27
  5.8 0.0 copy-start.12
  5.8 0.6 fusion.11.refs_3_
  6.4 0.0 copy-done
  6.4 1.0 convolution_convert_fusion.refs_6_
  7.5 0.7 compare_convert_fusion.refs_1_.refs_2_
  8.2 0.0 copy-done.9
  8.2 0.3 reshape.115
  8.5 0.2 copy.83
  8.7 0.2 fusion.21
  8.9 0.9 squeeze.49.refs_10_
  9.8 0.9 squeeze.48.refs_9_
  10.7 0.0 copy-done.12
  10.7 1.0 copy.68.refs_2_.refs_4_
  11.7 0.0 copy-done.6
  11.7 0.4 reshape.116
  12.1 0.1 copy.82
  12.2 0.8 squeeze.51.refs_12_
  13.0 0.8 squeeze.50.refs_11_
  13.8 0.0 copy-done.4
  13.9 0.8 copy.64
  14.7 0.5 reshape.114
  15.2 1.1 copy.81
  16.3 254.2 %shard_map.196 = (bf16[2,32,6144]{2,1,0:T(8,128)(2,1)}, bf16[8,16,1024]{2,1,0:T(8,128)(2,1)}, bf16[2,32,1024]{2,1,0:T(8,128)(2,1)}, bf16[4,32,768]{2,1,0:T(8,128...) custom-call(bf16[256,1024]{1,0:T(8,128)(2,1)} %bitcast.96, ...), custom_call_target="tpu_custom_call" | custom-call | flops 68719476736 | bytes 67108864 | tf_op jit(solution)/shard_map/pallas_call | solution.py:1043
  270.5 1.0 bitcast_convert_fusion
  271.5 0.2 copy.70
  271.7 0.1 add_divide_fusion
  271.9 0.6 fusion.12.refs_9_
  272.5 257.4 %shard_map.197 = (bf16[8,128,1024]{2,1,0:T(8,128)(2,1)}, bf16[8,128,1024]{2,1,0:T(8,128)(2,1)}, bf16[8,128,1024]{2,1,0:T(8,128)(2,1)}, bf16[8,128,1024]{2,1,0:T(...) custom-call(bf16[256,1024]{1,0:T(8,128)(2,1)} %bitcast.97, ...), custom_call_target="tpu_custom_call" | custom-call | flops 68719476736 | bytes 67108864 | tf_op jit(solution)/shard_map/pallas_call | solution.py:1043
  529.9 0.0 copy-start.10
  529.9 1.0 slice_reduce_fusion
  530.8 0.6 reshape.118
  531.5 0.8 convert_reduce_fusion.2
  532.3 1.1 slice_bitcast_fusion
  533.4 0.1 convert_element_type.81
  533.5 0.2 fusion.19
  533.8 0.0 copy-done.10
  533.8 0.4 reshape.122
  534.2 0.5 copy.75
  534.7 1.3 reshape.120
  536.0 0.1 copy.77
  536.1 0.7 copy.76
  536.8 1.4 reshape.121
  538.2 2.8 fusion.3
  541.0 0.0 copy-done.7
  541.1 0.8 copy.95
  541.8 0.8 copy.96
  542.6 0.0 copy-done.11
  542.6 0.7 copy.97
  543.4 1.0 copy.98
  544.3 1.1 copy.99
  545.5 0.0 copy-done.1
  (29 shorter events, 0.2 us)
Async XLA Ops:
  0.6 5.8 %copy-start = (bf16[1001,1024]{1,0:T(8,128)(2,1)S(1)}, bf16[1001,1024]{1,0:T(8,128)(2,1)}, u32[]{:S(2)}) copy-start(bf16[1001,1024]{1,0:T(8,128)(2,1)} %param.17) | copy-start | bytes 6150148
  0.7 7.5 %copy-start.9 = (bf16[2,32,3072]{2,1,0:T(8,128)(2,1)S(1)}, bf16[2,32,3072]{2,1,0:T(8,128)(2,1)}, u32[]{:S(2)}) copy-start(bf16[2,32,3072]{2,1,0:T(8,128)(2,1)} %param.19) | copy-start | bytes 1179652
  5.8 4.9 copy-start.12
  8.2 3.5 copy-start.6
  11.7 2.1 copy-start.4
  529.9 3.9 copy-start.10
  533.8 2.2 copy-start.5
  538.2 2.8 copy-start.7
  538.2 3.6 copy-start.8
  538.2 5.1 copy-start.3
  541.0 1.6 copy-start.11
  541.0 3.3 copy-start.2
  543.3 2.1 copy-start.1

commit v6 on v5

--- a/solution.py
+++ b/solution.py
@@ -490,7 +490,7 @@
 
 
 def mlp_back_segment(
-    hooks, dx, onehot, onehot_t, ada, ins, outs, dmid, items, held, mods, terms, moves, refs
+    hooks, begun, dx, onehot, onehot_t, ada, ins, outs, dmid, items, held, mods, terms, moves, refs
 ):
     wup_in, wdown_in, h_in, g_in, slope_in, result_in, mid_in = ins
     wup, wdown, hall, gall, slope, dwup, dwdown, result, mid_state = held
@@ -502,9 +502,11 @@
     load_up = mover.copy(wup_in, wup)
     later = [mover.copy(g_in, gall), mover.copy(h_in, hall)]
     later += [mover.copy(result_in, result), mover.copy(mid_in, mid_state)]
-    expand(onehot, ada, (1, 3), (gamma, scale))
+    if not begun:
+        expand(onehot, ada, (1, 3), (gamma, scale))
     hooks.start()
-    scaled_rows(dx, gamma, hbuf, spread)
+    if not begun:
+        scaled_rows(dx, gamma, hbuf, spread)
     hooks.sent()
     for one in (load_down, load_slope, load_up):
         one.wait()
@@ -1064,7 +1066,20 @@
     return r.spreads[turn] + [r.parts, r.out] + r.collects[turn]
 
 
-def forward_kernel(lead, layers, size, r):
+def whole_kernel(lead, layers, size, r):
+    wide = 3 * TILE
+    r.wqkv, r.wproj = r.wup.at[:, 0:wide], r.wdown.at[0:TILE]
+    r.qkv_buf, r.o_buf = r.gall.at[:, 0:wide], r.gall.at[:, wide : wide + TILE]
+    r.vt, r.rate_buf = r.dwdown.at[TILE : 2 * TILE], r.rates_buf
+    r.hidden, r.slope_buf = r.dwup, r.du
+    r.state, r.middle, r.branch_buf, r.result_buf = r.grad, r.dmid, r.load_a, r.load_b
+    if lead:
+        r.columns = r.hall.at[:, 0 : r.ada_in.shape[2]]
+    forward_part(lead, layers, size, r)
+    backward_part(layers, size, r)
+
+
+def forward_part(lead, layers, size, r):
     dps, blks = sizes()
     d, b = place()
     sibling, peer = partners()
@@ -1079,11 +1094,9 @@
             job = DpGather()
             job.bind(srcs, [one[layer] for one in dsts], r.gather_sems[2 * layer + part])
             gathers.append(job)
-    if lead:
-        arrived = greet_all()
-    else:
-        arrived = greet([sibling, peer, (d, 3 - b)] + gathers[0].partners)
+    arrived = greet_all()
     r.state[...] = r.tokens[...].astype(f32)
+    r.message[...] = jnp.zeros_like(r.message)
     arrived()
     swaps = [
         PieceSwap(
@@ -1109,15 +1122,15 @@
             r.columns,
             (r.dp_send, r.dp_recv, r.ada_send, r.ada_recv, r.ada_local),
         )
+        swaps[0].finish()
+        permutes[0].finish()
+        gathers[0].start_far()
+        gathers[0].start_near()
         for one in moves:
             one.wait()
         replies = modulations_answer(
             r.rows, r.columns, r.answers, r.quarters, (r.answer_send, r.answer_recv)
         )
-        swaps[0].finish()
-        permutes[0].finish()
-        gathers[0].start_far()
-        gathers[0].start_near()
         for one in permutes[1:]:
             one.start()
         share = Share(r.quarters, r.share_send, r.share_recv)
@@ -1179,6 +1192,11 @@
 
     def weights(ref, rows):
         return ref.reshape(rows, ref.shape[-1])
+
+    def begin_back():
+        hbuf, _, spread, _ = exchange(exchange_set(r, 0))
+        r.grad[...] = r.cotangent[...].astype(f32)
+        scaled_rows(r.grad, r.gamma, hbuf, spread)
 
     pending = []
     saver = Moves(r.save_sems)
@@ -1218,7 +1236,9 @@
             saver.copy(r.middle, r.mids.at[layer]),
         ]
         hooks = Hooks(need=partial(need_second, layer))
-        if not last:
+        if last:
+            hooks.c = begin_back
+        else:
             hooks.a, hooks.b, hooks.c = [partial(gathers[2 * layer + 2].step, i) for i in range(3)]
         mlp_segment(
             hooks,
@@ -1229,7 +1249,7 @@
             (r.wup, r.wdown),
             (r.h2.at[layer], r.g.at[layer], r.slope.at[layer]),
             r.result_buf,
-            r.state,
+            r.shift if last else r.state,
             (r.hidden, r.slope_buf),
             (r.gamma, r.scale, r.shift),
             r.moves.at[2 * layer + 1],
@@ -1240,12 +1260,12 @@
         pending = [saver.copy(r.result_buf, r.result.at[layer])]
         if not last:
             pending.append(saver.copy(r.state, r.states.at[layer]))
-    r.output[...] = r.state[...].astype(bf16)
+    r.output[...] = r.shift[...].astype(bf16)
     for one in pending:
         one.wait()
 
 
-def forward(size, tokens, onehot, keyc, keyr, qscale, w_down, proj, qkv_cols, up_cols, rows_in, ada_in, ada, qkv_shard, up_shard):
+def declare_forward(n, tokens, onehot, keyc, keyr, qscale, w_down, proj, qkv_cols, up_cols, rows_in, ada_in, ada, qkv_shard, up_shard):
     lead = ada_in is not None
     dps, blks = sizes()
     count = dps * blks
@@ -1254,7 +1274,6 @@
     length = rows * blks
     wide, ff = qkv_cols[0].shape[2], up_cols[0].shape[2]
     sems = pltpu.SemaphoreType.DMA
-    n = Names()
     vars(n.ins).update(
         tokens=(tokens, VMEM), onehot=(onehot, VMEM), keyc=(keyc, VMEM), keyr=(keyr, VMEM), qscale=(qscale, VMEM)
     )
@@ -1265,12 +1284,11 @@
         slots = rows_in.shape[0]
         columns = ada_in.shape[2]
         vars(n.outs).update(
-            ada=(low(layers, 2 * slots, count * columns // layers), VMEM),
             rows=(low(dps, slots, width), VMEM),
             proj_shard=(low(*proj.shape), ANY),
         )
         vars(n.scratch).update(
-            columns=pltpu.VMEM((width, columns), bf16),
+            ada=pltpu.VMEM((layers, 2 * slots, count * columns // layers), bf16),
             answers=pltpu.VMEM((dps, slots, columns), f32),
             quarters=pltpu.VMEM((blks, dps, slots, columns), f32),
             dp_send=sems((dps,)),
@@ -1287,7 +1305,7 @@
         )
     else:
         vars(n.ins).update(
-            ada=(ada, VMEM), proj_shard=(proj, ANY), qkv_first=(qkv_shard, ANY), up_first=(up_shard, ANY)
+            ada=(ada, VMEM), rows=(rows_in, VMEM), proj_shard=(proj, ANY), qkv_first=(qkv_shard, ANY), up_first=(up_shard, ANY)
         )
     moved_qkv, moved_up = (one if lead else one[1:] for one in (qkv_cols, up_cols))
     n.ins.qkv_cols = [(one, ANY) for one in moved_qkv]
@@ -1303,7 +1321,6 @@
     n.scratch.gather_sems = [[sems((2, dps)), sems((2, dps)), sems((2,))] for _ in range(2 * layers)]
     vars(n.outs).update(
         output=(low(rows, width), VMEM),
-        inverse=(shaped(layers, 4, 8, TILE), VMEM),
         h=(low(layers, length, width), ANY),
         qkv=(low(layers, length, wide), ANY),
         rates=(shaped(layers, length, 2 * TILE), ANY),
@@ -1316,40 +1333,29 @@
         result=(shaped(layers, rows, width), ANY),
         states=(shaped(layers, rows, width), ANY),
     )
-    big = pltpu.VMEM((rows, width), f32)
     vars(n.scratch).update(
-        state=big, middle=big, branch_buf=big, result_buf=big, gamma=big, scale=big, shift=big
-    )
-    vars(n.scratch).update(
-        wqkv=pltpu.VMEM((width, wide), bf16),
-        wproj=pltpu.VMEM((TILE, width), bf16),
-        wup=pltpu.VMEM((width, ff), bf16),
-        wdown=pltpu.VMEM((ff, width), bf16),
-        qkv_buf=pltpu.VMEM((length, wide), bf16),
-        vt=pltpu.VMEM((TILE, length), bf16),
-        rate_buf=pltpu.VMEM((length, 2 * TILE), f32),
-        o_buf=pltpu.VMEM((length, TILE), bf16),
-        hidden=pltpu.VMEM((length, ff), bf16),
-        slope_buf=pltpu.VMEM((length, ff), bf16),
+        shift=pltpu.VMEM((rows, width), f32),
+        inverse=pltpu.VMEM((layers, 4, 8, TILE), f32),
         moves=sems((2 * layers, 5)),
         save_sems=sems((5 * layers,)),
     )
-    add_exchanges(n, width)
-    return n.call(partial(forward_kernel, lead, layers, size), 8, 56)
-
-
-def backward_kernel(layers, size, r):
+    return n
+
+
+def backward_part(layers, size, r):
     dps, blks = sizes()
     d, b = place()
-    arrived = greet_all()
     width = r.grad.shape[1]
     rows = r.w_ada.shape[1]
     people = r.cond.shape[1]
-    r.grad[...] = r.cotangent[...].astype(f32)
-    arrived()
+    value = r.rows[...].astype(f32)
+    value = (value / (1.0 + jnp.exp(-value))).astype(bf16).reshape(people, width)
+    line = lax.broadcasted_iota(jnp.int32, (rows, width), 0) + flat_place() * rows
+    own_columns = (line == lax.broadcasted_iota(jnp.int32, (rows, width), 1)).astype(bf16)
+    r.cond[...] = mm_t(own_columns, value).astype(bf16)
 
     wides, narrows, swaps, permutes, items = {}, {}, {}, {}, {}
-    r.dadas = [r.near_dada] + r.far_dadas
+    r.dadas = r.near_dada + r.far_dadas
     for n in range(layers):
         wides[n], narrows[n] = DpScatter(), DpScatter()
         shared = r.wide
@@ -1358,14 +1364,31 @@
         narrows[n].bind([r.dwq[n], r.dwp[n]], [r.qkv_sum[n], r.proj_sum[n]], shared)
         for k, (src, dst) in enumerate(((r.up_sum, r.up_grad), (r.qkv_sum, r.qkv_grad))):
             swaps[k, n] = PieceSwap(
-                [(src[n], dst.at[n])], r.swap_send.at[2 * n + k], r.swap_recv.at[2 * n + k]
+                [(src[n], dst.at[n])], r.back_swap_send.at[2 * n + k], r.back_swap_recv.at[2 * n + k]
             )
         permutes[n] = Permute(
-            r.proj_sum[n], r.proj_grad.at[n], r.permute_send.at[n], r.permute_recv.at[n], True
+            r.proj_sum[n], r.proj_grad.at[n], r.back_permute_send.at[n], r.back_permute_recv.at[n], True
         )
         for part in range(2):
             at = 2 * n + part
             items[n, part] = Items(r.items[at], r.dadas[at], r.items_scratch[at])
+
+    def fold(layer, part):
+        dada = r.dadas[2 * layer + part]
+        if layer or part or not r.near_dada:
+            load = pltpu.make_async_copy(dada, r.dada, r.dada_sem)
+            load.start()
+            load.wait()
+            dada = r.dada
+        quarter = dada.shape[3]
+        total = r.message[0:rows, :]
+        for c in range(0, 3 * width, TILE):
+            at = (c // width) * 2 * width + part * width + c % width
+            inner = c % quarter
+            value = dada[c // quarter, :, :, inner : inner + TILE].reshape(people, TILE)
+            r.ada_grad[layer, :, at : at + TILE] = mm(r.cond[...], value)
+            total = total + mm_t(r.w_ada[layer, :, at : at + TILE], value)
+        r.message[0:rows, :] = total
 
     def wide_done(n):
         wides[n].finish()
@@ -1412,6 +1435,7 @@
         ff = r.slope.shape[2]
         mlp_back_segment(
             hooks,
+            top,
             r.grad,
             r.onehot,
             r.onehot_t,
@@ -1431,7 +1455,7 @@
             (r.wup, r.wdown, r.hall, r.gall, r.du, r.dwup, r.dwdown, r.load_a, r.load_b),
             (r.gamma, r.scale),
             (r.dgamma, r.dscale, r.dshift),
-            r.moves.at[2 * layer],
+            r.back_moves.at[2 * layer],
             exchange_set(r, 0),
         )
 
@@ -1458,6 +1482,9 @@
             if not top:
                 narrows[layer].acquire(r.credit.at[1])
             narrows[layer].start()
+            if not top:
+                items[above, 1].finish()
+                fold(above, 1)
 
         attend_back_segment(
             Hooks(
@@ -1509,48 +1536,29 @@
             ),
             (r.gamma, r.scale),
             (r.dgamma, r.dscale, r.dshift),
-            r.moves.at[2 * layer + 1],
+            r.back_moves.at[2 * layer + 1],
             exchange_set(r, 1),
         )
     items[0, 0].start()
     r.tokens_grad[...] = r.grad[...].astype(bf16)
+    items[1, 0].forward()
+    items[0, 0].sum()
     wides[0].own()
-    items[0, 0].sum()
-
-    def fold(layer, part, total):
-        dada = r.dadas[2 * layer + part]
-        if layer or part:
-            load = pltpu.make_async_copy(dada, r.dada, r.dada_sem)
-            load.start()
-            load.wait()
-            dada = r.dada
-        quarter = dada.shape[3]
-        for c in range(0, 3 * width, TILE):
-            at = (c // width) * 2 * width + part * width + c % width
-            inner = c % quarter
-            value = dada[c // quarter, :, :, inner : inner + TILE].reshape(people, TILE)
-            r.ada_grad[layer, :, at : at + TILE] = mm(r.cond[...], value)
-            total = total + mm_t(r.w_ada[layer, :, at : at + TILE], value)
-        return total
-
-    items[1, 1].finish()
-    total = fold(1, 1, jnp.zeros((rows, people), f32))
-    items[1, 0].forward()
+    items[1, 0].finish()
+    narrows[0].step(0)
+    fold(1, 0)
     items[0, 1].spread()
-    narrows[0].step(0)
-    items[1, 0].finish()
-    total = fold(1, 0, total)
+    narrows[0].step(1)
     items[0, 1].forward()
+    narrows[0].step(2)
+    items[0, 1].finish()
+    fold(0, 1)
     items[0, 0].spread()
-    narrows[0].step(1)
-    items[0, 1].finish()
-    total = fold(0, 1, total)
     items[0, 0].forward()
-    narrows[0].step(2)
+    narrows[0].own()
     items[0, 0].finish()
-    total = fold(0, 0, total)
+    fold(0, 0)
     message = r.message
-    message[0:rows, :] = total
     message[rows:, :] = r.notes[...]
     lane = lax.broadcasted_iota(jnp.int32, (TILE, people), 0)
     pick = (lane == lax.broadcasted_iota(jnp.int32, (TILE, people), 1) * size).astype(bf16)
@@ -1563,11 +1571,10 @@
     told.append(pltpu.make_async_copy(message, r.heard.at[b, d], r.told_send.at[0]))
     for one in told:
         one.start()
-    narrows[0].own()
     wide_done(0)
     for one in told:
         one.wait()
-    share = Share(r.heard, r.share_send, r.share_recv)
+    share = Share(r.heard, r.back_share_send, r.back_share_recv)
     share.start()
     share.forward()
     narrow_done(0)
@@ -1584,23 +1591,17 @@
     return mm(high, ones) + (mm(low, ones) + mm(least, ones))
 
 
-def backward(size, keep, extra):
+def declare_backward(n, layers, cotangent, w_ada, onehot_t, notes, wide, ff):
     dps, blks = sizes()
-    layers = keep.h.shape[0]
-    rows, width = extra.cotangent.shape
+    rows, width = cotangent.shape
     length = rows * blks
-    wide, ff = keep.qkv.shape[2], keep.slope.shape[2]
-    wrows = extra.w_ada.shape[1]
-    slots, people = extra.onehot_t.shape[0], extra.cond.shape[1]
+    wrows = w_ada.shape[1]
+    slots, people = onehot_t.shape[0], notes.shape[1]
     sems = pltpu.SemaphoreType.DMA
     low = partial(shaped, dtype=bf16)
-    n = Names()
-    for name, one in vars(extra).items():
-        vars(n.ins)[name] = (one, VMEM)
-    for name in vars(keep):
-        vars(n.ins)[name] = [(one, ANY) for one in flat(vars(keep)[name])]
-        if not isinstance(vars(keep)[name], list):
-            vars(n.ins)[name] = vars(n.ins)[name][0]
+    vars(n.ins).update(
+        cotangent=(cotangent, VMEM), w_ada=(w_ada, VMEM), onehot_t=(onehot_t, VMEM), notes=(notes, VMEM)
+    )
     pairs = dps // 2
 
     def scatter_scratch(shapes):
@@ -1617,8 +1618,9 @@
     n.outs.dwd = [(low(dps, ff // dps, width), ANY)] * layers
     n.outs.dwq = [(low(dps, blks * wrows, wide), ANY)] * layers
     n.outs.dwp = [(low(dps, TILE // dps, width), ANY)] * layers
-    n.outs.far_dadas = [(low(*whole), ANY)] * (sets - 1)
-    n.scratch.near_dada = pltpu.VMEM(whole, bf16)
+    near = [pltpu.VMEM(whole, bf16)] if people <= 128 else []
+    n.outs.far_dadas = [(low(*whole), ANY)] * (sets - len(near))
+    n.scratch.near_dada = near
     n.scratch.dada = pltpu.VMEM(whole, bf16)
     n.scratch.dada_sem = sems
     n.scratch.up_sum = [pltpu.VMEM((blks, wrows, ff), bf16)] * layers
@@ -1669,19 +1671,19 @@
         dvalues=pltpu.VMEM((length, TILE), f32),
         heads=pltpu.VMEM((layers, 1, TILE), f32),
         message=pltpu.VMEM((wrows + 8, people), f32),
-        moves=sems((2 * layers, 10)),
+        cond=pltpu.VMEM((wrows, people), bf16),
+        back_moves=sems((2 * layers, 10)),
         credit=pltpu.SemaphoreType.REGULAR((2,)),
-        permute_send=sems((layers,)),
-        permute_recv=sems((layers,)),
+        back_permute_send=sems((layers,)),
+        back_permute_recv=sems((layers,)),
         told_send=sems((dps,)),
         told_recv=sems((dps,)),
-        share_send=sems((3,)),
-        share_recv=sems((3,)),
+        back_share_send=sems((3,)),
+        back_share_recv=sems((3,)),
     )
-    n.scratch.swap_send = sems((2 * layers, 1, 4))
-    n.scratch.swap_recv = sems((2 * layers, 1, 4))
+    n.scratch.back_swap_send = sems((2 * layers, 1, 4))
+    n.scratch.back_swap_recv = sems((2 * layers, 1, 4))
     add_exchanges(n, width)
-    return n.call(partial(backward_kernel, layers, size), 9, 60)
 
 
 ANY = pl.BlockSpec(memory_space=pl.ANY)
@@ -1748,13 +1750,12 @@
     class_rows = mm(one_hot(names), class_table).astype(bf16)
     own_scale = lax.dynamic_slice_in_dim(head_scale, b * own_heads, own_heads, axis=1)
     qscales = jnp.repeat(jnp.exp(own_scale), size, axis=1)
-    common = (size, tokens[0], onehot, keyc, keyr, qscales[:, None, :], w_down)
+    common = (tokens[0], onehot, keyc, keyr, qscales[:, None, :], w_down)
     qkv_list, up_list = [qkv_cols[i] for i in range(layers)], [up_cols[i] for i in range(layers)]
-    if columns % 128 == 0 and wrows % 16 == 0:
-        kept = forward(*common, w_proj, qkv_list, up_list, class_rows, ada_cols, None, None, None)
-        ada = kept.ada
-        class_rows = kept.rows.reshape(dps * padded, width)
-        cond_all = jax.nn.silu(class_rows.astype(f32)).astype(bf16)
+    n = Names()
+    lead = columns % 128 == 0 and wrows % 16 == 0
+    if lead:
+        declare_forward(n, *common, w_proj, qkv_list, up_list, class_rows, ada_cols, None, None, None)
     else:
         to_heads = [(i, (i % dps) * blks + i // dps) for i in range(count)]
         proj_own = lax.ppermute(w_proj, ("dp", "blk"), to_heads)
@@ -1770,43 +1771,15 @@
         ada = jnp.concatenate([ada_high, ada_low], axis=1)
         qkv_shard = lax.all_to_all(qkv_cols[0], "blk", 0, 0, tiled=True)
         up_shard = lax.all_to_all(up_cols[0], "blk", 0, 0, tiled=True)
-        kept = forward(*common, proj_own, qkv_list, up_list, None, None, ada, qkv_shard, up_shard)
-    output = kept.output[None]
+        rows_all = class_rows.reshape(dps, padded, width)
+        declare_forward(n, *common, proj_own, qkv_list, up_list, rows_all, None, ada, qkv_shard, up_shard)
     lanes = dps * padded
     notes = jnp.pad(names.astype(f32)[None, :], ((layers, 7 - layers), (0, lanes - padded)))
-    cond_own = lax.dynamic_slice_in_dim(cond_all, (d * blks + b) * wrows, wrows, axis=1).T
-    keep = SimpleNamespace(
-        h=kept.h,
-        qkv=kept.qkv,
-        rates=kept.rates,
-        o=kept.o,
-        branch=kept.branch,
-        mids=kept.mids,
-        h2=kept.h2,
-        g=kept.g,
-        slope=kept.slope,
-        result=kept.result,
-        states=kept.states,
-        wq=kept.wq,
-        wp=kept.wp,
-        wu=kept.wu,
-        wd=kept.wd,
-    )
-    extra = SimpleNamespace(
-        tokens=tokens[0],
-        cotangent=cotangent[0],
-        onehot=onehot,
-        onehot_t=onehot_t,
-        keyc=keyc,
-        keyr=keyr,
-        qscale=qscales[:, None, :],
-        ada=ada,
-        inverse=kept.inverse,
-        cond=cond_own,
-        w_ada=w_ada,
-        notes=notes,
-    )
-    grads = backward(size, keep, extra)
+    declare_backward(n, layers, cotangent[0], w_ada, onehot_t, notes, 3 * piece, ff)
+    grads = n.call(partial(whole_kernel, lead, layers, size), 8, 60)
+    output = grads.output[None]
+    if lead:
+        class_rows = grads.rows.reshape(dps * padded, width)
     one = grads.qkv_grad.reshape(layers, blks, wrows, 3, piece)
     qkv_grad = one.transpose(0, 2, 3, 1, 4).reshape(layers, wrows, 3 * width).astype(f32)
     one = grads.up_grad.reshape(layers, blks, wrows, dps, ffrows)

time: 554 us -> 539 us (0.973)
  Pallas kernels: 512 us -> 498 us
    pallas_call x2 -> x1, Pallas kernels: 512 us -> 498 us  [call(): pl.pallas_call(lambda *refs: kernel(fill((self.ins, self.outs, self.scrat...]
where the time goes in v6:
time: 539 us; the launch traced here: 531 us
  Pallas kernels  498 us (92%)
  local copies, waits for them, and re-layouts  21.6 us (4%)
  other arithmetic  6.17 us (1%)
    pallas_call x1, Pallas kernels, call(): pl.pallas_call(lambda *refs: kernel(fill((self.ins, self.outs, self.scrat...  498 us

profile of v6, /device:TPU:7, one launch (start us, length us, event | category | flops | bytes accessed | tf_op | source)
XLA Modules:
  0.0 530.7 jit_solution(10250159049632724006)
XLA Ops:
  0.6 0.0 copy-start
  0.7 0.0 copy-start.9
  0.7 1.0 select_reduce_fusion.1
  1.7 0.2 reduce-window.8
  1.9 0.8 fusion.11
  2.7 0.1 pad_add_fusion.1
  2.8 0.7 convert_bitcast_fusion
  3.4 0.1 broadcast_in_dim.64
  3.5 0.7 broadcast_in_dim_reshape.3.refs_4_
  4.1 0.6 pad.9.refs_16_
  4.7 0.1 select_reduce_fusion
  4.9 0.7 convert_reduce_fusion.1
  5.6 0.1 dynamic_slice.24
  5.8 0.0 copy-start.13
  5.8 0.6 fusion.10.refs_15_
  6.4 0.0 copy-done
  6.4 1.0 convolution_convert_fusion.refs_6_
  7.5 0.7 compare_convert_fusion.refs_1_
  8.2 0.0 copy-done.9
  8.2 0.3 reshape.115
  8.5 0.2 copy.85
  8.7 0.2 fusion.19
  8.9 0.9 squeeze.48.refs_10_
  9.8 0.9 squeeze.47.refs_9_
  10.7 0.0 copy-done.13
  10.7 1.0 copy.72.refs_2_
  11.7 0.0 copy-done.6
  11.7 0.4 reshape.116
  12.1 0.1 copy.84
  12.2 0.8 squeeze.50.refs_12_
  13.0 0.8 squeeze.49.refs_11_
  13.8 0.0 copy-done.4
  13.8 0.8 copy.68
  14.7 0.5 reshape.114
  15.2 1.1 copy.83
  16.3 498.0 %shard_map.196 = (bf16[8,16,1024]{2,1,0:T(8,128)(2,1)}, bf16[2,32,1024]{2,1,0:T(8,128)(2,1)}, bf16[4,32,768]{2,1,0:T(8,128)(2,1)}, bf16[4,32,768]{2,1,0:T(8,128)...) custom-call(bf16[256,1024]{1,0:T(8,128)(2,1)} %bitcast.93, ...), custom_call_target="tpu_custom_call" | custom-call | flops 68719476736 | bytes 67108864 | tf_op jit(solution)/shard_map/pallas_call | solution.py:1045
  514.3 0.0 copy-start.11
  514.3 1.0 slice_reduce_fusion
  515.3 0.6 reshape.118
  515.9 0.8 convert_reduce_fusion.2
  516.7 1.1 slice_bitcast_fusion
  517.8 0.1 convert_element_type.74
  517.9 0.0 copy-done.11
  517.9 0.1 bitcast_convert_fusion
  518.0 0.2 copy.74
  518.2 0.2 fusion.17
  518.4 0.4 copy-done.10
  518.9 0.4 reshape.122
  519.3 0.5 copy.77
  519.8 1.3 reshape.120
  521.1 0.0 copy-done.5
  521.1 0.1 copy.79
  521.2 0.7 copy.78
  521.9 1.4 reshape.121
  523.3 2.8 fusion.3
  526.1 0.0 copy-done.8
  526.1 0.8 copy.97
  526.9 0.0 copy-done.7
  526.9 0.8 copy.98
  527.7 0.0 copy-done.12
  527.7 0.7 copy.99
  528.4 0.0 copy-done.3
  528.4 1.0 copy.100
  529.4 1.1 copy.101
  (28 shorter events, 0.2 us)
Async XLA Ops:
  0.6 5.8 %copy-start = (bf16[1001,1024]{1,0:T(8,128)(2,1)S(1)}, bf16[1001,1024]{1,0:T(8,128)(2,1)}, u32[]{:S(2)}) copy-start(bf16[1001,1024]{1,0:T(8,128)(2,1)} %param.17) | copy-start | bytes 6150148
  0.7 7.5 %copy-start.9 = (bf16[2,32,3072]{2,1,0:T(8,128)(2,1)S(1)}, bf16[2,32,3072]{2,1,0:T(8,128)(2,1)}, u32[]{:S(2)}) copy-start(bf16[2,32,3072]{2,1,0:T(8,128)(2,1)} %param.19) | copy-start | bytes 1179652
  5.8 4.9 copy-start.13
  8.2 3.5 copy-start.6
  11.7 2.1 copy-start.4
  514.3 3.6 copy-start.11
  517.8 1.0 copy-start.10
  518.8 2.2 copy-start.5
  523.3 2.8 copy-start.8
  523.3 3.6 copy-start.7
  526.1 1.6 copy-start.12
  526.1 2.3 copy-start.3
  526.9 2.5 copy-start.2
  528.4 2.1 copy-start.1

commit v7 on v6

--- a/solution.py
+++ b/solution.py
@@ -123,6 +123,15 @@
                 self.to_peer[c].wait_recv()
                 self.forward[c].start()
                 self.forward[c].wait_recv()
+
+    def ready(self):
+        for c in range(2):
+            self.to_sibling[c].wait_recv()
+        for c in range(2):
+            self.to_peer[c].wait_recv()
+            self.forward[c].start()
+        for c in range(2):
+            self.forward[c].wait_recv()
 
     def finish(self):
         for c in range(2):
@@ -187,11 +196,18 @@
         total = self.parts[span, :].astype(f32) + self.own[span, :].astype(f32)
         return total + self.far[span, :].astype(f32)
 
-    def finish(self):
+    def sent(self):
         self.home.wait_send()
         for c in range(2):
             self.cross[c].wait_send()
+
+    def over_sent(self):
+        for c in range(2):
             self.over[c].wait_send()
+
+    def finish(self):
+        self.sent()
+        self.over_sent()
 
 
 def spread_scratch(width):
@@ -400,6 +416,21 @@
         one.wait()
 
 
+def mlp_block(h, span, wup, wdown, hidden, slope, parts):
+    for n in range(0, wup.shape[1], TILE):
+        columns = slice(n, n + TILE)
+        up = mm(h, wup[:, columns])
+        square = up * up
+        bent = jnp.tanh(0.7978845608 * (up * (1.0 + 0.044715 * square)))
+        half = 0.5 * (1.0 + bent)
+        hidden[span, columns] = (up * half).astype(bf16)
+        inner = 0.7978845608 + (3.0 * 0.044715 * 0.7978845608) * square
+        slope[span, columns] = (half + 0.5 * up * (1.0 - bent * bent) * inner).astype(bf16)
+    g = hidden[span, :]
+    for n in range(0, parts.shape[1], TILE):
+        parts[span, n : n + TILE] = mm(g, wdown[:, n : n + TILE]).astype(bf16)
+
+
 def mlp_segment(
     hooks, x, onehot, ada, weights_in, weights, saves_out, result_out, x_out, held, mods, moves, refs
 ):
@@ -426,18 +457,7 @@
 
         span = pl.ds(pl.multiple_of(i * TILE, TILE), TILE)
         h = hbuf[span, :]
-        for n in range(0, wup.shape[1], TILE):
-            columns = slice(n, n + TILE)
-            up = mm(h, wup[:, columns])
-            square = up * up
-            bent = jnp.tanh(0.7978845608 * (up * (1.0 + 0.044715 * square)))
-            half = 0.5 * (1.0 + bent)
-            hidden[span, columns] = (up * half).astype(bf16)
-            inner = 0.7978845608 + (3.0 * 0.044715 * 0.7978845608) * square
-            slope[span, columns] = (half + 0.5 * up * (1.0 - bent * bent) * inner).astype(bf16)
-        g = hidden[span, :]
-        for n in range(0, parts.shape[1], TILE):
-            parts[span, n : n + TILE] = mm(g, wdown[:, n : n + TILE]).astype(bf16)
+        mlp_block(h, span, wup, wdown, hidden, slope, parts)
         collect.block_done(i)
 
     hooks.c()
@@ -489,8 +509,103 @@
     row_steps(0, TILE, added)
 
 
+def mlp_back_block(dm, span, wup, wdown, slope, parts):
+    for n in range(0, slope.shape[1], TILE):
+        columns = slice(n, n + TILE)
+        dg = mm_t(dm, wdown[columns, :])
+        slope[span, columns] = (dg * slope[span, columns].astype(f32)).astype(bf16)
+    du = slope[span, :]
+    for n in range(0, parts.shape[1], TILE):
+        parts[span, n : n + TILE] = mm_t(du, wup[n : n + TILE, :]).astype(bf16)
+
+
+def mlp_weight_grads(mover, hall, gall, dm, du, dwup, dwdown, outs):
+    @pl.loop(0, gall.shape[1] // TILE)
+    def _(k):
+        columns = pl.ds(pl.multiple_of(k * TILE, TILE), TILE)
+        for n in range(0, dm.shape[1], 2 * TILE):
+            dwdown[columns, n : n + 2 * TILE] = rows_mm(
+                gall[:, columns], dm[:, n : n + 2 * TILE]
+            ).astype(bf16)
+
+    save_down = mover.copy(dwdown, outs[1])
+
+    @pl.loop(0, hall.shape[1] // TILE)
+    def _(k):
+        columns = pl.ds(pl.multiple_of(k * TILE, TILE), TILE)
+        for n in range(0, du.shape[1], 2 * TILE):
+            dwup[columns, n : n + 2 * TILE] = rows_mm(
+                hall[:, columns], du[:, n : n + 2 * TILE]
+            ).astype(bf16)
+
+    save_up = mover.copy(dwup, outs[0])
+    save_down.wait()
+    save_up.wait()
+
+
+def mlp_top_segment(
+    hooks, x, dx, onehot, onehot_t, ada, cotangent, weights_in, weights, outs, result, x_out, items, held, mods, terms, moves, refs, back_refs, free
+):
+    hidden, du, dwup, dwdown = held
+    gamma, scale, shift = mods
+    wup, wdown = weights
+    dgamma, _, dshift = terms
+    refs = refs[:4] + [dgamma] + refs[5:]
+    hbuf, parts, spread, collect = exchange(refs)
+    back_hbuf, _, back_spread, back_collect = exchange(back_refs)
+    mover = Moves(moves)
+    expand(onehot, ada, (1, 3, 5), (gamma, scale, shift))
+    modulate_rows(x, scale, shift, hbuf, spread)
+    dx[...] = cotangent[...].astype(f32)
+    spread.ready()
+    scaled_rows(dx, gamma, back_hbuf, back_spread)
+    hooks.need()
+    loads = [mover.copy(a, b) for a, b in zip(weights_in, weights)]
+    for one in loads:
+        one.wait()
+
+    @pl.loop(0, 4)
+    def _(i):
+        span = pl.ds(pl.multiple_of(i * TILE, TILE), TILE)
+        mlp_block(hbuf[span, :], span, wup, wdown, hidden, du, parts)
+        collect.block_done(i)
+
+    collect.sent()
+    dshift[...] = parts[0:TILE, :]
+
+    @pl.loop(0, 4)
+    def _(i):
+        back_spread.wait_block(i)
+        span = pl.ds(pl.multiple_of(i * TILE, TILE), TILE)
+        mlp_back_block(back_hbuf[span, :], span, wup, wdown, du, parts)
+        back_collect.block_done(i)
+
+    mlp_weight_grads(mover, hbuf, hidden, back_hbuf, du, dwup, dwdown, outs)
+    spread.finish()
+    for other in partners():
+        pl.semaphore_signal(free, inc=1, device_id=other, device_id_type=MESH)
+    hooks.dw()
+    collect.wait()
+    collect.over_sent()
+
+    def added(at):
+        span = pl.ds(at, STEP)
+        total = dshift[span, :].astype(f32) + collect.own[span, :].astype(f32)
+        total = total + collect.far[span, :].astype(f32)
+        result[span, :] = total
+        x_out[span, :] = x[span, :] + gamma[span, :] * total
+
+    row_steps(0, TILE, added)
+    back_collect.wait()
+    back_rows(back_collect, x, dx, result, scale, terms, x)
+    item_sums(onehot_t, terms, items)
+    back_spread.finish()
+    back_collect.finish()
+    pl.semaphore_wait(free, 2)
+
+
 def mlp_back_segment(
-    hooks, begun, dx, onehot, onehot_t, ada, ins, outs, dmid, items, held, mods, terms, moves, refs
+    hooks, dx, onehot, onehot_t, ada, ins, outs, dmid, items, held, mods, terms, moves, refs
 ):
     wup_in, wdown_in, h_in, g_in, slope_in, result_in, mid_in = ins
     wup, wdown, hall, gall, slope, dwup, dwdown, result, mid_state = held
@@ -502,11 +617,9 @@
     load_up = mover.copy(wup_in, wup)
     later = [mover.copy(g_in, gall), mover.copy(h_in, hall)]
     later += [mover.copy(result_in, result), mover.copy(mid_in, mid_state)]
-    if not begun:
-        expand(onehot, ada, (1, 3), (gamma, scale))
+    expand(onehot, ada, (1, 3), (gamma, scale))
     hooks.start()
-    if not begun:
-        scaled_rows(dx, gamma, hbuf, spread)
+    scaled_rows(dx, gamma, hbuf, spread)
     hooks.sent()
     for one in (load_down, load_slope, load_up):
         one.wait()
@@ -522,40 +635,14 @@
 
         span = pl.ds(pl.multiple_of(i * TILE, TILE), TILE)
         dm = hbuf[span, :]
-        for n in range(0, slope.shape[1], TILE):
-            columns = slice(n, n + TILE)
-            dg = mm_t(dm, wdown[columns, :])
-            slope[span, columns] = (dg * slope[span, columns].astype(f32)).astype(bf16)
-        du = slope[span, :]
-        for n in range(0, parts.shape[1], TILE):
-            parts[span, n : n + TILE] = mm_t(du, wup[n : n + TILE, :]).astype(bf16)
+        mlp_back_block(dm, span, wup, wdown, slope, parts)
         collect.block_done(i)
 
     hooks.c()
     for one in later:
         one.wait()
 
-    @pl.loop(0, gall.shape[1] // TILE)
-    def _(k):
-        columns = pl.ds(pl.multiple_of(k * TILE, TILE), TILE)
-        for n in range(0, hbuf.shape[1], 2 * TILE):
-            dwdown[columns, n : n + 2 * TILE] = rows_mm(
-                gall[:, columns], hbuf[:, n : n + 2 * TILE]
-            ).astype(bf16)
-
-    save_down = mover.copy(dwdown, outs[1])
-
-    @pl.loop(0, hall.shape[1] // TILE)
-    def _(k):
-        columns = pl.ds(pl.multiple_of(k * TILE, TILE), TILE)
-        for n in range(0, slope.shape[1], 2 * TILE):
-            dwup[columns, n : n + 2 * TILE] = rows_mm(
-                hall[:, columns], slope[:, n : n + 2 * TILE]
-            ).astype(bf16)
-
-    save_up = mover.copy(dwup, outs[0])
-    save_down.wait()
-    save_up.wait()
+    mlp_weight_grads(mover, hall, gall, hbuf, slope, dwup, dwdown, outs)
     hooks.dw()
     collect.wait()
     back_rows(collect, mid_state, dx, result, scale, terms, dmid)
@@ -1075,8 +1162,8 @@
     r.state, r.middle, r.branch_buf, r.result_buf = r.grad, r.dmid, r.load_a, r.load_b
     if lead:
         r.columns = r.hall.at[:, 0 : r.ada_in.shape[2]]
-    forward_part(lead, layers, size, r)
-    backward_part(layers, size, r)
+    need_top, pending = forward_part(lead, layers, size, r)
+    backward_part(layers, size, r, need_top, pending)
 
 
 def forward_part(lead, layers, size, r):
@@ -1162,8 +1249,8 @@
         if layer == 0:
             job.step(1)
             job.step(2)
+        job.finish()
         following.start_near()
-        job.finish()
 
     def early(layer):
         if layer == 0:
@@ -1172,8 +1259,6 @@
             if lead:
                 for one in permutes[1:]:
                     one.finish()
-            for one in gathers[2:]:
-                one.start_far()
         else:
             gathers[2 * layer + 1].step(0)
 
@@ -1186,17 +1271,14 @@
     def need_second(layer):
         if layer == 0:
             gathers[1].step(2)
+            for one in gathers[2:]:
+                one.start_far()
         if layer + 1 < layers:
             gathers[2 * layer + 2].start_near()
         gathers[2 * layer + 1].finish()
 
     def weights(ref, rows):
         return ref.reshape(rows, ref.shape[-1])
-
-    def begin_back():
-        hbuf, _, spread, _ = exchange(exchange_set(r, 0))
-        r.grad[...] = r.cotangent[...].astype(f32)
-        scaled_rows(r.grad, r.gamma, hbuf, spread)
 
     pending = []
     saver = Moves(r.save_sems)
@@ -1235,11 +1317,10 @@
             saver.copy(r.branch_buf, r.branch.at[layer]),
             saver.copy(r.middle, r.mids.at[layer]),
         ]
+        if last:
+            return partial(need_second, layer), pending
         hooks = Hooks(need=partial(need_second, layer))
-        if last:
-            hooks.c = begin_back
-        else:
-            hooks.a, hooks.b, hooks.c = [partial(gathers[2 * layer + 2].step, i) for i in range(3)]
+        hooks.a, hooks.b, hooks.c = [partial(gathers[2 * layer + 2].step, i) for i in range(3)]
         mlp_segment(
             hooks,
             r.middle,
@@ -1249,7 +1330,7 @@
             (r.wup, r.wdown),
             (r.h2.at[layer], r.g.at[layer], r.slope.at[layer]),
             r.result_buf,
-            r.shift if last else r.state,
+            r.state,
             (r.hidden, r.slope_buf),
             (r.gamma, r.scale, r.shift),
             r.moves.at[2 * layer + 1],
@@ -1257,12 +1338,7 @@
         )
         for one in pending:
             one.wait()
-        pending = [saver.copy(r.result_buf, r.result.at[layer])]
-        if not last:
-            pending.append(saver.copy(r.state, r.states.at[layer]))
-    r.output[...] = r.shift[...].astype(bf16)
-    for one in pending:
-        one.wait()
+        pending = [saver.copy(r.result_buf, r.result.at[layer]), saver.copy(r.state, r.states.at[layer])]
 
 
 def declare_forward(n, tokens, onehot, keyc, keyr, qscale, w_down, proj, qkv_cols, up_cols, rows_in, ada_in, ada, qkv_shard, up_shard):
@@ -1342,7 +1418,7 @@
     return n
 
 
-def backward_part(layers, size, r):
+def backward_part(layers, size, r, need_top, pending):
     dps, blks = sizes()
     d, b = place()
     width = r.grad.shape[1]
@@ -1419,7 +1495,6 @@
         def late_mlp():
             if not top:
                 narrows[above].step(2)
-                items[above, 1].spread()
                 items[above, 0].sum()
 
         def done_mlp():
@@ -1433,31 +1508,62 @@
             hooks.sent = wides[above].own
             hooks.a, hooks.b = [partial(narrows[above].step, i) for i in range(2)]
         ff = r.slope.shape[2]
-        mlp_back_segment(
-            hooks,
-            top,
-            r.grad,
-            r.onehot,
-            r.onehot_t,
-            r.ada.at[layer],
-            (
-                weights(r.wu[layer], width),
-                weights(r.wd[layer], ff),
-                r.h2.at[layer],
-                r.g.at[layer],
-                r.slope.at[layer],
-                r.result.at[layer],
-                r.mids.at[layer],
-            ),
-            (weights(r.dwu[layer], width), weights(r.dwd[layer], ff)),
-            r.dmid,
-            r.items[2 * layer + 1],
-            (r.wup, r.wdown, r.hall, r.gall, r.du, r.dwup, r.dwdown, r.load_a, r.load_b),
-            (r.gamma, r.scale),
-            (r.dgamma, r.dscale, r.dshift),
-            r.back_moves.at[2 * layer],
-            exchange_set(r, 0),
-        )
+        if top:
+
+            def need():
+                need_top()
+                for one in pending:
+                    one.wait()
+
+            hooks.need = need
+            mlp_top_segment(
+                hooks,
+                r.dmid,
+                r.grad,
+                r.onehot,
+                r.onehot_t,
+                r.ada.at[layer],
+                r.cotangent,
+                (weights(r.wu[layer], width), weights(r.wd[layer], ff)),
+                (r.wup, r.wdown),
+                (weights(r.dwu[layer], width), weights(r.dwd[layer], ff)),
+                r.load_b,
+                r.shift,
+                r.items[2 * layer + 1],
+                (r.hidden, r.du, r.dwup, r.dwdown),
+                (r.gamma, r.scale, r.shift),
+                (r.dgamma, r.dscale, r.dshift),
+                r.back_moves.at[2 * layer],
+                exchange_set(r, 1),
+                exchange_set(r, 0),
+                r.credit.at[2],
+            )
+            r.output[...] = r.shift[...].astype(bf16)
+        else:
+            mlp_back_segment(
+                hooks,
+                r.grad,
+                r.onehot,
+                r.onehot_t,
+                r.ada.at[layer],
+                (
+                    weights(r.wu[layer], width),
+                    weights(r.wd[layer], ff),
+                    r.h2.at[layer],
+                    r.g.at[layer],
+                    r.slope.at[layer],
+                    r.result.at[layer],
+                    r.mids.at[layer],
+                ),
+                (weights(r.dwu[layer], width), weights(r.dwd[layer], ff)),
+                r.dmid,
+                r.items[2 * layer + 1],
+                (r.wup, r.wdown, r.hall, r.gall, r.du, r.dwup, r.dwdown, r.load_a, r.load_b),
+                (r.gamma, r.scale),
+                (r.dgamma, r.dscale, r.dshift),
+                r.back_moves.at[2 * layer],
+                exchange_set(r, 0),
+            )
 
         def begin_attend():
             items[layer, 1].start()
@@ -1465,6 +1571,7 @@
         def sent_attend():
             if not top:
                 narrows[above].own()
+                items[above, 1].spread()
 
         def second_attend():
             wides[layer].step(1)
@@ -1476,7 +1583,6 @@
             items[layer, 1].sum()
             if not top:
                 items[above, 1].forward()
-                items[above, 0].spread()
 
         def done_attend():
             if not top:
@@ -1485,6 +1591,7 @@
             if not top:
                 items[above, 1].finish()
                 fold(above, 1)
+                items[above, 0].spread()
 
         attend_back_segment(
             Hooks(
@@ -1543,19 +1650,18 @@
     r.tokens_grad[...] = r.grad[...].astype(bf16)
     items[1, 0].forward()
     items[0, 0].sum()
+    items[0, 1].spread()
     wides[0].own()
+    narrows[0].step(0)
     items[1, 0].finish()
-    narrows[0].step(0)
     fold(1, 0)
-    items[0, 1].spread()
+    items[0, 1].forward()
+    items[0, 0].spread()
     narrows[0].step(1)
-    items[0, 1].forward()
-    narrows[0].step(2)
     items[0, 1].finish()
     fold(0, 1)
-    items[0, 0].spread()
     items[0, 0].forward()
-    narrows[0].own()
+    narrows[0].step(2)
     items[0, 0].finish()
     fold(0, 0)
     message = r.message
@@ -1571,6 +1677,7 @@
     told.append(pltpu.make_async_copy(message, r.heard.at[b, d], r.told_send.at[0]))
     for one in told:
         one.start()
+    narrows[0].own()
     wide_done(0)
     for one in told:
         one.wait()
@@ -1673,7 +1780,7 @@
         message=pltpu.VMEM((wrows + 8, people), f32),
         cond=pltpu.VMEM((wrows, people), bf16),
         back_moves=sems((2 * layers, 10)),
-        credit=pltpu.SemaphoreType.REGULAR((2,)),
+        credit=pltpu.SemaphoreType.REGULAR((3,)),
         back_permute_send=sems((layers,)),
         back_permute_recv=sems((layers,)),
         told_send=sems((dps,)),

time: 539 us -> 503 us (0.933)
  Pallas kernels: 498 us -> 464 us
    pallas_call x1, Pallas kernels: 498 us -> 464 us  [call(): pl.pallas_call(lambda *refs: kernel(fill((self.ins, self.outs, self.scrat...]
where the time goes in v7:
time: 503 us; the launch traced here: 496 us
  Pallas kernels  464 us (92%)
  local copies, waits for them, and re-layouts  21.6 us (4%)
  other arithmetic  6.17 us (1%)
    pallas_call x1, Pallas kernels, call(): pl.pallas_call(lambda *refs: kernel(fill((self.ins, self.outs, self.scrat...  464 us

profile of v7, /device:TPU:7, one launch (start us, length us, event | category | flops | bytes accessed | tf_op | source)
XLA Modules:
  0.0 496.3 jit_solution(2962436121945389257)
XLA Ops:
  0.6 0.0 copy-start
  0.7 0.0 copy-start.9
  0.7 1.0 select_reduce_fusion.1
  1.7 0.2 reduce-window.8
  1.9 0.8 fusion.11
  2.7 0.1 pad_add_fusion.1
  2.8 0.7 convert_bitcast_fusion
  3.4 0.1 broadcast_in_dim.64
  3.5 0.7 broadcast_in_dim_reshape.3.refs_4_
  4.1 0.6 pad.9.refs_16_
  4.7 0.1 select_reduce_fusion
  4.9 0.7 convert_reduce_fusion.1
  5.6 0.1 dynamic_slice.24
  5.8 0.0 copy-start.13
  5.8 0.6 fusion.10.refs_15_
  6.4 0.0 copy-done
  6.4 1.0 convolution_convert_fusion.refs_6_
  7.5 0.7 compare_convert_fusion.refs_1_
  8.2 0.0 copy-done.9
  8.2 0.3 reshape.115
  8.5 0.2 copy.85
  8.7 0.2 fusion.19
  8.9 0.9 squeeze.48.refs_10_
  9.8 0.9 squeeze.47.refs_9_
  10.7 0.0 copy-done.13
  10.7 1.0 copy.72.refs_2_
  11.7 0.0 copy-done.6
  11.7 0.4 reshape.116
  12.1 0.1 copy.84
  12.2 0.8 squeeze.50.refs_12_
  13.0 0.8 squeeze.49.refs_11_
  13.8 0.0 copy-done.4
  13.8 0.8 copy.68
  14.7 0.5 reshape.114
  15.2 1.1 copy.83
  16.3 463.5 %shard_map.196 = (bf16[8,16,1024]{2,1,0:T(8,128)(2,1)}, bf16[2,32,1024]{2,1,0:T(8,128)(2,1)}, bf16[4,32,768]{2,1,0:T(8,128)(2,1)}, bf16[4,32,768]{2,1,0:T(8,128)...) custom-call(bf16[256,1024]{1,0:T(8,128)(2,1)} %bitcast.93, ...), custom_call_target="tpu_custom_call" | custom-call | flops 68719476736 | bytes 67108864 | tf_op jit(solution)/shard_map/pallas_call | solution.py:1132
  479.8 0.0 copy-start.11
  479.9 1.0 slice_reduce_fusion
  480.8 0.6 reshape.118
  481.5 0.8 convert_reduce_fusion.2
  482.3 1.1 slice_bitcast_fusion
  483.3 0.1 convert_element_type.74
  483.5 0.0 copy-done.11
  483.5 0.1 bitcast_convert_fusion
  483.6 0.2 copy.74
  483.8 0.2 fusion.17
  484.0 0.4 copy-done.10
  484.4 0.4 reshape.122
  484.8 0.5 copy.77
  485.4 1.3 reshape.120
  486.7 0.0 copy-done.5
  486.7 0.1 copy.79
  486.8 0.7 copy.78
  487.5 1.4 reshape.121
  488.9 2.8 fusion.3
  491.7 0.0 copy-done.8
  491.7 0.8 copy.97
  492.5 0.0 copy-done.7
  492.5 0.8 copy.98
  493.3 0.0 copy-done.12
  493.3 0.7 copy.99
  494.0 0.0 copy-done.3
  494.0 1.0 copy.100
  495.0 1.1 copy.101
  (28 shorter events, 0.2 us)
Async XLA Ops:
  0.6 5.8 %copy-start = (bf16[1001,1024]{1,0:T(8,128)(2,1)S(1)}, bf16[1001,1024]{1,0:T(8,128)(2,1)}, u32[]{:S(2)}) copy-start(bf16[1001,1024]{1,0:T(8,128)(2,1)} %param.17) | copy-start | bytes 6150148
  0.7 7.5 %copy-start.9 = (bf16[2,32,3072]{2,1,0:T(8,128)(2,1)S(1)}, bf16[2,32,3072]{2,1,0:T(8,128)(2,1)}, u32[]{:S(2)}) copy-start(bf16[2,32,3072]{2,1,0:T(8,128)(2,1)} %param.19) | copy-start | bytes 1179652
  5.8 4.9 copy-start.13
  8.2 3.5 copy-start.6
  11.7 2.1 copy-start.4
  479.8 3.6 copy-start.11
  483.4 1.0 copy-start.10
  484.4 2.2 copy-start.5
  488.9 2.8 copy-start.8
  488.9 3.6 copy-start.7
  491.7 1.6 copy-start.12
  491.7 2.3 copy-start.3
  492.5 2.5 copy-start.2
  494.0 2.1 copy-start.1

commit v8 on v7

--- a/solution.py
+++ b/solution.py
@@ -1575,14 +1575,12 @@
 
         def second_attend():
             wides[layer].step(1)
-            if not top:
-                narrow_done(above)
 
         def late_attend():
-            wides[layer].step(2)
             items[layer, 1].sum()
             if not top:
                 items[above, 1].forward()
+                narrow_done(above)
 
         def done_attend():
             if not top:
@@ -1599,6 +1597,7 @@
                 sent=sent_attend,
                 a=partial(wides[layer].step, 0),
                 b=second_attend,
+                c=partial(wides[layer].step, 2),
                 d=late_attend,
                 dw=done_attend,
             ),

time: 503 us -> 499 us (level)
  Pallas kernels: 464 us -> 458 us
    pallas_call x1, Pallas kernels: 464 us -> 458 us  [call(): pl.pallas_call(lambda *refs: kernel(fill((self.ins, self.outs, self.scrat...]
where the time goes in v8:
time: 499 us; the launch traced here: 491 us
  Pallas kernels  458 us (92%)
  local copies, waits for them, and re-layouts  21.6 us (4%)
  other arithmetic  6.17 us (1%)
    pallas_call x1, Pallas kernels, call(): pl.pallas_call(lambda *refs: kernel(fill((self.ins, self.outs, self.scrat...  458 us

profile of v8, /device:TPU:7, one launch (start us, length us, event | category | flops | bytes accessed | tf_op | source)
XLA Modules:
  0.0 490.8 jit_solution(14333775713049178889)
XLA Ops:
  0.6 0.0 copy-start
  0.7 0.0 copy-start.9
  0.7 1.0 select_reduce_fusion.1
  1.7 0.2 reduce-window.8
  1.9 0.8 fusion.11
  2.7 0.1 pad_add_fusion.1
  2.8 0.7 convert_bitcast_fusion
  3.4 0.1 broadcast_in_dim.64
  3.5 0.7 broadcast_in_dim_reshape.3.refs_4_
  4.1 0.6 pad.9.refs_16_
  4.7 0.1 select_reduce_fusion
  4.9 0.7 convert_reduce_fusion.1
  5.6 0.1 dynamic_slice.24
  5.8 0.0 copy-start.13
  5.8 0.6 fusion.10.refs_15_
  6.4 0.0 copy-done
  6.4 1.0 convolution_convert_fusion.refs_6_
  7.5 0.7 compare_convert_fusion.refs_1_
  8.2 0.0 copy-done.9
  8.2 0.3 reshape.115
  8.5 0.2 copy.85
  8.7 0.2 fusion.19
  8.9 0.9 squeeze.48.refs_10_
  9.8 0.9 squeeze.47.refs_9_
  10.7 0.0 copy-done.13
  10.7 1.0 copy.72.refs_2_
  11.7 0.0 copy-done.6
  11.7 0.4 reshape.116
  12.1 0.1 copy.84
  12.2 0.8 squeeze.50.refs_12_
  13.0 0.8 squeeze.49.refs_11_
  13.8 0.0 copy-done.4
  13.8 0.8 copy.68
  14.7 0.5 reshape.114
  15.2 1.1 copy.83
  16.3 458.0 %shard_map.196 = (bf16[8,16,1024]{2,1,0:T(8,128)(2,1)}, bf16[2,32,1024]{2,1,0:T(8,128)(2,1)}, bf16[4,32,768]{2,1,0:T(8,128)(2,1)}, bf16[4,32,768]{2,1,0:T(8,128)...) custom-call(bf16[256,1024]{1,0:T(8,128)(2,1)} %bitcast.93, ...), custom_call_target="tpu_custom_call" | custom-call | flops 68719476736 | bytes 67108864 | tf_op jit(solution)/shard_map/pallas_call | solution.py:1132
  474.4 0.0 copy-start.11
  474.4 1.0 slice_reduce_fusion
  475.3 0.6 reshape.118
  476.0 0.8 convert_reduce_fusion.2
  476.8 1.1 slice_bitcast_fusion
  477.9 0.1 convert_element_type.74
  478.0 0.0 copy-done.11
  478.0 0.1 bitcast_convert_fusion
  478.1 0.2 copy.74
  478.3 0.2 fusion.17
  478.5 0.4 copy-done.10
  478.9 0.4 reshape.122
  479.4 0.5 copy.77
  479.9 1.3 reshape.120
  481.2 0.0 copy-done.5
  481.2 0.1 copy.79
  481.3 0.7 copy.78
  482.0 1.4 reshape.121
  483.4 2.8 fusion.3
  486.2 0.0 copy-done.8
  486.2 0.8 copy.97
  487.0 0.0 copy-done.7
  487.0 0.8 copy.98
  487.8 0.0 copy-done.12
  487.8 0.7 copy.99
  488.5 1.0 copy.100
  489.5 1.1 copy.101
  490.6 0.0 copy-done.1
  (28 shorter events, 0.2 us)
Async XLA Ops:
  0.6 5.8 %copy-start = (bf16[1001,1024]{1,0:T(8,128)(2,1)S(1)}, bf16[1001,1024]{1,0:T(8,128)(2,1)}, u32[]{:S(2)}) copy-start(bf16[1001,1024]{1,0:T(8,128)(2,1)} %param.17) | copy-start | bytes 6150148
  0.7 7.5 %copy-start.9 = (bf16[2,32,3072]{2,1,0:T(8,128)(2,1)S(1)}, bf16[2,32,3072]{2,1,0:T(8,128)(2,1)}, u32[]{:S(2)}) copy-start(bf16[2,32,3072]{2,1,0:T(8,128)(2,1)} %param.19) | copy-start | bytes 1179652
  5.8 4.9 copy-start.13
  8.2 3.5 copy-start.6
  11.7 2.1 copy-start.4
  474.4 3.6 copy-start.11
  477.9 1.0 copy-start.10
  478.9 2.2 copy-start.5
  483.4 2.8 copy-start.8
  483.4 3.6 copy-start.7
  486.2 1.6 copy-start.12
  486.2 2.3 copy-start.3
  487.0 2.5 copy-start.2
  488.5 2.1 copy-start.1
